TPU v7x, 32 devices: a whole 2x2x4 slice. The times are simulated.
32 devices in a mesh: groups: 2 (over x), ctx: 16 (over z, y, core).
Axes of the slice: x: 2, y: 2, z: 4, core: 2. Of those that a mesh axis runs over, the one named last changes fastest.
Arguments:
- queries: bfloat16 [512, 4096], P(('groups', 'ctx')), parts along dimension 0, may hold values from -12 to 12
- new_key: bfloat16 [512, 512], P(('groups', 'ctx')), parts along dimension 0, may hold values from -8 to 8
- new_value: bfloat16 [512, 512], P(('groups', 'ctx')), parts along dimension 0, may hold values from -6 to 6
- key_cache: bfloat16 [32768, 512], P(('groups', 'ctx')), parts along dimension 0, may hold values from -8 to 8
- value_cache: bfloat16 [32768, 512], P(('groups', 'ctx')), parts along dimension 0, may hold values from -6 to 6
- cache_len: int32 [512], P('groups'), parts along dimension 0, may hold values from 1 to 16384
- out_weight: bfloat16 [4096, 2048], P('ctx'), may hold values from -0.09375 to 0.09375
- residual: bfloat16 [512, 2048], P(('groups', 'ctx')), parts along dimension 0, may hold values from -8 to 8
- norm_gain: bfloat16 [2048], replicated, may hold values from 0.099609375 to 1.8984375
- expert_ids: int32 [512, 8], P(('groups', 'ctx')), parts along dimension 0, may hold values from 0 to 31, all different within a row; in each aligned block of 16 rows (0 to 15, 16 to 31, ...) at most 4 rows name the same one
- route_weight: float32 [512, 8], P(('groups', 'ctx')), parts along dimension 0, may hold values from 0.1 to 1
- w_gate: bfloat16 [32, 2048, 768], P('ctx'), may hold values from -0.125 to 0.125
- w_up: bfloat16 [32, 2048, 768], P('ctx'), may hold values from -0.125 to 0.125
- w_down: bfloat16 [32, 768, 2048], P('ctx'), may hold values from -0.21875 to 0.21875
Outputs:
- layer_out: bfloat16 [512, 2048], P(('groups', 'ctx')), parts along dimension 0
There are 2 independent parts, one for each index of `groups`. A program takes and returns all parts, laid end to end along the dimension named above; an argument that names none is the same for every part. Nothing has to cross between parts.
Inputs may be any that keep to these rules, and one draw needn't show every extreme that they name: `expert_ids`: among the rows of one device no expert is named more than 4 times.
All inputs are finite; a program needn't handle non-finite values.
Results may differ from a plain program's by a relative error of at most 0.018.
Values may be sent and summed in bfloat16 or wider, within the bound.
No kernel may reach another device: no remote copies, remote signals or barrier semaphores. Data moves between devices by JAX's collectives and lax.ppermute only.
A program may use at most 192 MiB of HBM per device.

v0:
```python
import math

import jax
import jax.numpy as jnp
from jax import lax
from jax.sharding import PartitionSpec as P

D = 2048
HEADS = 32
KVH = 4
HD = 128
TOP = 8
EXP_DEV = 2
MOST = 4


def expert_block(arrived, w_gate, w_up, w_down, form_in, form_out):
    gate_proj = jnp.einsum(form_in, arrived, w_gate, preferred_element_type=jnp.float32)
    upward = jnp.einsum(form_in, arrived, w_up, preferred_element_type=jnp.float32)
    hidden = (jax.nn.silu(gate_proj) * upward).astype(jnp.bfloat16)
    return jnp.einsum(form_out, hidden, w_down, preferred_element_type=jnp.float32).astype(
        jnp.bfloat16
    )


def on_device(
    queries,
    new_key,
    new_value,
    key_cache,
    value_cache,
    cache_len,
    out_weight,
    residual,
    norm_gain,
    expert_ids,
    route_weight,
    w_gate,
    w_up,
    w_down,
):
    devices = lax.axis_size("ctx")
    my_index = lax.axis_index("ctx")
    local_rows = queries.shape[0]
    all_queries, all_new_keys, all_new_values = (
        lax.all_gather(queries, "ctx", axis=0, tiled=True),
        lax.all_gather(new_key, "ctx", axis=0, tiled=True),
        lax.all_gather(new_value, "ctx", axis=0, tiled=True),
    )
    total_rows = all_queries.shape[0]
    group_size = HEADS // KVH
    heads_here = out_weight.shape[0] // HD
    cache_here = key_cache.shape[0]
    score_scale = 1.0 / math.sqrt(HD)
    query_heads = all_queries.reshape(total_rows, KVH, group_size, HD)
    fresh_keys = all_new_keys.reshape(total_rows, KVH, HD)
    fresh_values = all_new_values.reshape(total_rows, KVH, HD)
    fresh_scores = (
        jnp.einsum("rgqd,rgd->rgq", query_heads, fresh_keys, preferred_element_type=jnp.float32)
        * score_scale
    )
    positions = my_index * cache_here + jnp.arange(cache_here, dtype=jnp.int32)
    visible = positions[None, :] < cache_len[:, None]
    cached_keys = key_cache.reshape(cache_here, KVH, HD)
    cached_values = value_cache.reshape(cache_here, KVH, HD)
    score_list = []
    maxima_list = []
    for kv_head in range(KVH):
        scores = (
            jnp.einsum(
                "rqd,pd->rqp",
                query_heads[:, kv_head],
                cached_keys[:, kv_head],
                preferred_element_type=jnp.float32,
            )
            * score_scale
        )
        scores = jnp.where(visible[:, None, :], scores, -jnp.inf)
        score_list.append(scores)
        maxima_list.append(jnp.maximum(fresh_scores[:, kv_head], jnp.max(scores, axis=-1)))
    local_peak = jnp.stack(maxima_list, axis=1).reshape(total_rows, HEADS)
    global_peak = lax.pmax(local_peak.astype(jnp.bfloat16), "ctx").astype(local_peak.dtype)
    peak_groups = global_peak.reshape(total_rows, KVH, group_size)
    numer_list = []
    denom_list = []
    for kv_head in range(KVH):
        weights = jnp.exp(score_list[kv_head] - peak_groups[:, kv_head, :, None]).astype(
            jnp.bfloat16
        )
        numer_list.append(
            jnp.einsum(
                "rqp,pd->rqd",
                weights,
                cached_values[:, kv_head],
                preferred_element_type=jnp.float32,
            )
        )
        denom_list.append(jnp.sum(weights.astype(jnp.float32), axis=-1))
    numerator = jnp.stack(numer_list, axis=1).reshape(total_rows, HEADS, HD)
    denominator = jnp.stack(denom_list, axis=1).reshape(total_rows, HEADS)
    own_numer, own_denom = (
        lax.psum_scatter(
            numerator.astype(jnp.bfloat16), "ctx", scatter_dimension=1, tiled=True
        ).astype(jnp.float32),
        lax.psum_scatter(
            denominator.astype(jnp.bfloat16), "ctx", scatter_dimension=1, tiled=True
        ).astype(jnp.float32),
    )
    head_start = my_index * heads_here
    own_fresh = lax.dynamic_slice_in_dim(
        fresh_scores.reshape(total_rows, HEADS), head_start, heads_here, 1
    )
    own_peak = lax.dynamic_slice_in_dim(global_peak, head_start, heads_here, 1)
    fresh_weight = lax.optimization_barrier(
        jnp.exp(own_fresh - own_peak).astype(jnp.bfloat16)
    ).astype(jnp.float32)
    value_heads = jnp.repeat(fresh_values, group_size, axis=1)
    own_values = lax.dynamic_slice_in_dim(value_heads, head_start, heads_here, 1).astype(
        jnp.float32
    )
    total_numer = own_numer + fresh_weight[..., None] * own_values
    total_denom = own_denom + fresh_weight
    attended = (
        (total_numer / total_denom[..., None])
        .astype(jnp.bfloat16)
        .reshape(total_rows, heads_here * HD)
    )
    attn_out = lax.psum_scatter(
        jnp.dot(attended, out_weight, preferred_element_type=jnp.float32).astype(jnp.bfloat16),
        "ctx",
        scatter_dimension=0,
        tiled=True,
    ).astype(jnp.float32)
    after_attention = lax.optimization_barrier(
        (residual.astype(jnp.float32) + attn_out).astype(jnp.bfloat16)
    )
    middle = after_attention.astype(jnp.float32)
    inv_rms = lax.rsqrt(jnp.mean(middle * middle, axis=-1, keepdims=True) + 1e-06)
    normed = (middle * inv_rms * norm_gain.astype(jnp.float32)[None, :]).astype(jnp.bfloat16)
    expert_count = EXP_DEV * devices
    slots_all = expert_count * MOST
    flat_ids = expert_ids.reshape(-1)
    one_hot = (flat_ids[:, None] == jnp.arange(expert_count, dtype=jnp.int32)[None, :]).astype(
        jnp.int32
    )
    slot_rank = jnp.sum((jnp.cumsum(one_hot, axis=0) - 1) * one_hot, axis=1)
    target = flat_ids * MOST + slot_rank
    chooser = (target[None, :] == jnp.arange(slots_all, dtype=jnp.int32)[:, None]).reshape(
        slots_all, local_rows, TOP
    )
    chooser = jnp.any(chooser, axis=2).astype(jnp.bfloat16)
    outgoing = jnp.dot(chooser, normed, preferred_element_type=jnp.float32).astype(jnp.bfloat16)
    outgoing = outgoing.reshape(devices, EXP_DEV, MOST, D)
    produced = expert_block(
        lax.all_to_all(outgoing, "ctx", split_axis=0, concat_axis=0, tiled=True),
        w_gate,
        w_up,
        w_down,
        "semd,edf->semf",
        "semf,efd->semd",
    )
    returned = lax.all_to_all(produced, "ctx", split_axis=0, concat_axis=0, tiled=True).reshape(
        slots_all, D
    )
    picked = jnp.take(returned, target, axis=0).reshape(local_rows, TOP, D)
    mixed = jnp.sum(route_weight[..., None] * picked.astype(jnp.float32), axis=1)
    return (middle + mixed).astype(jnp.bfloat16)


def solution(mesh):
    placed = (
        P(("groups", "ctx"), None),
        P(("groups", "ctx"), None),
        P(("groups", "ctx"), None),
        P(("groups", "ctx"), None),
        P(("groups", "ctx"), None),
        P("groups"),
        P("ctx", None),
        P(("groups", "ctx"), None),
        P(),
        P(("groups", "ctx"), None),
        P(("groups", "ctx"), None),
        P("ctx", None, None),
        P("ctx", None, None),
        P("ctx", None, None),
    )
    return jax.shard_map(
        on_device, mesh=mesh, in_specs=placed, out_specs=P(("groups", "ctx"), None), check_vma=False
    )
```

profile of v0, /device:TPU:0, one launch (start us, length us, event | category | flops | bytes accessed | tf_op | source)
XLA Modules:
  0.0 365.3 jit_solution(17394293425251557948)
XLA Ops:
  6.5 0.7 all-gather.2.cloned.1.call-update
  7.3 2.3 copy.67
  9.6 24.5 %all_gather.10 = bf16[256,512]{1,0:T(8,128)(2,1)S(1)} all-gather(bf16[16,512]{1,0:T(8,128)(2,1)} %param.15), channel_id=1, replica_groups=mesh['groups'=2,'ctx'=16] {'ctx'}, dimensions={0}, use_global_device_ids=true | all-gather | bytes 278528 | tf_op jit(solution)/shard_map/all_gather | solution.py:47
  34.1 1.0 copy.111
  35.2 2.3 copy.75
  37.4 0.9 broadcast_compare_fusion
  38.3 15.4 %all-gather.2.cloned.1.call-done = bf16[256,4096]{1,0:T(8,128)(2,1)} async-done(((bf16[16,4096]{1,0:T(8,128)(2,1)}), bf16[256,4096]{1,0:T(8,128)(2,1)}) %all-gather.2.cloned.1.call-update) | async-done | bytes 2097168 | tf_op jit(solution)/shard_map/all_gather | solution.py:46
  53.8 3.3 copy.65
  57.1 1.3 copy-done.4
  58.4 2.2 fusion.32
  60.6 2.8 fusion.33
  63.5 0.8 copy-done.5
  64.3 4.9 %fusion.34 = f32[256,8,1024]{2,0,1:T(8,128)} fusion(bf16[256,4,8,128]{0,3,2,1:T(8,128)(2,1)S(1)} %bitcast.169, bf16[1024,4,128]{0,2,1:T(8,128)(2,1)S(1)} %bitcast.174), kind=kOutput, calls=%fused_computation.43 | convolution fusion | flops 536870912 | bytes 9175040 | tf_op jit(solution)/shard_map/rqd,pd->rqp/dot_general | solution.py:70
  69.2 0.5 multiply_reduce_fusion
  69.7 9.3 %fusion = (bf16[256,8]{0,1:T(8,128)(2,1)S(1)}, bf16[256,8]{0,1:T(8,128)(2,1)S(1)}, bf16[256,8]{0,1:T(8,128)(2,1)S(1)}, bf16[256,8]{0,1:T(8,128)(2,1)S(1)}, f32[256,8,1024]{2,0,1:T(8,128)}) fusion(pred[256,1024]{1,0:T(8,128)(4,1)S(1)} %broadcast_compare_fusion, f32[256,8,1024]{2,0,1:T(8,128)} %fusion.34, f32[256,8,1024]{2,0,1:T(8,128)S(1)} %fusion.33, ...), kind=kOutput, calls=%fused_computation.9 | convolution fusion | flops 562028544 | bytes 34619392 | tf_op jit(solution)/shard_map/rqd,pd->rqp/dot_general | solution.py:70
  79.1 59.5 %pmax.7 = bf16[256,32]{0,1:T(8,128)(2,1)S(1)} all-reduce(bf16[256,32]{0,1:T(8,128)(2,1)S(1)} %maximum_bitcast_fusion), channel_id=1, replica_groups=mesh['groups'=2,'ctx'=16] {'ctx'}, use_global_device_ids=true, to_apply=%region_4.5 | all-reduce | flops 8192 | bytes 32768 | tf_op jit(solution)/shard_map/pmax | solution.py:82
  138.6 5.7 %fusion.17 = bf16[256,1,8,128]{3,0,2,1:T(8,128)(2,1)S(1)} fusion(bf16[1024,4,128]{0,2,1:T(8,128)(2,1)S(1)} %bitcast.177, f32[256,8,1024]{2,0,1:T(8,128)} %fusion.34, f32[256,8]{0,1:T(8,128)S(1)} %get-tuple-element.18, pred[256,1024]{1,0:T(8,128)(4,1)S(1)} %broadcast_compare_fusion), kind=kOutput, calls=%fused_computation.30 | convolution fusion | flops 545521664 | bytes 9445376 | tf_op jit(solution)/shard_map/rqp,pd->rqd/dot_general | solution.py:91
  144.3 2.2 fusion.18
  146.6 0.4 slice-done.1
  147.0 2.3 fusion.19
  149.3 0.2 slice-done.3
  149.5 2.2 fusion.16
  151.7 0.3 pad_maximum_fusion
  152.0 2.9 copy.80
  155.0 17.8 %all_gather.11 = bf16[256,512]{1,0:T(8,128)(2,1)S(1)} all-gather(bf16[16,512]{1,0:T(8,128)(2,1)S(1)} %copy-done.10), channel_id=1, replica_groups=mesh['groups'=2,'ctx'=16] {'ctx'}, dimensions={0}, use_global_device_ids=true | all-gather | bytes 278528 | tf_op jit(solution)/shard_map/all_gather | solution.py:48
  172.9 0.1 copy.98
  173.0 0.6 dynamic-slice
  174.4 13.8 %fusion.60 = (bf16[256,8]{0,1:T(8,128)(2,1)S(1)}, bf16[256,8]{0,1:T(8,128)(2,1)S(1)}, bf16[256,8]{0,1:T(8,128)(2,1)S(1)}, bf16[256,8]{0,1:T(8,128)(2,1)S(1)}) fusion(f32[256,8]{0,1:T(8,128)S(1)} %get-tuple-element.15, f32[256,8,1024]{2,0,1:T(8,128)} %get-tuple-element.25, pred[256,1024]{1,0:T(8,128)(4,1)S(1)} %broadcast_compare_fusion, ...), kind=kLoop, calls=%fused_computation.105 | loop fusion | flops 41934848 | bytes 33865728 | tf_op jit(solution)/shard_map/reduce_sum | solution.py:98
  188.1 60.0 %all-reduce = bf16[256,32]{0,1:T(8,128)(2,1)S(1)} all-reduce(bf16[256,32]{0,1:T(8,128)(2,1)S(1)} %maximum_bitcast_fusion.1), channel_id=3, replica_groups=mesh['groups'=2,'ctx'=16] {'ctx'}, use_global_device_ids=true, to_apply=%region_10.11.clone | all-reduce | flops 8192 | bytes 32768
  248.1 0.2 broadcast_in_dim.53
  248.4 1.0 divide_convert_fusion
  249.3 1.5 convolution_convert_fusion
  251.1 0.2 reduce_window_sum.11
  251.3 0.2 select_reduce_fusion
  251.7 53.9 %reduce-scatter.5.cloned.1.call-done = bf16[16,2048]{1,0:T(8,128)(2,1)} async-done(((bf16[256,2048]{1,0:T(8,128)(2,1)}), bf16[16,2048]{1,0:T(8,128)(2,1)}) %reduce-scatter.5.cloned.1.call-update) | async-done | bytes 65552 | tf_op jit(solution)/shard_map/reduce_scatter | solution.py:128
  305.6 0.9 add_convert_fusion
  306.4 0.1 fusion.43
  306.6 0.4 convolution_convert_fusion.1
  307.0 0.2 reshape.159
  307.2 18.0 %all_to_all.10 = bf16[16,2,4,2048]{3,2,1,0:T(4,128)(2,1)S(1)} all-to-all(bf16[16,2,4,2048]{3,2,1,0:T(4,128)(2,1)S(1)} %reshape.159), channel_id=1, replica_groups=mesh['groups'=2,'ctx'=16] {'ctx'}, dimensions={0} | all-to-all | bytes 1048576 | tf_op jit(solution)/shard_map/all_to_all | solution.py:155
  325.2 4.1 %fusion.20 = f32[16,2,4,768]{3,0,2,1:T(8,128)S(1)} fusion(bf16[2,2048,768]{2,1,0:T(8,128)(2,1)} %param.25, bf16[16,2,4,2048]{3,2,1,0:T(4,128)(2,1)S(1)} %all_to_all.10), kind=kOutput, calls=%fused_computation.33 | convolution fusion | flops 402653184 | bytes 7208960 | tf_op jit(solution)/shard_map/semd,edf->semf/dot_general | solution.py:18
  329.3 7.1 %fusion.13 = bf16[16,2,4,2048]{3,0,2,1:T(8,128)(2,1)S(1)} fusion(bf16[2,768,2048]{2,1,0:T(8,128)(2,1)} %param.27, bf16[2,2048,768]{2,1,0:T(8,128)(2,1)} %param.26, bf16[16,2,4,2048]{3,2,1,0:T(4,128)(2,1)S(1)} %all_to_all.10, f32[16,2,4,768]{3,0,2,1:T(8,128)S(1)} %fusion.20), kind=kOutput, calls=%fused_computation.23 | convolution fusion | flops 806158336 | bytes 14024704 | tf_op jit(solution)/shard_map/semf,efd->semd/dot_general | solution.py:21
  336.4 1.2 copy.87
  337.6 4.1 %all-to-all-start.1 = ((bf16[16,2,4,2048]{3,2,1,0:T(4,128)(2,1)}), bf16[16,2,4,2048]{3,2,1,0:T(4,128)(2,1)S(1)}, u32[]{:S(2)}, u32[]{:S(2)}) async-start(bf16[16,2,4,2048]{3,2,1,0:T(4,128)(2,1)} %copy.87), calls=%async_computation.3 | async-start | bytes 1048576 | tf_op jit(solution)/shard_map/all_to_all | solution.py:162
  341.9 14.3 %all-to-all-done.1 = bf16[16,2,4,2048]{3,2,1,0:T(4,128)(2,1)S(1)} async-done(((bf16[16,2,4,2048]{3,2,1,0:T(4,128)(2,1)}), bf16[16,2,4,2048]{3,2,1,0:T(4,128)(2,1)S(1)}, u32[]{:S(2)}, u32[]{:S(2)}) %all-to-all-start.1) | async-done | bytes 524320 | tf_op jit(solution)/shard_map/all_to_all | solution.py:162
  356.2 0.9 gather_fusion
  357.2 0.9 multiply_reduce_fusion.1
  358.1 0.6 fusion.46
  (68 shorter events, 1.2 us)
Async XLA Ops:
  6.5 242.8 %copy-start = (bf16[256,2048]{1,0:T(8,128)(2,1)S(1)}, bf16[256,2048]{1,0:T(8,128)(2,1)}, u32[]{:S(2)}) copy-start(bf16[256,2048]{1,0:T(8,128)(2,1)} %param.20) | copy-start | bytes 3145732
  6.5 47.2 %all-gather.2.cloned.1.call-start = ((), (), s32[]{:S(2)}) async-start(), calls=%async_computation.4 | async-start | bytes 2228224 | tf_op jit(solution)/shard_map/all_gather | solution.py:46
  7.3 240.9 %reduce-scatter.3.cloned.1.call-start = ((), (), s32[]{:S(2)}) async-start(), calls=%async_computation.5 | async-start | bytes 2228224 | tf_op jit(solution)/shard_map/reduce_scatter | solution.py:102
  57.1 1.3 copy-start.4
  57.1 3.5 copy-start.6
  60.6 9.1 %copy-start.1 = (f32[256,8,1024]{2,0,1:T(8,128)}, f32[256,8,1024]{2,0,1:T(8,128)S(1)}, u32[]{:S(2)}) copy-start(f32[256,8,1024]{2,0,1:T(8,128)S(1)} %fusion.32) | copy-start | bytes 25165828
  60.6 3.7 %copy-start.5 = (bf16[256,4096]{0,1:T(8,128)(2,1)S(1)}, bf16[256,4096]{0,1:T(8,128)(2,1)}, u32[]{:S(2)}) copy-start(bf16[256,4096]{0,1:T(8,128)(2,1)} %copy-done.4) | copy-start | bytes 6291460
  60.6 8.6 %copy-start.7 = (f32[256,4,128]{0,2,1:T(8,128)S(1)}, f32[256,4,128]{0,2,1:T(8,128)}, u32[]{:S(2)}) copy-start(f32[256,4,128]{0,2,1:T(8,128)} %copy.111) | copy-start | bytes 1572868
  64.3 14.7 %copy-start.2 = (f32[256,8,1024]{2,0,1:T(8,128)}, f32[256,8,1024]{2,0,1:T(8,128)S(1)}, u32[]{:S(2)}) copy-start(f32[256,8,1024]{2,0,1:T(8,128)S(1)} %fusion.33) | copy-start | bytes 25165828
  69.7 68.8 %copy-start.8 = (bf16[1024,512]{0,1:T(8,128)(2,1)S(1)}, bf16[1024,512]{0,1:T(8,128)(2,1)}, u32[]{:S(2)}) copy-start(bf16[1024,512]{0,1:T(8,128)(2,1)} %copy.75) | copy-start | bytes 3145732
  138.5 5.8 %copy-start.3 = (f32[256,8,1024]{2,0,1:T(8,128)S(1)}, f32[256,8,1024]{2,0,1:T(8,128)}, u32[]{:S(2)}) copy-start(f32[256,8,1024]{2,0,1:T(8,128)} %copy-done.2) | copy-start | bytes 25165828
  138.6 8.0 %slice-start = ((s8[8388608]{0:T(1024)(128)(4,1)}), s8[4194304]{0:T(1024)(128)(4,1)S(1)}, s32[]{:S(2)}) async-start(s8[8388608]{0:T(1024)(128)(4,1)} %bitcast.162), calls=%async_computation.7 | async-start | bytes 8388608
  144.3 2.7 slice-start.1
  144.3 5.0 %slice-start.2 = ((s8[8388608]{0:T(1024)(128)(4,1)}), s8[4194304]{0:T(1024)(128)(4,1)S(1)}, s32[]{:S(2)}) async-start(s8[8388608]{0:T(1024)(128)(4,1)} %bitcast.164), calls=%async_computation.9 | async-start | bytes 8388608
  147.0 2.4 slice-start.3
  151.7 3.3 copy-start.10
  151.7 21.3 %copy-start.14 = (u32[32]{0:T(128)S(1)}, u32[32]{0:T(128)}, u32[]{:S(2)}) copy-start(u32[32]{0:T(128)} %constant.69) | copy-start | bytes 388
  155.0 150.6 %reduce-scatter.5.cloned.1.call-start = ((), (), s32[]{:S(2)}) async-start(), calls=%async_computation.6 | async-start | bytes 1114112 | tf_op jit(solution)/shard_map/reduce_scatter | solution.py:128
  174.3 76.5 %copy-start.11 = (s32[16,8]{0,1:T(8,128)S(1)}, s32[16,8]{0,1:T(8,128)}, u32[]{:S(2)}) copy-start(s32[16,8]{0,1:T(8,128)} %param.23) | copy-start | bytes 1540
  174.3 77.2 %copy-start.12 = (bf16[2048]{0:T(1024)(128)(2,1)S(1)}, bf16[2048]{0:T(1024)(128)(2,1)}, u32[]{:S(2)}) copy-start(bf16[2048]{0:T(1024)(128)(2,1)} %param.22) | copy-start | bytes 12292
  174.3 131.2 %copy-start.9 = (bf16[16,2048]{1,0:T(8,128)(2,1)S(1)}, bf16[16,2048]{1,0:T(8,128)(2,1)}, u32[]{:S(2)}) copy-start(bf16[16,2048]{1,0:T(8,128)(2,1)} %param.21) | copy-start | bytes 196612
  329.3 12.5 %copy-start.13 = (f32[16,8]{0,1:T(8,128)S(1)}, f32[16,8]{0,1:T(8,128)}, u32[]{:S(2)}) copy-start(f32[16,8]{0,1:T(8,128)} %param.24) | copy-start | bytes 1540
  337.6 18.6 %all-to-all-start.1 = ((bf16[16,2,4,2048]{3,2,1,0:T(4,128)(2,1)}), bf16[16,2,4,2048]{3,2,1,0:T(4,128)(2,1)S(1)}, u32[]{:S(2)}, u32[]{:S(2)}) async-start(bf16[16,2,4,2048]{3,2,1,0:T(4,128)(2,1)} %copy.87), calls=%async_computation.3 | async-start | bytes 1048576 | tf_op jit(solution)/shard_map/all_to_all | solution.py:162
Sparse Core Ops, SparseCore 0:
  9.5 44.2 all-gather.1
  155.1 58.7 reduce-scatter.2
  250.9 54.6 reduce-scatter.4
where the time goes:
time: 366 us; the launch traced here: 365 us
  blocking collectives  180 us (49%)
  waiting for transfers between devices  84.4 us (23%)
  matrix products  44.6 us (12%)
  other arithmetic  19.6 us (5%)
  local copies, waits for them, and re-layouts  18.5 us (5%)
  between operations  14.2 us (4%)
  starting transfers between devices  4.17 us (1%)
    unnamed x1, blocking collectives  60 us
    pmax x1, blocking collectives, on_device(): lax.pmax(local_peak.astype(jnp.bfloat16), 'ctx').astype(local_peak.dtype)  59.5 us
    reduce_scatter x1, waiting for transfers between devices, on_device(): lax.psum_scatter(jnp.dot(attended, out_weight, preferred_element_type=jnp...  53.9 us
    all_gather x1, blocking collectives, on_device(): lax.all_gather(new_key, 'ctx', axis=0, tiled=True)  24.5 us
    dot_general x4, matrix products, on_device(): jnp.einsum('rqd,pd->rqp', query_heads[:, kv_head], cached_keys[:, kv_head...  19.3 us
    all_to_all x1, blocking collectives, on_device(): lax.all_to_all(outgoing, 'ctx', split_axis=0, concat_axis=0, tiled=True)  18 us
    all_gather x1, blocking collectives, on_device(): lax.all_gather(new_value, 'ctx', axis=0, tiled=True)  17.8 us
    all_gather x1, waiting for transfers between devices, on_device(): lax.all_gather(queries, 'ctx', axis=0, tiled=True)  15.4 us
  transfers between devices with their start and end apart: 4, of which 3 were waited for; matrix products, arithmetic and copies ran while one was open for 6% of the time, Pallas kernels for 0%

commit v1 on v0

v1 whole, which is shorter than its diff:
```python
import functools
import math

import jax
import jax.numpy as jnp
from jax import lax
from jax.experimental import pallas as pl
from jax.experimental.pallas import tpu as pltpu
from jax.sharding import PartitionSpec as P

HD = 128
MOST = 4
CORES = 2
STATS = 16
MASKED = -1e30
FLOOR = -1e20
LOG2E = math.log2(math.e)
MIB = 1024 * 1024
F32 = jnp.float32
BF16 = jnp.bfloat16


def nt_dot(a, b):
    return lax.dot_general(a, b, (((1,), (1,)), ((), ())), preferred_element_type=F32)


def nn_dot(a, b):
    return lax.dot_general(a, b, (((1,), (0,)), ((), ())), preferred_element_type=F32)


def attention_body(chips, heads_chip, spare, place, *refs):
    query_refs = refs[:chips]
    key_own, key_other, value_own, value_other, key_fresh, value_fresh, lens, out, q_rows, v_turned, hidden = refs[chips:]
    owner = pl.program_id(0)
    chip, start_own, start_other = place[0], place[1], place[2]
    home_rows = query_refs[0].shape[0]
    rows = chips * home_rows
    cache_here = key_own.shape[0]

    @pl.when(owner == 0)
    def _():
        for part, start in enumerate((start_own, start_other)):
            positions = start + lax.broadcasted_iota(jnp.int32, (cache_here, rows), 0)
            hidden[part * cache_here : (part + 1) * cache_here, :] = jnp.where(
                positions < lens[...], 0.0, MASKED
            )
        token = lax.broadcasted_iota(jnp.int32, (home_rows, rows), 0)
        column = lax.broadcasted_iota(jnp.int32, (home_rows, rows), 1)
        hidden[2 * cache_here :, :] = jnp.where(token + chip * home_rows == column, 0.0, MASKED)

    @pl.when(owner % spare == 0)
    def _():
        v_turned[:HD, :cache_here] = value_own[...].T
        v_turned[:HD, cache_here : 2 * cache_here] = value_other[...].T
        v_turned[HD:, :] = jnp.ones_like(v_turned[HD:, :])

    for shift in range(chips):
        source = lax.rem(chip + chips - shift, chips)
        q_rows[pl.ds(pl.multiple_of(source * home_rows, home_rows), home_rows), :] = query_refs[shift][...]

    value_new = value_fresh[...].astype(F32).T.astype(BF16)
    peaks, highs, lows = [], [], []
    pair = min(2, heads_chip)
    for first in range(0, heads_chip, pair):
        q = jnp.concatenate(
            [q_rows[:, h * HD : (h + 1) * HD] for h in range(first, first + pair)], axis=0
        )
        mask = jnp.concatenate([hidden[...]] * pair, axis=1)
        s_own = nt_dot(key_own[...], q) + mask[:cache_here]
        s_other = nt_dot(key_other[...], q) + mask[cache_here : 2 * cache_here]
        s_new = nt_dot(key_fresh[...], q) + mask[2 * cache_here :]
        peak = jnp.maximum(
            jnp.maximum(jnp.max(s_own, axis=0, keepdims=True), jnp.max(s_other, axis=0, keepdims=True)),
            jnp.max(s_new, axis=0, keepdims=True),
        )
        scale = 1.0 / math.sqrt(HD)
        peak = jnp.maximum(peak * scale, FLOOR).astype(BF16).astype(F32)
        lift = peak * LOG2E
        p_own = jnp.exp2(s_own * (scale * LOG2E) - lift).astype(BF16)
        p_other = jnp.exp2(s_other * (scale * LOG2E) - lift).astype(BF16)
        p_new = jnp.exp2(s_new * (scale * LOG2E) - lift).astype(BF16)
        total = nn_dot(v_turned[:, :cache_here], p_own) + nn_dot(v_turned[:, cache_here:], p_other)
        numer = total[:HD] + nn_dot(value_new, p_new)
        denom = total[HD : HD + 1] + jnp.sum(p_new.astype(F32), axis=0, keepdims=True)
        for k in range(pair):
            cols = slice(k * rows, (k + 1) * rows)
            out[0, (first + k) * HD : (first + k + 1) * HD, :] = numer[:, cols].astype(BF16)
            high = denom[:, cols].astype(BF16).astype(F32)
            peaks.append(peak[:, cols])
            highs.append(high)
            lows.append(denom[:, cols] - high)
    stats = peaks + highs + lows
    stats = stats + [jnp.zeros_like(stats[0])] * (STATS - len(stats))
    out[0, heads_chip * HD :, :] = jnp.concatenate(stats, axis=0).astype(BF16)


def attention(place, query_parts, keys, values, new_key, new_value, lens, heads_chip, group_size):
    chips = len(query_parts)
    home_rows = query_parts[0].shape[0]
    rows = chips * home_rows
    cache_here = keys[0].shape[0]
    spare = max(1, group_size // heads_chip)
    kv = lambda j, place: (0, j * heads_chip // group_size)
    height = heads_chip * HD + STATS
    total_positions = 2 * cache_here + home_rows
    work = rows * heads_chip * chips * total_positions
    return pl.pallas_call(
        functools.partial(attention_body, chips, heads_chip, spare),
        grid_spec=pltpu.PrefetchScalarGridSpec(
            num_scalar_prefetch=1,
            grid=(chips,),
            in_specs=[pl.BlockSpec((home_rows, heads_chip * HD), lambda j, place: (0, j))] * chips
            + [pl.BlockSpec((cache_here, HD), kv)] * 4
            + [pl.BlockSpec((home_rows, HD), kv)] * 2
            + [pl.BlockSpec((1, rows), lambda j, place: (0, 0))],
            out_specs=pl.BlockSpec((1, height, rows), lambda j, place: (j, 0, 0)),
            scratch_shapes=[
                pltpu.VMEM((rows, heads_chip * HD), BF16),
                pltpu.VMEM((HD + STATS, 2 * cache_here), BF16),
                pltpu.VMEM((total_positions, rows), F32),
            ],
        ),
        out_shape=jax.ShapeDtypeStruct((chips, height, rows), BF16),
        compiler_params=pltpu.CompilerParams(vmem_limit_bytes=40 * MIB),
        cost_estimate=pl.CostEstimate(
            flops=4 * work * HD, bytes_accessed=8 * MIB, transcendentals=work
        ),
        name="attention",
    )(place, *query_parts, *keys, *values, new_key, new_value, lens)


def project_body(heads_chip, place, parts, weight_own, weight_other, out, turned):
    core = place[3]
    chips = parts.shape[0]
    base = heads_chip * HD
    stats = parts[:, base:, :].astype(F32)
    peaks = stats[:, :heads_chip]
    top = jnp.max(peaks, axis=0, keepdims=True)
    share = jnp.exp(peaks - top)
    totals = stats[:, heads_chip : 2 * heads_chip] + stats[:, 2 * heads_chip : 3 * heads_chip]
    denom = jnp.sum(share * totals, axis=0)
    half = heads_chip // CORES
    for h in range(heads_chip):
        numer = None
        for s in range(chips):
            term = parts[s, h * HD : (h + 1) * HD, :].astype(F32) * share[s, h : h + 1, :]
            numer = term if numer is None else numer + term
        attended = (numer / denom[h : h + 1, :]).T.astype(BF16)
        turned[h // half, :, (h % half) * HD : (h % half + 1) * HD] = attended
    product = nn_dot(turned[core], weight_own[...]) + nn_dot(turned[1 - core], weight_other[...])
    out[...] = product.astype(BF16)


def project(place, parts, weight_own, weight_other, heads_chip):
    rows = parts.shape[2]
    width = weight_own.shape[1]
    vmem = pl.BlockSpec(memory_space=pltpu.VMEM)
    return pl.pallas_call(
        functools.partial(project_body, heads_chip),
        in_specs=[pl.BlockSpec(memory_space=pltpu.SMEM), vmem, vmem, vmem],
        out_specs=vmem,
        out_shape=jax.ShapeDtypeStruct((rows, width), BF16),
        scratch_shapes=[pltpu.VMEM((CORES, rows, weight_own.shape[0]), BF16)],
        compiler_params=pltpu.CompilerParams(vmem_limit_bytes=32 * MIB),
        cost_estimate=pl.CostEstimate(
            flops=2 * rows * width * heads_chip * HD, bytes_accessed=4 * MIB, transcendentals=0
        ),
        name="project",
    )(place, parts, weight_own, weight_other)


def norm_body(parts, residual, gain, chooser, middle_out, sent):
    total = parts[0].astype(F32)
    for s in range(1, parts.shape[0]):
        total = total + parts[s].astype(F32)
    middle = (residual[...].astype(F32) + total).astype(BF16)
    middle_out[...] = middle
    middle = middle.astype(F32)
    inv_rms = lax.rsqrt(jnp.mean(middle * middle, axis=-1, keepdims=True) + 1e-06)
    normed = (middle * inv_rms * gain[...].astype(F32)).astype(BF16)
    sent[...] = nn_dot(chooser[...], normed).astype(BF16)


def norm_and_dispatch(parts, residual, gain, chooser):
    vmem = pl.BlockSpec(memory_space=pltpu.VMEM)
    rows, width = residual.shape
    return pl.pallas_call(
        norm_body,
        in_specs=[vmem] * 4,
        out_specs=[vmem] * 2,
        out_shape=[
            jax.ShapeDtypeStruct((rows, width), BF16),
            jax.ShapeDtypeStruct((chooser.shape[0], width), BF16),
        ],
        compiler_params=pltpu.CompilerParams(vmem_limit_bytes=24 * MIB),
        cost_estimate=pl.CostEstimate(
            flops=2 * chooser.shape[0] * rows * width, bytes_accessed=2 * MIB, transcendentals=0
        ),
        name="norm_and_dispatch",
    )(parts, residual, gain, chooser)


def experts_body(experts, arrived, w_gate, w_up, w_down, out, total):
    expert, chunk = pl.program_id(0), pl.program_id(1)
    rows = arrived.shape[0]
    gate = nn_dot(arrived[...], w_gate[0])
    upward = nn_dot(arrived[...], w_up[0])
    hidden = gate / (1.0 + jnp.exp(-gate)) * upward
    slot = lax.broadcasted_iota(jnp.int32, hidden.shape, 0)
    mine = lax.rem(slot, experts * MOST) // MOST == expert
    hidden = jnp.where(mine, hidden, 0.0).astype(BF16)
    product = nn_dot(hidden, w_down[0])
    first = (expert == 0) & (chunk == 0)
    last = (expert == pl.num_programs(0) - 1) & (chunk == pl.num_programs(1) - 1)

    @pl.when(first)
    def _():
        total[...] = product

    @pl.when(jnp.logical_not(first))
    def _():
        total[...] += product

    @pl.when(last)
    def _():
        out[...] = total[...].astype(BF16)


def run_experts(arrived, w_gate, w_up, w_down):
    rows, width = arrived.shape
    experts, _, hidden = w_gate.shape
    block = 256
    return pl.pallas_call(
        functools.partial(experts_body, experts),
        grid=(experts, hidden // block),
        in_specs=[
            pl.BlockSpec((rows, width), lambda e, f: (0, 0)),
            pl.BlockSpec((1, width, block), lambda e, f: (e, 0, f)),
            pl.BlockSpec((1, width, block), lambda e, f: (e, 0, f)),
            pl.BlockSpec((1, block, width), lambda e, f: (e, f, 0)),
        ],
        out_specs=pl.BlockSpec((rows, width), lambda e, f: (0, 0)),
        out_shape=jax.ShapeDtypeStruct((rows, width), BF16),
        scratch_shapes=[pltpu.VMEM((rows, width), F32)],
        compiler_params=pltpu.CompilerParams(vmem_limit_bytes=32 * MIB),
        cost_estimate=pl.CostEstimate(
            flops=6 * rows * width * experts * hidden,
            bytes_accessed=6 * width * experts * hidden,
            transcendentals=rows * experts * hidden,
        ),
        name="experts",
    )(arrived, w_gate, w_up, w_down)


def mix_body(returned, coarse, fine, middle, out):
    values = returned[...]
    mixed = nn_dot(coarse[...], values) + nn_dot(fine[...], values)
    out[...] = (middle[...].astype(F32) + mixed).astype(BF16)


def mix(returned, coarse, fine, middle):
    vmem = pl.BlockSpec(memory_space=pltpu.VMEM)
    return pl.pallas_call(
        mix_body,
        in_specs=[vmem] * 4,
        out_specs=vmem,
        out_shape=jax.ShapeDtypeStruct(middle.shape, BF16),
        compiler_params=pltpu.CompilerParams(vmem_limit_bytes=16 * MIB),
        name="mix",
    )(returned, coarse, fine, middle)


def on_device(
    queries,
    new_key,
    new_value,
    key_cache,
    value_cache,
    cache_len,
    out_weight,
    residual,
    norm_gain,
    expert_ids,
    route_weight,
    w_gate,
    w_up,
    w_down,
):
    devices = lax.axis_size("ctx")
    chips = devices // CORES
    index = lax.axis_index("ctx")
    chip, core = index // CORES, index % CORES
    home_rows, width = residual.shape
    top = expert_ids.shape[1]
    heads = queries.shape[1] // HD
    group_size = heads // (key_cache.shape[1] // HD)
    heads_chip = heads // chips
    cache_here = key_cache.shape[0]
    same_core = [[CORES * j + c for j in range(chips)] for c in range(CORES)]
    swap = [(i, i ^ 1) for i in range(devices)]

    query_parts = [queries] + [
        lax.ppermute(
            queries,
            "ctx",
            [(i, (i + CORES * shift) % devices) for i in range(devices)],
        )
        for shift in range(1, chips)
    ]
    key_other = lax.ppermute(key_cache, "ctx", swap)
    value_other = lax.ppermute(value_cache, "ctx", swap)
    weight_other = lax.ppermute(out_weight, "ctx", swap)

    place = jnp.stack([chip, index * cache_here, (index ^ 1) * cache_here, core]).astype(jnp.int32)
    lens = lax.dynamic_index_in_dim(
        cache_len.reshape(chips, CORES, home_rows), core, axis=1, keepdims=False
    ).reshape(1, chips * home_rows)

    flat_ids = expert_ids.reshape(-1)
    picks = jnp.arange(flat_ids.shape[0])
    earlier = (flat_ids[:, None] == flat_ids[None, :]) & (picks[None, :] < picks[:, None])
    target = (flat_ids * MOST + jnp.sum(earlier, axis=1, dtype=jnp.int32)).reshape(home_rows, top)
    experts = w_gate.shape[0]
    slots = experts * devices * MOST
    takes = target[:, :, None] == jnp.arange(slots, dtype=jnp.int32)
    chooser = jnp.any(takes, axis=1).T.astype(BF16)
    spread = jnp.sum(jnp.where(takes, route_weight[:, :, None], 0.0), axis=1)
    coarse = spread.astype(BF16)
    fine = (spread - coarse.astype(F32)).astype(BF16)

    sums = attention(
        place,
        query_parts,
        (key_cache, key_other),
        (value_cache, value_other),
        new_key,
        new_value,
        lens,
        heads_chip,
        group_size,
    )
    gathered = lax.all_to_all(
        sums, "ctx", split_axis=0, concat_axis=0, axis_index_groups=same_core, tiled=True
    )
    share = project(place, gathered, out_weight, weight_other, heads_chip)
    shares = lax.all_to_all(
        share.reshape(chips, home_rows, width),
        "ctx",
        split_axis=0,
        concat_axis=0,
        axis_index_groups=same_core,
        tiled=True,
    )
    middle, outgoing = norm_and_dispatch(shares, residual, norm_gain.reshape(1, width), chooser)
    arrived = lax.all_to_all(
        outgoing.reshape(devices, experts * MOST, width), "ctx", split_axis=0, concat_axis=0, tiled=True
    )
    produced = run_experts(arrived.reshape(slots, width), w_gate, w_up, w_down)
    returned = lax.all_to_all(
        produced.reshape(devices, experts * MOST, width), "ctx", split_axis=0, concat_axis=0, tiled=True
    )
    return mix(returned.reshape(slots, width), coarse, fine, middle)


def solution(mesh):
    placed = (
        P(("groups", "ctx"), None),
        P(("groups", "ctx"), None),
        P(("groups", "ctx"), None),
        P(("groups", "ctx"), None),
        P(("groups", "ctx"), None),
        P("groups"),
        P("ctx", None),
        P(("groups", "ctx"), None),
        P(),
        P(("groups", "ctx"), None),
        P(("groups", "ctx"), None),
        P("ctx", None, None),
        P("ctx", None, None),
        P("ctx", None, None),
    )
    return jax.shard_map(
        on_device, mesh=mesh, in_specs=placed, out_specs=P(("groups", "ctx"), None), check_vma=False
    )
```

time: 366 us -> 171 us (0.47)
  blocking collectives: 180 us -> 18 us
  matrix products: 44.6 us -> 0 us
  starting transfers between devices: 4.17 us -> 41.4 us
  Pallas kernels: 0 us -> 31.7 us
  waiting for transfers between devices: 84.4 us -> 60.3 us
  other arithmetic: 19.6 us -> 0.5 us
  between operations: 14.2 us -> 0.15 us
    unnamed x1 -> x0, blocking collectives: 60 us -> none
    pmax x1 -> x0, blocking collectives: 59.5 us -> none  [on_device(): lax.pmax(local_peak.astype(jnp.bfloat16), 'ctx').astype(local_peak.dtype)]
    reduce_scatter x2 -> x0, waiting for transfers between devices: 53.9 us -> none  [the longest x1 53.9 us: on_device(): lax.psum_scatter(jnp.dot(attended, out_weight, preferred_element_type=jnp...]
    dot_general x12 -> x0, matrix products: 44.6 us -> none  [the longest x4 19.3 us: on_device(): jnp.einsum('rqd,pd->rqp', query_heads[:, kv_head], cached_keys[:, kv_head...]
    all_gather x2 -> x0, blocking collectives: 42.3 us -> none  [the longest x1 24.5 us: on_device(): lax.all_gather(new_key, 'ctx', axis=0, tiled=True)]
    all_to_all x1 -> x3, waiting for transfers between devices: 14.3 us -> 51 us  [the longest x1 22.9 us: on_device(): lax.all_to_all(sums, 'ctx', split_axis=0, concat_axis=0, axis_index_group...]
    pallas_call x0 -> x5, Pallas kernels: none -> 31.7 us  [the longest x1 21.6 us: attention(): pl.pallas_call(functools.partial(attention_body, chips, heads_chip, spare...]
    ppermute x0 -> x10, starting transfers between devices: none -> 27.5 us  [the longest x7 26.9 us: on_device(): lax.ppermute(queries, 'ctx', [(i, (i + CORES * shift) % devices) for i in...]
  transfers between devices with their start and end apart: 4 -> 13, of which waited for: 3 -> 7; matrix products, arithmetic and copies ran while one was open for 6% -> 1% of each run, Pallas kernels for 0% -> 0%
where the time goes in v1:
time: 171 us; the launch traced here: 170 us
  waiting for transfers between devices  60.3 us (35%)
  starting transfers between devices  41.4 us (24%)
  Pallas kernels  31.7 us (19%)
  blocking collectives  18 us (11%)
  local copies, waits for them, and re-layouts  17.6 us (10%)
    ppermute x7, starting transfers between devices, on_device(): lax.ppermute(queries, 'ctx', [(i, (i + CORES * shift) % devices) for i in...  26.9 us
    all_to_all x1, waiting for transfers between devices, on_device(): lax.all_to_all(sums, 'ctx', split_axis=0, concat_axis=0, axis_index_group...  22.9 us
    pallas_call x1, Pallas kernels, attention(): pl.pallas_call(functools.partial(attention_body, chips, heads_chip, spare...  21.6 us
    all_to_all x1, blocking collectives, on_device(): lax.all_to_all(outgoing.reshape(devices, experts * MOST, width), 'ctx', s...  18 us
    unnamed x36, local copies, waits for them, and re-layouts  16.4 us
    all_to_all x1, waiting for transfers between devices, on_device(): lax.all_to_all(produced.reshape(devices, experts * MOST, width), 'ctx', s...  14.3 us
    all_to_all x1, waiting for transfers between devices, on_device(): lax.all_to_all(share.reshape(chips, home_rows, width), 'ctx', split_axis=...  13.9 us
    pallas_call x1, Pallas kernels, run_experts(): pl.pallas_call(functools.partial(experts_body, experts), grid=(experts, h...  6.73 us
  transfers between devices with their start and end apart: 13, of which 7 were waited for; matrix products, arithmetic and copies ran while one was open for 1% of the time, Pallas kernels for 0%

profile of v1, /device:TPU:0, one launch (start us, length us, event | category | flops | bytes accessed | tf_op | source)
XLA Modules:
  0.0 169.7 jit_solution(17105971210167864557)
XLA Ops:
  0.0 0.5 collective-permute-start.7
  0.5 3.0 %collective-permute-start = (bf16[16,4096]{1,0:T(8,128)(2,1)}, bf16[16,4096]{1,0:T(8,128)(2,1)S(1)}, u32[]{:S(2)}, u32[]{:S(2)}) collective-permute-start(bf16[16,4096]{1,0:T(8,128)(2,1)} %refs_0_.1), channel_id=1, source_target_pairs={{0,2},{1,3},{2,4},{3,5},{4,6},{5,7},{6,8},{7,9},{8,10},{9,11},{10,... | collective-permute-start | bytes 393224 | tf_op jit(solution)/shard_map/ppermute | solution.py:303
  3.5 1.6 collective-permute-start.1
  5.1 2.5 %collective-permute-start.2 = (bf16[16,4096]{1,0:T(8,128)(2,1)}, bf16[16,4096]{1,0:T(8,128)(2,1)S(1)}, u32[]{:S(2)}, u32[]{:S(2)}) collective-permute-start(bf16[16,4096]{1,0:T(8,128)(2,1)} %refs_0_.1), channel_id=1, source_target_pairs={{0,6},{1,7},{2,8},{3,9},{4,10},{5,11},{6,12},{7,13},{8,14},{9,15},... | collective-permute-start | bytes 393224 | tf_op jit(solution)/shard_map/ppermute | solution.py:303
  7.6 3.5 %collective-permute-done.refs_1_ = bf16[16,4096]{1,0:T(8,128)(2,1)S(1)} collective-permute-done((bf16[16,4096]{1,0:T(8,128)(2,1)}, bf16[16,4096]{1,0:T(8,128)(2,1)S(1)}, u32[]{:S(2)}, u32[]{:S(2)}) %collective-permute-start) | collective-permute-done | bytes 131104 | tf_op jit(solution)/shard_map/ppermute | solution.py:303
  11.1 0.9 collective-permute-start.3
  12.0 14.0 %collective-permute-start.4 = (bf16[16,4096]{1,0:T(8,128)(2,1)}, bf16[16,4096]{1,0:T(8,128)(2,1)}, u32[]{:S(2)}, u32[]{:S(2)}) collective-permute-start(bf16[16,4096]{1,0:T(8,128)(2,1)} %refs_0_.1), channel_id=1, source_target_pairs={{0,10},{1,11},{2,12},{3,13},{4,14},{5,15},{6,0},{7,1},{8,2},{9,3},... | collective-permute-start | bytes 393224 | tf_op jit(solution)/shard_map/ppermute | solution.py:303
  26.1 0.6 copy-done.8
  26.7 3.7 %collective-permute-start.5 = (bf16[16,4096]{1,0:T(8,128)(2,1)}, bf16[16,4096]{1,0:T(8,128)(2,1)}, u32[]{:S(2)}, u32[]{:S(2)}) collective-permute-start(bf16[16,4096]{1,0:T(8,128)(2,1)} %refs_0_.1), channel_id=1, source_target_pairs={{0,12},{1,13},{2,14},{3,15},{4,0},{5,1},{6,2},{7,3},{8,4},{9,5},{1... | collective-permute-start | bytes 393224 | tf_op jit(solution)/shard_map/ppermute | solution.py:303
  30.4 0.7 copy-done.10
  31.1 1.2 collective-permute-start.6
  32.3 0.8 reshape.35
  33.1 0.1 reshape.36.refs_14_
  33.2 0.1 pad_add_fusion.place
  33.2 1.4 collective-permute-done.5.refs_6_
  34.6 1.8 %collective-permute-done.6.refs_7_ = bf16[16,4096]{1,0:T(8,128)(2,1)} collective-permute-done((bf16[16,4096]{1,0:T(8,128)(2,1)}, bf16[16,4096]{1,0:T(8,128)(2,1)}, u32[]{:S(2)}, u32[]{:S(2)}) %collective-permute-start.6) | collective-permute-done | bytes 131104 | tf_op jit(solution)/shard_map/ppermute | solution.py:303
  36.4 1.2 copy-done.5
  37.6 1.2 copy-done.6
  38.8 0.9 copy-done.7
  39.7 0.9 copy-done.9
  40.6 0.9 copy-done.11
  41.5 0.7 copy-done.12
  42.3 0.7 copy-done.13
  43.0 21.6 %attention.1 = bf16[8,528,128]{2,1,0:T(8,128)(2,1)} custom-call(s32[4]{0:T(128)S(1)} %pad_add_fusion.place, bf16[16,4096]{1,0:T(8,128)(2,1)S(1)} %copy-done.7, bf16[16,4096]{1,0:T(8,128)(2,1)S(1)} %collective-permute-done.refs_1_, bf16[16,4096]{1,0:T(8,128)(2,1)S(1)} %collective-permute-done.1.refs_2_, bf16[16,4096]{1,0:T(8,128)(2,1)S(1)} %copy-done.9, ...), custom_call_target="tpu_custom_call" | custom-call | flops 4328521728 | bytes 8388608 | tf_op jit(solution)/shard_map/attention/pallas_call | solution.py:107
  64.6 6.3 %all-to-all-start = ((bf16[8,528,128]{2,1,0:T(8,128)(2,1)}), bf16[8,528,128]{2,1,0:T(8,128)(2,1)S(1)}, u32[]{:S(2)}, u32[]{:S(2)}) async-start(bf16[8,528,128]{2,1,0:T(8,128)(2,1)} %attention.1), calls=%async_computation | async-start | bytes 2162688 | tf_op jit(solution)/shard_map/all_to_all | solution.py:342
  70.9 0.1 collective-permute-start.9
  71.0 2.6 %collective-permute-done.9.weight_other = bf16[256,2048]{1,0:T(8,128)(2,1)S(1)} collective-permute-done((bf16[256,2048]{1,0:T(8,128)(2,1)S(1)}, bf16[256,2048]{1,0:T(8,128)(2,1)S(1)}, u32[]{:S(2)}, u32[]{:S(2)}) %collective-permute-start.9) | collective-permute-done | bytes 1048608 | tf_op jit(solution)/shard_map/ppermute | solution.py:312
  73.6 22.9 %all-to-all-done.parts = bf16[8,528,128]{2,1,0:T(8,128)(2,1)S(1)} async-done(((bf16[8,528,128]{2,1,0:T(8,128)(2,1)}), bf16[8,528,128]{2,1,0:T(8,128)(2,1)S(1)}, u32[]{:S(2)}, u32[]{:S(2)}) %all-to-all-start) | async-done | bytes 1081376 | tf_op jit(solution)/shard_map/all_to_all | solution.py:342
  96.5 2.1 %project.1 = bf16[128,2048]{1,0:T(8,128)(2,1)} custom-call(s32[4]{0:T(128)S(1)} %pad_add_fusion.place, bf16[8,528,128]{2,1,0:T(8,128)(2,1)S(1)} %all-to-all-done.parts, bf16[256,2048]{1,0:T(8,128)(2,1)S(1)} %copy-done.3, bf16[256,2048]{1,0:T(8,128)(2,1)S(1)} %collective-permute-done.9.weight_other), custom_call_target="tpu_custom_call" | custom-call | flops 268435456 | bytes 4194304 | tf_op jit(solution)/shard_map/project/pallas_call | solution.py:158
  98.6 3.5 %all-to-all-start.1 = ((bf16[8,16,2048]{2,1,0:T(8,128)(2,1)}), bf16[8,16,2048]{2,1,0:T(8,128)(2,1)S(1)}, u32[]{:S(2)}, u32[]{:S(2)}) async-start(bf16[8,16,2048]{2,1,0:T(8,128)(2,1)} %bitcast.4), calls=%async_computation.1 | async-start | bytes 1048576 | tf_op jit(solution)/shard_map/all_to_all | solution.py:346
  102.1 0.1 copy.21
  102.1 0.1 eq.30
  102.2 0.2 convert_reduce_fusion
  102.4 0.1 reduce_sum.21
  102.5 0.1 fusion
  102.6 0.1 copy.23
  102.8 13.9 %all-to-all-done.1.parts = bf16[8,16,2048]{2,1,0:T(8,128)(2,1)S(1)} async-done(((bf16[8,16,2048]{2,1,0:T(8,128)(2,1)}), bf16[8,16,2048]{2,1,0:T(8,128)(2,1)S(1)}, u32[]{:S(2)}, u32[]{:S(2)}) %all-to-all-start.1) | async-done | bytes 524320 | tf_op jit(solution)/shard_map/all_to_all | solution.py:346
  116.7 0.4 norm_and_dispatch.1
  117.1 18.0 %all_to_all.20 = bf16[16,8,2048]{2,1,0:T(8,128)(2,1)S(1)} all-to-all(bf16[16,8,2048]{2,1,0:T(8,128)(2,1)S(1)} %bitcast.12), channel_id=1, replica_groups=mesh['groups'=2,'ctx'=16] {'ctx'}, dimensions={0} | all-to-all | bytes 1048576 | tf_op jit(solution)/shard_map/all_to_all | solution.py:355
  135.1 2.8 %copy-done = bf16[2,2048,768]{2,1,0:T(8,128)(2,1)S(1)} copy-done((bf16[2,2048,768]{2,1,0:T(8,128)(2,1)S(1)}, bf16[2,2048,768]{2,1,0:T(8,128)(2,1)}, u32[]{:S(2)}) %copy-start) | copy-done | bytes 6291480
  137.9 2.8 %copy-done.1 = bf16[2,2048,768]{2,1,0:T(8,128)(2,1)S(1)} copy-done((bf16[2,2048,768]{2,1,0:T(8,128)(2,1)S(1)}, bf16[2,2048,768]{2,1,0:T(8,128)(2,1)}, u32[]{:S(2)}) %copy-start.1) | copy-done | bytes 6291480
  140.7 2.8 %copy-done.2 = bf16[2,768,2048]{2,1,0:T(8,128)(2,1)S(1)} copy-done((bf16[2,768,2048]{2,1,0:T(8,128)(2,1)S(1)}, bf16[2,768,2048]{2,1,0:T(8,128)(2,1)}, u32[]{:S(2)}) %copy-start.2) | copy-done | bytes 6291480
  143.5 6.7 %experts.1 = bf16[128,2048]{1,0:T(8,128)(2,1)} custom-call(bf16[128,2048]{1,0:T(8,128)(2,1)S(1)} %bitcast.10, bf16[2,2048,768]{2,1,0:T(8,128)(2,1)S(1)} %copy-done, bf16[2,2048,768]{2,1,0:T(8,128)(2,1)S(1)} %copy-done.1, bf16[2,768,2048]{2,1,0:T(8,128)(2,1)S(1)} %copy-done.2), custom_call_target="tpu_custom_call" | custom-call | flops 2415919104 | bytes 18874368 | tf_op jit(solution)/shard_map/experts/pallas_call | solution.py:233
  150.2 4.1 %all-to-all-start.3 = ((bf16[16,8,2048]{2,1,0:T(8,128)(2,1)}), bf16[16,8,2048]{2,1,0:T(8,128)(2,1)S(1)}, u32[]{:S(2)}, u32[]{:S(2)}) async-start(bf16[16,8,2048]{2,1,0:T(8,128)(2,1)} %bitcast.8), calls=%async_computation.3 | async-start | bytes 1048576 | tf_op jit(solution)/shard_map/all_to_all | solution.py:359
  154.3 0.1 copy.24
  154.4 0.1 select_reduce_fusion
  154.5 14.3 %all-to-all-done.3 = bf16[16,8,2048]{2,1,0:T(8,128)(2,1)S(1)} async-done(((bf16[16,8,2048]{2,1,0:T(8,128)(2,1)}), bf16[16,8,2048]{2,1,0:T(8,128)(2,1)S(1)}, u32[]{:S(2)}, u32[]{:S(2)}) %all-to-all-start.3) | async-done | bytes 524320 | tf_op jit(solution)/shard_map/all_to_all | solution.py:359
  168.8 0.9 mix.1
  (34 shorter events, 0.2 us)
Async XLA Ops:
  0.0 36.4 %collective-permute-start.7 = (bf16[1024,512]{1,0:T(8,128)(2,1)}, bf16[1024,512]{1,0:T(8,128)(2,1)S(1)}, u32[]{:S(2)}, u32[]{:S(2)}) collective-permute-start(bf16[1024,512]{1,0:T(8,128)(2,1)} %refs_8_.1), channel_id=1, source_target_pairs={{0,1},{1,0},{2,3},{3,2},{4,5},{5,4},{6,7},{7,6},{8,9},{9,8},{10,11... | collective-permute-start | bytes 3145736 | tf_op jit(solution)/shard_map/ppermute | solution.py:310
  0.5 35.9 %collective-permute-start.8 = (bf16[1024,512]{1,0:T(8,128)(2,1)}, bf16[1024,512]{1,0:T(8,128)(2,1)S(1)}, u32[]{:S(2)}, u32[]{:S(2)}) collective-permute-start(bf16[1024,512]{1,0:T(8,128)(2,1)} %refs_10_.1), channel_id=1, source_target_pairs={{0,1},{1,0},{2,3},{3,2},{4,5},{5,4},{6,7},{7,6},{8,9},{9,8},{10,11... | collective-permute-start | bytes 3145736 | tf_op jit(solution)/shard_map/ppermute | solution.py:311
  0.5 10.6 %collective-permute-start = (bf16[16,4096]{1,0:T(8,128)(2,1)}, bf16[16,4096]{1,0:T(8,128)(2,1)S(1)}, u32[]{:S(2)}, u32[]{:S(2)}) collective-permute-start(bf16[16,4096]{1,0:T(8,128)(2,1)} %refs_0_.1), channel_id=1, source_target_pairs={{0,2},{1,3},{2,4},{3,5},{4,6},{5,7},{6,8},{7,9},{8,10},{9,11},{10,... | collective-permute-start | bytes 393224 | tf_op jit(solution)/shard_map/ppermute | solution.py:303
  3.5 8.5 %collective-permute-start.1 = (bf16[16,4096]{1,0:T(8,128)(2,1)}, bf16[16,4096]{1,0:T(8,128)(2,1)S(1)}, u32[]{:S(2)}, u32[]{:S(2)}) collective-permute-start(bf16[16,4096]{1,0:T(8,128)(2,1)} %refs_0_.1), channel_id=1, source_target_pairs={{0,4},{1,5},{2,6},{3,7},{4,8},{5,9},{6,10},{7,11},{8,12},{9,13},{1... | collective-permute-start | bytes 393224 | tf_op jit(solution)/shard_map/ppermute | solution.py:303
  5.1 21.0 %collective-permute-start.2 = (bf16[16,4096]{1,0:T(8,128)(2,1)}, bf16[16,4096]{1,0:T(8,128)(2,1)S(1)}, u32[]{:S(2)}, u32[]{:S(2)}) collective-permute-start(bf16[16,4096]{1,0:T(8,128)(2,1)} %refs_0_.1), channel_id=1, source_target_pairs={{0,6},{1,7},{2,8},{3,9},{4,10},{5,11},{6,12},{7,13},{8,14},{9,15},... | collective-permute-start | bytes 393224 | tf_op jit(solution)/shard_map/ppermute | solution.py:303
  11.1 19.3 %collective-permute-start.3 = (bf16[16,4096]{1,0:T(8,128)(2,1)}, bf16[16,4096]{1,0:T(8,128)(2,1)S(1)}, u32[]{:S(2)}, u32[]{:S(2)}) collective-permute-start(bf16[16,4096]{1,0:T(8,128)(2,1)} %refs_0_.1), channel_id=1, source_target_pairs={{0,8},{1,9},{2,10},{3,11},{4,12},{5,13},{6,14},{7,15},{8,0},{9,1},... | collective-permute-start | bytes 393224 | tf_op jit(solution)/shard_map/ppermute | solution.py:303
  12.0 21.2 %collective-permute-start.4 = (bf16[16,4096]{1,0:T(8,128)(2,1)}, bf16[16,4096]{1,0:T(8,128)(2,1)}, u32[]{:S(2)}, u32[]{:S(2)}) collective-permute-start(bf16[16,4096]{1,0:T(8,128)(2,1)} %refs_0_.1), channel_id=1, source_target_pairs={{0,10},{1,11},{2,12},{3,13},{4,14},{5,15},{6,0},{7,1},{8,2},{9,3},... | collective-permute-start | bytes 393224 | tf_op jit(solution)/shard_map/ppermute | solution.py:303
  26.1 0.7 copy-start.8
  26.7 7.9 %collective-permute-start.5 = (bf16[16,4096]{1,0:T(8,128)(2,1)}, bf16[16,4096]{1,0:T(8,128)(2,1)}, u32[]{:S(2)}, u32[]{:S(2)}) collective-permute-start(bf16[16,4096]{1,0:T(8,128)(2,1)} %refs_0_.1), channel_id=1, source_target_pairs={{0,12},{1,13},{2,14},{3,15},{4,0},{5,1},{6,2},{7,3},{8,4},{9,5},{1... | collective-permute-start | bytes 393224 | tf_op jit(solution)/shard_map/ppermute | solution.py:303
  30.4 0.7 copy-start.10
  31.1 5.3 %collective-permute-start.6 = (bf16[16,4096]{1,0:T(8,128)(2,1)}, bf16[16,4096]{1,0:T(8,128)(2,1)}, u32[]{:S(2)}, u32[]{:S(2)}) collective-permute-start(bf16[16,4096]{1,0:T(8,128)(2,1)} %refs_0_.1), channel_id=1, source_target_pairs={{0,14},{1,15},{2,0},{3,1},{4,2},{5,3},{6,4},{7,5},{8,6},{9,7},{10,... | collective-permute-start | bytes 393224 | tf_op jit(solution)/shard_map/ppermute | solution.py:303
  33.2 37.7 %copy-start.3 = (bf16[256,2048]{1,0:T(8,128)(2,1)S(1)}, bf16[256,2048]{1,0:T(8,128)(2,1)}, u32[]{:S(2)}) copy-start(bf16[256,2048]{1,0:T(8,128)(2,1)} %weight_own.1) | copy-start | bytes 3145732
  36.4 1.2 copy-start.5
  37.6 1.2 copy-start.6
  38.8 0.9 copy-start.7
  39.7 0.9 copy-start.9
  40.6 0.9 copy-start.11
  41.5 0.7 copy-start.12
  42.3 0.7 copy-start.13
  64.6 37.5 %copy-start.14 = (s32[16,8]{0,1:T(8,128)S(1)}, s32[16,8]{0,1:T(8,128)}, u32[]{:S(2)}) copy-start(s32[16,8]{0,1:T(8,128)} %param.23) | copy-start | bytes 1540
  64.6 38.2 %copy-start.15 = (bf16[2048]{0:T(1024)(128)(2,1)S(1)}, bf16[2048]{0:T(1024)(128)(2,1)}, u32[]{:S(2)}) copy-start(bf16[2048]{0:T(1024)(128)(2,1)} %param.22) | copy-start | bytes 12292
  64.6 52.0 %copy-start.4 = (bf16[16,2048]{1,0:T(8,128)(2,1)S(1)}, bf16[16,2048]{1,0:T(8,128)(2,1)}, u32[]{:S(2)}) copy-start(bf16[16,2048]{1,0:T(8,128)(2,1)} %residual.1) | copy-start | bytes 196612
  64.6 31.9 %all-to-all-start = ((bf16[8,528,128]{2,1,0:T(8,128)(2,1)}), bf16[8,528,128]{2,1,0:T(8,128)(2,1)S(1)}, u32[]{:S(2)}, u32[]{:S(2)}) async-start(bf16[8,528,128]{2,1,0:T(8,128)(2,1)} %attention.1), calls=%async_computation | async-start | bytes 2162688 | tf_op jit(solution)/shard_map/all_to_all | solution.py:342
  70.9 2.7 %collective-permute-start.9 = (bf16[256,2048]{1,0:T(8,128)(2,1)S(1)}, bf16[256,2048]{1,0:T(8,128)(2,1)S(1)}, u32[]{:S(2)}, u32[]{:S(2)}) collective-permute-start(bf16[256,2048]{1,0:T(8,128)(2,1)S(1)} %copy-done.3), channel_id=1, source_target_pairs={{0,1},{1,0},{2,3},{3,2},{4,5},{5,4},{6,7},{7,6},{8,9},{9,8},{10,11... | collective-permute-start | bytes 3145736 | tf_op jit(solution)/shard_map/ppermute | solution.py:312
  98.6 18.1 %all-to-all-start.1 = ((bf16[8,16,2048]{2,1,0:T(8,128)(2,1)}), bf16[8,16,2048]{2,1,0:T(8,128)(2,1)S(1)}, u32[]{:S(2)}, u32[]{:S(2)}) async-start(bf16[8,16,2048]{2,1,0:T(8,128)(2,1)} %bitcast.4), calls=%async_computation.1 | async-start | bytes 1048576 | tf_op jit(solution)/shard_map/all_to_all | solution.py:346
  135.1 2.8 %copy-start = (bf16[2,2048,768]{2,1,0:T(8,128)(2,1)S(1)}, bf16[2,2048,768]{2,1,0:T(8,128)(2,1)}, u32[]{:S(2)}) copy-start(bf16[2,2048,768]{2,1,0:T(8,128)(2,1)} %w_gate.1) | copy-start | bytes 18874372
  137.9 2.8 %copy-start.1 = (bf16[2,2048,768]{2,1,0:T(8,128)(2,1)S(1)}, bf16[2,2048,768]{2,1,0:T(8,128)(2,1)}, u32[]{:S(2)}) copy-start(bf16[2,2048,768]{2,1,0:T(8,128)(2,1)} %w_up.1) | copy-start | bytes 18874372
  140.7 2.8 %copy-start.2 = (bf16[2,768,2048]{2,1,0:T(8,128)(2,1)S(1)}, bf16[2,768,2048]{2,1,0:T(8,128)(2,1)}, u32[]{:S(2)}) copy-start(bf16[2,768,2048]{2,1,0:T(8,128)(2,1)} %w_down.1) | copy-start | bytes 18874372
  143.5 10.8 %copy-start.16 = (f32[16,8]{0,1:T(8,128)S(1)}, f32[16,8]{0,1:T(8,128)}, u32[]{:S(2)}) copy-start(f32[16,8]{0,1:T(8,128)} %param.24) | copy-start | bytes 1540
  150.2 18.6 %all-to-all-start.3 = ((bf16[16,8,2048]{2,1,0:T(8,128)(2,1)}), bf16[16,8,2048]{2,1,0:T(8,128)(2,1)S(1)}, u32[]{:S(2)}, u32[]{:S(2)}) async-start(bf16[16,8,2048]{2,1,0:T(8,128)(2,1)} %bitcast.8), calls=%async_computation.3 | async-start | bytes 1048576 | tf_op jit(solution)/shard_map/all_to_all | solution.py:359

commit v2 on v1

v2 whole, which is shorter than its diff:
```python
import functools
import math

import jax
import jax.numpy as jnp
from jax import lax
from jax.experimental import pallas as pl
from jax.experimental.pallas import tpu as pltpu
from jax.sharding import PartitionSpec as P

HD = 128
MOST = 4
CORES = 2
STATS = 16
MASKED = -1e30
FLOOR = -1e20
LOG2E = math.log2(math.e)
MIB = 1024 * 1024
F32 = jnp.float32
BF16 = jnp.bfloat16


def nt_dot(a, b):
    return lax.dot_general(a, b, (((1,), (1,)), ((), ())), preferred_element_type=F32)


def nn_dot(a, b):
    return lax.dot_general(a, b, (((1,), (0,)), ((), ())), preferred_element_type=F32)


def attention_body(shape, place, own_q, other_q, key_own, key_other, value_own, value_other, key_fresh, value_fresh, lens, out, *scratch):
    owners, heads_owner, home_rows, rows, cache_here, step = shape
    q_rows, v_turned, hidden, scores, probs = scratch
    chip, start_own, start_other, pair_place = place[0], place[1], place[2], place[4]
    rings = rows // home_rows // 2

    @pl.when(pl.program_id(0) == 0)
    def _():
        for part, start in enumerate((start_own, start_other)):
            positions = start + lax.broadcasted_iota(jnp.int32, (cache_here, rows), 0)
            hidden[part * cache_here : (part + 1) * cache_here, :] = jnp.where(
                positions < lens[...], 0.0, MASKED
            )
        token = lax.broadcasted_iota(jnp.int32, (home_rows, rows), 0)
        column = lax.broadcasted_iota(jnp.int32, (home_rows, rows), 1)
        hidden[2 * cache_here :, :] = jnp.where(token + chip * home_rows == column, 0.0, MASKED)
        v_turned[HD:, :] = jnp.ones_like(v_turned[HD:, :])

    v_turned[:HD, :cache_here] = value_own[...].T
    v_turned[:HD, cache_here:] = value_other[...].T
    value_new = value_fresh[...].astype(F32).T.astype(BF16)
    for ring in range(rings):
        taken = slice(ring * home_rows, (ring + 1) * home_rows)
        for piece, side in ((own_q, pair_place), (other_q, 1 - pair_place)):
            spot = pl.multiple_of((2 * ring + side) * home_rows, home_rows)
            q_rows[pl.ds(spot, home_rows), :] = piece[taken, :]

    heads = owners * heads_owner
    wide = min(2, heads)
    groups = heads // wide
    factor = LOG2E / math.sqrt(HD)
    pieces = [(key_own, 0, i) for i in range(0, cache_here, step)]
    pieces += [(key_other, cache_here, i) for i in range(0, cache_here, step)]
    queries, highest, fresh = [], [], []
    for group in range(groups):
        scaled = jnp.concatenate(
            [q_rows[:, (group * wide + k) * HD : (group * wide + k + 1) * HD] for k in range(wide)], axis=0
        ).astype(F32) * factor
        coarse = scaled.astype(BF16)
        fine = (scaled - coarse.astype(F32)).astype(BF16)
        queries.append(jnp.concatenate([coarse, fine], axis=1))

    def score(group, piece):
        source, base, i = piece
        keys = source[i : i + step, :]
        s = nt_dot(jnp.concatenate([keys, keys], axis=1), queries[group])
        s = s + jnp.concatenate([hidden[base + i : base + i + step, :]] * wide, axis=1)
        scores[group % 2, base + i : base + i + step, :] = s
        return jnp.max(s.reshape(step // 8, 8, wide * rows), axis=0)

    def weigh(group, piece, lift):
        _, base, i = piece
        s = scores[group % 2, base + i : base + i + step, :]
        probs[group % 2, base + i : base + i + step, :] = jnp.exp2(s - lift).astype(BF16)

    def finish_peak(group, run):
        keys = key_fresh[...]
        s = nt_dot(jnp.concatenate([keys, keys], axis=1), queries[group])
        s = s + jnp.concatenate([hidden[2 * cache_here :, :]] * wide, axis=1)
        peak = jnp.maximum(jnp.max(run, axis=0, keepdims=True), jnp.max(s, axis=0, keepdims=True))
        peak = jnp.maximum(peak, FLOOR).astype(BF16).astype(F32)
        return peak, jnp.exp2(s - peak).astype(BF16)

    stats = [[None] * (3 * heads_owner) for _ in range(owners)]

    def total(group, peak, p_new):
        sums = nn_dot(v_turned[...], probs[group % 2])
        numer = sums[:HD] + nn_dot(value_new, p_new)
        denom = sums[HD : HD + 1] + jnp.sum(p_new.astype(F32), axis=0, keepdims=True)
        for k in range(wide):
            owner, h = divmod(group * wide + k, heads_owner)
            cols = slice(k * rows, (k + 1) * rows)
            out[owner, h * HD : (h + 1) * HD, :] = numer[:, cols].astype(BF16)
            high = denom[:, cols].astype(BF16).astype(F32)
            stats[owner][h] = peak[:, cols]
            stats[owner][heads_owner + h] = high
            stats[owner][2 * heads_owner + h] = denom[:, cols] - high

    previous = None
    for group in range(groups + 1):
        run = None
        for piece in pieces:
            if group < groups:
                top = score(group, piece)
                run = top if run is None else jnp.maximum(run, top)
            if previous is not None:
                weigh(group - 1, piece, previous[0])
        if previous is not None:
            total(group - 1, *previous)
        if group < groups:
            previous = finish_peak(group, run)
    for owner in range(owners):
        filled = stats[owner] + [jnp.zeros_like(stats[owner][0])] * (STATS - len(stats[owner]))
        out[owner, heads_owner * HD :, :] = jnp.concatenate(filled, axis=0).astype(BF16)


def attention(place, own_q, other_q, keys, values, new_key, new_value, lens, chips, kv_heads):
    rows = lens.shape[1]
    home_rows = new_key.shape[0]
    cache_here = keys[0].shape[0]
    heads_owner = own_q.shape[1] // HD // chips
    owners = chips // kv_heads
    height = heads_owner * HD + STATS
    step = 256
    wide = min(2, owners * heads_owner)
    kv = lambda g, place: (0, g)
    shape = (owners, heads_owner, home_rows, rows, cache_here, step)
    work = rows * heads_owner * chips * 2 * cache_here
    return pl.pallas_call(
        functools.partial(attention_body, shape),
        grid_spec=pltpu.PrefetchScalarGridSpec(
            num_scalar_prefetch=1,
            grid=(kv_heads,),
            in_specs=[pl.BlockSpec((own_q.shape[0], owners * heads_owner * HD), kv)] * 2
            + [pl.BlockSpec((cache_here, HD), kv)] * 4
            + [pl.BlockSpec((home_rows, HD), kv)] * 2
            + [pl.BlockSpec((1, rows), lambda g, place: (0, 0))],
            out_specs=pl.BlockSpec((owners, height, rows), lambda g, place: (g, 0, 0)),
            scratch_shapes=[
                pltpu.VMEM((rows, owners * heads_owner * HD), BF16),
                pltpu.VMEM((HD + STATS, 2 * cache_here), BF16),
                pltpu.VMEM((2 * cache_here + home_rows, rows), F32),
                pltpu.VMEM((2, 2 * cache_here, wide * rows), F32),
                pltpu.VMEM((2, 2 * cache_here, wide * rows), BF16),
            ],
        ),
        out_shape=jax.ShapeDtypeStruct((chips, height, rows), BF16),
        compiler_params=pltpu.CompilerParams(vmem_limit_bytes=56 * MIB),
        cost_estimate=pl.CostEstimate(
            flops=6 * work * HD, bytes_accessed=8 * MIB, transcendentals=work
        ),
        name="attention",
    )(place, own_q, other_q, *keys, *values, new_key, new_value, lens)


def project_body(place, *refs):
    *chunks, weight_own, weight_other, out, turned = refs
    core = place[3]
    for chunk, parts in enumerate(chunks):
        chips, height, _ = parts.shape
        base = height - STATS
        heads = base // HD
        stats = parts[:, base:, :].astype(F32)
        peaks = stats[:, :heads]
        share = jnp.exp2(peaks - jnp.max(peaks, axis=0, keepdims=True))
        totals = stats[:, heads : 2 * heads] + stats[:, 2 * heads : 3 * heads]
        denom = jnp.sum(share * totals, axis=0)
        for h in range(heads):
            numer = None
            for s in range(chips):
                term = parts[s, h * HD : (h + 1) * HD, :].astype(F32) * share[s, h : h + 1, :]
                numer = term if numer is None else numer + term
            turned[chunk, :, h * HD : (h + 1) * HD] = (numer / denom[h : h + 1, :]).T.astype(BF16)
    product = nn_dot(turned[core], weight_own[...]) + nn_dot(turned[1 - core], weight_other[...])
    out[...] = product.astype(BF16)


def project(place, chunks, weight_own, weight_other):
    rows = chunks[0].shape[2]
    depth, width = weight_own.shape
    vmem = pl.BlockSpec(memory_space=pltpu.VMEM)
    return pl.pallas_call(
        project_body,
        in_specs=[pl.BlockSpec(memory_space=pltpu.SMEM)] + [vmem] * (len(chunks) + 2),
        out_specs=vmem,
        out_shape=jax.ShapeDtypeStruct((rows, width), BF16),
        scratch_shapes=[pltpu.VMEM((CORES, rows, depth), BF16)],
        compiler_params=pltpu.CompilerParams(vmem_limit_bytes=32 * MIB),
        cost_estimate=pl.CostEstimate(
            flops=4 * rows * width * depth, bytes_accessed=4 * MIB, transcendentals=0
        ),
        name="project",
    )(place, *chunks, weight_own, weight_other)


def norm_body(parts, residual, gain, chooser, middle_out, sent):
    total = parts[0].astype(F32)
    for s in range(1, parts.shape[0]):
        total = total + parts[s].astype(F32)
    middle = (residual[...].astype(F32) + total).astype(BF16)
    middle_out[...] = middle
    middle = middle.astype(F32)
    inv_rms = lax.rsqrt(jnp.mean(middle * middle, axis=-1, keepdims=True) + 1e-06)
    normed = (middle * inv_rms * gain[...].astype(F32)).astype(BF16)
    sent[...] = nn_dot(chooser[...], normed).astype(BF16)


def norm_and_dispatch(parts, residual, gain, chooser):
    vmem = pl.BlockSpec(memory_space=pltpu.VMEM)
    rows, width = residual.shape
    return pl.pallas_call(
        norm_body,
        in_specs=[vmem] * 4,
        out_specs=[vmem] * 2,
        out_shape=[
            jax.ShapeDtypeStruct((rows, width), BF16),
            jax.ShapeDtypeStruct((chooser.shape[0], width), BF16),
        ],
        compiler_params=pltpu.CompilerParams(vmem_limit_bytes=24 * MIB),
        cost_estimate=pl.CostEstimate(
            flops=2 * chooser.shape[0] * rows * width, bytes_accessed=2 * MIB, transcendentals=0
        ),
        name="norm_and_dispatch",
    )(parts, residual, gain, chooser)


def experts_body(experts, arrived, w_gate, w_up, w_down, out, total):
    expert, chunk = pl.program_id(0), pl.program_id(1)
    rows = arrived.shape[0]
    gate = nn_dot(arrived[...], w_gate[0])
    upward = nn_dot(arrived[...], w_up[0])
    hidden = gate / (1.0 + jnp.exp(-gate)) * upward
    slot = lax.broadcasted_iota(jnp.int32, hidden.shape, 0)
    mine = lax.rem(slot, experts * MOST) // MOST == expert
    hidden = jnp.where(mine, hidden, 0.0).astype(BF16)
    product = nn_dot(hidden, w_down[0])
    first = (expert == 0) & (chunk == 0)
    last = (expert == pl.num_programs(0) - 1) & (chunk == pl.num_programs(1) - 1)

    @pl.when(first)
    def _():
        total[...] = product

    @pl.when(jnp.logical_not(first))
    def _():
        total[...] += product

    @pl.when(last)
    def _():
        out[...] = total[...].astype(BF16)


def run_experts(arrived, w_gate, w_up, w_down):
    rows, width = arrived.shape
    experts, _, hidden = w_gate.shape
    block = 256
    return pl.pallas_call(
        functools.partial(experts_body, experts),
        grid=(experts, hidden // block),
        in_specs=[
            pl.BlockSpec((rows, width), lambda e, f: (0, 0)),
            pl.BlockSpec((1, width, block), lambda e, f: (e, 0, f)),
            pl.BlockSpec((1, width, block), lambda e, f: (e, 0, f)),
            pl.BlockSpec((1, block, width), lambda e, f: (e, f, 0)),
        ],
        out_specs=pl.BlockSpec((rows, width), lambda e, f: (0, 0)),
        out_shape=jax.ShapeDtypeStruct((rows, width), BF16),
        scratch_shapes=[pltpu.VMEM((rows, width), F32)],
        compiler_params=pltpu.CompilerParams(vmem_limit_bytes=60 * MIB),
        cost_estimate=pl.CostEstimate(
            flops=6 * rows * width * experts * hidden,
            bytes_accessed=6 * width * experts * hidden,
            transcendentals=rows * experts * hidden,
        ),
        name="experts",
    )(arrived, w_gate, w_up, w_down)


def mix_body(returned, coarse, fine, middle, out):
    values = returned[...]
    mixed = nn_dot(coarse[...], values) + nn_dot(fine[...], values)
    out[...] = (middle[...].astype(F32) + mixed).astype(BF16)


def mix(returned, coarse, fine, middle):
    vmem = pl.BlockSpec(memory_space=pltpu.VMEM)
    return pl.pallas_call(
        mix_body,
        in_specs=[vmem] * 4,
        out_specs=vmem,
        out_shape=jax.ShapeDtypeStruct(middle.shape, BF16),
        compiler_params=pltpu.CompilerParams(vmem_limit_bytes=16 * MIB),
        name="mix",
    )(returned, coarse, fine, middle)


def on_device(
    queries,
    new_key,
    new_value,
    key_cache,
    value_cache,
    cache_len,
    out_weight,
    residual,
    norm_gain,
    expert_ids,
    route_weight,
    w_gate,
    w_up,
    w_down,
):
    devices = lax.axis_size("ctx")
    chips = devices // CORES
    index = lax.axis_index("ctx")
    chip, core = index // CORES, index % CORES
    home_rows, width = residual.shape
    top = expert_ids.shape[1]
    heads_here = out_weight.shape[0] // HD
    cache_here = key_cache.shape[0]
    same_core = [[CORES * j + c for j in range(chips)] for c in range(CORES)]
    swap = [(i, i ^ 1) for i in range(devices)]

    along = [
        [CORES * (2 * ring + side) + c for ring in range(chips // 2)]
        for side in range(2)
        for c in range(CORES)
    ]
    across = [(i, i ^ CORES) for i in range(devices)]

    key_other = lax.ppermute(key_cache, "ctx", swap)
    value_other = lax.ppermute(value_cache, "ctx", swap)
    by_owner = queries.reshape(home_rows, chips, CORES, heads_here * HD)
    query_chunks = []
    for chunk in range(CORES):
        part = by_owner[:, :, chunk].reshape(home_rows, chips * heads_here * HD)
        mine = lax.all_gather(part, "ctx", axis=0, axis_index_groups=along, tiled=True)
        query_chunks.append((mine, lax.ppermute(mine, "ctx", across)))
    weight_other = lax.ppermute(out_weight, "ctx", swap)

    place = jnp.stack([chip, index * cache_here, (index ^ 1) * cache_here, core, chip % 2]).astype(jnp.int32)
    lens = lax.dynamic_index_in_dim(
        cache_len.reshape(chips, CORES, home_rows), core, axis=1, keepdims=False
    ).reshape(1, chips * home_rows)

    flat_ids = expert_ids.reshape(-1)
    picks = jnp.arange(flat_ids.shape[0])
    earlier = (flat_ids[:, None] == flat_ids[None, :]) & (picks[None, :] < picks[:, None])
    target = (flat_ids * MOST + jnp.sum(earlier, axis=1, dtype=jnp.int32)).reshape(home_rows, top)
    experts = w_gate.shape[0]
    slots = experts * devices * MOST
    takes = target[:, :, None] == jnp.arange(slots, dtype=jnp.int32)
    chooser = jnp.any(takes, axis=1).T.astype(BF16)
    spread = jnp.sum(jnp.where(takes, route_weight[:, :, None], 0.0), axis=1)
    coarse = spread.astype(BF16)
    fine = (spread - coarse.astype(F32)).astype(BF16)

    gathered = []
    for own_q, other_q in query_chunks:
        sums = attention(
            place,
            own_q,
            other_q,
            (key_cache, key_other),
            (value_cache, value_other),
            new_key,
            new_value,
            lens,
            chips,
            key_cache.shape[1] // HD,
        )
        gathered.append(
            lax.all_to_all(
                sums, "ctx", split_axis=0, concat_axis=0, axis_index_groups=same_core, tiled=True
            )
        )
    share = project(place, gathered, out_weight, weight_other)
    shares = lax.all_to_all(
        share.reshape(chips, home_rows, width),
        "ctx",
        split_axis=0,
        concat_axis=0,
        axis_index_groups=same_core,
        tiled=True,
    )
    middle, outgoing = norm_and_dispatch(shares, residual, norm_gain.reshape(1, width), chooser)
    arrived = lax.all_to_all(
        outgoing.reshape(devices, experts * MOST, width), "ctx", split_axis=0, concat_axis=0, tiled=True
    )
    produced = run_experts(arrived.reshape(slots, width), w_gate, w_up, w_down)
    returned = lax.all_to_all(
        produced.reshape(devices, experts * MOST, width), "ctx", split_axis=0, concat_axis=0, tiled=True
    )
    return mix(returned.reshape(slots, width), coarse, fine, middle)


def solution(mesh):
    placed = (
        P(("groups", "ctx"), None),
        P(("groups", "ctx"), None),
        P(("groups", "ctx"), None),
        P(("groups", "ctx"), None),
        P(("groups", "ctx"), None),
        P("groups"),
        P("ctx", None),
        P(("groups", "ctx"), None),
        P(),
        P(("groups", "ctx"), None),
        P(("groups", "ctx"), None),
        P("ctx", None, None),
        P("ctx", None, None),
        P("ctx", None, None),
    )
    return jax.shard_map(
        on_device, mesh=mesh, in_specs=placed, out_specs=P(("groups", "ctx"), None), check_vma=False
    )
```

time: 171 us -> 159 us (0.930)
  blocking collectives: 18 us -> 52.3 us
  waiting for transfers between devices: 60.3 us -> 41.8 us
  starting transfers between devices: 41.4 us -> 23.1 us
  local copies, waits for them, and re-layouts: 17.6 us -> 5.91 us
  Pallas kernels: 31.7 us -> 34.3 us
    all_gather x0 -> x2, blocking collectives: none -> 34.2 us  [on_device(): lax.all_gather(part, 'ctx', axis=0, axis_index_groups=along, tiled=True)]
    ppermute x7 -> x2, starting transfers between devices: 26.9 us -> 3.41 us  [on_device(): query_chunks.append((mine, lax.ppermute(mine, 'ctx', across)))]
    unnamed x36 -> x26, local copies, waits for them, and re-layouts: 16.4 us -> 1.99 us
    all_to_all x1 -> x2, waiting for transfers between devices: 22.9 us -> 10.6 us  [on_device(): lax.all_to_all(sums, 'ctx', split_axis=0, concat_axis=0, axis_index_group...]
    all_to_all x1 -> x2, starting transfers between devices: 6.29 us -> 11.4 us  [on_device(): lax.all_to_all(sums, 'ctx', split_axis=0, concat_axis=0, axis_index_group...]
    all_to_all x1, waiting for transfers between devices: 13.9 us -> 9.56 us  [on_device(): lax.all_to_all(share.reshape(chips, home_rows, width), 'ctx', split_axis=...]
    pallas_call x1, Pallas kernels: 6.73 us -> 10.8 us  [run_experts(): pl.pallas_call(functools.partial(experts_body, experts), grid=(experts, h...]
    ppermute x1, waiting for transfers between devices: 2.65 us -> 0.01 us  [on_device(): weight_other = lax.ppermute(out_weight, 'ctx', swap)]
  transfers between devices with their start and end apart: 13 -> 9, of which waited for: 7 -> 5; matrix products, arithmetic and copies ran while one was open for 1% -> 3% of each run, Pallas kernels for 0% -> 6%
where the time goes in v2:
time: 159 us; the launch traced here: 158 us
  blocking collectives  52.3 us (33%)
  waiting for transfers between devices  41.8 us (26%)
  Pallas kernels  34.3 us (22%)
  starting transfers between devices  23.1 us (15%)
  local copies, waits for them, and re-layouts  5.91 us (4%)
    all_gather x2, blocking collectives, on_device(): lax.all_gather(part, 'ctx', axis=0, axis_index_groups=along, tiled=True)  34.2 us
    pallas_call x2, Pallas kernels, attention(): pl.pallas_call(functools.partial(attention_body, shape), grid_spec=pltpu....  20.1 us
    all_to_all x1, blocking collectives, on_device(): lax.all_to_all(outgoing.reshape(devices, experts * MOST, width), 'ctx', s...  18.2 us
    all_to_all x1, waiting for transfers between devices, on_device(): lax.all_to_all(produced.reshape(devices, experts * MOST, width), 'ctx', s...  14.3 us
    all_to_all x2, starting transfers between devices, on_device(): lax.all_to_all(sums, 'ctx', split_axis=0, concat_axis=0, axis_index_group...  11.4 us
    pallas_call x1, Pallas kernels, run_experts(): pl.pallas_call(functools.partial(experts_body, experts), grid=(experts, h...  10.8 us
    all_to_all x2, waiting for transfers between devices, on_device(): lax.all_to_all(sums, 'ctx', split_axis=0, concat_axis=0, axis_index_group...  10.6 us
    all_to_all x1, waiting for transfers between devices, on_device(): lax.all_to_all(share.reshape(chips, home_rows, width), 'ctx', split_axis=...  9.56 us
  transfers between devices with their start and end apart: 9, of which 5 were waited for; matrix products, arithmetic and copies ran while one was open for 3% of the time, Pallas kernels for 6%

profile of v2, /device:TPU:0, one launch (start us, length us, event | category | flops | bytes accessed | tf_op | source)
XLA Modules:
  0.0 158.1 jit_solution(2548677061816930104)
XLA Ops:
  0.0 0.5 collective-permute-start.1
  0.5 0.1 collective-permute-start.2
  0.5 1.0 reshape.38
  1.5 0.5 slice_reduce_fusion
  2.1 15.5 %all_gather.7.own_q = bf16[64,2048]{1,0:T(8,128)(2,1)S(1)} all-gather(bf16[16,2048]{1,0:T(8,128)(2,1)S(1)} %bitcast.20), channel_id=1, replica_groups={{0,4,8,12},{1,5,9,13},{2,6,10,14},{3,7,11,15},{16,20,24,28},{17,21,25,2..., dimensions={0}, use_global_device_ids=true | all-gather | bytes 327680 | tf_op jit(solution)/shard_map/all_gather | solution.py:347
  17.5 1.5 collective-permute-start.3
  19.1 0.8 reshape.39
  19.9 0.7 reshape.40.lens
  20.5 0.7 stack.23.place
  21.2 2.8 %collective-permute-done.3.other_q = bf16[64,2048]{1,0:T(8,128)(2,1)S(1)} collective-permute-done((bf16[64,2048]{1,0:T(8,128)(2,1)S(1)}, bf16[64,2048]{1,0:T(8,128)(2,1)S(1)}, u32[]{:S(2)}, u32[]{:S(2)}) %collective-permute-start.3) | collective-permute-done | bytes 262176 | tf_op jit(solution)/shard_map/ppermute | solution.py:348
  24.0 0.0 collective-permute-done.1.key_other
  24.0 0.0 collective-permute-done.2.value_other
  24.0 0.7 copy-done.9
  24.7 0.4 copy-done.8
  25.1 10.1 %attention.3 = bf16[8,272,128]{2,1,0:T(8,128)(2,1)} custom-call(s32[5]{0:T(128)} %stack.23.place, bf16[64,2048]{1,0:T(8,128)(2,1)} %copy-done.3, bf16[64,2048]{1,0:T(8,128)(2,1)} %copy-done.9, bf16[1024,512]{1,0:T(8,128)(2,1)} %key_own.3, bf16[1024,512]{1,0:T(8,128)(2,1)} %copy-done.8, bf16[1024,512]{1,0:T(8,128)(2,1)} %value_own.3, ...), custom_call_target="tpu_custom_call" | custom-call | flops 3221225472 | bytes 8388608 | tf_op jit(solution)/shard_map/attention/pallas_call | solution.py:139
  35.2 6.1 %all-to-all-start.1 = ((bf16[8,272,128]{2,1,0:T(8,128)(2,1)}), bf16[8,272,128]{2,1,0:T(8,128)(2,1)S(1)}, u32[]{:S(2)}, u32[]{:S(2)}) async-start(bf16[8,272,128]{2,1,0:T(8,128)(2,1)} %attention.3), calls=%async_computation.1 | async-start | bytes 1114112 | tf_op jit(solution)/shard_map/all_to_all | solution.py:383
  41.3 18.7 %all_gather.6.own_q = bf16[64,2048]{1,0:T(8,128)(2,1)S(1)} all-gather(bf16[16,2048]{1,0:T(8,128)(2,1)S(1)} %bitcast.21), channel_id=1, replica_groups={{0,4,8,12},{1,5,9,13},{2,6,10,14},{3,7,11,15},{16,20,24,28},{17,21,25,2..., dimensions={0}, use_global_device_ids=true | all-gather | bytes 327680 | tf_op jit(solution)/shard_map/all_gather | solution.py:347
  60.0 0.0 copy-start.1
  60.0 1.9 %collective-permute-start = (bf16[64,2048]{1,0:T(8,128)(2,1)S(1)}, bf16[64,2048]{1,0:T(8,128)(2,1)S(1)}, u32[]{:S(2)}, u32[]{:S(2)}) collective-permute-start(bf16[64,2048]{1,0:T(8,128)(2,1)S(1)} %all_gather.6.own_q), channel_id=1, source_target_pairs={{0,2},{1,3},{2,0},{3,1},{4,6},{5,7},{6,4},{7,5},{8,10},{9,11},{10,... | collective-permute-start | bytes 786440 | tf_op jit(solution)/shard_map/ppermute | solution.py:348
  61.9 0.0 collective-permute-start.4
  61.9 4.5 %collective-permute-done.other_q = bf16[64,2048]{1,0:T(8,128)(2,1)S(1)} collective-permute-done((bf16[64,2048]{1,0:T(8,128)(2,1)S(1)}, bf16[64,2048]{1,0:T(8,128)(2,1)S(1)}, u32[]{:S(2)}, u32[]{:S(2)}) %collective-permute-start) | collective-permute-done | bytes 262176 | tf_op jit(solution)/shard_map/ppermute | solution.py:348
  66.4 0.0 copy-done.4
  66.4 0.7 copy-done.10
  67.2 10.1 %attention.2 = bf16[8,272,128]{2,1,0:T(8,128)(2,1)} custom-call(s32[5]{0:T(128)} %stack.23.place, bf16[64,2048]{1,0:T(8,128)(2,1)} %copy-done.4, bf16[64,2048]{1,0:T(8,128)(2,1)} %copy-done.10, bf16[1024,512]{1,0:T(8,128)(2,1)} %key_own.3, bf16[1024,512]{1,0:T(8,128)(2,1)} %copy-done.8, bf16[1024,512]{1,0:T(8,128)(2,1)} %value_own.3, ...), custom_call_target="tpu_custom_call" | custom-call | flops 3221225472 | bytes 8388608 | tf_op jit(solution)/shard_map/attention/pallas_call | solution.py:139
  77.2 0.0 all-to-all-done.1.refs_1_
  77.2 5.3 %all-to-all-start = ((bf16[8,272,128]{2,1,0:T(8,128)(2,1)}), bf16[8,272,128]{2,1,0:T(8,128)(2,1)S(1)}, u32[]{:S(2)}, u32[]{:S(2)}) async-start(bf16[8,272,128]{2,1,0:T(8,128)(2,1)} %attention.2), calls=%async_computation | async-start | bytes 1114112 | tf_op jit(solution)/shard_map/all_to_all | solution.py:383
  82.5 0.0 collective-permute-done.4.refs_3_
  82.5 10.6 %all-to-all-done.refs_0_ = bf16[8,272,128]{2,1,0:T(8,128)(2,1)S(1)} async-done(((bf16[8,272,128]{2,1,0:T(8,128)(2,1)}), bf16[8,272,128]{2,1,0:T(8,128)(2,1)S(1)}, u32[]{:S(2)}, u32[]{:S(2)}) %all-to-all-start) | async-done | bytes 557088 | tf_op jit(solution)/shard_map/all_to_all | solution.py:383
  93.2 0.0 copy-done.2
  93.2 2.1 %project.1 = bf16[128,2048]{1,0:T(8,128)(2,1)} custom-call(s32[5]{0:T(128)S(1)} %copy-done.2, bf16[8,272,128]{2,1,0:T(8,128)(2,1)S(1)} %all-to-all-done.refs_0_, bf16[8,272,128]{2,1,0:T(8,128)(2,1)S(1)} %all-to-all-done.1.refs_1_, bf16[256,2048]{1,0:T(8,128)(2,1)S(1)} %copy-done, bf16[256,2048]{1,0:T(8,128)(2,1)S(1)} %collective-permute-done.4.refs_3_), custom_call_target="tpu_custom_call" | custom-call | flops 268435456 | bytes 4194304 | tf_op jit(solution)/shard_map/project/pallas_call | solution.py:192
  95.2 3.7 %all-to-all-start.2 = ((bf16[8,16,2048]{2,1,0:T(8,128)(2,1)}), bf16[8,16,2048]{2,1,0:T(8,128)(2,1)S(1)}, u32[]{:S(2)}, u32[]{:S(2)}) async-start(bf16[8,16,2048]{2,1,0:T(8,128)(2,1)} %bitcast.5), calls=%async_computation.2 | async-start | bytes 1048576 | tf_op jit(solution)/shard_map/all_to_all | solution.py:388
  98.9 0.0 copy-done.5
  98.9 0.1 copy.27
  99.0 0.1 eq.31
  99.1 0.2 convert_reduce_fusion
  99.3 0.1 reduce_sum.21
  99.4 0.1 fusion
  99.5 0.1 copy.29
  99.6 0.0 copy-done.6
  99.6 9.6 %all-to-all-done.2.parts = bf16[8,16,2048]{2,1,0:T(8,128)(2,1)S(1)} async-done(((bf16[8,16,2048]{2,1,0:T(8,128)(2,1)}), bf16[8,16,2048]{2,1,0:T(8,128)(2,1)S(1)}, u32[]{:S(2)}, u32[]{:S(2)}) %all-to-all-start.2) | async-done | bytes 524320 | tf_op jit(solution)/shard_map/all_to_all | solution.py:388
  109.2 0.4 norm_and_dispatch.1
  109.7 18.2 %all_to_all.25 = bf16[16,8,2048]{2,1,0:T(8,128)(2,1)} all-to-all(bf16[16,8,2048]{2,1,0:T(8,128)(2,1)S(1)} %bitcast.16), channel_id=1, replica_groups=mesh['groups'=2,'ctx'=16] {'ctx'}, dimensions={0} | all-to-all | bytes 1048576 | tf_op jit(solution)/shard_map/all_to_all | solution.py:397
  127.8 10.8 %experts.1 = bf16[128,2048]{1,0:T(8,128)(2,1)} custom-call(bf16[128,2048]{1,0:T(8,128)(2,1)} %bitcast.19, bf16[2,2048,768]{2,1,0:T(8,128)(2,1)} %w_gate.1, bf16[2,2048,768]{2,1,0:T(8,128)(2,1)} %w_up.1, bf16[2,768,2048]{2,1,0:T(8,128)(2,1)} %w_down.1), custom_call_target="tpu_custom_call" | custom-call | flops 2415919104 | bytes 18874368 | tf_op jit(solution)/shard_map/experts/pallas_call | solution.py:267
  138.6 4.1 %all-to-all-start.4 = ((bf16[16,8,2048]{2,1,0:T(8,128)(2,1)}), bf16[16,8,2048]{2,1,0:T(8,128)(2,1)S(1)}, u32[]{:S(2)}, u32[]{:S(2)}) async-start(bf16[16,8,2048]{2,1,0:T(8,128)(2,1)} %bitcast.18), calls=%async_computation.4 | async-start | bytes 1048576 | tf_op jit(solution)/shard_map/all_to_all | solution.py:401
  142.7 0.1 copy.30
  142.8 0.1 select_reduce_fusion
  142.9 14.3 %all-to-all-done.4 = bf16[16,8,2048]{2,1,0:T(8,128)(2,1)S(1)} async-done(((bf16[16,8,2048]{2,1,0:T(8,128)(2,1)}), bf16[16,8,2048]{2,1,0:T(8,128)(2,1)S(1)}, u32[]{:S(2)}, u32[]{:S(2)}) %all-to-all-start.4) | async-done | bytes 524320 | tf_op jit(solution)/shard_map/all_to_all | solution.py:401
  157.2 0.9 mix.1
  (21 shorter events, 0.1 us)
Async XLA Ops:
  0.0 24.0 %collective-permute-start.1 = (bf16[1024,512]{1,0:T(8,128)(2,1)}, bf16[1024,512]{1,0:T(8,128)(2,1)S(1)}, u32[]{:S(2)}, u32[]{:S(2)}) collective-permute-start(bf16[1024,512]{1,0:T(8,128)(2,1)} %key_own.3), channel_id=1, source_target_pairs={{0,1},{1,0},{2,3},{3,2},{4,5},{5,4},{6,7},{7,6},{8,9},{9,8},{10,11... | collective-permute-start | bytes 3145736 | tf_op jit(solution)/shard_map/ppermute | solution.py:341
  0.5 23.6 %collective-permute-start.2 = (bf16[1024,512]{1,0:T(8,128)(2,1)}, bf16[1024,512]{1,0:T(8,128)(2,1)}, u32[]{:S(2)}, u32[]{:S(2)}) collective-permute-start(bf16[1024,512]{1,0:T(8,128)(2,1)} %value_own.3), channel_id=1, source_target_pairs={{0,1},{1,0},{2,3},{3,2},{4,5},{5,4},{6,7},{7,6},{8,9},{9,8},{10,11... | collective-permute-start | bytes 3145736 | tf_op jit(solution)/shard_map/ppermute | solution.py:342
  17.5 6.5 %copy-start.3 = (bf16[64,2048]{1,0:T(8,128)(2,1)}, bf16[64,2048]{1,0:T(8,128)(2,1)S(1)}, u32[]{:S(2)}) copy-start(bf16[64,2048]{1,0:T(8,128)(2,1)S(1)} %all_gather.7.own_q) | copy-start | bytes 786436
  17.5 6.5 %collective-permute-start.3 = (bf16[64,2048]{1,0:T(8,128)(2,1)S(1)}, bf16[64,2048]{1,0:T(8,128)(2,1)S(1)}, u32[]{:S(2)}, u32[]{:S(2)}) collective-permute-start(bf16[64,2048]{1,0:T(8,128)(2,1)S(1)} %all_gather.7.own_q), channel_id=1, source_target_pairs={{0,2},{1,3},{2,0},{3,1},{4,6},{5,7},{6,4},{7,5},{8,10},{9,11},{10,... | collective-permute-start | bytes 786440 | tf_op jit(solution)/shard_map/ppermute | solution.py:348
  21.2 40.7 %copy-start = (bf16[256,2048]{1,0:T(8,128)(2,1)S(1)}, bf16[256,2048]{1,0:T(8,128)(2,1)}, u32[]{:S(2)}) copy-start(bf16[256,2048]{1,0:T(8,128)(2,1)} %refs_2_.1) | copy-start | bytes 3145732
  24.0 0.7 copy-start.9
  24.0 1.1 copy-start.8
  35.2 42.1 %all-to-all-start.1 = ((bf16[8,272,128]{2,1,0:T(8,128)(2,1)}), bf16[8,272,128]{2,1,0:T(8,128)(2,1)S(1)}, u32[]{:S(2)}, u32[]{:S(2)}) async-start(bf16[8,272,128]{2,1,0:T(8,128)(2,1)} %attention.3), calls=%async_computation.1 | async-start | bytes 1114112 | tf_op jit(solution)/shard_map/all_to_all | solution.py:383
  60.0 6.5 %copy-start.4 = (bf16[64,2048]{1,0:T(8,128)(2,1)}, bf16[64,2048]{1,0:T(8,128)(2,1)S(1)}, u32[]{:S(2)}) copy-start(bf16[64,2048]{1,0:T(8,128)(2,1)S(1)} %all_gather.6.own_q) | copy-start | bytes 786436
  60.0 33.2 %copy-start.2 = (s32[5]{0:T(128)S(1)}, s32[5]{0:T(128)}, u32[]{:S(2)}) copy-start(s32[5]{0:T(128)} %stack.23.place) | copy-start | bytes 64
  60.0 38.9 %copy-start.5 = (s32[16,8]{0,1:T(8,128)S(1)}, s32[16,8]{0,1:T(8,128)}, u32[]{:S(2)}) copy-start(s32[16,8]{0,1:T(8,128)} %param.23) | copy-start | bytes 1540
  60.0 39.6 %copy-start.6 = (bf16[2048]{0:T(1024)(128)(2,1)S(1)}, bf16[2048]{0:T(1024)(128)(2,1)}, u32[]{:S(2)}) copy-start(bf16[2048]{0:T(1024)(128)(2,1)} %param.22) | copy-start | bytes 12292
  60.0 49.2 %copy-start.1 = (bf16[16,2048]{1,0:T(8,128)(2,1)S(1)}, bf16[16,2048]{1,0:T(8,128)(2,1)}, u32[]{:S(2)}) copy-start(bf16[16,2048]{1,0:T(8,128)(2,1)} %residual.1) | copy-start | bytes 196612
  60.0 6.4 %collective-permute-start = (bf16[64,2048]{1,0:T(8,128)(2,1)S(1)}, bf16[64,2048]{1,0:T(8,128)(2,1)S(1)}, u32[]{:S(2)}, u32[]{:S(2)}) collective-permute-start(bf16[64,2048]{1,0:T(8,128)(2,1)S(1)} %all_gather.6.own_q), channel_id=1, source_target_pairs={{0,2},{1,3},{2,0},{3,1},{4,6},{5,7},{6,4},{7,5},{8,10},{9,11},{10,... | collective-permute-start | bytes 786440 | tf_op jit(solution)/shard_map/ppermute | solution.py:348
  61.9 20.6 %collective-permute-start.4 = (bf16[256,2048]{1,0:T(8,128)(2,1)S(1)}, bf16[256,2048]{1,0:T(8,128)(2,1)S(1)}, u32[]{:S(2)}, u32[]{:S(2)}) collective-permute-start(bf16[256,2048]{1,0:T(8,128)(2,1)S(1)} %copy-done), channel_id=1, source_target_pairs={{0,1},{1,0},{2,3},{3,2},{4,5},{5,4},{6,7},{7,6},{8,9},{9,8},{10,11... | collective-permute-start | bytes 3145736 | tf_op jit(solution)/shard_map/ppermute | solution.py:349
  66.4 0.7 copy-start.10
  77.2 15.9 %all-to-all-start = ((bf16[8,272,128]{2,1,0:T(8,128)(2,1)}), bf16[8,272,128]{2,1,0:T(8,128)(2,1)S(1)}, u32[]{:S(2)}, u32[]{:S(2)}) async-start(bf16[8,272,128]{2,1,0:T(8,128)(2,1)} %attention.2), calls=%async_computation | async-start | bytes 1114112 | tf_op jit(solution)/shard_map/all_to_all | solution.py:383
  95.2 14.0 %all-to-all-start.2 = ((bf16[8,16,2048]{2,1,0:T(8,128)(2,1)}), bf16[8,16,2048]{2,1,0:T(8,128)(2,1)S(1)}, u32[]{:S(2)}, u32[]{:S(2)}) async-start(bf16[8,16,2048]{2,1,0:T(8,128)(2,1)} %bitcast.5), calls=%async_computation.2 | async-start | bytes 1048576 | tf_op jit(solution)/shard_map/all_to_all | solution.py:388
  127.8 14.9 %copy-start.7 = (f32[16,8]{0,1:T(8,128)S(1)}, f32[16,8]{0,1:T(8,128)}, u32[]{:S(2)}) copy-start(f32[16,8]{0,1:T(8,128)} %param.24) | copy-start | bytes 1540
  138.6 18.6 %all-to-all-start.4 = ((bf16[16,8,2048]{2,1,0:T(8,128)(2,1)}), bf16[16,8,2048]{2,1,0:T(8,128)(2,1)S(1)}, u32[]{:S(2)}, u32[]{:S(2)}) async-start(bf16[16,8,2048]{2,1,0:T(8,128)(2,1)} %bitcast.18), calls=%async_computation.4 | async-start | bytes 1048576 | tf_op jit(solution)/shard_map/all_to_all | solution.py:401

commit v3 on v2

--- a/solution.py
+++ b/solution.py
@@ -31,7 +31,7 @@
 def attention_body(shape, place, own_q, other_q, key_own, key_other, value_own, value_other, key_fresh, value_fresh, lens, out, *scratch):
     owners, heads_owner, home_rows, rows, cache_here, step = shape
     q_rows, v_turned, hidden, scores, probs = scratch
-    chip, start_own, start_other, pair_place = place[0], place[1], place[2], place[4]
+    chip, start_own, start_other, pair_place, ring_place = place[0], place[1], place[2], place[4], place[5]
     rings = rows // home_rows // 2
 
     @pl.when(pl.program_id(0) == 0)
@@ -52,7 +52,7 @@
     for ring in range(rings):
         taken = slice(ring * home_rows, (ring + 1) * home_rows)
         for piece, side in ((own_q, pair_place), (other_q, 1 - pair_place)):
-            spot = pl.multiple_of((2 * ring + side) * home_rows, home_rows)
+            spot = pl.multiple_of((2 * (ring ^ ring_place) + side) * home_rows, home_rows)
             q_rows[pl.ds(spot, home_rows), :] = piece[taken, :]
 
     heads = owners * heads_owner
@@ -81,7 +81,7 @@
     def weigh(group, piece, lift):
         _, base, i = piece
         s = scores[group % 2, base + i : base + i + step, :]
-        probs[group % 2, base + i : base + i + step, :] = jnp.exp2(s - lift).astype(BF16)
+        probs[group % 2, base + i : base + i + step, :] = jnp.exp2((s - lift).astype(BF16))
 
     def finish_peak(group, run):
         keys = key_fresh[...]
@@ -89,7 +89,7 @@
         s = s + jnp.concatenate([hidden[2 * cache_here :, :]] * wide, axis=1)
         peak = jnp.maximum(jnp.max(run, axis=0, keepdims=True), jnp.max(s, axis=0, keepdims=True))
         peak = jnp.maximum(peak, FLOOR).astype(BF16).astype(F32)
-        return peak, jnp.exp2(s - peak).astype(BF16)
+        return peak, jnp.exp2((s - peak).astype(BF16))
 
     stats = [[None] * (3 * heads_owner) for _ in range(owners)]
 
@@ -331,24 +331,23 @@
     same_core = [[CORES * j + c for j in range(chips)] for c in range(CORES)]
     swap = [(i, i ^ 1) for i in range(devices)]
 
-    along = [
-        [CORES * (2 * ring + side) + c for ring in range(chips // 2)]
-        for side in range(2)
-        for c in range(CORES)
-    ]
     across = [(i, i ^ CORES) for i in range(devices)]
 
-    key_other = lax.ppermute(key_cache, "ctx", swap)
-    value_other = lax.ppermute(value_cache, "ctx", swap)
     by_owner = queries.reshape(home_rows, chips, CORES, heads_here * HD)
     query_chunks = []
     for chunk in range(CORES):
-        part = by_owner[:, :, chunk].reshape(home_rows, chips * heads_here * HD)
-        mine = lax.all_gather(part, "ctx", axis=0, axis_index_groups=along, tiled=True)
+        mine = by_owner[:, :, chunk].reshape(home_rows, chips * heads_here * HD)
+        stride = 2 * CORES
+        while stride < devices:
+            step = [(i, i ^ stride) for i in range(devices)]
+            mine = jnp.concatenate([mine, lax.ppermute(mine, "ctx", step)], axis=0)
+            stride *= 2
         query_chunks.append((mine, lax.ppermute(mine, "ctx", across)))
+    key_other = lax.ppermute(key_cache, "ctx", swap)
+    value_other = lax.ppermute(value_cache, "ctx", swap)
     weight_other = lax.ppermute(out_weight, "ctx", swap)
 
-    place = jnp.stack([chip, index * cache_here, (index ^ 1) * cache_here, core, chip % 2]).astype(jnp.int32)
+    place = jnp.stack([chip, index * cache_here, (index ^ 1) * cache_here, core, chip % 2, chip // 2]).astype(jnp.int32)
     lens = lax.dynamic_index_in_dim(
         cache_len.reshape(chips, CORES, home_rows), core, axis=1, keepdims=False
     ).reshape(1, chips * home_rows)

time: 159 us -> 149 us (0.937)
  blocking collectives: 52.3 us -> 18.1 us
  waiting for transfers between devices: 41.8 us -> 60 us
  starting transfers between devices: 23.1 us -> 30.2 us
    all_gather x2 -> x0, blocking collectives: 34.2 us -> none  [on_device(): lax.all_gather(part, 'ctx', axis=0, axis_index_groups=along, tiled=True)]
    ppermute x0 -> x4, waiting for transfers between devices: none -> 6.91 us  [on_device(): mine = jnp.concatenate([mine, lax.ppermute(mine, 'ctx', step)], axis=0)]
    ppermute x0 -> x4, starting transfers between devices: none -> 6.87 us  [on_device(): mine = jnp.concatenate([mine, lax.ppermute(mine, 'ctx', step)], axis=0)]
    ppermute x2, waiting for transfers between devices: 7.35 us -> 12 us  [on_device(): query_chunks.append((mine, lax.ppermute(mine, 'ctx', across)))]
    all_to_all x1, waiting for transfers between devices: 9.56 us -> 13 us  [on_device(): lax.all_to_all(share.reshape(chips, home_rows, width), 'ctx', split_axis=...]
    all_to_all x2, waiting for transfers between devices: 10.6 us -> 13.8 us  [on_device(): lax.all_to_all(sums, 'ctx', split_axis=0, concat_axis=0, axis_index_group...]
  transfers between devices with their start and end apart: 9 -> 13, of which waited for: 5 -> 7; matrix products, arithmetic and copies ran while one was open for 3% -> 2% of each run, Pallas kernels for 6% -> 13%
where the time goes in v3:
time: 149 us; the launch traced here: 148 us
  waiting for transfers between devices  60 us (40%)
  Pallas kernels  33.5 us (22%)
  starting transfers between devices  30.2 us (20%)
  blocking collectives  18.1 us (12%)
  local copies, waits for them, and re-layouts  5.49 us (4%)
    pallas_call x2, Pallas kernels, attention(): pl.pallas_call(functools.partial(attention_body, shape), grid_spec=pltpu....  19.2 us
    all_to_all x1, blocking collectives, on_device(): lax.all_to_all(outgoing.reshape(devices, experts * MOST, width), 'ctx', s...  18.1 us
    all_to_all x1, waiting for transfers between devices, on_device(): lax.all_to_all(produced.reshape(devices, experts * MOST, width), 'ctx', s...  14.3 us
    all_to_all x2, waiting for transfers between devices, on_device(): lax.all_to_all(sums, 'ctx', split_axis=0, concat_axis=0, axis_index_group...  13.8 us
    all_to_all x1, waiting for transfers between devices, on_device(): lax.all_to_all(share.reshape(chips, home_rows, width), 'ctx', split_axis=...  13 us
    ppermute x2, waiting for transfers between devices, on_device(): query_chunks.append((mine, lax.ppermute(mine, 'ctx', across)))  12 us
    all_to_all x2, starting transfers between devices, on_device(): lax.all_to_all(sums, 'ctx', split_axis=0, concat_axis=0, axis_index_group...  11.2 us
    pallas_call x1, Pallas kernels, run_experts(): pl.pallas_call(functools.partial(experts_body, experts), grid=(experts, h...  10.8 us
  transfers between devices with their start and end apart: 13, of which 7 were waited for; matrix products, arithmetic and copies ran while one was open for 2% of the time, Pallas kernels for 13%

profile of v3, /device:TPU:0, one launch (start us, length us, event | category | flops | bytes accessed | tf_op | source)
XLA Modules:
  0.0 147.9 jit_solution(12457457357646234103)
XLA Ops:
  0.0 1.0 reshape.38
  1.0 0.5 slice_reduce_fusion
  1.5 3.1 %collective-permute-start.5 = (bf16[16,2048]{1,0:T(8,128)(2,1)S(1)}, bf16[16,2048]{1,0:T(8,128)(2,1)S(1)}, u32[]{:S(2)}, u32[]{:S(2)}) collective-permute-start(bf16[16,2048]{1,0:T(8,128)(2,1)S(1)} %bitcast.24), channel_id=1, source_target_pairs={{0,4},{1,5},{2,6},{3,7},{4,0},{5,1},{6,2},{7,3},{8,12},{9,13},{10,... | collective-permute-start | bytes 196616 | tf_op jit(solution)/shard_map/ppermute | solution.py:343
  4.6 0.0 collective-permute-start.3
  4.6 0.5 collective-permute-start.4
  5.2 0.1 collective-permute-start
  5.3 1.7 %collective-permute-done.5 = bf16[16,2048]{1,0:T(8,128)(2,1)S(1)} collective-permute-done((bf16[16,2048]{1,0:T(8,128)(2,1)S(1)}, bf16[16,2048]{1,0:T(8,128)(2,1)S(1)}, u32[]{:S(2)}, u32[]{:S(2)}) %collective-permute-start.5) | collective-permute-done | bytes 65568 | tf_op jit(solution)/shard_map/ppermute | solution.py:343
  7.0 2.9 %collective-permute-start.6 = (bf16[32,2048]{1,0:T(8,128)(2,1)S(1)}, bf16[32,2048]{1,0:T(8,128)(2,1)S(1)}, u32[]{:S(2)}, u32[]{:S(2)}) collective-permute-start(bf16[32,2048]{1,0:T(8,128)(2,1)S(1)} %pad_maximum_fusion.1), channel_id=1, source_target_pairs={{0,8},{1,9},{2,10},{3,11},{4,12},{5,13},{6,14},{7,15},{8,0},{9,1},... | collective-permute-start | bytes 393224 | tf_op jit(solution)/shard_map/ppermute | solution.py:343
  10.0 5.2 %collective-permute-done.6 = bf16[32,2048]{1,0:T(8,128)(2,1)S(1)} collective-permute-done((bf16[32,2048]{1,0:T(8,128)(2,1)S(1)}, bf16[32,2048]{1,0:T(8,128)(2,1)S(1)}, u32[]{:S(2)}, u32[]{:S(2)}) %collective-permute-start.6) | collective-permute-done | bytes 131104 | tf_op jit(solution)/shard_map/ppermute | solution.py:343
  15.2 1.7 %collective-permute-start.7 = (bf16[64,2048]{1,0:T(8,128)(2,1)S(1)}, bf16[64,2048]{1,0:T(8,128)(2,1)S(1)}, u32[]{:S(2)}, u32[]{:S(2)}) collective-permute-start(bf16[64,2048]{1,0:T(8,128)(2,1)S(1)} %constant_dynamic-update-slice_fusion.3.own_q), channel_id=1, source_target_pairs={{0,2},{1,3},{2,0},{3,1},{4,6},{5,7},{6,4},{7,5},{8,10},{9,11},{10,... | collective-permute-start | bytes 786440 | tf_op jit(solution)/shard_map/ppermute | solution.py:345
  16.9 0.8 reshape.39
  17.7 0.6 reshape.40.lens
  18.4 0.6 stack.27.place
  19.0 0.0 collective-permute-done
  19.0 0.0 copy-start
  19.0 0.7 collective-permute-start.1
  19.7 1.9 %collective-permute-done.7.other_q = bf16[64,2048]{1,0:T(8,128)(2,1)S(1)} collective-permute-done((bf16[64,2048]{1,0:T(8,128)(2,1)S(1)}, bf16[64,2048]{1,0:T(8,128)(2,1)S(1)}, u32[]{:S(2)}, u32[]{:S(2)}) %collective-permute-start.7) | collective-permute-done | bytes 262176 | tf_op jit(solution)/shard_map/ppermute | solution.py:345
  21.6 0.0 collective-permute-done.3.key_other
  21.7 0.0 collective-permute-done.4.value_other
  21.7 0.7 copy-done.8
  22.4 9.6 %attention.3 = bf16[8,272,128]{2,1,0:T(8,128)(2,1)} custom-call(s32[6]{0:T(128)} %stack.27.place, bf16[64,2048]{1,0:T(8,128)(2,1)} %copy-done.4, bf16[64,2048]{1,0:T(8,128)(2,1)} %copy-done.8, bf16[1024,512]{1,0:T(8,128)(2,1)} %key_own.3, bf16[1024,512]{1,0:T(8,128)(2,1)} %collective-permute-done.3.key_other, bf16[1024,512]{1,0:T(8,128)(2,1)} %value_own.3, ...), custom_call_target="tpu_custom_call" | custom-call | flops 3221225472 | bytes 8388608 | tf_op jit(solution)/shard_map/attention/pallas_call | solution.py:139
  32.0 6.6 %all-to-all-start.1 = ((bf16[8,272,128]{2,1,0:T(8,128)(2,1)}), bf16[8,272,128]{2,1,0:T(8,128)(2,1)S(1)}, u32[]{:S(2)}, u32[]{:S(2)}) async-start(bf16[8,272,128]{2,1,0:T(8,128)(2,1)} %attention.3), calls=%async_computation.1 | async-start | bytes 1114112 | tf_op jit(solution)/shard_map/all_to_all | solution.py:382
  38.7 0.0 copy-start.5
  38.7 0.0 copy-start.6
  38.7 0.0 copy-start.1
  38.7 2.1 %collective-permute-start.2 = (bf16[64,2048]{1,0:T(8,128)(2,1)S(1)}, bf16[64,2048]{1,0:T(8,128)(2,1)S(1)}, u32[]{:S(2)}, u32[]{:S(2)}) collective-permute-start(bf16[64,2048]{1,0:T(8,128)(2,1)S(1)} %constant_dynamic-update-slice_fusion.own_q), channel_id=1, source_target_pairs={{0,2},{1,3},{2,0},{3,1},{4,6},{5,7},{6,4},{7,5},{8,10},{9,11},{10,... | collective-permute-start | bytes 786440 | tf_op jit(solution)/shard_map/ppermute | solution.py:345
  40.8 10.1 %collective-permute-done.2.other_q = bf16[64,2048]{1,0:T(8,128)(2,1)S(1)} collective-permute-done((bf16[64,2048]{1,0:T(8,128)(2,1)S(1)}, bf16[64,2048]{1,0:T(8,128)(2,1)S(1)}, u32[]{:S(2)}, u32[]{:S(2)}) %collective-permute-start.2) | collective-permute-done | bytes 262176 | tf_op jit(solution)/shard_map/ppermute | solution.py:345
  50.9 0.7 copy-done.9
  51.6 9.6 %attention.2 = bf16[8,272,128]{2,1,0:T(8,128)(2,1)} custom-call(s32[6]{0:T(128)} %stack.27.place, bf16[64,2048]{1,0:T(8,128)(2,1)} %copy-done.3, bf16[64,2048]{1,0:T(8,128)(2,1)} %copy-done.9, bf16[1024,512]{1,0:T(8,128)(2,1)} %key_own.3, bf16[1024,512]{1,0:T(8,128)(2,1)} %collective-permute-done.3.key_other, bf16[1024,512]{1,0:T(8,128)(2,1)} %value_own.3, ...), custom_call_target="tpu_custom_call" | custom-call | flops 3221225472 | bytes 8388608 | tf_op jit(solution)/shard_map/attention/pallas_call | solution.py:139
  61.2 4.6 %all-to-all-start = ((bf16[8,272,128]{2,1,0:T(8,128)(2,1)}), bf16[8,272,128]{2,1,0:T(8,128)(2,1)S(1)}, u32[]{:S(2)}, u32[]{:S(2)}) async-start(bf16[8,272,128]{2,1,0:T(8,128)(2,1)} %attention.2), calls=%async_computation | async-start | bytes 1114112 | tf_op jit(solution)/shard_map/all_to_all | solution.py:382
  65.8 13.8 %all-to-all-done.refs_0_ = bf16[8,272,128]{2,1,0:T(8,128)(2,1)S(1)} async-done(((bf16[8,272,128]{2,1,0:T(8,128)(2,1)}), bf16[8,272,128]{2,1,0:T(8,128)(2,1)S(1)}, u32[]{:S(2)}, u32[]{:S(2)}) %all-to-all-start) | async-done | bytes 557088 | tf_op jit(solution)/shard_map/all_to_all | solution.py:382
  79.6 2.1 %project.1 = bf16[128,2048]{1,0:T(8,128)(2,1)} custom-call(s32[6]{0:T(128)S(1)} %copy-done.2, bf16[8,272,128]{2,1,0:T(8,128)(2,1)S(1)} %all-to-all-done.refs_0_, bf16[8,272,128]{2,1,0:T(8,128)(2,1)S(1)} %all-to-all-done.1.refs_1_, bf16[256,2048]{1,0:T(8,128)(2,1)S(1)} %copy-done, bf16[256,2048]{1,0:T(8,128)(2,1)S(1)} %collective-permute-done.8.refs_3_), custom_call_target="tpu_custom_call" | custom-call | flops 268435456 | bytes 4194304 | tf_op jit(solution)/shard_map/project/pallas_call | solution.py:192
  81.7 3.7 %all-to-all-start.2 = ((bf16[8,16,2048]{2,1,0:T(8,128)(2,1)}), bf16[8,16,2048]{2,1,0:T(8,128)(2,1)S(1)}, u32[]{:S(2)}, u32[]{:S(2)}) async-start(bf16[8,16,2048]{2,1,0:T(8,128)(2,1)} %bitcast.6), calls=%async_computation.2 | async-start | bytes 1048576 | tf_op jit(solution)/shard_map/all_to_all | solution.py:387
  85.4 0.1 copy.27
  85.4 0.1 eq.31
  85.5 0.2 convert_reduce_fusion
  85.7 0.1 reduce_sum.21
  85.8 0.1 fusion
  85.9 0.1 copy.29
  86.1 13.0 %all-to-all-done.2.parts = bf16[8,16,2048]{2,1,0:T(8,128)(2,1)S(1)} async-done(((bf16[8,16,2048]{2,1,0:T(8,128)(2,1)}), bf16[8,16,2048]{2,1,0:T(8,128)(2,1)S(1)}, u32[]{:S(2)}, u32[]{:S(2)}) %all-to-all-start.2) | async-done | bytes 524320 | tf_op jit(solution)/shard_map/all_to_all | solution.py:387
  99.1 0.4 norm_and_dispatch.1
  99.5 18.1 %all_to_all.25 = bf16[16,8,2048]{2,1,0:T(8,128)(2,1)} all-to-all(bf16[16,8,2048]{2,1,0:T(8,128)(2,1)S(1)} %bitcast.17), channel_id=1, replica_groups=mesh['groups'=2,'ctx'=16] {'ctx'}, dimensions={0} | all-to-all | bytes 1048576 | tf_op jit(solution)/shard_map/all_to_all | solution.py:396
  117.6 10.8 %experts.1 = bf16[128,2048]{1,0:T(8,128)(2,1)} custom-call(bf16[128,2048]{1,0:T(8,128)(2,1)} %bitcast.20, bf16[2,2048,768]{2,1,0:T(8,128)(2,1)} %w_gate.1, bf16[2,2048,768]{2,1,0:T(8,128)(2,1)} %w_up.1, bf16[2,768,2048]{2,1,0:T(8,128)(2,1)} %w_down.1), custom_call_target="tpu_custom_call" | custom-call | flops 2415919104 | bytes 18874368 | tf_op jit(solution)/shard_map/experts/pallas_call | solution.py:267
  128.5 4.1 %all-to-all-start.4 = ((bf16[16,8,2048]{2,1,0:T(8,128)(2,1)}), bf16[16,8,2048]{2,1,0:T(8,128)(2,1)S(1)}, u32[]{:S(2)}, u32[]{:S(2)}) async-start(bf16[16,8,2048]{2,1,0:T(8,128)(2,1)} %bitcast.19), calls=%async_computation.4 | async-start | bytes 1048576 | tf_op jit(solution)/shard_map/all_to_all | solution.py:400
  132.6 0.1 copy.30
  132.6 0.1 select_reduce_fusion
  132.8 14.3 %all-to-all-done.4 = bf16[16,8,2048]{2,1,0:T(8,128)(2,1)S(1)} async-done(((bf16[16,8,2048]{2,1,0:T(8,128)(2,1)}), bf16[16,8,2048]{2,1,0:T(8,128)(2,1)S(1)}, u32[]{:S(2)}, u32[]{:S(2)}) %all-to-all-start.4) | async-done | bytes 524320 | tf_op jit(solution)/shard_map/all_to_all | solution.py:400
  147.0 0.9 mix.1
  (33 shorter events, 0.2 us)
Async XLA Ops:
  1.5 5.5 %collective-permute-start.5 = (bf16[16,2048]{1,0:T(8,128)(2,1)S(1)}, bf16[16,2048]{1,0:T(8,128)(2,1)S(1)}, u32[]{:S(2)}, u32[]{:S(2)}) collective-permute-start(bf16[16,2048]{1,0:T(8,128)(2,1)S(1)} %bitcast.24), channel_id=1, source_target_pairs={{0,4},{1,5},{2,6},{3,7},{4,0},{5,1},{6,2},{7,3},{8,12},{9,13},{10,... | collective-permute-start | bytes 196616 | tf_op jit(solution)/shard_map/ppermute | solution.py:343
  4.6 17.0 %collective-permute-start.3 = (bf16[1024,512]{1,0:T(8,128)(2,1)}, bf16[1024,512]{1,0:T(8,128)(2,1)}, u32[]{:S(2)}, u32[]{:S(2)}) collective-permute-start(bf16[1024,512]{1,0:T(8,128)(2,1)} %key_own.3), channel_id=1, source_target_pairs={{0,1},{1,0},{2,3},{3,2},{4,5},{5,4},{6,7},{7,6},{8,9},{9,8},{10,11... | collective-permute-start | bytes 3145736 | tf_op jit(solution)/shard_map/ppermute | solution.py:346
  4.6 17.0 %collective-permute-start.4 = (bf16[1024,512]{1,0:T(8,128)(2,1)}, bf16[1024,512]{1,0:T(8,128)(2,1)}, u32[]{:S(2)}, u32[]{:S(2)}) collective-permute-start(bf16[1024,512]{1,0:T(8,128)(2,1)} %value_own.3), channel_id=1, source_target_pairs={{0,1},{1,0},{2,3},{3,2},{4,5},{5,4},{6,7},{7,6},{8,9},{9,8},{10,11... | collective-permute-start | bytes 3145736 | tf_op jit(solution)/shard_map/ppermute | solution.py:347
  5.2 13.8 %collective-permute-start = (bf16[16,2048]{1,0:T(8,128)(2,1)S(1)}, bf16[16,2048]{1,0:T(8,128)(2,1)S(1)}, u32[]{:S(2)}, u32[]{:S(2)}) collective-permute-start(bf16[16,2048]{1,0:T(8,128)(2,1)S(1)} %bitcast.21), channel_id=1, source_target_pairs={{0,4},{1,5},{2,6},{3,7},{4,0},{5,1},{6,2},{7,3},{8,12},{9,13},{10,... | collective-permute-start | bytes 196616 | tf_op jit(solution)/shard_map/ppermute | solution.py:343
  7.0 8.1 %collective-permute-start.6 = (bf16[32,2048]{1,0:T(8,128)(2,1)S(1)}, bf16[32,2048]{1,0:T(8,128)(2,1)S(1)}, u32[]{:S(2)}, u32[]{:S(2)}) collective-permute-start(bf16[32,2048]{1,0:T(8,128)(2,1)S(1)} %pad_maximum_fusion.1), channel_id=1, source_target_pairs={{0,8},{1,9},{2,10},{3,11},{4,12},{5,13},{6,14},{7,15},{8,0},{9,1},... | collective-permute-start | bytes 393224 | tf_op jit(solution)/shard_map/ppermute | solution.py:343
  15.2 6.5 %copy-start.4 = (bf16[64,2048]{1,0:T(8,128)(2,1)}, bf16[64,2048]{1,0:T(8,128)(2,1)S(1)}, u32[]{:S(2)}) copy-start(bf16[64,2048]{1,0:T(8,128)(2,1)S(1)} %constant_dynamic-update-slice_fusion.3.own_q) | copy-start | bytes 786436
  15.2 6.4 %collective-permute-start.7 = (bf16[64,2048]{1,0:T(8,128)(2,1)S(1)}, bf16[64,2048]{1,0:T(8,128)(2,1)S(1)}, u32[]{:S(2)}, u32[]{:S(2)}) collective-permute-start(bf16[64,2048]{1,0:T(8,128)(2,1)S(1)} %constant_dynamic-update-slice_fusion.3.own_q), channel_id=1, source_target_pairs={{0,2},{1,3},{2,0},{3,1},{4,6},{5,7},{6,4},{7,5},{8,10},{9,11},{10,... | collective-permute-start | bytes 786440 | tf_op jit(solution)/shard_map/ppermute | solution.py:345
  19.0 21.8 %copy-start = (bf16[256,2048]{1,0:T(8,128)(2,1)S(1)}, bf16[256,2048]{1,0:T(8,128)(2,1)}, u32[]{:S(2)}) copy-start(bf16[256,2048]{1,0:T(8,128)(2,1)} %refs_2_.1) | copy-start | bytes 3145732
  19.0 19.6 %collective-permute-start.1 = (bf16[32,2048]{1,0:T(8,128)(2,1)S(1)}, bf16[32,2048]{1,0:T(8,128)(2,1)S(1)}, u32[]{:S(2)}, u32[]{:S(2)}) collective-permute-start(bf16[32,2048]{1,0:T(8,128)(2,1)S(1)} %pad_maximum_fusion), channel_id=1, source_target_pairs={{0,8},{1,9},{2,10},{3,11},{4,12},{5,13},{6,14},{7,15},{8,0},{9,1},... | collective-permute-start | bytes 393224 | tf_op jit(solution)/shard_map/ppermute | solution.py:343
  21.6 0.7 copy-start.8
  32.0 29.2 %all-to-all-start.1 = ((bf16[8,272,128]{2,1,0:T(8,128)(2,1)}), bf16[8,272,128]{2,1,0:T(8,128)(2,1)S(1)}, u32[]{:S(2)}, u32[]{:S(2)}) async-start(bf16[8,272,128]{2,1,0:T(8,128)(2,1)} %attention.3), calls=%async_computation.1 | async-start | bytes 1114112 | tf_op jit(solution)/shard_map/all_to_all | solution.py:382
  38.7 12.2 %copy-start.3 = (bf16[64,2048]{1,0:T(8,128)(2,1)}, bf16[64,2048]{1,0:T(8,128)(2,1)S(1)}, u32[]{:S(2)}) copy-start(bf16[64,2048]{1,0:T(8,128)(2,1)S(1)} %constant_dynamic-update-slice_fusion.own_q) | copy-start | bytes 786436
  38.7 40.9 %copy-start.2 = (s32[6]{0:T(128)S(1)}, s32[6]{0:T(128)}, u32[]{:S(2)}) copy-start(s32[6]{0:T(128)} %stack.27.place) | copy-start | bytes 76
  38.7 46.7 %copy-start.5 = (s32[16,8]{0,1:T(8,128)S(1)}, s32[16,8]{0,1:T(8,128)}, u32[]{:S(2)}) copy-start(s32[16,8]{0,1:T(8,128)} %param.23) | copy-start | bytes 1540
  38.7 47.3 %copy-start.6 = (bf16[2048]{0:T(1024)(128)(2,1)S(1)}, bf16[2048]{0:T(1024)(128)(2,1)}, u32[]{:S(2)}) copy-start(bf16[2048]{0:T(1024)(128)(2,1)} %param.22) | copy-start | bytes 12292
  38.7 60.3 %copy-start.1 = (bf16[16,2048]{1,0:T(8,128)(2,1)S(1)}, bf16[16,2048]{1,0:T(8,128)(2,1)}, u32[]{:S(2)}) copy-start(bf16[16,2048]{1,0:T(8,128)(2,1)} %residual.1) | copy-start | bytes 196612
  38.7 12.2 %collective-permute-start.2 = (bf16[64,2048]{1,0:T(8,128)(2,1)S(1)}, bf16[64,2048]{1,0:T(8,128)(2,1)S(1)}, u32[]{:S(2)}, u32[]{:S(2)}) collective-permute-start(bf16[64,2048]{1,0:T(8,128)(2,1)S(1)} %constant_dynamic-update-slice_fusion.own_q), channel_id=1, source_target_pairs={{0,2},{1,3},{2,0},{3,1},{4,6},{5,7},{6,4},{7,5},{8,10},{9,11},{10,... | collective-permute-start | bytes 786440 | tf_op jit(solution)/shard_map/ppermute | solution.py:345
  40.8 24.9 %collective-permute-start.8 = (bf16[256,2048]{1,0:T(8,128)(2,1)S(1)}, bf16[256,2048]{1,0:T(8,128)(2,1)S(1)}, u32[]{:S(2)}, u32[]{:S(2)}) collective-permute-start(bf16[256,2048]{1,0:T(8,128)(2,1)S(1)} %copy-done), channel_id=1, source_target_pairs={{0,1},{1,0},{2,3},{3,2},{4,5},{5,4},{6,7},{7,6},{8,9},{9,8},{10,11... | collective-permute-start | bytes 3145736 | tf_op jit(solution)/shard_map/ppermute | solution.py:348
  50.9 0.7 copy-start.9
  61.2 18.4 %all-to-all-start = ((bf16[8,272,128]{2,1,0:T(8,128)(2,1)}), bf16[8,272,128]{2,1,0:T(8,128)(2,1)S(1)}, u32[]{:S(2)}, u32[]{:S(2)}) async-start(bf16[8,272,128]{2,1,0:T(8,128)(2,1)} %attention.2), calls=%async_computation | async-start | bytes 1114112 | tf_op jit(solution)/shard_map/all_to_all | solution.py:382
  81.7 17.4 %all-to-all-start.2 = ((bf16[8,16,2048]{2,1,0:T(8,128)(2,1)}), bf16[8,16,2048]{2,1,0:T(8,128)(2,1)S(1)}, u32[]{:S(2)}, u32[]{:S(2)}) async-start(bf16[8,16,2048]{2,1,0:T(8,128)(2,1)} %bitcast.6), calls=%async_computation.2 | async-start | bytes 1048576 | tf_op jit(solution)/shard_map/all_to_all | solution.py:387
  117.6 14.9 %copy-start.7 = (f32[16,8]{0,1:T(8,128)S(1)}, f32[16,8]{0,1:T(8,128)}, u32[]{:S(2)}) copy-start(f32[16,8]{0,1:T(8,128)} %param.24) | copy-start | bytes 1540
  128.5 18.6 %all-to-all-start.4 = ((bf16[16,8,2048]{2,1,0:T(8,128)(2,1)}), bf16[16,8,2048]{2,1,0:T(8,128)(2,1)S(1)}, u32[]{:S(2)}, u32[]{:S(2)}) async-start(bf16[16,8,2048]{2,1,0:T(8,128)(2,1)} %bitcast.19), calls=%async_computation.4 | async-start | bytes 1048576 | tf_op jit(solution)/shard_map/all_to_all | solution.py:400

commit v4 on v3

--- a/solution.py
+++ b/solution.py
@@ -30,7 +30,7 @@
 
 def attention_body(shape, place, own_q, other_q, key_own, key_other, value_own, value_other, key_fresh, value_fresh, lens, out, *scratch):
     owners, heads_owner, home_rows, rows, cache_here, step = shape
-    q_rows, v_turned, hidden, scores, probs = scratch
+    q_rows, v_turned, hidden, scores = scratch
     chip, start_own, start_other, pair_place, ring_place = place[0], place[1], place[2], place[4], place[5]
     rings = rows // home_rows // 2
 
@@ -56,71 +56,43 @@
             q_rows[pl.ds(spot, home_rows), :] = piece[taken, :]
 
     heads = owners * heads_owner
-    wide = min(2, heads)
-    groups = heads // wide
     factor = LOG2E / math.sqrt(HD)
     pieces = [(key_own, 0, i) for i in range(0, cache_here, step)]
     pieces += [(key_other, cache_here, i) for i in range(0, cache_here, step)]
-    queries, highest, fresh = [], [], []
-    for group in range(groups):
-        scaled = jnp.concatenate(
-            [q_rows[:, (group * wide + k) * HD : (group * wide + k + 1) * HD] for k in range(wide)], axis=0
-        ).astype(F32) * factor
-        coarse = scaled.astype(BF16)
-        fine = (scaled - coarse.astype(F32)).astype(BF16)
-        queries.append(jnp.concatenate([coarse, fine], axis=1))
-
-    def score(group, piece):
-        source, base, i = piece
-        keys = source[i : i + step, :]
-        s = nt_dot(jnp.concatenate([keys, keys], axis=1), queries[group])
-        s = s + jnp.concatenate([hidden[base + i : base + i + step, :]] * wide, axis=1)
-        scores[group % 2, base + i : base + i + step, :] = s
-        return jnp.max(s.reshape(step // 8, 8, wide * rows), axis=0)
-
-    def weigh(group, piece, lift):
-        _, base, i = piece
-        s = scores[group % 2, base + i : base + i + step, :]
-        probs[group % 2, base + i : base + i + step, :] = jnp.exp2((s - lift).astype(BF16))
-
-    def finish_peak(group, run):
-        keys = key_fresh[...]
-        s = nt_dot(jnp.concatenate([keys, keys], axis=1), queries[group])
-        s = s + jnp.concatenate([hidden[2 * cache_here :, :]] * wide, axis=1)
-        peak = jnp.maximum(jnp.max(run, axis=0, keepdims=True), jnp.max(s, axis=0, keepdims=True))
-        peak = jnp.maximum(peak, FLOOR).astype(BF16).astype(F32)
-        return peak, jnp.exp2((s - peak).astype(BF16))
-
-    stats = [[None] * (3 * heads_owner) for _ in range(owners)]
-
-    def total(group, peak, p_new):
-        sums = nn_dot(v_turned[...], probs[group % 2])
-        numer = sums[:HD] + nn_dot(value_new, p_new)
-        denom = sums[HD : HD + 1] + jnp.sum(p_new.astype(F32), axis=0, keepdims=True)
-        for k in range(wide):
-            owner, h = divmod(group * wide + k, heads_owner)
-            cols = slice(k * rows, (k + 1) * rows)
+    scaled = jnp.concatenate([q_rows[:, h * HD : (h + 1) * HD] for h in range(heads)], axis=0)
+    scaled = scaled.astype(F32) * factor
+    coarse = scaled.astype(BF16)
+    fine = (scaled - coarse.astype(F32)).astype(BF16)
+    queries = jnp.concatenate([coarse, fine], axis=1)
+
+    def score(keys, mask):
+        s = nt_dot(jnp.concatenate([keys, keys], axis=1), queries)
+        return s + jnp.concatenate([mask] * heads, axis=1)
+
+    s_new = score(key_fresh[...], hidden[2 * cache_here :, :])
+    run = jnp.max(s_new.reshape(home_rows // 8, 8, heads * rows), axis=0)
+    for source, base, i in pieces:
+        s = score(source[i : i + step, :], hidden[base + i : base + i + step, :])
+        scores[base + i : base + i + step, :] = s
+        run = jnp.maximum(run, jnp.max(s.reshape(step // 8, 8, heads * rows), axis=0))
+    peak = jnp.maximum(jnp.max(run, axis=0, keepdims=True), FLOOR).astype(BF16).astype(F32)
+    p_new = jnp.exp2((s_new - peak).astype(BF16))
+    sums = None
+    for _, base, i in pieces:
+        at = slice(base + i, base + i + step)
+        p = jnp.exp2((scores[at, :] - peak).astype(BF16))
+        term = nn_dot(v_turned[:, at], p)
+        sums = term if sums is None else sums + term
+    numer = sums[:HD] + nn_dot(value_new, p_new)
+    denom = sums[HD : HD + 1] + jnp.sum(p_new.astype(F32), axis=0, keepdims=True)
+    high = denom.astype(BF16).astype(F32)
+    low = denom - high
+    for owner in range(owners):
+        across = [slice((owner * heads_owner + h) * rows, (owner * heads_owner + h + 1) * rows) for h in range(heads_owner)]
+        for h, cols in enumerate(across):
             out[owner, h * HD : (h + 1) * HD, :] = numer[:, cols].astype(BF16)
-            high = denom[:, cols].astype(BF16).astype(F32)
-            stats[owner][h] = peak[:, cols]
-            stats[owner][heads_owner + h] = high
-            stats[owner][2 * heads_owner + h] = denom[:, cols] - high
-
-    previous = None
-    for group in range(groups + 1):
-        run = None
-        for piece in pieces:
-            if group < groups:
-                top = score(group, piece)
-                run = top if run is None else jnp.maximum(run, top)
-            if previous is not None:
-                weigh(group - 1, piece, previous[0])
-        if previous is not None:
-            total(group - 1, *previous)
-        if group < groups:
-            previous = finish_peak(group, run)
-    for owner in range(owners):
-        filled = stats[owner] + [jnp.zeros_like(stats[owner][0])] * (STATS - len(stats[owner]))
+        filled = [kind[:, cols] for kind in (peak, high, low) for cols in across]
+        filled += [jnp.zeros_like(filled[0])] * (STATS - len(filled))
         out[owner, heads_owner * HD :, :] = jnp.concatenate(filled, axis=0).astype(BF16)
 
 
@@ -132,7 +104,6 @@
     owners = chips // kv_heads
     height = heads_owner * HD + STATS
     step = 256
-    wide = min(2, owners * heads_owner)
     kv = lambda g, place: (0, g)
     shape = (owners, heads_owner, home_rows, rows, cache_here, step)
     work = rows * heads_owner * chips * 2 * cache_here
@@ -150,8 +121,7 @@
                 pltpu.VMEM((rows, owners * heads_owner * HD), BF16),
                 pltpu.VMEM((HD + STATS, 2 * cache_here), BF16),
                 pltpu.VMEM((2 * cache_here + home_rows, rows), F32),
-                pltpu.VMEM((2, 2 * cache_here, wide * rows), F32),
-                pltpu.VMEM((2, 2 * cache_here, wide * rows), BF16),
+                pltpu.VMEM((2 * cache_here, owners * heads_owner * rows), F32),
             ],
         ),
         out_shape=jax.ShapeDtypeStruct((chips, height, rows), BF16),
@@ -203,7 +173,7 @@
     )(place, *chunks, weight_own, weight_other)
 
 
-def norm_body(parts, residual, gain, chooser, middle_out, sent):
+def norm_body(parts, residual, gain, chooser, done, middle_out, sent):
     total = parts[0].astype(F32)
     for s in range(1, parts.shape[0]):
         total = total + parts[s].astype(F32)
@@ -215,12 +185,12 @@
     sent[...] = nn_dot(chooser[...], normed).astype(BF16)
 
 
-def norm_and_dispatch(parts, residual, gain, chooser):
+def norm_and_dispatch(parts, residual, gain, chooser, done):
     vmem = pl.BlockSpec(memory_space=pltpu.VMEM)
     rows, width = residual.shape
     return pl.pallas_call(
         norm_body,
-        in_specs=[vmem] * 4,
+        in_specs=[vmem] * 5,
         out_specs=[vmem] * 2,
         out_shape=[
             jax.ShapeDtypeStruct((rows, width), BF16),
@@ -231,55 +201,75 @@
             flops=2 * chooser.shape[0] * rows * width, bytes_accessed=2 * MIB, transcendentals=0
         ),
         name="norm_and_dispatch",
-    )(parts, residual, gain, chooser)
-
-
-def experts_body(experts, arrived, w_gate, w_up, w_down, out, total):
-    expert, chunk = pl.program_id(0), pl.program_id(1)
-    rows = arrived.shape[0]
-    gate = nn_dot(arrived[...], w_gate[0])
-    upward = nn_dot(arrived[...], w_up[0])
-    hidden = gate / (1.0 + jnp.exp(-gate)) * upward
-    slot = lax.broadcasted_iota(jnp.int32, hidden.shape, 0)
-    mine = lax.rem(slot, experts * MOST) // MOST == expert
-    hidden = jnp.where(mine, hidden, 0.0).astype(BF16)
-    product = nn_dot(hidden, w_down[0])
-    first = (expert == 0) & (chunk == 0)
-    last = (expert == pl.num_programs(0) - 1) & (chunk == pl.num_programs(1) - 1)
-
-    @pl.when(first)
-    def _():
-        total[...] = product
-
-    @pl.when(jnp.logical_not(first))
-    def _():
-        total[...] += product
-
-    @pl.when(last)
-    def _():
-        out[...] = total[...].astype(BF16)
+    )(parts, residual, gain, chooser, done)
+
+
+def fetch_body(after, gate, up, down, gate_out, up_out, down_out, done, sems):
+    copies = [
+        pltpu.make_async_copy(source, held, sems.at[k])
+        for k, (source, held) in enumerate(((gate, gate_out), (up, up_out), (down, down_out)))
+    ]
+    for copy in copies:
+        copy.start()
+    for copy in copies:
+        copy.wait()
+    done[...] = jnp.zeros_like(done)
+
+
+def fetch(after, weights):
+    anywhere = pl.BlockSpec(memory_space=pl.ANY)
+    return pl.pallas_call(
+        fetch_body,
+        in_specs=[anywhere] * (1 + len(weights)),
+        out_specs=[pl.BlockSpec(memory_space=pltpu.VMEM)] * (1 + len(weights)),
+        out_shape=[pltpu.VMEM(w.shape, w.dtype) for w in weights]
+        + [jax.ShapeDtypeStruct((8, HD), F32)],
+        scratch_shapes=[pltpu.SemaphoreType.DMA((len(weights),))],
+        compiler_params=pltpu.CompilerParams(vmem_limit_bytes=1 * MIB),
+        cost_estimate=pl.CostEstimate(
+            flops=0, bytes_accessed=2 * sum(w.size * 2 for w in weights), transcendentals=0
+        ),
+        name="fetch",
+    )(after, *weights)
+
+
+def experts_body(arrived, w_gate, w_up, w_down, out):
+    experts, _, depth = w_gate.shape
+    rows, width = arrived.shape
+    slot = lax.broadcasted_iota(jnp.int32, (rows, 1), 0)
+    values = arrived[...]
+    step = 256
+    hidden = []
+    for e in range(experts):
+        mine = lax.rem(slot, experts * MOST) // MOST == e
+        parts = []
+        for f in range(0, depth, step):
+            gate = nn_dot(values, w_gate[e, :, f : f + step])
+            upward = nn_dot(values, w_up[e, :, f : f + step])
+            part = gate / (1.0 + jnp.exp(-gate)) * upward
+            parts.append(jnp.where(mine, part, 0.0).astype(BF16))
+        hidden.append(jnp.concatenate(parts, axis=1))
+    step = 512
+    for c in range(0, width, step):
+        total = nn_dot(hidden[0], w_down[0, :, c : c + step])
+        for e in range(1, experts):
+            total = total + nn_dot(hidden[e], w_down[e, :, c : c + step])
+        out[:, c : c + step] = total.astype(BF16)
 
 
 def run_experts(arrived, w_gate, w_up, w_down):
     rows, width = arrived.shape
     experts, _, hidden = w_gate.shape
-    block = 256
-    return pl.pallas_call(
-        functools.partial(experts_body, experts),
-        grid=(experts, hidden // block),
-        in_specs=[
-            pl.BlockSpec((rows, width), lambda e, f: (0, 0)),
-            pl.BlockSpec((1, width, block), lambda e, f: (e, 0, f)),
-            pl.BlockSpec((1, width, block), lambda e, f: (e, 0, f)),
-            pl.BlockSpec((1, block, width), lambda e, f: (e, f, 0)),
-        ],
-        out_specs=pl.BlockSpec((rows, width), lambda e, f: (0, 0)),
+    vmem = pl.BlockSpec(memory_space=pltpu.VMEM)
+    return pl.pallas_call(
+        experts_body,
+        in_specs=[vmem] * 4,
+        out_specs=vmem,
         out_shape=jax.ShapeDtypeStruct((rows, width), BF16),
-        scratch_shapes=[pltpu.VMEM((rows, width), F32)],
-        compiler_params=pltpu.CompilerParams(vmem_limit_bytes=60 * MIB),
+        compiler_params=pltpu.CompilerParams(vmem_limit_bytes=24 * MIB),
         cost_estimate=pl.CostEstimate(
             flops=6 * rows * width * experts * hidden,
-            bytes_accessed=6 * width * experts * hidden,
+            bytes_accessed=2 * MIB,
             transcendentals=rows * experts * hidden,
         ),
         name="experts",
@@ -365,7 +355,7 @@
     fine = (spread - coarse.astype(F32)).astype(BF16)
 
     gathered = []
-    for own_q, other_q in query_chunks:
+    for chunk, (own_q, other_q) in enumerate(query_chunks):
         sums = attention(
             place,
             own_q,
@@ -378,12 +368,17 @@
             chips,
             key_cache.shape[1] // HD,
         )
+        if chunk + 1 < len(query_chunks):
+            own_next, other_next = query_chunks[chunk + 1]
+            sums, other_next = lax.optimization_barrier((sums, other_next))
+            query_chunks[chunk + 1] = (own_next, other_next)
         gathered.append(
             lax.all_to_all(
                 sums, "ctx", split_axis=0, concat_axis=0, axis_index_groups=same_core, tiled=True
             )
         )
     share = project(place, gathered, out_weight, weight_other)
+    *held, done = fetch(share, (w_gate, w_up, w_down))
     shares = lax.all_to_all(
         share.reshape(chips, home_rows, width),
         "ctx",
@@ -392,11 +387,11 @@
         axis_index_groups=same_core,
         tiled=True,
     )
-    middle, outgoing = norm_and_dispatch(shares, residual, norm_gain.reshape(1, width), chooser)
+    middle, outgoing = norm_and_dispatch(shares, residual, norm_gain.reshape(1, width), chooser, done)
     arrived = lax.all_to_all(
         outgoing.reshape(devices, experts * MOST, width), "ctx", split_axis=0, concat_axis=0, tiled=True
     )
-    produced = run_experts(arrived.reshape(slots, width), w_gate, w_up, w_down)
+    produced = run_experts(arrived.reshape(slots, width), *held)
     returned = lax.all_to_all(
         produced.reshape(devices, experts * MOST, width), "ctx", split_axis=0, concat_axis=0, tiled=True
     )

time: 149 us -> 155 us (1.040)
  local copies, waits for them, and re-layouts: 5.49 us -> 29.7 us
  waiting for transfers between devices: 60 us -> 47 us
  Pallas kernels: 33.5 us -> 28.7 us
  blocking collectives: 18.1 us -> 20.4 us
  starting transfers between devices: 30.2 us -> 28.1 us
    unnamed x28 -> x48, local copies, waits for them, and re-layouts: 1.63 us -> 25.8 us
    all_to_all x1, waiting for transfers between devices: 13 us -> 0.01 us  [on_device(): lax.all_to_all(share.reshape(chips, home_rows, width), 'ctx', split_axis=...]
    ppermute x2, waiting for transfers between devices: 12 us -> 5.48 us  [on_device(): query_chunks.append((mine, lax.ppermute(mine, 'ctx', across)))]
    pallas_call x2 -> x3, Pallas kernels: 11.2 us -> 5.22 us  [the longest x1 3.5 us: run_experts(): pl.pallas_call(experts_body, in_specs=[vmem] * 4, out_specs=vmem, out_sha...]
    all_to_all x2, waiting for transfers between devices: 13.8 us -> 18.2 us  [on_device(): lax.all_to_all(sums, 'ctx', split_axis=0, concat_axis=0, axis_index_group...]
    all_to_all x2, starting transfers between devices: 11.2 us -> 8.81 us  [on_device(): lax.all_to_all(sums, 'ctx', split_axis=0, concat_axis=0, axis_index_group...]
    all_to_all x1, blocking collectives: 18.1 us -> 20.4 us  [on_device(): lax.all_to_all(outgoing.reshape(devices, experts * MOST, width), 'ctx', s...]
    ppermute x4, waiting for transfers between devices: 6.91 us -> 8.99 us  [on_device(): mine = jnp.concatenate([mine, lax.ppermute(mine, 'ctx', step)], axis=0)]
  transfers between devices with their start and end apart: 13 -> 13, of which waited for: 7 -> 6; matrix products, arithmetic and copies ran while one was open for 2% -> 2% of each run, Pallas kernels for 13% -> 14%
where the time goes in v4:
time: 155 us
  waiting for transfers between devices  47 us (30%)
  local copies, waits for them, and re-layouts  29.7 us (19%)
  Pallas kernels  28.7 us (19%)
  starting transfers between devices  28.1 us (18%)
  blocking collectives  20.4 us (13%)
    unnamed x48, local copies, waits for them, and re-layouts  25.8 us
    pallas_call x2, Pallas kernels, attention(): pl.pallas_call(functools.partial(attention_body, shape), grid_spec=pltpu....  20.5 us
    all_to_all x1, blocking collectives, on_device(): lax.all_to_all(outgoing.reshape(devices, experts * MOST, width), 'ctx', s...  20.4 us
    all_to_all x2, waiting for transfers between devices, on_device(): lax.all_to_all(sums, 'ctx', split_axis=0, concat_axis=0, axis_index_group...  18.2 us
    all_to_all x1, waiting for transfers between devices, on_device(): lax.all_to_all(produced.reshape(devices, experts * MOST, width), 'ctx', s...  14.3 us
    ppermute x4, waiting for transfers between devices, on_device(): mine = jnp.concatenate([mine, lax.ppermute(mine, 'ctx', step)], axis=0)  8.99 us
    all_to_all x2, starting transfers between devices, on_device(): lax.all_to_all(sums, 'ctx', split_axis=0, concat_axis=0, axis_index_group...  8.81 us
    ppermute x4, starting transfers between devices, on_device(): mine = jnp.concatenate([mine, lax.ppermute(mine, 'ctx', step)], axis=0)  7.3 us
  transfers between devices with their start and end apart: 13, of which 6 were waited for; matrix products, arithmetic and copies ran while one was open for 2% of the time, Pallas kernels for 14%

profile of v4, /device:TPU:0, one launch (start us, length us, event | category | flops | bytes accessed | tf_op | source)
XLA Modules:
  0.0 154.7 jit_solution(2623325323422788794)
XLA Ops:
  0.0 1.0 reshape.38
  1.0 0.5 slice_reduce_fusion
  1.5 3.1 %collective-permute-start = (bf16[16,2048]{1,0:T(8,128)(2,1)S(1)}, bf16[16,2048]{1,0:T(8,128)(2,1)S(1)}, u32[]{:S(2)}, u32[]{:S(2)}) collective-permute-start(bf16[16,2048]{1,0:T(8,128)(2,1)S(1)} %bitcast.23), channel_id=1, source_target_pairs={{0,4},{1,5},{2,6},{3,7},{4,0},{5,1},{6,2},{7,3},{8,12},{9,13},{10,... | collective-permute-start | bytes 196616 | tf_op jit(solution)/shard_map/ppermute | solution.py:333
  4.7 0.1 collective-permute-start.5
  4.8 0.5 collective-permute-start.4
  5.4 0.8 reshape.39
  6.2 0.7 reshape.40.lens
  6.8 0.7 stack.27.place
  7.5 3.0 %collective-permute-start.1 = (bf16[32,2048]{1,0:T(8,128)(2,1)S(1)}, bf16[32,2048]{1,0:T(8,128)(2,1)S(1)}, u32[]{:S(2)}, u32[]{:S(2)}) collective-permute-start(bf16[32,2048]{1,0:T(8,128)(2,1)S(1)} %pad_maximum_fusion), channel_id=1, source_target_pairs={{0,8},{1,9},{2,10},{3,11},{4,12},{5,13},{6,14},{7,15},{8,0},{9,1},... | collective-permute-start | bytes 393224 | tf_op jit(solution)/shard_map/ppermute | solution.py:333
  10.6 1.1 collective-permute-start.6
  11.7 8.8 %collective-permute-done.1 = bf16[32,2048]{1,0:T(8,128)(2,1)S(1)} collective-permute-done((bf16[32,2048]{1,0:T(8,128)(2,1)S(1)}, bf16[32,2048]{1,0:T(8,128)(2,1)S(1)}, u32[]{:S(2)}, u32[]{:S(2)}) %collective-permute-start.1) | collective-permute-done | bytes 131104 | tf_op jit(solution)/shard_map/ppermute | solution.py:333
  20.5 2.0 %collective-permute-start.2 = (bf16[64,2048]{1,0:T(8,128)(2,1)S(1)}, bf16[64,2048]{1,0:T(8,128)(2,1)S(1)}, u32[]{:S(2)}, u32[]{:S(2)}) collective-permute-start(bf16[64,2048]{1,0:T(8,128)(2,1)S(1)} %constant_dynamic-update-slice_fusion.own_q), channel_id=1, source_target_pairs={{0,2},{1,3},{2,0},{3,1},{4,6},{5,7},{6,4},{7,5},{8,10},{9,11},{10,... | collective-permute-start | bytes 786440 | tf_op jit(solution)/shard_map/ppermute | solution.py:335
  22.4 0.2 collective-permute-done.6
  22.7 1.6 %collective-permute-start.7 = (bf16[64,2048]{1,0:T(8,128)(2,1)S(1)}, bf16[64,2048]{1,0:T(8,128)(2,1)S(1)}, u32[]{:S(2)}, u32[]{:S(2)}) collective-permute-start(bf16[64,2048]{1,0:T(8,128)(2,1)S(1)} %constant_dynamic-update-slice_fusion.3.own_q), channel_id=1, source_target_pairs={{0,2},{1,3},{2,0},{3,1},{4,6},{5,7},{6,4},{7,5},{8,10},{9,11},{10,... | collective-permute-start | bytes 786440 | tf_op jit(solution)/shard_map/ppermute | solution.py:335
  24.3 5.5 %collective-permute-done.2.other_q = bf16[64,2048]{1,0:T(8,128)(2,1)S(1)} collective-permute-done((bf16[64,2048]{1,0:T(8,128)(2,1)S(1)}, bf16[64,2048]{1,0:T(8,128)(2,1)S(1)}, u32[]{:S(2)}, u32[]{:S(2)}) %collective-permute-start.2) | collective-permute-done | bytes 262176 | tf_op jit(solution)/shard_map/ppermute | solution.py:335
  29.8 0.7 copy-done.19
  30.5 0.3 copy-done.17
  30.8 10.3 %attention.2 = bf16[8,272,128]{2,1,0:T(8,128)(2,1)} custom-call(s32[6]{0:T(128)} %stack.27.place, bf16[64,2048]{1,0:T(8,128)(2,1)} %copy-done.13, bf16[64,2048]{1,0:T(8,128)(2,1)} %copy-done.19, bf16[1024,512]{1,0:T(8,128)(2,1)} %key_own.3, bf16[1024,512]{1,0:T(8,128)(2,1)} %copy-done.17, bf16[1024,512]{1,0:T(8,128)(2,1)} %value_own.3, ...), custom_call_target="tpu_custom_call" | custom-call | flops 3221225472 | bytes 8388608 | tf_op jit(solution)/shard_map/attention/pallas_call | solution.py:110
  41.1 5.2 %all-to-all-start = ((bf16[8,272,128]{2,1,0:T(8,128)(2,1)}), bf16[8,272,128]{2,1,0:T(8,128)(2,1)S(1)}, u32[]{:S(2)}, u32[]{:S(2)}) async-start(bf16[8,272,128]{2,1,0:T(8,128)(2,1)} %attention.2), calls=%async_computation | async-start | bytes 1114112 | tf_op jit(solution)/shard_map/all_to_all | solution.py:376
  46.4 10.3 %attention.3 = bf16[8,272,128]{2,1,0:T(8,128)(2,1)} custom-call(s32[6]{0:T(128)} %stack.27.place, bf16[64,2048]{1,0:T(8,128)(2,1)} %copy-done.12, bf16[64,2048]{1,0:T(8,128)(2,1)} %copy-done.18, bf16[1024,512]{1,0:T(8,128)(2,1)} %key_own.3, bf16[1024,512]{1,0:T(8,128)(2,1)} %copy-done.17, bf16[1024,512]{1,0:T(8,128)(2,1)} %value_own.3, ...), custom_call_target="tpu_custom_call" | custom-call | flops 3221225472 | bytes 8388608 | tf_op jit(solution)/shard_map/attention/pallas_call | solution.py:110
  56.7 3.0 %all-to-all-done.refs_0_ = bf16[8,272,128]{2,1,0:T(8,128)(2,1)S(1)} async-done(((bf16[8,272,128]{2,1,0:T(8,128)(2,1)}), bf16[8,272,128]{2,1,0:T(8,128)(2,1)S(1)}, u32[]{:S(2)}, u32[]{:S(2)}) %all-to-all-start) | async-done | bytes 557088 | tf_op jit(solution)/shard_map/all_to_all | solution.py:376
  59.8 3.6 %all-to-all-start.1 = ((bf16[8,272,128]{2,1,0:T(8,128)(2,1)}), bf16[8,272,128]{2,1,0:T(8,128)(2,1)S(1)}, u32[]{:S(2)}, u32[]{:S(2)}) async-start(bf16[8,272,128]{2,1,0:T(8,128)(2,1)} %attention.3), calls=%async_computation.1 | async-start | bytes 1114112 | tf_op jit(solution)/shard_map/all_to_all | solution.py:376
  63.4 15.2 %all-to-all-done.1.refs_1_ = bf16[8,272,128]{2,1,0:T(8,128)(2,1)S(1)} async-done(((bf16[8,272,128]{2,1,0:T(8,128)(2,1)}), bf16[8,272,128]{2,1,0:T(8,128)(2,1)S(1)}, u32[]{:S(2)}, u32[]{:S(2)}) %all-to-all-start.1) | async-done | bytes 557088 | tf_op jit(solution)/shard_map/all_to_all | solution.py:376
  78.6 2.1 %project.1.after = bf16[128,2048]{1,0:T(8,128)(2,1)} custom-call(s32[6]{0:T(128)S(1)} %copy-done.11, bf16[8,272,128]{2,1,0:T(8,128)(2,1)S(1)} %all-to-all-done.refs_0_, bf16[8,272,128]{2,1,0:T(8,128)(2,1)S(1)} %all-to-all-done.1.refs_1_, bf16[256,2048]{1,0:T(8,128)(2,1)S(1)} %copy-done.9, bf16[256,2048]{1,0:T(8,128)(2,1)S(1)} %collective-permute-done.8.refs_3_), custom_call_target="tpu_custom_call" | custom-call | flops 268435456 | bytes 4194304 | tf_op jit(solution)/shard_map/project/pallas_call | solution.py:162
  80.7 3.6 %all-to-all-start.2 = ((bf16[8,16,2048]{2,1,0:T(8,128)(2,1)}), bf16[8,16,2048]{2,1,0:T(8,128)(2,1)S(1)}, u32[]{:S(2)}, u32[]{:S(2)}) async-start(bf16[8,16,2048]{2,1,0:T(8,128)(2,1)} %bitcast.6), calls=%async_computation.2 | async-start | bytes 1048576 | tf_op jit(solution)/shard_map/all_to_all | solution.py:382
  84.3 0.1 copy.27
  84.4 0.1 eq.31
  84.5 0.2 convert_reduce_fusion
  84.6 0.1 reduce_sum.21
  84.8 0.1 fusion
  84.9 0.1 copy.29
  85.0 2.8 %copy-done.6 = bf16[2,2048,768]{2,1,0:T(8,128)(2,1)S(1)} copy-done((bf16[2,2048,768]{2,1,0:T(8,128)(2,1)S(1)}, bf16[2,2048,768]{2,1,0:T(8,128)(2,1)}, u32[]{:S(2)}) %copy-start.6) | copy-done | bytes 6291480
  87.8 2.8 %copy-done.7 = bf16[2,2048,768]{2,1,0:T(8,128)(2,1)S(1)} copy-done((bf16[2,2048,768]{2,1,0:T(8,128)(2,1)S(1)}, bf16[2,2048,768]{2,1,0:T(8,128)(2,1)}, u32[]{:S(2)}) %copy-start.7) | copy-done | bytes 6291480
  90.6 2.8 %copy-done.8 = bf16[2,768,2048]{2,1,0:T(8,128)(2,1)S(1)} copy-done((bf16[2,768,2048]{2,1,0:T(8,128)(2,1)S(1)}, bf16[2,768,2048]{2,1,0:T(8,128)(2,1)}, u32[]{:S(2)}) %copy-start.8) | copy-done | bytes 6291480
  93.4 1.3 fetch.1
  94.7 2.6 %copy-done = bf16[2,2048,768]{2,1,0:T(8,128)(2,1)} copy-done((bf16[2,2048,768]{2,1,0:T(8,128)(2,1)}, bf16[2,2048,768]{2,1,0:T(8,128)(2,1)S(1)}, u32[]{:S(2)}) %copy-start) | copy-done | bytes 6291480
  97.3 2.6 %copy-done.2 = bf16[2,2048,768]{2,1,0:T(8,128)(2,1)} copy-done((bf16[2,2048,768]{2,1,0:T(8,128)(2,1)}, bf16[2,2048,768]{2,1,0:T(8,128)(2,1)S(1)}, u32[]{:S(2)}) %copy-start.2) | copy-done | bytes 6291480
  99.9 2.6 %copy-done.4 = bf16[2,768,2048]{2,1,0:T(8,128)(2,1)} copy-done((bf16[2,768,2048]{2,1,0:T(8,128)(2,1)}, bf16[2,768,2048]{2,1,0:T(8,128)(2,1)S(1)}, u32[]{:S(2)}) %copy-start.4) | copy-done | bytes 6291480
  102.5 0.4 norm_and_dispatch.1
  103.0 20.4 %all_to_all.25 = bf16[16,8,2048]{2,1,0:T(8,128)(2,1)S(1)} all-to-all(bf16[16,8,2048]{2,1,0:T(8,128)(2,1)S(1)} %bitcast.18), channel_id=1, replica_groups=mesh['groups'=2,'ctx'=16] {'ctx'}, dimensions={0} | all-to-all | bytes 1048576 | tf_op jit(solution)/shard_map/all_to_all | solution.py:391
  123.3 2.8 %copy-done.1 = bf16[2,2048,768]{2,1,0:T(8,128)(2,1)S(1)} copy-done((bf16[2,2048,768]{2,1,0:T(8,128)(2,1)S(1)}, bf16[2,2048,768]{2,1,0:T(8,128)(2,1)}, u32[]{:S(2)}) %copy-start.1) | copy-done | bytes 6291480
  126.1 2.8 %copy-done.3 = bf16[2,2048,768]{2,1,0:T(8,128)(2,1)S(1)} copy-done((bf16[2,2048,768]{2,1,0:T(8,128)(2,1)S(1)}, bf16[2,2048,768]{2,1,0:T(8,128)(2,1)}, u32[]{:S(2)}) %copy-start.3) | copy-done | bytes 6291480
  128.9 2.8 %copy-done.5 = bf16[2,768,2048]{2,1,0:T(8,128)(2,1)S(1)} copy-done((bf16[2,768,2048]{2,1,0:T(8,128)(2,1)S(1)}, bf16[2,768,2048]{2,1,0:T(8,128)(2,1)}, u32[]{:S(2)}) %copy-start.5) | copy-done | bytes 6291480
  131.7 3.5 %experts.1 = bf16[128,2048]{1,0:T(8,128)(2,1)} custom-call(bf16[128,2048]{1,0:T(8,128)(2,1)S(1)} %bitcast.16, bf16[2,2048,768]{2,1,0:T(8,128)(2,1)S(1)} %copy-done.1, bf16[2,2048,768]{2,1,0:T(8,128)(2,1)S(1)} %copy-done.3, bf16[2,768,2048]{2,1,0:T(8,128)(2,1)S(1)} %copy-done.5), custom_call_target="tpu_custom_call" | custom-call | flops 2415919104 | bytes 2097152 | tf_op jit(solution)/shard_map/experts/pallas_call | solution.py:264
  135.2 4.1 %all-to-all-start.4 = ((bf16[16,8,2048]{2,1,0:T(8,128)(2,1)}), bf16[16,8,2048]{2,1,0:T(8,128)(2,1)S(1)}, u32[]{:S(2)}, u32[]{:S(2)}) async-start(bf16[16,8,2048]{2,1,0:T(8,128)(2,1)} %bitcast.10), calls=%async_computation.4 | async-start | bytes 1048576 | tf_op jit(solution)/shard_map/all_to_all | solution.py:395
  139.4 0.1 select_reduce_fusion
  139.5 14.3 %all-to-all-done.4 = bf16[16,8,2048]{2,1,0:T(8,128)(2,1)S(1)} async-done(((bf16[16,8,2048]{2,1,0:T(8,128)(2,1)}), bf16[16,8,2048]{2,1,0:T(8,128)(2,1)S(1)}, u32[]{:S(2)}, u32[]{:S(2)}) %all-to-all-start.4) | async-done | bytes 524320 | tf_op jit(solution)/shard_map/all_to_all | solution.py:395
  153.8 0.9 mix.1
  (54 shorter events, 0.4 us)
Async XLA Ops:
  1.5 6.0 %collective-permute-start = (bf16[16,2048]{1,0:T(8,128)(2,1)S(1)}, bf16[16,2048]{1,0:T(8,128)(2,1)S(1)}, u32[]{:S(2)}, u32[]{:S(2)}) collective-permute-start(bf16[16,2048]{1,0:T(8,128)(2,1)S(1)} %bitcast.23), channel_id=1, source_target_pairs={{0,4},{1,5},{2,6},{3,7},{4,0},{5,1},{6,2},{7,3},{8,12},{9,13},{10,... | collective-permute-start | bytes 196616 | tf_op jit(solution)/shard_map/ppermute | solution.py:333
  4.7 5.9 %collective-permute-start.5 = (bf16[16,2048]{1,0:T(8,128)(2,1)S(1)}, bf16[16,2048]{1,0:T(8,128)(2,1)S(1)}, u32[]{:S(2)}, u32[]{:S(2)}) collective-permute-start(bf16[16,2048]{1,0:T(8,128)(2,1)S(1)} %bitcast.20), channel_id=1, source_target_pairs={{0,4},{1,5},{2,6},{3,7},{4,0},{5,1},{6,2},{7,3},{8,12},{9,13},{10,... | collective-permute-start | bytes 196616 | tf_op jit(solution)/shard_map/ppermute | solution.py:333
  4.7 25.1 %collective-permute-start.3 = (bf16[1024,512]{1,0:T(8,128)(2,1)}, bf16[1024,512]{1,0:T(8,128)(2,1)S(1)}, u32[]{:S(2)}, u32[]{:S(2)}) collective-permute-start(bf16[1024,512]{1,0:T(8,128)(2,1)} %key_own.3), channel_id=1, source_target_pairs={{0,1},{1,0},{2,3},{3,2},{4,5},{5,4},{6,7},{7,6},{8,9},{9,8},{10,11... | collective-permute-start | bytes 3145736 | tf_op jit(solution)/shard_map/ppermute | solution.py:336
  4.8 25.0 %collective-permute-start.4 = (bf16[1024,512]{1,0:T(8,128)(2,1)}, bf16[1024,512]{1,0:T(8,128)(2,1)}, u32[]{:S(2)}, u32[]{:S(2)}) collective-permute-start(bf16[1024,512]{1,0:T(8,128)(2,1)} %value_own.3), channel_id=1, source_target_pairs={{0,1},{1,0},{2,3},{3,2},{4,5},{5,4},{6,7},{7,6},{8,9},{9,8},{10,11... | collective-permute-start | bytes 3145736 | tf_op jit(solution)/shard_map/ppermute | solution.py:337
  7.5 12.9 %collective-permute-start.1 = (bf16[32,2048]{1,0:T(8,128)(2,1)S(1)}, bf16[32,2048]{1,0:T(8,128)(2,1)S(1)}, u32[]{:S(2)}, u32[]{:S(2)}) collective-permute-start(bf16[32,2048]{1,0:T(8,128)(2,1)S(1)} %pad_maximum_fusion), channel_id=1, source_target_pairs={{0,8},{1,9},{2,10},{3,11},{4,12},{5,13},{6,14},{7,15},{8,0},{9,1},... | collective-permute-start | bytes 393224 | tf_op jit(solution)/shard_map/ppermute | solution.py:333
  10.6 12.1 %collective-permute-start.6 = (bf16[32,2048]{1,0:T(8,128)(2,1)S(1)}, bf16[32,2048]{1,0:T(8,128)(2,1)S(1)}, u32[]{:S(2)}, u32[]{:S(2)}) collective-permute-start(bf16[32,2048]{1,0:T(8,128)(2,1)S(1)} %pad_maximum_fusion.1), channel_id=1, source_target_pairs={{0,8},{1,9},{2,10},{3,11},{4,12},{5,13},{6,14},{7,15},{8,0},{9,1},... | collective-permute-start | bytes 393224 | tf_op jit(solution)/shard_map/ppermute | solution.py:333
  20.5 9.3 %copy-start.13 = (bf16[64,2048]{1,0:T(8,128)(2,1)}, bf16[64,2048]{1,0:T(8,128)(2,1)S(1)}, u32[]{:S(2)}) copy-start(bf16[64,2048]{1,0:T(8,128)(2,1)S(1)} %constant_dynamic-update-slice_fusion.own_q) | copy-start | bytes 786436
  20.5 9.3 %collective-permute-start.2 = (bf16[64,2048]{1,0:T(8,128)(2,1)S(1)}, bf16[64,2048]{1,0:T(8,128)(2,1)S(1)}, u32[]{:S(2)}, u32[]{:S(2)}) collective-permute-start(bf16[64,2048]{1,0:T(8,128)(2,1)S(1)} %constant_dynamic-update-slice_fusion.own_q), channel_id=1, source_target_pairs={{0,2},{1,3},{2,0},{3,1},{4,6},{5,7},{6,4},{7,5},{8,10},{9,11},{10,... | collective-permute-start | bytes 786440 | tf_op jit(solution)/shard_map/ppermute | solution.py:335
  22.7 18.5 %copy-start.12 = (bf16[64,2048]{1,0:T(8,128)(2,1)}, bf16[64,2048]{1,0:T(8,128)(2,1)S(1)}, u32[]{:S(2)}) copy-start(bf16[64,2048]{1,0:T(8,128)(2,1)S(1)} %constant_dynamic-update-slice_fusion.3.own_q) | copy-start | bytes 786436
  22.7 23.7 %copy-start.9 = (bf16[256,2048]{1,0:T(8,128)(2,1)S(1)}, bf16[256,2048]{1,0:T(8,128)(2,1)}, u32[]{:S(2)}) copy-start(bf16[256,2048]{1,0:T(8,128)(2,1)} %refs_2_.1) | copy-start | bytes 3145732
  22.7 18.4 %collective-permute-start.7 = (bf16[64,2048]{1,0:T(8,128)(2,1)S(1)}, bf16[64,2048]{1,0:T(8,128)(2,1)S(1)}, u32[]{:S(2)}, u32[]{:S(2)}) collective-permute-start(bf16[64,2048]{1,0:T(8,128)(2,1)S(1)} %constant_dynamic-update-slice_fusion.3.own_q), channel_id=1, source_target_pairs={{0,2},{1,3},{2,0},{3,1},{4,6},{5,7},{6,4},{7,5},{8,10},{9,11},{10,... | collective-permute-start | bytes 786440 | tf_op jit(solution)/shard_map/ppermute | solution.py:335
  29.8 0.7 copy-start.19
  29.8 1.0 copy-start.17
  41.1 5.3 %copy-start.18 = (bf16[64,2048]{1,0:T(8,128)(2,1)}, bf16[64,2048]{1,0:T(8,128)(2,1)S(1)}, u32[]{:S(2)}) copy-start(bf16[64,2048]{1,0:T(8,128)(2,1)S(1)} %collective-permute-done.7.other_q) | copy-start | bytes 786436
  41.1 18.7 %all-to-all-start = ((bf16[8,272,128]{2,1,0:T(8,128)(2,1)}), bf16[8,272,128]{2,1,0:T(8,128)(2,1)S(1)}, u32[]{:S(2)}, u32[]{:S(2)}) async-start(bf16[8,272,128]{2,1,0:T(8,128)(2,1)} %attention.2), calls=%async_computation | async-start | bytes 1114112 | tf_op jit(solution)/shard_map/all_to_all | solution.py:376
  46.3 32.3 %copy-start.11 = (s32[6]{0:T(128)S(1)}, s32[6]{0:T(128)}, u32[]{:S(2)}) copy-start(s32[6]{0:T(128)} %stack.27.place) | copy-start | bytes 76
  46.3 38.0 %copy-start.14 = (s32[16,8]{0,1:T(8,128)S(1)}, s32[16,8]{0,1:T(8,128)}, u32[]{:S(2)}) copy-start(s32[16,8]{0,1:T(8,128)} %param.23) | copy-start | bytes 1540
  46.3 38.5 %copy-start.15 = (bf16[2048]{0:T(1024)(128)(2,1)S(1)}, bf16[2048]{0:T(1024)(128)(2,1)}, u32[]{:S(2)}) copy-start(bf16[2048]{0:T(1024)(128)(2,1)} %param.22) | copy-start | bytes 12292
  46.4 17.0 %collective-permute-start.8 = (bf16[256,2048]{1,0:T(8,128)(2,1)S(1)}, bf16[256,2048]{1,0:T(8,128)(2,1)S(1)}, u32[]{:S(2)}, u32[]{:S(2)}) collective-permute-start(bf16[256,2048]{1,0:T(8,128)(2,1)S(1)} %copy-done.9), channel_id=1, source_target_pairs={{0,1},{1,0},{2,3},{3,2},{4,5},{5,4},{6,7},{7,6},{8,9},{9,8},{10,11... | collective-permute-start | bytes 3145736 | tf_op jit(solution)/shard_map/ppermute | solution.py:338
  59.8 18.8 %all-to-all-start.1 = ((bf16[8,272,128]{2,1,0:T(8,128)(2,1)}), bf16[8,272,128]{2,1,0:T(8,128)(2,1)S(1)}, u32[]{:S(2)}, u32[]{:S(2)}) async-start(bf16[8,272,128]{2,1,0:T(8,128)(2,1)} %attention.3), calls=%async_computation.1 | async-start | bytes 1114112 | tf_op jit(solution)/shard_map/all_to_all | solution.py:376
  80.7 21.9 %all-to-all-start.2 = ((bf16[8,16,2048]{2,1,0:T(8,128)(2,1)}), bf16[8,16,2048]{2,1,0:T(8,128)(2,1)S(1)}, u32[]{:S(2)}, u32[]{:S(2)}) async-start(bf16[8,16,2048]{2,1,0:T(8,128)(2,1)} %bitcast.6), calls=%async_computation.2 | async-start | bytes 1048576 | tf_op jit(solution)/shard_map/all_to_all | solution.py:382
  85.0 2.8 %copy-start.6 = (bf16[2,2048,768]{2,1,0:T(8,128)(2,1)S(1)}, bf16[2,2048,768]{2,1,0:T(8,128)(2,1)}, u32[]{:S(2)}) copy-start(bf16[2,2048,768]{2,1,0:T(8,128)(2,1)} %gate.1) | copy-start | bytes 18874372
  87.8 2.8 %copy-start.7 = (bf16[2,2048,768]{2,1,0:T(8,128)(2,1)S(1)}, bf16[2,2048,768]{2,1,0:T(8,128)(2,1)}, u32[]{:S(2)}) copy-start(bf16[2,2048,768]{2,1,0:T(8,128)(2,1)} %up.1) | copy-start | bytes 18874372
  90.6 2.8 %copy-start.8 = (bf16[2,768,2048]{2,1,0:T(8,128)(2,1)S(1)}, bf16[2,768,2048]{2,1,0:T(8,128)(2,1)}, u32[]{:S(2)}) copy-start(bf16[2,768,2048]{2,1,0:T(8,128)(2,1)} %down.1) | copy-start | bytes 18874372
  93.4 9.1 %copy-start.10 = (bf16[16,2048]{1,0:T(8,128)(2,1)S(1)}, bf16[16,2048]{1,0:T(8,128)(2,1)}, u32[]{:S(2)}) copy-start(bf16[16,2048]{1,0:T(8,128)(2,1)} %residual.1) | copy-start | bytes 196612
  94.7 2.7 %copy-start = (bf16[2,2048,768]{2,1,0:T(8,128)(2,1)}, bf16[2,2048,768]{2,1,0:T(8,128)(2,1)S(1)}, u32[]{:S(2)}) copy-start(bf16[2,2048,768]{2,1,0:T(8,128)(2,1)S(1)} %get-tuple-element.17.w_gate) | copy-start | bytes 18874372
  97.3 2.6 %copy-start.2 = (bf16[2,2048,768]{2,1,0:T(8,128)(2,1)}, bf16[2,2048,768]{2,1,0:T(8,128)(2,1)S(1)}, u32[]{:S(2)}) copy-start(bf16[2,2048,768]{2,1,0:T(8,128)(2,1)S(1)} %get-tuple-element.18.w_up) | copy-start | bytes 18874372
  99.9 2.6 %copy-start.4 = (bf16[2,768,2048]{2,1,0:T(8,128)(2,1)}, bf16[2,768,2048]{2,1,0:T(8,128)(2,1)S(1)}, u32[]{:S(2)}) copy-start(bf16[2,768,2048]{2,1,0:T(8,128)(2,1)S(1)} %get-tuple-element.19.w_down) | copy-start | bytes 18874372
  123.3 2.8 %copy-start.1 = (bf16[2,2048,768]{2,1,0:T(8,128)(2,1)S(1)}, bf16[2,2048,768]{2,1,0:T(8,128)(2,1)}, u32[]{:S(2)}) copy-start(bf16[2,2048,768]{2,1,0:T(8,128)(2,1)} %copy-done) | copy-start | bytes 18874372
  126.1 2.8 %copy-start.3 = (bf16[2,2048,768]{2,1,0:T(8,128)(2,1)S(1)}, bf16[2,2048,768]{2,1,0:T(8,128)(2,1)}, u32[]{:S(2)}) copy-start(bf16[2,2048,768]{2,1,0:T(8,128)(2,1)} %copy-done.2) | copy-start | bytes 18874372
  128.9 2.8 %copy-start.5 = (bf16[2,768,2048]{2,1,0:T(8,128)(2,1)S(1)}, bf16[2,768,2048]{2,1,0:T(8,128)(2,1)}, u32[]{:S(2)}) copy-start(bf16[2,768,2048]{2,1,0:T(8,128)(2,1)} %copy-done.4) | copy-start | bytes 18874372
  131.7 7.6 %copy-start.16 = (f32[16,8]{0,1:T(8,128)S(1)}, f32[16,8]{0,1:T(8,128)}, u32[]{:S(2)}) copy-start(f32[16,8]{0,1:T(8,128)} %param.24) | copy-start | bytes 1540
  135.2 18.6 %all-to-all-start.4 = ((bf16[16,8,2048]{2,1,0:T(8,128)(2,1)}), bf16[16,8,2048]{2,1,0:T(8,128)(2,1)S(1)}, u32[]{:S(2)}, u32[]{:S(2)}) async-start(bf16[16,8,2048]{2,1,0:T(8,128)(2,1)} %bitcast.10), calls=%async_computation.4 | async-start | bytes 1048576 | tf_op jit(solution)/shard_map/all_to_all | solution.py:395

commit v5 on v4

--- a/solution.py
+++ b/solution.py
@@ -30,7 +30,7 @@
 
 def attention_body(shape, place, own_q, other_q, key_own, key_other, value_own, value_other, key_fresh, value_fresh, lens, out, *scratch):
     owners, heads_owner, home_rows, rows, cache_here, step = shape
-    q_rows, v_turned, hidden, scores = scratch
+    q_rows, q_turned, hidden, scores = scratch
     chip, start_own, start_other, pair_place, ring_place = place[0], place[1], place[2], place[4], place[5]
     rings = rows // home_rows // 2
 
@@ -44,10 +44,7 @@
         token = lax.broadcasted_iota(jnp.int32, (home_rows, rows), 0)
         column = lax.broadcasted_iota(jnp.int32, (home_rows, rows), 1)
         hidden[2 * cache_here :, :] = jnp.where(token + chip * home_rows == column, 0.0, MASKED)
-        v_turned[HD:, :] = jnp.ones_like(v_turned[HD:, :])
-
-    v_turned[:HD, :cache_here] = value_own[...].T
-    v_turned[:HD, cache_here:] = value_other[...].T
+
     value_new = value_fresh[...].astype(F32).T.astype(BF16)
     for ring in range(rings):
         taken = slice(ring * home_rows, (ring + 1) * home_rows)
@@ -57,31 +54,31 @@
 
     heads = owners * heads_owner
     factor = LOG2E / math.sqrt(HD)
-    pieces = [(key_own, 0, i) for i in range(0, cache_here, step)]
-    pieces += [(key_other, cache_here, i) for i in range(0, cache_here, step)]
-    scaled = jnp.concatenate([q_rows[:, h * HD : (h + 1) * HD] for h in range(heads)], axis=0)
-    scaled = scaled.astype(F32) * factor
-    coarse = scaled.astype(BF16)
-    fine = (scaled - coarse.astype(F32)).astype(BF16)
-    queries = jnp.concatenate([coarse, fine], axis=1)
+    pieces = [(key_own, value_own, 0, i) for i in range(0, cache_here, step)]
+    pieces += [(key_other, value_other, cache_here, i) for i in range(0, cache_here, step)]
+    for h in range(heads):
+        scaled = q_rows[:, h * HD : (h + 1) * HD].T.astype(F32) * factor
+        coarse = scaled.astype(BF16)
+        q_turned[:HD, h * rows : (h + 1) * rows] = coarse
+        q_turned[HD:, h * rows : (h + 1) * rows] = (scaled - coarse.astype(F32)).astype(BF16)
 
     def score(keys, mask):
-        s = nt_dot(jnp.concatenate([keys, keys], axis=1), queries)
+        s = nn_dot(jnp.concatenate([keys, keys], axis=1), q_turned[...])
         return s + jnp.concatenate([mask] * heads, axis=1)
 
     s_new = score(key_fresh[...], hidden[2 * cache_here :, :])
     run = jnp.max(s_new.reshape(home_rows // 8, 8, heads * rows), axis=0)
-    for source, base, i in pieces:
+    for source, _, base, i in pieces:
         s = score(source[i : i + step, :], hidden[base + i : base + i + step, :])
         scores[base + i : base + i + step, :] = s
         run = jnp.maximum(run, jnp.max(s.reshape(step // 8, 8, heads * rows), axis=0))
     peak = jnp.maximum(jnp.max(run, axis=0, keepdims=True), FLOOR).astype(BF16).astype(F32)
     p_new = jnp.exp2((s_new - peak).astype(BF16))
     sums = None
-    for _, base, i in pieces:
-        at = slice(base + i, base + i + step)
-        p = jnp.exp2((scores[at, :] - peak).astype(BF16))
-        term = nn_dot(v_turned[:, at], p)
+    ones = jnp.ones((STATS, step), BF16)
+    for _, source, base, i in pieces:
+        p = jnp.exp2((scores[base + i : base + i + step, :] - peak).astype(BF16))
+        term = nn_dot(jnp.concatenate([source[:, i : i + step], ones], axis=0), p)
         sums = term if sums is None else sums + term
     numer = sums[:HD] + nn_dot(value_new, p_new)
     denom = sums[HD : HD + 1] + jnp.sum(p_new.astype(F32), axis=0, keepdims=True)
@@ -103,7 +100,7 @@
     heads_owner = own_q.shape[1] // HD // chips
     owners = chips // kv_heads
     height = heads_owner * HD + STATS
-    step = 256
+    step = 512
     kv = lambda g, place: (0, g)
     shape = (owners, heads_owner, home_rows, rows, cache_here, step)
     work = rows * heads_owner * chips * 2 * cache_here
@@ -113,24 +110,25 @@
             num_scalar_prefetch=1,
             grid=(kv_heads,),
             in_specs=[pl.BlockSpec((own_q.shape[0], owners * heads_owner * HD), kv)] * 2
-            + [pl.BlockSpec((cache_here, HD), kv)] * 4
+            + [pl.BlockSpec((cache_here, HD), kv)] * 2
+            + [pl.BlockSpec((HD, cache_here), lambda g, place: (g, 0))] * 2
             + [pl.BlockSpec((home_rows, HD), kv)] * 2
             + [pl.BlockSpec((1, rows), lambda g, place: (0, 0))],
             out_specs=pl.BlockSpec((owners, height, rows), lambda g, place: (g, 0, 0)),
             scratch_shapes=[
                 pltpu.VMEM((rows, owners * heads_owner * HD), BF16),
-                pltpu.VMEM((HD + STATS, 2 * cache_here), BF16),
+                pltpu.VMEM((2 * HD, owners * heads_owner * rows), BF16),
                 pltpu.VMEM((2 * cache_here + home_rows, rows), F32),
                 pltpu.VMEM((2 * cache_here, owners * heads_owner * rows), F32),
             ],
         ),
         out_shape=jax.ShapeDtypeStruct((chips, height, rows), BF16),
-        compiler_params=pltpu.CompilerParams(vmem_limit_bytes=56 * MIB),
+        compiler_params=pltpu.CompilerParams(vmem_limit_bytes=24 * MIB),
         cost_estimate=pl.CostEstimate(
             flops=6 * work * HD, bytes_accessed=8 * MIB, transcendentals=work
         ),
         name="attention",
-    )(place, own_q, other_q, *keys, *values, new_key, new_value, lens)
+    )(place, own_q, other_q, pltpu.with_memory_space_constraint(keys[0], pltpu.HBM), keys[1], *values, new_key, new_value, lens)
 
 
 def project_body(place, *refs):
@@ -173,7 +171,7 @@
     )(place, *chunks, weight_own, weight_other)
 
 
-def norm_body(parts, residual, gain, chooser, done, middle_out, sent):
+def norm_body(parts, residual, gain, chooser, middle_out, sent):
     total = parts[0].astype(F32)
     for s in range(1, parts.shape[0]):
         total = total + parts[s].astype(F32)
@@ -185,12 +183,12 @@
     sent[...] = nn_dot(chooser[...], normed).astype(BF16)
 
 
-def norm_and_dispatch(parts, residual, gain, chooser, done):
+def norm_and_dispatch(parts, residual, gain, chooser):
     vmem = pl.BlockSpec(memory_space=pltpu.VMEM)
     rows, width = residual.shape
     return pl.pallas_call(
         norm_body,
-        in_specs=[vmem] * 5,
+        in_specs=[vmem] * 4,
         out_specs=[vmem] * 2,
         out_shape=[
             jax.ShapeDtypeStruct((rows, width), BF16),
@@ -201,10 +199,10 @@
             flops=2 * chooser.shape[0] * rows * width, bytes_accessed=2 * MIB, transcendentals=0
         ),
         name="norm_and_dispatch",
-    )(parts, residual, gain, chooser, done)
-
-
-def fetch_body(after, gate, up, down, gate_out, up_out, down_out, done, sems):
+    )(parts, residual, gain, chooser)
+
+
+def fetch_body(after, gate, up, down, gate_out, up_out, down_out, sems):
     copies = [
         pltpu.make_async_copy(source, held, sems.at[k])
         for k, (source, held) in enumerate(((gate, gate_out), (up, up_out), (down, down_out)))
@@ -213,24 +211,22 @@
         copy.start()
     for copy in copies:
         copy.wait()
-    done[...] = jnp.zeros_like(done)
 
 
 def fetch(after, weights):
-    anywhere = pl.BlockSpec(memory_space=pl.ANY)
+    hbm = pl.BlockSpec(memory_space=pltpu.HBM)
     return pl.pallas_call(
         fetch_body,
-        in_specs=[anywhere] * (1 + len(weights)),
-        out_specs=[pl.BlockSpec(memory_space=pltpu.VMEM)] * (1 + len(weights)),
-        out_shape=[pltpu.VMEM(w.shape, w.dtype) for w in weights]
-        + [jax.ShapeDtypeStruct((8, HD), F32)],
+        in_specs=[pl.BlockSpec(memory_space=pl.ANY)] + [hbm] * len(weights),
+        out_specs=[pl.BlockSpec(memory_space=pltpu.VMEM)] * len(weights),
+        out_shape=[pltpu.VMEM(w.shape, w.dtype) for w in weights],
         scratch_shapes=[pltpu.SemaphoreType.DMA((len(weights),))],
-        compiler_params=pltpu.CompilerParams(vmem_limit_bytes=1 * MIB),
+        compiler_params=pltpu.CompilerParams(vmem_limit_bytes=2 * MIB),
         cost_estimate=pl.CostEstimate(
             flops=0, bytes_accessed=2 * sum(w.size * 2 for w in weights), transcendentals=0
         ),
         name="fetch",
-    )(after, *weights)
+    )(after, *[pltpu.with_memory_space_constraint(w, pltpu.HBM) for w in weights])
 
 
 def experts_body(arrived, w_gate, w_up, w_down, out):
@@ -266,7 +262,7 @@
         in_specs=[vmem] * 4,
         out_specs=vmem,
         out_shape=jax.ShapeDtypeStruct((rows, width), BF16),
-        compiler_params=pltpu.CompilerParams(vmem_limit_bytes=24 * MIB),
+        compiler_params=pltpu.CompilerParams(vmem_limit_bytes=16 * MIB),
         cost_estimate=pl.CostEstimate(
             flops=6 * rows * width * experts * hidden,
             bytes_accessed=2 * MIB,
@@ -324,17 +320,20 @@
     across = [(i, i ^ CORES) for i in range(devices)]
 
     by_owner = queries.reshape(home_rows, chips, CORES, heads_here * HD)
+    value_turned = value_cache.T
+    key_other = lax.ppermute(key_cache, "ctx", swap)
+    value_other = lax.ppermute(value_turned, "ctx", swap)
     query_chunks = []
     for chunk in range(CORES):
         mine = by_owner[:, :, chunk].reshape(home_rows, chips * heads_here * HD)
         stride = 2 * CORES
         while stride < devices:
+            if chunk and 2 * stride >= devices:
+                mine, _ = lax.optimization_barrier((mine, query_chunks[0][0]))
             step = [(i, i ^ stride) for i in range(devices)]
             mine = jnp.concatenate([mine, lax.ppermute(mine, "ctx", step)], axis=0)
             stride *= 2
         query_chunks.append((mine, lax.ppermute(mine, "ctx", across)))
-    key_other = lax.ppermute(key_cache, "ctx", swap)
-    value_other = lax.ppermute(value_cache, "ctx", swap)
     weight_other = lax.ppermute(out_weight, "ctx", swap)
 
     place = jnp.stack([chip, index * cache_here, (index ^ 1) * cache_here, core, chip % 2, chip // 2]).astype(jnp.int32)
@@ -361,7 +360,7 @@
             own_q,
             other_q,
             (key_cache, key_other),
-            (value_cache, value_other),
+            (value_turned, value_other),
             new_key,
             new_value,
             lens,
@@ -378,7 +377,6 @@
             )
         )
     share = project(place, gathered, out_weight, weight_other)
-    *held, done = fetch(share, (w_gate, w_up, w_down))
     shares = lax.all_to_all(
         share.reshape(chips, home_rows, width),
         "ctx",
@@ -387,7 +385,8 @@
         axis_index_groups=same_core,
         tiled=True,
     )
-    middle, outgoing = norm_and_dispatch(shares, residual, norm_gain.reshape(1, width), chooser, done)
+    middle, outgoing = norm_and_dispatch(shares, residual, norm_gain.reshape(1, width), chooser)
+    held = fetch(middle, (w_gate, w_up, w_down))
     arrived = lax.all_to_all(
         outgoing.reshape(devices, experts * MOST, width), "ctx", split_axis=0, concat_axis=0, tiled=True
     )

time: 155 us -> 150 us (0.968)
  blocking collectives: 20.4 us -> 0 us
  waiting for transfers between devices: 47 us -> 62.3 us
  local copies, waits for them, and re-layouts: 29.7 us -> 22.1 us
  Pallas kernels: 28.7 us -> 34.6 us
    all_to_all x1 -> x0, blocking collectives: 20.4 us -> none  [on_device(): lax.all_to_all(outgoing.reshape(devices, experts * MOST, width), 'ctx', s...]
    all_to_all x1, waiting for transfers between devices: 0.01 us -> 13.7 us  [on_device(): lax.all_to_all(share.reshape(chips, home_rows, width), 'ctx', split_axis=...]
    unnamed x48 -> x38, local copies, waits for them, and re-layouts: 25.8 us -> 19.4 us
    pallas_call x2, Pallas kernels: 1.73 us -> 7.66 us  [the longest x1 6.43 us: fetch(): pl.pallas_call(fetch_body, in_specs=[pl.BlockSpec(memory_space=pl.ANY)] +...]
    ppermute x4, waiting for transfers between devices: 8.99 us -> 14.8 us  [on_device(): mine = jnp.concatenate([mine, lax.ppermute(mine, 'ctx', step)], axis=0)]
    ppermute x2, waiting for transfers between devices: 5.48 us -> 0.01 us  [on_device(): query_chunks.append((mine, lax.ppermute(mine, 'ctx', across)))]
    all_to_all x0 -> x1, starting transfers between devices: none -> 3.74 us  [on_device(): lax.all_to_all(outgoing.reshape(devices, experts * MOST, width), 'ctx', s...]
    all_to_all x1, starting transfers between devices: 4.1 us -> 5.86 us  [on_device(): lax.all_to_all(produced.reshape(devices, experts * MOST, width), 'ctx', s...]
  transfers between devices with their start and end apart: 13 -> 14, of which waited for: 6 -> 7; matrix products, arithmetic and copies ran while one was open for 2% -> 2% of each run, Pallas kernels for 14% -> 18%
where the time goes in v5:
time: 150 us; the launch traced here: 149 us
  waiting for transfers between devices  62.3 us (42%)
  Pallas kernels  34.6 us (23%)
  starting transfers between devices  29.6 us (20%)
  local copies, waits for them, and re-layouts  22.1 us (15%)
    pallas_call x2, Pallas kernels, attention(): pl.pallas_call(functools.partial(attention_body, shape), grid_spec=pltpu....  19.8 us
    unnamed x38, local copies, waits for them, and re-layouts  19.4 us
    all_to_all x2, waiting for transfers between devices, on_device(): lax.all_to_all(sums, 'ctx', split_axis=0, concat_axis=0, axis_index_group...  19.3 us
    ppermute x4, waiting for transfers between devices, on_device(): mine = jnp.concatenate([mine, lax.ppermute(mine, 'ctx', step)], axis=0)  14.8 us
    all_to_all x1, waiting for transfers between devices, on_device(): lax.all_to_all(produced.reshape(devices, experts * MOST, width), 'ctx', s...  14.3 us
    all_to_all x1, waiting for transfers between devices, on_device(): lax.all_to_all(share.reshape(chips, home_rows, width), 'ctx', split_axis=...  13.7 us
    all_to_all x2, starting transfers between devices, on_device(): lax.all_to_all(sums, 'ctx', split_axis=0, concat_axis=0, axis_index_group...  7.21 us
    pallas_call x1, Pallas kernels, fetch(): pl.pallas_call(fetch_body, in_specs=[pl.BlockSpec(memory_space=pl.ANY)] +...  6.43 us
  transfers between devices with their start and end apart: 14, of which 7 were waited for; matrix products, arithmetic and copies ran while one was open for 2% of the time, Pallas kernels for 18%

profile of v5, /device:TPU:0, one launch (start us, length us, event | category | flops | bytes accessed | tf_op | source)
XLA Modules:
  0.0 149.3 jit_solution(3270054983597299889)
XLA Ops:
  0.0 1.0 reshape.38
  1.0 0.5 slice_reduce_fusion
  1.5 3.1 %collective-permute-start = (bf16[16,2048]{1,0:T(8,128)(2,1)S(1)}, bf16[16,2048]{1,0:T(8,128)(2,1)S(1)}, u32[]{:S(2)}, u32[]{:S(2)}) collective-permute-start(bf16[16,2048]{1,0:T(8,128)(2,1)S(1)} %bitcast.23), channel_id=1, source_target_pairs={{0,4},{1,5},{2,6},{3,7},{4,0},{5,1},{6,2},{7,3},{8,12},{9,13},{10,... | collective-permute-start | bytes 196616 | tf_op jit(solution)/shard_map/ppermute | solution.py:334
  4.7 0.1 collective-permute-start.5
  4.7 1.5 copy.28
  6.2 0.1 collective-permute-start.4
  6.3 0.5 collective-permute-start.3
  6.8 0.8 reshape.39
  7.6 0.1 reshape.40.lens
  7.7 0.1 stack.27.place
  7.8 3.1 %collective-permute-start.1 = (bf16[32,2048]{1,0:T(8,128)(2,1)S(1)}, bf16[32,2048]{1,0:T(8,128)(2,1)S(1)}, u32[]{:S(2)}, u32[]{:S(2)}) collective-permute-start(bf16[32,2048]{1,0:T(8,128)(2,1)S(1)} %pad_maximum_fusion), channel_id=1, source_target_pairs={{0,8},{1,9},{2,10},{3,11},{4,12},{5,13},{6,14},{7,15},{8,0},{9,1},... | collective-permute-start | bytes 393224 | tf_op jit(solution)/shard_map/ppermute | solution.py:334
  10.9 6.5 %collective-permute-done.1 = bf16[32,2048]{1,0:T(8,128)(2,1)S(1)} collective-permute-done((bf16[32,2048]{1,0:T(8,128)(2,1)S(1)}, bf16[32,2048]{1,0:T(8,128)(2,1)S(1)}, u32[]{:S(2)}, u32[]{:S(2)}) %collective-permute-start.1) | collective-permute-done | bytes 131104 | tf_op jit(solution)/shard_map/ppermute | solution.py:334
  17.4 1.6 %collective-permute-start.2 = (bf16[64,2048]{1,0:T(8,128)(2,1)S(1)}, bf16[64,2048]{1,0:T(8,128)(2,1)S(1)}, u32[]{:S(2)}, u32[]{:S(2)}) collective-permute-start(bf16[64,2048]{1,0:T(8,128)(2,1)S(1)} %constant_dynamic-update-slice_fusion.own_q), channel_id=1, source_target_pairs={{0,2},{1,3},{2,0},{3,1},{4,6},{5,7},{6,4},{7,5},{8,10},{9,11},{10,... | collective-permute-start | bytes 786440 | tf_op jit(solution)/shard_map/ppermute | solution.py:336
  19.1 8.3 %collective-permute-done.6 = bf16[32,2048]{1,0:T(8,128)(2,1)S(1)} collective-permute-done((bf16[32,2048]{1,0:T(8,128)(2,1)S(1)}, bf16[32,2048]{1,0:T(8,128)(2,1)S(1)}, u32[]{:S(2)}, u32[]{:S(2)}) %collective-permute-start.6) | collective-permute-done | bytes 131104 | tf_op jit(solution)/shard_map/ppermute | solution.py:334
  27.4 0.6 collective-permute-start.7
  28.0 0.7 copy-done.8
  28.8 0.7 copy-done.10
  29.5 9.9 %attention.2 = bf16[8,272,128]{2,1,0:T(8,128)(2,1)} custom-call(s32[6]{0:T(128)S(1)} %stack.27.place, bf16[64,2048]{1,0:T(8,128)(2,1)S(1)} %constant_dynamic-update-slice_fusion.own_q, bf16[64,2048]{1,0:T(8,128)(2,1)S(1)} %collective-permute-done.2.other_q, bf16[1024,512]{1,0:T(8,128)(2,1)} %key_own.3, bf16[1024,512]{1,0:T(8,128)(2,1)} %collective-permute-done.3.key_other, ...), custom_call_target="tpu_custom_call" | custom-call | flops 3221225472 | bytes 8388608 | tf_op jit(solution)/shard_map/attention/pallas_call | solution.py:107
  39.4 3.6 %all-to-all-start = ((bf16[8,272,128]{2,1,0:T(8,128)(2,1)}), bf16[8,272,128]{2,1,0:T(8,128)(2,1)S(1)}, u32[]{:S(2)}, u32[]{:S(2)}) async-start(bf16[8,272,128]{2,1,0:T(8,128)(2,1)} %attention.2), calls=%async_computation | async-start | bytes 1114112 | tf_op jit(solution)/shard_map/all_to_all | solution.py:375
  43.0 0.1 collective-permute-start.8
  43.1 9.9 %attention.3 = bf16[8,272,128]{2,1,0:T(8,128)(2,1)} custom-call(s32[6]{0:T(128)S(1)} %stack.27.place, bf16[64,2048]{1,0:T(8,128)(2,1)S(1)} %constant_dynamic-update-slice_fusion.3.own_q, bf16[64,2048]{1,0:T(8,128)(2,1)S(1)} %collective-permute-done.7.other_q, bf16[1024,512]{1,0:T(8,128)(2,1)} %key_own.3, bf16[1024,512]{1,0:T(8,128)(2,1)} %collective-permute-done.3.key_other, ...), custom_call_target="tpu_custom_call" | custom-call | flops 3221225472 | bytes 8388608 | tf_op jit(solution)/shard_map/attention/pallas_call | solution.py:107
  53.0 4.5 %all-to-all-done.refs_0_ = bf16[8,272,128]{2,1,0:T(8,128)(2,1)S(1)} async-done(((bf16[8,272,128]{2,1,0:T(8,128)(2,1)}), bf16[8,272,128]{2,1,0:T(8,128)(2,1)S(1)}, u32[]{:S(2)}, u32[]{:S(2)}) %all-to-all-start) | async-done | bytes 557088 | tf_op jit(solution)/shard_map/all_to_all | solution.py:375
  57.4 3.6 %all-to-all-start.1 = ((bf16[8,272,128]{2,1,0:T(8,128)(2,1)}), bf16[8,272,128]{2,1,0:T(8,128)(2,1)S(1)}, u32[]{:S(2)}, u32[]{:S(2)}) async-start(bf16[8,272,128]{2,1,0:T(8,128)(2,1)} %attention.3), calls=%async_computation.1 | async-start | bytes 1114112 | tf_op jit(solution)/shard_map/all_to_all | solution.py:375
  61.1 14.9 %all-to-all-done.1.refs_1_ = bf16[8,272,128]{2,1,0:T(8,128)(2,1)S(1)} async-done(((bf16[8,272,128]{2,1,0:T(8,128)(2,1)}), bf16[8,272,128]{2,1,0:T(8,128)(2,1)S(1)}, u32[]{:S(2)}, u32[]{:S(2)}) %all-to-all-start.1) | async-done | bytes 557088 | tf_op jit(solution)/shard_map/all_to_all | solution.py:375
  75.9 2.8 %project.1 = bf16[128,2048]{1,0:T(8,128)(2,1)} custom-call(s32[6]{0:T(128)S(1)} %stack.27.place, bf16[8,272,128]{2,1,0:T(8,128)(2,1)S(1)} %all-to-all-done.refs_0_, bf16[8,272,128]{2,1,0:T(8,128)(2,1)S(1)} %all-to-all-done.1.refs_1_, bf16[256,2048]{1,0:T(8,128)(2,1)S(1)} %copy-done.6, bf16[256,2048]{1,0:T(8,128)(2,1)} %collective-permute-done.8.refs_3_), custom_call_target="tpu_custom_call" | custom-call | flops 268435456 | bytes 4194304 | tf_op jit(solution)/shard_map/project/pallas_call | solution.py:160
  78.7 3.6 %all-to-all-start.2 = ((bf16[8,16,2048]{2,1,0:T(8,128)(2,1)}), bf16[8,16,2048]{2,1,0:T(8,128)(2,1)S(1)}, u32[]{:S(2)}, u32[]{:S(2)}) async-start(bf16[8,16,2048]{2,1,0:T(8,128)(2,1)} %bitcast.7), calls=%async_computation.2 | async-start | bytes 1048576 | tf_op jit(solution)/shard_map/all_to_all | solution.py:380
  82.4 0.1 copy.30
  82.4 0.1 eq.31
  82.5 0.2 convert_reduce_fusion
  82.7 0.1 reduce_sum.21
  82.8 0.1 fusion
  83.0 0.1 copy.32
  83.1 13.7 %all-to-all-done.2.parts = bf16[8,16,2048]{2,1,0:T(8,128)(2,1)S(1)} async-done(((bf16[8,16,2048]{2,1,0:T(8,128)(2,1)}), bf16[8,16,2048]{2,1,0:T(8,128)(2,1)S(1)}, u32[]{:S(2)}, u32[]{:S(2)}) %all-to-all-start.2) | async-done | bytes 524320 | tf_op jit(solution)/shard_map/all_to_all | solution.py:380
  96.8 1.2 norm_and_dispatch.1
  98.1 3.7 %all-to-all-start.3 = ((bf16[16,8,2048]{2,1,0:T(8,128)(2,1)}), bf16[16,8,2048]{2,1,0:T(8,128)(2,1)S(1)}, u32[]{:S(2)}, u32[]{:S(2)}) async-start(bf16[16,8,2048]{2,1,0:T(8,128)(2,1)} %bitcast.9), calls=%async_computation.3 | async-start | bytes 1048576 | tf_op jit(solution)/shard_map/all_to_all | solution.py:390
  101.8 6.4 %fetch.1 = (bf16[2,2048,768]{2,1,0:T(8,128)(2,1)S(1)}, bf16[2,2048,768]{2,1,0:T(8,128)(2,1)S(1)}, bf16[2,768,2048]{2,1,0:T(8,128)(2,1)S(1)}) custom-call(bf16[16,2048]{1,0:T(8,128)(2,1)S(1)} %get-tuple-element.17.after.middle, bf16[2,2048,768]{2,1,0:T(8,128)(2,1)} %gate.1, bf16[2,2048,768]{2,1,0:T(8,128)(2,1)} %up.1, bf16[2,768,2048]{2,1,0:T(8,128)(2,1)} %down.1), custom_call_target="tpu_custom_call" | custom-call | bytes 37748736 | tf_op jit(solution)/shard_map/fetch/pallas_call | solution.py:218
  108.3 2.7 %copy-done = bf16[2,2048,768]{2,1,0:T(8,128)(2,1)} copy-done((bf16[2,2048,768]{2,1,0:T(8,128)(2,1)}, bf16[2,2048,768]{2,1,0:T(8,128)(2,1)S(1)}, u32[]{:S(2)}) %copy-start) | copy-done | bytes 6291480
  110.9 2.6 %copy-done.2 = bf16[2,2048,768]{2,1,0:T(8,128)(2,1)} copy-done((bf16[2,2048,768]{2,1,0:T(8,128)(2,1)}, bf16[2,2048,768]{2,1,0:T(8,128)(2,1)S(1)}, u32[]{:S(2)}) %copy-start.2) | copy-done | bytes 6291480
  113.5 2.6 %copy-done.4 = bf16[2,768,2048]{2,1,0:T(8,128)(2,1)} copy-done((bf16[2,768,2048]{2,1,0:T(8,128)(2,1)}, bf16[2,768,2048]{2,1,0:T(8,128)(2,1)S(1)}, u32[]{:S(2)}) %copy-start.4) | copy-done | bytes 6291480
  116.1 0.2 all-to-all-done.3
  116.3 2.8 %copy-done.1 = bf16[2,2048,768]{2,1,0:T(8,128)(2,1)S(1)} copy-done((bf16[2,2048,768]{2,1,0:T(8,128)(2,1)S(1)}, bf16[2,2048,768]{2,1,0:T(8,128)(2,1)}, u32[]{:S(2)}) %copy-start.1) | copy-done | bytes 6291480
  119.1 2.8 %copy-done.3 = bf16[2,2048,768]{2,1,0:T(8,128)(2,1)S(1)} copy-done((bf16[2,2048,768]{2,1,0:T(8,128)(2,1)S(1)}, bf16[2,2048,768]{2,1,0:T(8,128)(2,1)}, u32[]{:S(2)}) %copy-start.3) | copy-done | bytes 6291480
  121.9 2.8 %copy-done.5 = bf16[2,768,2048]{2,1,0:T(8,128)(2,1)S(1)} copy-done((bf16[2,768,2048]{2,1,0:T(8,128)(2,1)S(1)}, bf16[2,768,2048]{2,1,0:T(8,128)(2,1)}, u32[]{:S(2)}) %copy-start.5) | copy-done | bytes 6291480
  124.6 3.5 %experts.1 = bf16[128,2048]{1,0:T(8,128)(2,1)} custom-call(bf16[128,2048]{1,0:T(8,128)(2,1)S(1)} %bitcast.17, bf16[2,2048,768]{2,1,0:T(8,128)(2,1)S(1)} %copy-done.1, bf16[2,2048,768]{2,1,0:T(8,128)(2,1)S(1)} %copy-done.3, bf16[2,768,2048]{2,1,0:T(8,128)(2,1)S(1)} %copy-done.5), custom_call_target="tpu_custom_call" | custom-call | flops 2415919104 | bytes 2097152 | tf_op jit(solution)/shard_map/experts/pallas_call | solution.py:260
  128.1 5.9 %all-to-all-start.4 = ((bf16[16,8,2048]{2,1,0:T(8,128)(2,1)}), bf16[16,8,2048]{2,1,0:T(8,128)(2,1)S(1)}, u32[]{:S(2)}, u32[]{:S(2)}) async-start(bf16[16,8,2048]{2,1,0:T(8,128)(2,1)} %bitcast.11), calls=%async_computation.4 | async-start | bytes 1048576 | tf_op jit(solution)/shard_map/all_to_all | solution.py:394
  134.1 0.1 select_reduce_fusion
  134.2 14.3 %all-to-all-done.4 = bf16[16,8,2048]{2,1,0:T(8,128)(2,1)S(1)} async-done(((bf16[16,8,2048]{2,1,0:T(8,128)(2,1)}), bf16[16,8,2048]{2,1,0:T(8,128)(2,1)S(1)}, u32[]{:S(2)}, u32[]{:S(2)}) %all-to-all-start.4) | async-done | bytes 524320 | tf_op jit(solution)/shard_map/all_to_all | solution.py:394
  148.5 0.9 mix.1
  (45 shorter events, 0.3 us)
Async XLA Ops:
  1.5 6.2 %collective-permute-start = (bf16[16,2048]{1,0:T(8,128)(2,1)S(1)}, bf16[16,2048]{1,0:T(8,128)(2,1)S(1)}, u32[]{:S(2)}, u32[]{:S(2)}) collective-permute-start(bf16[16,2048]{1,0:T(8,128)(2,1)S(1)} %bitcast.23), channel_id=1, source_target_pairs={{0,4},{1,5},{2,6},{3,7},{4,0},{5,1},{6,2},{7,3},{8,12},{9,13},{10,... | collective-permute-start | bytes 196616 | tf_op jit(solution)/shard_map/ppermute | solution.py:334
  4.7 6.2 %collective-permute-start.5 = (bf16[16,2048]{1,0:T(8,128)(2,1)S(1)}, bf16[16,2048]{1,0:T(8,128)(2,1)S(1)}, u32[]{:S(2)}, u32[]{:S(2)}) collective-permute-start(bf16[16,2048]{1,0:T(8,128)(2,1)S(1)} %bitcast.26), channel_id=1, source_target_pairs={{0,4},{1,5},{2,6},{3,7},{4,0},{5,1},{6,2},{7,3},{8,12},{9,13},{10,... | collective-permute-start | bytes 196616 | tf_op jit(solution)/shard_map/ppermute | solution.py:334
  6.2 21.8 %collective-permute-start.4 = (bf16[512,1024]{1,0:T(8,128)(2,1)S(1)}, bf16[512,1024]{1,0:T(8,128)(2,1)}, u32[]{:S(2)}, u32[]{:S(2)}) collective-permute-start(bf16[512,1024]{1,0:T(8,128)(2,1)S(1)} %bitcast.19), channel_id=1, source_target_pairs={{0,1},{1,0},{2,3},{3,2},{4,5},{5,4},{6,7},{7,6},{8,9},{9,8},{10,11... | collective-permute-start | bytes 3145736 | tf_op jit(solution)/shard_map/ppermute | solution.py:325
  6.3 21.7 %collective-permute-start.3 = (bf16[1024,512]{1,0:T(8,128)(2,1)}, bf16[1024,512]{1,0:T(8,128)(2,1)}, u32[]{:S(2)}, u32[]{:S(2)}) collective-permute-start(bf16[1024,512]{1,0:T(8,128)(2,1)} %key_own.3), channel_id=1, source_target_pairs={{0,1},{1,0},{2,3},{3,2},{4,5},{5,4},{6,7},{7,6},{8,9},{9,8},{10,11... | collective-permute-start | bytes 3145736 | tf_op jit(solution)/shard_map/ppermute | solution.py:324
  7.8 9.6 %collective-permute-start.1 = (bf16[32,2048]{1,0:T(8,128)(2,1)S(1)}, bf16[32,2048]{1,0:T(8,128)(2,1)S(1)}, u32[]{:S(2)}, u32[]{:S(2)}) collective-permute-start(bf16[32,2048]{1,0:T(8,128)(2,1)S(1)} %pad_maximum_fusion), channel_id=1, source_target_pairs={{0,8},{1,9},{2,10},{3,11},{4,12},{5,13},{6,14},{7,15},{8,0},{9,1},... | collective-permute-start | bytes 393224 | tf_op jit(solution)/shard_map/ppermute | solution.py:334
  17.4 10.6 %collective-permute-start.2 = (bf16[64,2048]{1,0:T(8,128)(2,1)S(1)}, bf16[64,2048]{1,0:T(8,128)(2,1)S(1)}, u32[]{:S(2)}, u32[]{:S(2)}) collective-permute-start(bf16[64,2048]{1,0:T(8,128)(2,1)S(1)} %constant_dynamic-update-slice_fusion.own_q), channel_id=1, source_target_pairs={{0,2},{1,3},{2,0},{3,1},{4,6},{5,7},{6,4},{7,5},{8,10},{9,11},{10,... | collective-permute-start | bytes 786440 | tf_op jit(solution)/shard_map/ppermute | solution.py:336
  19.1 8.3 %collective-permute-start.6 = (bf16[32,2048]{1,0:T(8,128)(2,1)S(1)}, bf16[32,2048]{1,0:T(8,128)(2,1)S(1)}, u32[]{:S(2)}, u32[]{:S(2)}) collective-permute-start(bf16[32,2048]{1,0:T(8,128)(2,1)S(1)} %pad_maximum_fusion.1), channel_id=1, source_target_pairs={{0,8},{1,9},{2,10},{3,11},{4,12},{5,13},{6,14},{7,15},{8,0},{9,1},... | collective-permute-start | bytes 393224 | tf_op jit(solution)/shard_map/ppermute | solution.py:334
  27.4 15.7 %copy-start.9 = (bf16[16,512]{1,0:T(8,128)(2,1)S(1)}, bf16[16,512]{1,0:T(8,128)(2,1)}, u32[]{:S(2)}) copy-start(bf16[16,512]{1,0:T(8,128)(2,1)} %key_fresh.3) | copy-start | bytes 49156
  27.4 15.7 %copy-start.11 = (bf16[16,512]{1,0:T(8,128)(2,1)S(1)}, bf16[16,512]{1,0:T(8,128)(2,1)}, u32[]{:S(2)}) copy-start(bf16[16,512]{1,0:T(8,128)(2,1)} %value_fresh.3) | copy-start | bytes 49156
  27.4 15.5 %copy-start.6 = (bf16[256,2048]{1,0:T(8,128)(2,1)S(1)}, bf16[256,2048]{1,0:T(8,128)(2,1)}, u32[]{:S(2)}) copy-start(bf16[256,2048]{1,0:T(8,128)(2,1)} %refs_2_.1) | copy-start | bytes 3145732
  27.4 12.0 %collective-permute-start.7 = (bf16[64,2048]{1,0:T(8,128)(2,1)S(1)}, bf16[64,2048]{1,0:T(8,128)(2,1)S(1)}, u32[]{:S(2)}, u32[]{:S(2)}) collective-permute-start(bf16[64,2048]{1,0:T(8,128)(2,1)S(1)} %constant_dynamic-update-slice_fusion.3.own_q), channel_id=1, source_target_pairs={{0,2},{1,3},{2,0},{3,1},{4,6},{5,7},{6,4},{7,5},{8,10},{9,11},{10,... | collective-permute-start | bytes 786440 | tf_op jit(solution)/shard_map/ppermute | solution.py:336
  28.0 0.7 copy-start.8
  28.7 0.7 copy-start.10
  39.4 18.1 %all-to-all-start = ((bf16[8,272,128]{2,1,0:T(8,128)(2,1)}), bf16[8,272,128]{2,1,0:T(8,128)(2,1)S(1)}, u32[]{:S(2)}, u32[]{:S(2)}) async-start(bf16[8,272,128]{2,1,0:T(8,128)(2,1)} %attention.2), calls=%async_computation | async-start | bytes 1114112 | tf_op jit(solution)/shard_map/all_to_all | solution.py:375
  42.9 39.4 %copy-start.12 = (s32[16,8]{0,1:T(8,128)S(1)}, s32[16,8]{0,1:T(8,128)}, u32[]{:S(2)}) copy-start(s32[16,8]{0,1:T(8,128)} %param.23) | copy-start | bytes 1540
  42.9 40.0 %copy-start.13 = (bf16[2048]{0:T(1024)(128)(2,1)S(1)}, bf16[2048]{0:T(1024)(128)(2,1)}, u32[]{:S(2)}) copy-start(bf16[2048]{0:T(1024)(128)(2,1)} %param.22) | copy-start | bytes 12292
  43.0 53.9 %copy-start.7 = (bf16[16,2048]{1,0:T(8,128)(2,1)S(1)}, bf16[16,2048]{1,0:T(8,128)(2,1)}, u32[]{:S(2)}) copy-start(bf16[16,2048]{1,0:T(8,128)(2,1)} %residual.1) | copy-start | bytes 196612
  43.0 18.1 %collective-permute-start.8 = (bf16[256,2048]{1,0:T(8,128)(2,1)S(1)}, bf16[256,2048]{1,0:T(8,128)(2,1)}, u32[]{:S(2)}, u32[]{:S(2)}) collective-permute-start(bf16[256,2048]{1,0:T(8,128)(2,1)S(1)} %copy-done.6), channel_id=1, source_target_pairs={{0,1},{1,0},{2,3},{3,2},{4,5},{5,4},{6,7},{7,6},{8,9},{9,8},{10,11... | collective-permute-start | bytes 3145736 | tf_op jit(solution)/shard_map/ppermute | solution.py:337
  57.4 18.5 %all-to-all-start.1 = ((bf16[8,272,128]{2,1,0:T(8,128)(2,1)}), bf16[8,272,128]{2,1,0:T(8,128)(2,1)S(1)}, u32[]{:S(2)}, u32[]{:S(2)}) async-start(bf16[8,272,128]{2,1,0:T(8,128)(2,1)} %attention.3), calls=%async_computation.1 | async-start | bytes 1114112 | tf_op jit(solution)/shard_map/all_to_all | solution.py:375
  78.7 18.1 %all-to-all-start.2 = ((bf16[8,16,2048]{2,1,0:T(8,128)(2,1)}), bf16[8,16,2048]{2,1,0:T(8,128)(2,1)S(1)}, u32[]{:S(2)}, u32[]{:S(2)}) async-start(bf16[8,16,2048]{2,1,0:T(8,128)(2,1)} %bitcast.7), calls=%async_computation.2 | async-start | bytes 1048576 | tf_op jit(solution)/shard_map/all_to_all | solution.py:380
  98.1 18.2 %all-to-all-start.3 = ((bf16[16,8,2048]{2,1,0:T(8,128)(2,1)}), bf16[16,8,2048]{2,1,0:T(8,128)(2,1)S(1)}, u32[]{:S(2)}, u32[]{:S(2)}) async-start(bf16[16,8,2048]{2,1,0:T(8,128)(2,1)} %bitcast.9), calls=%async_computation.3 | async-start | bytes 1048576 | tf_op jit(solution)/shard_map/all_to_all | solution.py:390
  108.2 2.7 %copy-start = (bf16[2,2048,768]{2,1,0:T(8,128)(2,1)}, bf16[2,2048,768]{2,1,0:T(8,128)(2,1)S(1)}, u32[]{:S(2)}) copy-start(bf16[2,2048,768]{2,1,0:T(8,128)(2,1)S(1)} %get-tuple-element.18.w_gate) | copy-start | bytes 18874372
  110.9 2.6 %copy-start.2 = (bf16[2,2048,768]{2,1,0:T(8,128)(2,1)}, bf16[2,2048,768]{2,1,0:T(8,128)(2,1)S(1)}, u32[]{:S(2)}) copy-start(bf16[2,2048,768]{2,1,0:T(8,128)(2,1)S(1)} %get-tuple-element.19.w_up) | copy-start | bytes 18874372
  113.5 2.6 %copy-start.4 = (bf16[2,768,2048]{2,1,0:T(8,128)(2,1)}, bf16[2,768,2048]{2,1,0:T(8,128)(2,1)S(1)}, u32[]{:S(2)}) copy-start(bf16[2,768,2048]{2,1,0:T(8,128)(2,1)S(1)} %get-tuple-element.20.w_down) | copy-start | bytes 18874372
  116.3 2.8 %copy-start.1 = (bf16[2,2048,768]{2,1,0:T(8,128)(2,1)S(1)}, bf16[2,2048,768]{2,1,0:T(8,128)(2,1)}, u32[]{:S(2)}) copy-start(bf16[2,2048,768]{2,1,0:T(8,128)(2,1)} %copy-done) | copy-start | bytes 18874372
  119.1 2.8 %copy-start.3 = (bf16[2,2048,768]{2,1,0:T(8,128)(2,1)S(1)}, bf16[2,2048,768]{2,1,0:T(8,128)(2,1)}, u32[]{:S(2)}) copy-start(bf16[2,2048,768]{2,1,0:T(8,128)(2,1)} %copy-done.2) | copy-start | bytes 18874372
  121.8 2.8 %copy-start.5 = (bf16[2,768,2048]{2,1,0:T(8,128)(2,1)S(1)}, bf16[2,768,2048]{2,1,0:T(8,128)(2,1)}, u32[]{:S(2)}) copy-start(bf16[2,768,2048]{2,1,0:T(8,128)(2,1)} %copy-done.4) | copy-start | bytes 18874372
  124.6 9.4 %copy-start.14 = (f32[16,8]{0,1:T(8,128)S(1)}, f32[16,8]{0,1:T(8,128)}, u32[]{:S(2)}) copy-start(f32[16,8]{0,1:T(8,128)} %param.24) | copy-start | bytes 1540
  128.1 20.3 %all-to-all-start.4 = ((bf16[16,8,2048]{2,1,0:T(8,128)(2,1)}), bf16[16,8,2048]{2,1,0:T(8,128)(2,1)S(1)}, u32[]{:S(2)}, u32[]{:S(2)}) async-start(bf16[16,8,2048]{2,1,0:T(8,128)(2,1)} %bitcast.11), calls=%async_computation.4 | async-start | bytes 1048576 | tf_op jit(solution)/shard_map/all_to_all | solution.py:394

commit v6 on v5

--- a/solution.py
+++ b/solution.py
@@ -30,9 +30,13 @@
 
 def attention_body(shape, place, own_q, other_q, key_own, key_other, value_own, value_other, key_fresh, value_fresh, lens, out, *scratch):
     owners, heads_owner, home_rows, rows, cache_here, step = shape
-    q_rows, q_turned, hidden, scores = scratch
+    q_rows, q_turned, hidden, scores, peaks = scratch
     chip, start_own, start_other, pair_place, ring_place = place[0], place[1], place[2], place[4], place[5]
     rings = rows // home_rows // 2
+    heads = owners * heads_owner
+    wide = heads * rows
+    now = lax.rem(pl.program_id(0), 2)
+    before = 1 - now
 
     @pl.when(pl.program_id(0) == 0)
     def _():
@@ -44,51 +48,60 @@
         token = lax.broadcasted_iota(jnp.int32, (home_rows, rows), 0)
         column = lax.broadcasted_iota(jnp.int32, (home_rows, rows), 1)
         hidden[2 * cache_here :, :] = jnp.where(token + chip * home_rows == column, 0.0, MASKED)
-
-    value_new = value_fresh[...].astype(F32).T.astype(BF16)
+        scores[1] = jnp.zeros_like(scores[1])
+        peaks[1] = jnp.zeros_like(peaks[1])
+
     for ring in range(rings):
         taken = slice(ring * home_rows, (ring + 1) * home_rows)
         for piece, side in ((own_q, pair_place), (other_q, 1 - pair_place)):
             spot = pl.multiple_of((2 * (ring ^ ring_place) + side) * home_rows, home_rows)
             q_rows[pl.ds(spot, home_rows), :] = piece[taken, :]
 
-    heads = owners * heads_owner
     factor = LOG2E / math.sqrt(HD)
-    pieces = [(key_own, value_own, 0, i) for i in range(0, cache_here, step)]
-    pieces += [(key_other, value_other, cache_here, i) for i in range(0, cache_here, step)]
     for h in range(heads):
         scaled = q_rows[:, h * HD : (h + 1) * HD].T.astype(F32) * factor
         coarse = scaled.astype(BF16)
         q_turned[:HD, h * rows : (h + 1) * rows] = coarse
         q_turned[HD:, h * rows : (h + 1) * rows] = (scaled - coarse.astype(F32)).astype(BF16)
 
-    def score(keys, mask):
+    run = [None]
+    sums = [None]
+    old_peak = peaks[before, :1, :]
+
+    def score(keys, at):
         s = nn_dot(jnp.concatenate([keys, keys], axis=1), q_turned[...])
-        return s + jnp.concatenate([mask] * heads, axis=1)
-
-    s_new = score(key_fresh[...], hidden[2 * cache_here :, :])
-    run = jnp.max(s_new.reshape(home_rows // 8, 8, heads * rows), axis=0)
-    for source, _, base, i in pieces:
-        s = score(source[i : i + step, :], hidden[base + i : base + i + step, :])
-        scores[base + i : base + i + step, :] = s
-        run = jnp.maximum(run, jnp.max(s.reshape(step // 8, 8, heads * rows), axis=0))
-    peak = jnp.maximum(jnp.max(run, axis=0, keepdims=True), FLOOR).astype(BF16).astype(F32)
-    p_new = jnp.exp2((s_new - peak).astype(BF16))
-    sums = None
-    ones = jnp.ones((STATS, step), BF16)
-    for _, source, base, i in pieces:
-        p = jnp.exp2((scores[base + i : base + i + step, :] - peak).astype(BF16))
-        term = nn_dot(jnp.concatenate([source[:, i : i + step], ones], axis=0), p)
-        sums = term if sums is None else sums + term
-    numer = sums[:HD] + nn_dot(value_new, p_new)
-    denom = sums[HD : HD + 1] + jnp.sum(p_new.astype(F32), axis=0, keepdims=True)
+        s = s + jnp.concatenate([hidden[at, :]] * heads, axis=1)
+        scores[now, at, :] = s
+        most = jnp.max(s.reshape(s.shape[0] // 8, 8, wide), axis=0)
+        run[0] = most if run[0] is None else jnp.maximum(run[0], most)
+
+    def weigh(values, at):
+        p = jnp.exp2((scores[before, at, :] - old_peak).astype(BF16))
+        ones = jnp.ones((STATS, values.shape[1]), BF16)
+        term = nn_dot(jnp.concatenate([values, ones], axis=0), p)
+        sums[0] = term if sums[0] is None else sums[0] + term
+
+    fresh_at = slice(2 * cache_here, 2 * cache_here + home_rows)
+    weigh(value_fresh[...].astype(F32).T.astype(BF16), fresh_at)
+    score(key_fresh[...], fresh_at)
+    for base, keys, values in ((0, key_own, value_own), (cache_here, key_other, value_other)):
+        for i in range(0, cache_here, step):
+            at = slice(base + i, base + i + step)
+            weigh(values[:, i : i + step], at)
+            score(keys[i : i + step, :], at)
+    peak = jnp.maximum(jnp.max(run[0], axis=0, keepdims=True), FLOOR).astype(BF16).astype(F32)
+    peaks[now] = jnp.broadcast_to(peak, peaks.shape[1:])
+
+    numer = sums[0][:HD]
+    denom = sums[0][HD : HD + 1]
     high = denom.astype(BF16).astype(F32)
     low = denom - high
     for owner in range(owners):
-        across = [slice((owner * heads_owner + h) * rows, (owner * heads_owner + h + 1) * rows) for h in range(heads_owner)]
+        first = owner * heads_owner
+        across = [slice((first + h) * rows, (first + h + 1) * rows) for h in range(heads_owner)]
         for h, cols in enumerate(across):
             out[owner, h * HD : (h + 1) * HD, :] = numer[:, cols].astype(BF16)
-        filled = [kind[:, cols] for kind in (peak, high, low) for cols in across]
+        filled = [kind[:, cols] for kind in (old_peak, high, low) for cols in across]
         filled += [jnp.zeros_like(filled[0])] * (STATS - len(filled))
         out[owner, heads_owner * HD :, :] = jnp.concatenate(filled, axis=0).astype(BF16)
 
@@ -99,31 +112,37 @@
     cache_here = keys[0].shape[0]
     heads_owner = own_q.shape[1] // HD // chips
     owners = chips // kv_heads
+    wide = owners * heads_owner * rows
     height = heads_owner * HD + STATS
-    step = 512
-    kv = lambda g, place: (0, g)
+    step = 256
+    positions = 2 * cache_here + home_rows
+    this = lambda g, place: (0, jnp.minimum(g, kv_heads - 1))
+    last = lambda g, place: (0, jnp.maximum(g - 1, 0))
     shape = (owners, heads_owner, home_rows, rows, cache_here, step)
     work = rows * heads_owner * chips * 2 * cache_here
     return pl.pallas_call(
         functools.partial(attention_body, shape),
         grid_spec=pltpu.PrefetchScalarGridSpec(
             num_scalar_prefetch=1,
-            grid=(kv_heads,),
-            in_specs=[pl.BlockSpec((own_q.shape[0], owners * heads_owner * HD), kv)] * 2
-            + [pl.BlockSpec((cache_here, HD), kv)] * 2
-            + [pl.BlockSpec((HD, cache_here), lambda g, place: (g, 0))] * 2
-            + [pl.BlockSpec((home_rows, HD), kv)] * 2
+            grid=(kv_heads + 1,),
+            in_specs=[pl.BlockSpec((own_q.shape[0], owners * heads_owner * HD), this)] * 2
+            + [pl.BlockSpec((cache_here, HD), this)] * 2
+            + [pl.BlockSpec((HD, cache_here), lambda g, place: (jnp.maximum(g - 1, 0), 0))] * 2
+            + [pl.BlockSpec((home_rows, HD), this), pl.BlockSpec((home_rows, HD), last)]
             + [pl.BlockSpec((1, rows), lambda g, place: (0, 0))],
-            out_specs=pl.BlockSpec((owners, height, rows), lambda g, place: (g, 0, 0)),
+            out_specs=pl.BlockSpec(
+                (owners, height, rows), lambda g, place: (jnp.maximum(g - 1, 0), 0, 0)
+            ),
             scratch_shapes=[
                 pltpu.VMEM((rows, owners * heads_owner * HD), BF16),
-                pltpu.VMEM((2 * HD, owners * heads_owner * rows), BF16),
-                pltpu.VMEM((2 * cache_here + home_rows, rows), F32),
-                pltpu.VMEM((2 * cache_here, owners * heads_owner * rows), F32),
+                pltpu.VMEM((2 * HD, wide), BF16),
+                pltpu.VMEM((positions, rows), F32),
+                pltpu.VMEM((2, positions, wide), F32),
+                pltpu.VMEM((2, 8, wide), F32),
             ],
         ),
         out_shape=jax.ShapeDtypeStruct((chips, height, rows), BF16),
-        compiler_params=pltpu.CompilerParams(vmem_limit_bytes=24 * MIB),
+        compiler_params=pltpu.CompilerParams(vmem_limit_bytes=32 * MIB),
         cost_estimate=pl.CostEstimate(
             flops=6 * work * HD, bytes_accessed=8 * MIB, transcendentals=work
         ),
@@ -202,74 +221,71 @@
     )(parts, residual, gain, chooser)
 
 
-def fetch_body(after, gate, up, down, gate_out, up_out, down_out, sems):
-    copies = [
-        pltpu.make_async_copy(source, held, sems.at[k])
-        for k, (source, held) in enumerate(((gate, gate_out), (up, up_out), (down, down_out)))
-    ]
-    for copy in copies:
-        copy.start()
-    for copy in copies:
-        copy.wait()
-
-
-def fetch(after, weights):
-    hbm = pl.BlockSpec(memory_space=pltpu.HBM)
-    return pl.pallas_call(
-        fetch_body,
-        in_specs=[pl.BlockSpec(memory_space=pl.ANY)] + [hbm] * len(weights),
-        out_specs=[pl.BlockSpec(memory_space=pltpu.VMEM)] * len(weights),
-        out_shape=[pltpu.VMEM(w.shape, w.dtype) for w in weights],
-        scratch_shapes=[pltpu.SemaphoreType.DMA((len(weights),))],
-        compiler_params=pltpu.CompilerParams(vmem_limit_bytes=2 * MIB),
-        cost_estimate=pl.CostEstimate(
-            flops=0, bytes_accessed=2 * sum(w.size * 2 for w in weights), transcendentals=0
-        ),
-        name="fetch",
-    )(after, *[pltpu.with_memory_space_constraint(w, pltpu.HBM) for w in weights])
-
-
-def experts_body(arrived, w_gate, w_up, w_down, out):
+def experts_body(step, arrived, w_gate, w_up, w_down, out, gate_held, up_held, down_held, sems):
     experts, _, depth = w_gate.shape
     rows, width = arrived.shape
+    pieces = [(e, f) for e in range(experts) for f in range(0, depth, step)]
+    copies = []
+    for n, (e, f) in enumerate(pieces):
+        down = pl.ds(f, step)
+        copies.append(
+            [
+                pltpu.make_async_copy(w_gate.at[e, :, down], gate_held.at[n], sems.at[n, 0]),
+                pltpu.make_async_copy(w_up.at[e, :, down], up_held.at[n], sems.at[n, 1]),
+                pltpu.make_async_copy(w_down.at[e, down, :], down_held.at[n], sems.at[n, 2]),
+            ]
+        )
+    for piece in copies:
+        for copy in piece[:2]:
+            copy.start()
+    for piece in copies:
+        piece[2].start()
     slot = lax.broadcasted_iota(jnp.int32, (rows, 1), 0)
     values = arrived[...]
-    step = 256
     hidden = []
-    for e in range(experts):
+    for n, (e, f) in enumerate(pieces):
+        copies[n][0].wait()
+        copies[n][1].wait()
+        gate = nn_dot(values, gate_held[n])
+        upward = nn_dot(values, up_held[n])
+        part = gate / (1.0 + jnp.exp(-gate)) * upward
         mine = lax.rem(slot, experts * MOST) // MOST == e
-        parts = []
-        for f in range(0, depth, step):
-            gate = nn_dot(values, w_gate[e, :, f : f + step])
-            upward = nn_dot(values, w_up[e, :, f : f + step])
-            part = gate / (1.0 + jnp.exp(-gate)) * upward
-            parts.append(jnp.where(mine, part, 0.0).astype(BF16))
-        hidden.append(jnp.concatenate(parts, axis=1))
-    step = 512
-    for c in range(0, width, step):
-        total = nn_dot(hidden[0], w_down[0, :, c : c + step])
-        for e in range(1, experts):
-            total = total + nn_dot(hidden[e], w_down[e, :, c : c + step])
-        out[:, c : c + step] = total.astype(BF16)
+        hidden.append(jnp.where(mine, part, 0.0).astype(BF16))
+    total = None
+    for n in range(len(pieces)):
+        copies[n][2].wait()
+        term = nn_dot(hidden[n], down_held[n])
+        total = term if total is None else total + term
+    out[...] = total.astype(BF16)
 
 
 def run_experts(arrived, w_gate, w_up, w_down):
     rows, width = arrived.shape
-    experts, _, hidden = w_gate.shape
+    experts, _, depth = w_gate.shape
+    step = 256
+    pieces = experts * depth // step
     vmem = pl.BlockSpec(memory_space=pltpu.VMEM)
+    hbm = pl.BlockSpec(memory_space=pltpu.HBM)
+    weights = [pltpu.with_memory_space_constraint(w, pltpu.HBM) for w in (w_gate, w_up, w_down)]
     return pl.pallas_call(
-        experts_body,
-        in_specs=[vmem] * 4,
+        functools.partial(experts_body, step),
+        in_specs=[vmem] + [hbm] * 3,
         out_specs=vmem,
         out_shape=jax.ShapeDtypeStruct((rows, width), BF16),
-        compiler_params=pltpu.CompilerParams(vmem_limit_bytes=16 * MIB),
+        scratch_shapes=[
+            pltpu.VMEM((pieces, width, step), BF16),
+            pltpu.VMEM((pieces, width, step), BF16),
+            pltpu.VMEM((pieces, step, width), BF16),
+            pltpu.SemaphoreType.DMA((pieces, 3)),
+        ],
+        compiler_params=pltpu.CompilerParams(vmem_limit_bytes=44 * MIB),
         cost_estimate=pl.CostEstimate(
-            flops=6 * rows * width * experts * hidden,
-            bytes_accessed=2 * MIB,
-            transcendentals=rows * experts * hidden,
+            flops=6 * rows * width * experts * depth,
+            bytes_accessed=6 * width * experts * depth,
+            transcendentals=rows * experts * depth,
         ),
         name="experts",
-    )(arrived, w_gate, w_up, w_down)
+    )(arrived, *weights)
 
 
 def mix_body(returned, coarse, fine, middle, out):
@@ -319,20 +335,25 @@
 
     across = [(i, i ^ CORES) for i in range(devices)]
 
-    by_owner = queries.reshape(home_rows, chips, CORES, heads_here * HD)
-    value_turned = value_cache.T
+    def chunk_of(part, chunk):
+        by_owner = part.reshape(part.shape[0], chips, CORES, heads_here * HD)
+        return by_owner[:, :, chunk].reshape(part.shape[0], chips * heads_here * HD)
+
+    strides = [CORES << k for k in range(1, (chips // 2).bit_length())]
+    hops = [[(i, i ^ stride) for i in range(devices)] for stride in strides]
+    arrived_first = lax.ppermute(queries, "ctx", hops[0])
     key_other = lax.ppermute(key_cache, "ctx", swap)
+    both = jnp.concatenate([queries, arrived_first], axis=0)
+    both, value_late = lax.optimization_barrier((both, value_cache))
+    value_turned = value_late.T
     value_other = lax.ppermute(value_turned, "ctx", swap)
     query_chunks = []
     for chunk in range(CORES):
-        mine = by_owner[:, :, chunk].reshape(home_rows, chips * heads_here * HD)
-        stride = 2 * CORES
-        while stride < devices:
-            if chunk and 2 * stride >= devices:
+        mine = chunk_of(both, chunk)
+        for hop in hops[1:]:
+            if chunk and hop is hops[-1]:
                 mine, _ = lax.optimization_barrier((mine, query_chunks[0][0]))
-            step = [(i, i ^ stride) for i in range(devices)]
-            mine = jnp.concatenate([mine, lax.ppermute(mine, "ctx", step)], axis=0)
-            stride *= 2
+            mine = jnp.concatenate([mine, lax.ppermute(mine, "ctx", hop)], axis=0)
         query_chunks.append((mine, lax.ppermute(mine, "ctx", across)))
     weight_other = lax.ppermute(out_weight, "ctx", swap)
 
@@ -386,11 +407,10 @@
         tiled=True,
     )
     middle, outgoing = norm_and_dispatch(shares, residual, norm_gain.reshape(1, width), chooser)
-    held = fetch(middle, (w_gate, w_up, w_down))
     arrived = lax.all_to_all(
         outgoing.reshape(devices, experts * MOST, width), "ctx", split_axis=0, concat_axis=0, tiled=True
     )
-    produced = run_experts(arrived.reshape(slots, width), *held)
+    produced = run_experts(arrived.reshape(slots, width), w_gate, w_up, w_down)
     returned = lax.all_to_all(
         produced.reshape(devices, experts * MOST, width), "ctx", split_axis=0, concat_axis=0, tiled=True
     )

time: 150 us -> 159 us (1.060)
  blocking collectives: 0 us -> 18 us
  local copies, waits for them, and re-layouts: 22.1 us -> 6.46 us
  waiting for transfers between devices: 62.3 us -> 75.3 us
  starting transfers between devices: 29.6 us -> 23.3 us
    all_to_all x0 -> x1, blocking collectives: none -> 18 us  [on_device(): lax.all_to_all(outgoing.reshape(devices, experts * MOST, width), 'ctx', s...]
    unnamed x38 -> x22, local copies, waits for them, and re-layouts: 19.4 us -> 2.45 us
    all_to_all x2, waiting for transfers between devices: 19.3 us -> 29.1 us  [on_device(): lax.all_to_all(sums, 'ctx', split_axis=0, concat_axis=0, axis_index_group...]
    all_to_all x1 -> x0, starting transfers between devices: 3.74 us -> none  [on_device(): lax.all_to_all(outgoing.reshape(devices, experts * MOST, width), 'ctx', s...]
    ppermute x4 -> x3, waiting for transfers between devices: 14.8 us -> 18.2 us  [the longest x2 15.4 us: on_device(): mine = jnp.concatenate([mine, lax.ppermute(mine, 'ctx', hop)], axis=0)]
    pallas_call x2, Pallas kernels: 19.8 us -> 22.3 us  [attention(): pl.pallas_call(functools.partial(attention_body, shape), grid_spec=pltpu....]
    pallas_call x2 -> x1, Pallas kernels: 9.92 us -> 7.87 us  [run_experts(): pl.pallas_call(functools.partial(experts_body, step), in_specs=[vmem] + [...]
    all_to_all x1, starting transfers between devices: 5.86 us -> 4.1 us  [on_device(): lax.all_to_all(produced.reshape(devices, experts * MOST, width), 'ctx', s...]
  transfers between devices with their start and end apart: 14 -> 12, of which waited for: 7 -> 7; matrix products, arithmetic and copies ran while one was open for 2% -> 4% of each run, Pallas kernels for 18% -> 7%
where the time goes in v6:
time: 159 us; the launch traced here: 158 us
  waiting for transfers between devices  75.3 us (47%)
  Pallas kernels  33.5 us (21%)
  starting transfers between devices  23.3 us (15%)
  blocking collectives  18 us (11%)
  local copies, waits for them, and re-layouts  6.46 us (4%)
    all_to_all x2, waiting for transfers between devices, on_device(): lax.all_to_all(sums, 'ctx', split_axis=0, concat_axis=0, axis_index_group...  29.1 us
    pallas_call x2, Pallas kernels, attention(): pl.pallas_call(functools.partial(attention_body, shape), grid_spec=pltpu....  22.3 us
    all_to_all x1, blocking collectives, on_device(): lax.all_to_all(outgoing.reshape(devices, experts * MOST, width), 'ctx', s...  18 us
    ppermute x2, waiting for transfers between devices, on_device(): mine = jnp.concatenate([mine, lax.ppermute(mine, 'ctx', hop)], axis=0)  15.4 us
    all_to_all x1, waiting for transfers between devices, on_device(): lax.all_to_all(produced.reshape(devices, experts * MOST, width), 'ctx', s...  14.3 us
    all_to_all x1, waiting for transfers between devices, on_device(): lax.all_to_all(share.reshape(chips, home_rows, width), 'ctx', split_axis=...  13.7 us
    pallas_call x1, Pallas kernels, run_experts(): pl.pallas_call(functools.partial(experts_body, step), in_specs=[vmem] + [...  7.87 us
    all_to_all x2, starting transfers between devices, on_device(): lax.all_to_all(sums, 'ctx', split_axis=0, concat_axis=0, axis_index_group...  7.31 us
  transfers between devices with their start and end apart: 12, of which 7 were waited for; matrix products, arithmetic and copies ran while one was open for 4% of the time, Pallas kernels for 7%

profile of v6, /device:TPU:0, one launch (start us, length us, event | category | flops | bytes accessed | tf_op | source)
XLA Modules:
  0.0 158.2 jit_solution(16611505440457915067)
XLA Ops:
  0.0 3.0 %collective-permute-start = (bf16[16,4096]{1,0:T(8,128)(2,1)}, bf16[16,4096]{1,0:T(8,128)(2,1)S(1)}, u32[]{:S(2)}, u32[]{:S(2)}) collective-permute-start(bf16[16,4096]{1,0:T(8,128)(2,1)} %param.14), channel_id=1, source_target_pairs={{0,4},{1,5},{2,6},{3,7},{4,0},{5,1},{6,2},{7,3},{8,12},{9,13},{10,... | collective-permute-start | bytes 393224 | tf_op jit(solution)/shard_map/ppermute | solution.py:344
  3.0 0.0 collective-permute-start.3
  3.0 0.8 reshape.40
  3.8 0.1 reshape.41.lens
  3.9 0.1 stack.27.place
  4.0 2.7 %collective-permute-done = bf16[16,4096]{1,0:T(8,128)(2,1)S(1)} collective-permute-done((bf16[16,4096]{1,0:T(8,128)(2,1)}, bf16[16,4096]{1,0:T(8,128)(2,1)S(1)}, u32[]{:S(2)}, u32[]{:S(2)}) %collective-permute-start) | collective-permute-done | bytes 131104 | tf_op jit(solution)/shard_map/ppermute | solution.py:344
  6.7 0.9 pad_maximum_fusion
  7.7 0.2 reshape.39
  7.8 1.5 copy.28
  9.3 0.1 collective-permute-start.4
  9.4 1.1 slice_reduce_fusion
  10.5 2.8 %collective-permute-start.1 = (bf16[32,2048]{1,0:T(8,128)(2,1)S(1)}, bf16[32,2048]{1,0:T(8,128)(2,1)S(1)}, u32[]{:S(2)}, u32[]{:S(2)}) collective-permute-start(bf16[32,2048]{1,0:T(8,128)(2,1)S(1)} %bitcast.26), channel_id=1, source_target_pairs={{0,8},{1,9},{2,10},{3,11},{4,12},{5,13},{6,14},{7,15},{8,0},{9,1},... | collective-permute-start | bytes 393224 | tf_op jit(solution)/shard_map/ppermute | solution.py:356
  13.4 6.9 %collective-permute-done.1 = bf16[32,2048]{1,0:T(8,128)(2,1)S(1)} collective-permute-done((bf16[32,2048]{1,0:T(8,128)(2,1)S(1)}, bf16[32,2048]{1,0:T(8,128)(2,1)S(1)}, u32[]{:S(2)}, u32[]{:S(2)}) %collective-permute-start.1) | collective-permute-done | bytes 131104 | tf_op jit(solution)/shard_map/ppermute | solution.py:356
  20.3 1.6 %collective-permute-start.2 = (bf16[64,2048]{1,0:T(8,128)(2,1)S(1)}, bf16[64,2048]{1,0:T(8,128)(2,1)S(1)}, u32[]{:S(2)}, u32[]{:S(2)}) collective-permute-start(bf16[64,2048]{1,0:T(8,128)(2,1)S(1)} %constant_dynamic-update-slice_fusion.own_q), channel_id=1, source_target_pairs={{0,2},{1,3},{2,0},{3,1},{4,6},{5,7},{6,4},{7,5},{8,10},{9,11},{10,... | collective-permute-start | bytes 786440 | tf_op jit(solution)/shard_map/ppermute | solution.py:357
  22.0 0.0 collective-permute-start.5
  22.0 8.5 %collective-permute-done.5 = bf16[32,2048]{1,0:T(8,128)(2,1)S(1)} collective-permute-done((bf16[32,2048]{1,0:T(8,128)(2,1)S(1)}, bf16[32,2048]{1,0:T(8,128)(2,1)S(1)}, u32[]{:S(2)}, u32[]{:S(2)}) %collective-permute-start.5) | collective-permute-done | bytes 131104 | tf_op jit(solution)/shard_map/ppermute | solution.py:356
  30.5 0.7 collective-permute-start.6
  31.2 0.0 collective-permute-done.2.other_q
  31.2 0.0 copy-start.3
  31.2 0.7 copy-done.3
  31.9 0.7 copy-done.4
  32.6 10.8 %attention.2 = bf16[8,272,128]{2,1,0:T(8,128)(2,1)S(1)} custom-call(s32[6]{0:T(128)S(1)} %stack.27.place, bf16[64,2048]{1,0:T(8,128)(2,1)S(1)} %constant_dynamic-update-slice_fusion.own_q, bf16[64,2048]{1,0:T(8,128)(2,1)S(1)} %collective-permute-done.2.other_q, bf16[1024,512]{1,0:T(8,128)(2,1)} %key_own.3, ...), custom_call_target="tpu_custom_call" | custom-call | flops 3221225472 | bytes 8388608 | tf_op jit(solution)/shard_map/attention/pallas_call | solution.py:123
  43.5 0.8 copy-done.1
  44.3 0.0 collective-permute-done.6.other_q
  44.3 11.4 %attention.3 = bf16[8,272,128]{2,1,0:T(8,128)(2,1)} custom-call(s32[6]{0:T(128)S(1)} %stack.27.place, bf16[64,2048]{1,0:T(8,128)(2,1)S(1)} %constant_dynamic-update-slice_fusion.2.own_q, bf16[64,2048]{1,0:T(8,128)(2,1)S(1)} %collective-permute-done.6.other_q, bf16[1024,512]{1,0:T(8,128)(2,1)} %key_own.3, ...), custom_call_target="tpu_custom_call" | custom-call | flops 3221225472 | bytes 8388608 | tf_op jit(solution)/shard_map/attention/pallas_call | solution.py:123
  55.7 3.7 %all-to-all-start.1 = ((bf16[8,272,128]{2,1,0:T(8,128)(2,1)}), bf16[8,272,128]{2,1,0:T(8,128)(2,1)S(1)}, u32[]{:S(2)}, u32[]{:S(2)}) async-start(bf16[8,272,128]{2,1,0:T(8,128)(2,1)} %attention.3), calls=%async_computation.1 | async-start | bytes 1114112 | tf_op jit(solution)/shard_map/all_to_all | solution.py:396
  59.4 0.1 collective-permute-start.7
  59.5 14.3 %all-to-all-done.1.refs_1_ = bf16[8,272,128]{2,1,0:T(8,128)(2,1)S(1)} async-done(((bf16[8,272,128]{2,1,0:T(8,128)(2,1)}), bf16[8,272,128]{2,1,0:T(8,128)(2,1)S(1)}, u32[]{:S(2)}, u32[]{:S(2)}) %all-to-all-start.1) | async-done | bytes 557088 | tf_op jit(solution)/shard_map/all_to_all | solution.py:396
  73.8 3.6 %all-to-all-start = ((bf16[8,272,128]{2,1,0:T(8,128)(2,1)}), bf16[8,272,128]{2,1,0:T(8,128)(2,1)S(1)}, u32[]{:S(2)}, u32[]{:S(2)}) async-start(bf16[8,272,128]{2,1,0:T(8,128)(2,1)} %copy-done.1), calls=%async_computation | async-start | bytes 1114112 | tf_op jit(solution)/shard_map/all_to_all | solution.py:396
  77.4 0.0 collective-permute-done.7.refs_3_
  77.4 14.8 %all-to-all-done.refs_0_ = bf16[8,272,128]{2,1,0:T(8,128)(2,1)S(1)} async-done(((bf16[8,272,128]{2,1,0:T(8,128)(2,1)}), bf16[8,272,128]{2,1,0:T(8,128)(2,1)S(1)}, u32[]{:S(2)}, u32[]{:S(2)}) %all-to-all-start) | async-done | bytes 557088 | tf_op jit(solution)/shard_map/all_to_all | solution.py:396
  92.2 2.1 %project.1 = bf16[128,2048]{1,0:T(8,128)(2,1)} custom-call(s32[6]{0:T(128)S(1)} %stack.27.place, bf16[8,272,128]{2,1,0:T(8,128)(2,1)S(1)} %all-to-all-done.refs_0_, bf16[8,272,128]{2,1,0:T(8,128)(2,1)S(1)} %all-to-all-done.1.refs_1_, bf16[256,2048]{1,0:T(8,128)(2,1)S(1)} %copy-done, bf16[256,2048]{1,0:T(8,128)(2,1)S(1)} %collective-permute-done.7.refs_3_), custom_call_target="tpu_custom_call" | custom-call | flops 268435456 | bytes 4194304 | tf_op jit(solution)/shard_map/project/pallas_call | solution.py:179
  94.3 3.6 %all-to-all-start.2 = ((bf16[8,16,2048]{2,1,0:T(8,128)(2,1)}), bf16[8,16,2048]{2,1,0:T(8,128)(2,1)S(1)}, u32[]{:S(2)}, u32[]{:S(2)}) async-start(bf16[8,16,2048]{2,1,0:T(8,128)(2,1)} %bitcast.7), calls=%async_computation.2 | async-start | bytes 1048576 | tf_op jit(solution)/shard_map/all_to_all | solution.py:401
  97.9 0.1 copy.30
  98.0 0.1 eq.31
  98.1 0.2 convert_reduce_fusion
  98.3 0.1 reduce_sum.21
  98.4 0.1 fusion
  98.5 0.1 copy.32
  98.7 13.7 %all-to-all-done.2.parts = bf16[8,16,2048]{2,1,0:T(8,128)(2,1)S(1)} async-done(((bf16[8,16,2048]{2,1,0:T(8,128)(2,1)}), bf16[8,16,2048]{2,1,0:T(8,128)(2,1)S(1)}, u32[]{:S(2)}, u32[]{:S(2)}) %all-to-all-start.2) | async-done | bytes 524320 | tf_op jit(solution)/shard_map/all_to_all | solution.py:401
  112.4 0.4 norm_and_dispatch.1
  112.8 18.0 %all_to_all.25 = bf16[16,8,2048]{2,1,0:T(8,128)(2,1)S(1)} all-to-all(bf16[16,8,2048]{2,1,0:T(8,128)(2,1)S(1)} %bitcast.22), channel_id=1, replica_groups=mesh['groups'=2,'ctx'=16] {'ctx'}, dimensions={0} | all-to-all | bytes 1048576 | tf_op jit(solution)/shard_map/all_to_all | solution.py:410
  130.8 7.9 %experts.1 = bf16[128,2048]{1,0:T(8,128)(2,1)} custom-call(bf16[128,2048]{1,0:T(8,128)(2,1)S(1)} %bitcast.17, bf16[2,2048,768]{2,1,0:T(8,128)(2,1)} %w_gate.1, bf16[2,2048,768]{2,1,0:T(8,128)(2,1)} %w_up.1, bf16[2,768,2048]{2,1,0:T(8,128)(2,1)} %w_down.1), custom_call_target="tpu_custom_call" | custom-call | flops 2415919104 | bytes 18874368 | tf_op jit(solution)/shard_map/experts/pallas_call | solution.py:270
  138.7 4.1 %all-to-all-start.4 = ((bf16[16,8,2048]{2,1,0:T(8,128)(2,1)}), bf16[16,8,2048]{2,1,0:T(8,128)(2,1)S(1)}, u32[]{:S(2)}, u32[]{:S(2)}) async-start(bf16[16,8,2048]{2,1,0:T(8,128)(2,1)} %bitcast.11), calls=%async_computation.4 | async-start | bytes 1048576 | tf_op jit(solution)/shard_map/all_to_all | solution.py:414
  142.8 0.1 copy.33
  142.9 0.1 select_reduce_fusion
  143.0 14.3 %all-to-all-done.4 = bf16[16,8,2048]{2,1,0:T(8,128)(2,1)S(1)} async-done(((bf16[16,8,2048]{2,1,0:T(8,128)(2,1)}), bf16[16,8,2048]{2,1,0:T(8,128)(2,1)S(1)}, u32[]{:S(2)}, u32[]{:S(2)}) %all-to-all-start.4) | async-done | bytes 524320 | tf_op jit(solution)/shard_map/all_to_all | solution.py:414
  157.3 0.9 mix.1
  (25 shorter events, 0.2 us)
Async XLA Ops:
  0.0 6.7 %collective-permute-start = (bf16[16,4096]{1,0:T(8,128)(2,1)}, bf16[16,4096]{1,0:T(8,128)(2,1)S(1)}, u32[]{:S(2)}, u32[]{:S(2)}) collective-permute-start(bf16[16,4096]{1,0:T(8,128)(2,1)} %param.14), channel_id=1, source_target_pairs={{0,4},{1,5},{2,6},{3,7},{4,0},{5,1},{6,2},{7,3},{8,12},{9,13},{10,... | collective-permute-start | bytes 393224 | tf_op jit(solution)/shard_map/ppermute | solution.py:344
  3.0 28.1 %collective-permute-start.3 = (bf16[1024,512]{1,0:T(8,128)(2,1)}, bf16[1024,512]{1,0:T(8,128)(2,1)S(1)}, u32[]{:S(2)}, u32[]{:S(2)}) collective-permute-start(bf16[1024,512]{1,0:T(8,128)(2,1)} %key_own.3), channel_id=1, source_target_pairs={{0,1},{1,0},{2,3},{3,2},{4,5},{5,4},{6,7},{7,6},{8,9},{9,8},{10,11... | collective-permute-start | bytes 3145736 | tf_op jit(solution)/shard_map/ppermute | solution.py:345
  9.3 21.8 %collective-permute-start.4 = (bf16[512,1024]{1,0:T(8,128)(2,1)S(1)}, bf16[512,1024]{1,0:T(8,128)(2,1)S(1)}, u32[]{:S(2)}, u32[]{:S(2)}) collective-permute-start(bf16[512,1024]{1,0:T(8,128)(2,1)S(1)} %bitcast.19), channel_id=1, source_target_pairs={{0,1},{1,0},{2,3},{3,2},{4,5},{5,4},{6,7},{7,6},{8,9},{9,8},{10,11... | collective-permute-start | bytes 3145736 | tf_op jit(solution)/shard_map/ppermute | solution.py:349
  10.5 9.8 %collective-permute-start.1 = (bf16[32,2048]{1,0:T(8,128)(2,1)S(1)}, bf16[32,2048]{1,0:T(8,128)(2,1)S(1)}, u32[]{:S(2)}, u32[]{:S(2)}) collective-permute-start(bf16[32,2048]{1,0:T(8,128)(2,1)S(1)} %bitcast.26), channel_id=1, source_target_pairs={{0,8},{1,9},{2,10},{3,11},{4,12},{5,13},{6,14},{7,15},{8,0},{9,1},... | collective-permute-start | bytes 393224 | tf_op jit(solution)/shard_map/ppermute | solution.py:356
  20.3 10.8 %collective-permute-start.2 = (bf16[64,2048]{1,0:T(8,128)(2,1)S(1)}, bf16[64,2048]{1,0:T(8,128)(2,1)S(1)}, u32[]{:S(2)}, u32[]{:S(2)}) collective-permute-start(bf16[64,2048]{1,0:T(8,128)(2,1)S(1)} %constant_dynamic-update-slice_fusion.own_q), channel_id=1, source_target_pairs={{0,2},{1,3},{2,0},{3,1},{4,6},{5,7},{6,4},{7,5},{8,10},{9,11},{10,... | collective-permute-start | bytes 786440 | tf_op jit(solution)/shard_map/ppermute | solution.py:357
  22.0 8.5 %collective-permute-start.5 = (bf16[32,2048]{1,0:T(8,128)(2,1)S(1)}, bf16[32,2048]{1,0:T(8,128)(2,1)S(1)}, u32[]{:S(2)}, u32[]{:S(2)}) collective-permute-start(bf16[32,2048]{1,0:T(8,128)(2,1)S(1)} %bitcast.24), channel_id=1, source_target_pairs={{0,8},{1,9},{2,10},{3,11},{4,12},{5,13},{6,14},{7,15},{8,0},{9,1},... | collective-permute-start | bytes 393224 | tf_op jit(solution)/shard_map/ppermute | solution.py:356
  30.5 13.8 %collective-permute-start.6 = (bf16[64,2048]{1,0:T(8,128)(2,1)S(1)}, bf16[64,2048]{1,0:T(8,128)(2,1)S(1)}, u32[]{:S(2)}, u32[]{:S(2)}) collective-permute-start(bf16[64,2048]{1,0:T(8,128)(2,1)S(1)} %constant_dynamic-update-slice_fusion.2.own_q), channel_id=1, source_target_pairs={{0,2},{1,3},{2,0},{3,1},{4,6},{5,7},{6,4},{7,5},{8,10},{9,11},{10,... | collective-permute-start | bytes 786440 | tf_op jit(solution)/shard_map/ppermute | solution.py:357
  31.2 0.7 copy-start.3
  31.9 0.7 copy-start.4
  43.5 0.8 copy-start.1
  44.3 15.1 %copy-start = (bf16[256,2048]{1,0:T(8,128)(2,1)S(1)}, bf16[256,2048]{1,0:T(8,128)(2,1)}, u32[]{:S(2)}) copy-start(bf16[256,2048]{1,0:T(8,128)(2,1)} %refs_2_.1) | copy-start | bytes 3145732
  55.7 42.2 %copy-start.5 = (s32[16,8]{0,1:T(8,128)S(1)}, s32[16,8]{0,1:T(8,128)}, u32[]{:S(2)}) copy-start(s32[16,8]{0,1:T(8,128)} %param.23) | copy-start | bytes 1540
  55.7 42.9 %copy-start.6 = (bf16[2048]{0:T(1024)(128)(2,1)S(1)}, bf16[2048]{0:T(1024)(128)(2,1)}, u32[]{:S(2)}) copy-start(bf16[2048]{0:T(1024)(128)(2,1)} %param.22) | copy-start | bytes 12292
  55.7 56.7 %copy-start.2 = (bf16[16,2048]{1,0:T(8,128)(2,1)S(1)}, bf16[16,2048]{1,0:T(8,128)(2,1)}, u32[]{:S(2)}) copy-start(bf16[16,2048]{1,0:T(8,128)(2,1)} %residual.1) | copy-start | bytes 196612
  55.7 18.1 %all-to-all-start.1 = ((bf16[8,272,128]{2,1,0:T(8,128)(2,1)}), bf16[8,272,128]{2,1,0:T(8,128)(2,1)S(1)}, u32[]{:S(2)}, u32[]{:S(2)}) async-start(bf16[8,272,128]{2,1,0:T(8,128)(2,1)} %attention.3), calls=%async_computation.1 | async-start | bytes 1114112 | tf_op jit(solution)/shard_map/all_to_all | solution.py:396
  59.4 18.0 %collective-permute-start.7 = (bf16[256,2048]{1,0:T(8,128)(2,1)S(1)}, bf16[256,2048]{1,0:T(8,128)(2,1)S(1)}, u32[]{:S(2)}, u32[]{:S(2)}) collective-permute-start(bf16[256,2048]{1,0:T(8,128)(2,1)S(1)} %copy-done), channel_id=1, source_target_pairs={{0,1},{1,0},{2,3},{3,2},{4,5},{5,4},{6,7},{7,6},{8,9},{9,8},{10,11... | collective-permute-start | bytes 3145736 | tf_op jit(solution)/shard_map/ppermute | solution.py:358
  73.8 18.4 %all-to-all-start = ((bf16[8,272,128]{2,1,0:T(8,128)(2,1)}), bf16[8,272,128]{2,1,0:T(8,128)(2,1)S(1)}, u32[]{:S(2)}, u32[]{:S(2)}) async-start(bf16[8,272,128]{2,1,0:T(8,128)(2,1)} %copy-done.1), calls=%async_computation | async-start | bytes 1114112 | tf_op jit(solution)/shard_map/all_to_all | solution.py:396
  94.3 18.1 %all-to-all-start.2 = ((bf16[8,16,2048]{2,1,0:T(8,128)(2,1)}), bf16[8,16,2048]{2,1,0:T(8,128)(2,1)S(1)}, u32[]{:S(2)}, u32[]{:S(2)}) async-start(bf16[8,16,2048]{2,1,0:T(8,128)(2,1)} %bitcast.7), calls=%async_computation.2 | async-start | bytes 1048576 | tf_op jit(solution)/shard_map/all_to_all | solution.py:401
  130.8 12.0 %copy-start.7 = (f32[16,8]{0,1:T(8,128)S(1)}, f32[16,8]{0,1:T(8,128)}, u32[]{:S(2)}) copy-start(f32[16,8]{0,1:T(8,128)} %param.24) | copy-start | bytes 1540
  138.7 18.6 %all-to-all-start.4 = ((bf16[16,8,2048]{2,1,0:T(8,128)(2,1)}), bf16[16,8,2048]{2,1,0:T(8,128)(2,1)S(1)}, u32[]{:S(2)}, u32[]{:S(2)}) async-start(bf16[16,8,2048]{2,1,0:T(8,128)(2,1)} %bitcast.11), calls=%async_computation.4 | async-start | bytes 1048576 | tf_op jit(solution)/shard_map/all_to_all | solution.py:414

commit v7 on v6

v7 whole, which is shorter than its diff:
```python
import functools
import math

import jax
import jax.numpy as jnp
from jax import lax
from jax.experimental import pallas as pl
from jax.experimental.pallas import tpu as pltpu
from jax.sharding import PartitionSpec as P

HD = 128
MOST = 4
CORES = 2
STATS = 16
MASKED = -1e30
FLOOR = -1e20
LOG2E = math.log2(math.e)
MIB = 1024 * 1024
F32 = jnp.float32
BF16 = jnp.bfloat16


def nt_dot(a, b):
    return lax.dot_general(a, b, (((1,), (1,)), ((), ())), preferred_element_type=F32)


def nn_dot(a, b):
    return lax.dot_general(a, b, (((1,), (0,)), ((), ())), preferred_element_type=F32)


def attention_body(shape, place, own_q, other_q, key_own, key_other, value_own, value_other, key_fresh, value_fresh, lens, row_ids, out, *scratch):
    rings, ring_heads, home_rows, side_rows, cache_here, step = shape
    q_rows, q_turned, hidden, scores, probs = scratch
    chip, start_own, start_other, side_here = place[0], place[1], place[2], place[4]
    pack = HD // side_rows
    groups = ring_heads // pack

    @pl.when(pl.program_id(0) == 0)
    def _():
        lanes = lens.shape[1]
        for part, start in enumerate((start_own, start_other)):
            positions = start + lax.broadcasted_iota(jnp.int32, (cache_here, lanes), 0)
            hidden[part * cache_here : (part + 1) * cache_here, :] = jnp.where(
                positions < lens[...], 0.0, MASKED
            )
        token = chip * home_rows + lax.broadcasted_iota(jnp.int32, (home_rows, lanes), 0)
        hidden[2 * cache_here :, :] = jnp.where(token == row_ids[...], 0.0, MASKED)

    for piece, side in ((own_q, side_here), (other_q, 1 - side_here)):
        q_rows[side] = piece[...]

    factor = LOG2E / math.sqrt(HD)
    spots = [(r, s, k) for r in range(rings) for s in range(2) for k in range(groups)]
    for n, (r, s, k) in enumerate(spots):
        first = r * ring_heads + k * pack
        block = jnp.concatenate(
            [q_rows[s, :, h * HD : (h + 1) * HD] for h in range(first, first + pack)], axis=0
        )
        scaled = block.T.astype(F32) * factor
        coarse = scaled.astype(BF16)
        q_turned[:HD, n * HD : (n + 1) * HD] = coarse
        q_turned[HD:, n * HD : (n + 1) * HD] = (scaled - coarse.astype(F32)).astype(BF16)
    wide = len(spots) * HD

    def score(keys, at):
        s = nn_dot(jnp.concatenate([keys, keys], axis=1), q_turned[...])
        return s + jnp.concatenate([hidden[at, s * HD : (s + 1) * HD] for _, s, _ in spots], axis=1)

    s_new = score(key_fresh[...], slice(2 * cache_here, 2 * cache_here + home_rows))
    run = jnp.max(s_new.reshape(home_rows // 8, 8, wide), axis=0)
    pieces = [(part, i) for part in range(2) for i in range(0, cache_here, step)]
    for part, i in pieces:
        at = slice(part * cache_here + i, part * cache_here + i + step)
        s = score((key_own, key_other)[part][i : i + step, :], at)
        scores[at, :] = s
        run = jnp.maximum(run, jnp.max(s.reshape(step // 8, 8, wide), axis=0))
    peak = jnp.maximum(jnp.max(run, axis=0, keepdims=True), FLOOR).astype(BF16).astype(F32)
    p_new = jnp.exp2((s_new - peak).astype(BF16))
    for part, i in pieces:
        at = slice(part * cache_here + i, part * cache_here + i + step)
        probs[at, :] = jnp.exp2((scores[at, :] - peak).astype(BF16))
    ones = jnp.ones((STATS, cache_here), BF16)
    sums = nn_dot(jnp.concatenate([value_own[...], ones], axis=0), probs[:cache_here, :])
    sums = sums + nn_dot(jnp.concatenate([value_other[...], ones], axis=0), probs[cache_here:, :])
    numer = sums[:HD] + nn_dot(value_fresh[...].astype(F32).T.astype(BF16), p_new)
    denom = sums[HD : HD + 1] + jnp.sum(p_new.astype(F32), axis=0, keepdims=True)
    high = denom.astype(BF16).astype(F32)
    low = denom - high
    for owner in range(2 * rings):
        lanes = [slice((owner * groups + k) * HD, (owner * groups + k + 1) * HD) for k in range(groups)]
        for k, cols in enumerate(lanes):
            out[owner, k * HD : (k + 1) * HD, :] = numer[:, cols].astype(BF16)
        filled = [kind[:, cols] for kind in (peak, high, low) for cols in lanes]
        filled += [jnp.zeros_like(filled[0])] * (STATS - len(filled))
        out[owner, groups * HD :, :] = jnp.concatenate(filled, axis=0).astype(BF16)


def attention(place, own_q, other_q, keys, values, new_key, new_value, lens, row_ids, chips, kv_heads):
    side_rows = own_q.shape[0]
    home_rows = new_key.shape[0]
    cache_here = keys[0].shape[0]
    rings = chips // 2 // kv_heads
    columns = own_q.shape[1] // kv_heads
    ring_heads = columns // HD // rings
    wide = 2 * side_rows * columns // HD
    height = ring_heads * side_rows + STATS
    step = 512
    positions = 2 * cache_here + home_rows
    kv = lambda g, place: (0, g)
    whole = lambda g, place: (0, 0)
    shape = (rings, ring_heads, home_rows, side_rows, cache_here, step)
    work = wide * kv_heads * 2 * cache_here
    return pl.pallas_call(
        functools.partial(attention_body, shape),
        grid_spec=pltpu.PrefetchScalarGridSpec(
            num_scalar_prefetch=1,
            grid=(kv_heads,),
            in_specs=[pl.BlockSpec((side_rows, columns), kv)] * 2
            + [pl.BlockSpec((cache_here, HD), kv)] * 2
            + [pl.BlockSpec((HD, cache_here), lambda g, place: (g, 0))] * 2
            + [pl.BlockSpec((home_rows, HD), kv)] * 2
            + [pl.BlockSpec(lens.shape, whole)] * 2,
            out_specs=pl.BlockSpec((2 * rings, height, HD), lambda g, place: (g, 0, 0)),
            scratch_shapes=[
                pltpu.VMEM((2, side_rows, columns), BF16),
                pltpu.VMEM((2 * HD, wide), BF16),
                pltpu.VMEM((positions, 2 * HD), F32),
                pltpu.VMEM((2 * cache_here, wide), F32),
                pltpu.VMEM((2 * cache_here, wide), BF16),
            ],
        ),
        out_shape=jax.ShapeDtypeStruct((chips, height, HD), BF16),
        compiler_params=pltpu.CompilerParams(vmem_limit_bytes=32 * MIB),
        cost_estimate=pl.CostEstimate(
            flops=6 * work * HD, bytes_accessed=8 * MIB, transcendentals=work
        ),
        name="attention",
    )(
        place,
        own_q,
        other_q,
        pltpu.with_memory_space_constraint(keys[0], pltpu.HBM),
        keys[1],
        *values,
        new_key,
        new_value,
        lens,
        row_ids,
    )


def project_body(side_rows, place, *refs):
    *chunks, same_own, same_other, across_own, across_other, out, turned = refs
    core, side = place[3], place[4]
    pack = HD // side_rows
    for chunk, parts in enumerate(chunks):
        chips, height, _ = parts.shape
        base = height - STATS
        groups = base // HD
        owner_heads = groups * pack // 2
        stats = parts[:, base:, :].astype(F32)
        peaks = stats[:, :groups]
        share = jnp.exp2(peaks - jnp.max(peaks, axis=0, keepdims=True))
        totals = stats[:, groups : 2 * groups] + stats[:, 2 * groups : 3 * groups]
        denom = jnp.sum(share * totals, axis=0)
        for k in range(groups):
            numer = None
            for s in range(chips):
                term = parts[s, k * HD : (k + 1) * HD, :].astype(F32) * share[s, k : k + 1, :]
                numer = term if numer is None else numer + term
            attended = (numer / denom[k : k + 1, :]).T.astype(BF16)
            for j in range(pack):
                owner, h = divmod(k * pack + j, owner_heads)
                turned[owner, chunk, :, h * HD : (h + 1) * HD] = attended[
                    j * side_rows : (j + 1) * side_rows
                ]
    product = nn_dot(turned[side, core], same_own[...]) + nn_dot(turned[side, 1 - core], same_other[...])
    product = product + nn_dot(turned[1 - side, core], across_own[...])
    product = product + nn_dot(turned[1 - side, 1 - core], across_other[...])
    out[...] = product.astype(BF16)


def project(place, chunks, weights, side_rows):
    depth, width = weights[0].shape
    vmem = pl.BlockSpec(memory_space=pltpu.VMEM)
    return pl.pallas_call(
        functools.partial(project_body, side_rows),
        in_specs=[pl.BlockSpec(memory_space=pltpu.SMEM)] + [vmem] * (len(chunks) + len(weights)),
        out_specs=vmem,
        out_shape=jax.ShapeDtypeStruct((side_rows, width), BF16),
        scratch_shapes=[pltpu.VMEM((2, CORES, side_rows, depth), BF16)],
        compiler_params=pltpu.CompilerParams(vmem_limit_bytes=32 * MIB),
        cost_estimate=pl.CostEstimate(
            flops=8 * side_rows * width * depth, bytes_accessed=6 * MIB, transcendentals=0
        ),
        name="project",
    )(place, *chunks, *weights)


def norm_body(parts, residual, gain, chooser, middle_out, sent):
    total = parts[0].astype(F32)
    for s in range(1, parts.shape[0]):
        total = total + parts[s].astype(F32)
    middle = (residual[...].astype(F32) + total).astype(BF16)
    middle_out[...] = middle
    middle = middle.astype(F32)
    inv_rms = lax.rsqrt(jnp.mean(middle * middle, axis=-1, keepdims=True) + 1e-06)
    normed = (middle * inv_rms * gain[...].astype(F32)).astype(BF16)
    sent[...] = nn_dot(chooser[...], normed).astype(BF16)


def norm_and_dispatch(parts, residual, gain, chooser):
    vmem = pl.BlockSpec(memory_space=pltpu.VMEM)
    rows, width = residual.shape
    return pl.pallas_call(
        norm_body,
        in_specs=[vmem] * 4,
        out_specs=[vmem] * 2,
        out_shape=[
            jax.ShapeDtypeStruct((rows, width), BF16),
            jax.ShapeDtypeStruct((chooser.shape[0], width), BF16),
        ],
        compiler_params=pltpu.CompilerParams(vmem_limit_bytes=24 * MIB),
        cost_estimate=pl.CostEstimate(
            flops=2 * chooser.shape[0] * rows * width, bytes_accessed=2 * MIB, transcendentals=0
        ),
        name="norm_and_dispatch",
    )(parts, residual, gain, chooser)


def experts_body(step, arrived, w_gate, w_up, w_down, out, gate_held, up_held, down_held, sems):
    experts, _, depth = w_gate.shape
    rows, width = arrived.shape
    pieces = [(e, f) for e in range(experts) for f in range(0, depth, step)]
    copies = []
    for n, (e, f) in enumerate(pieces):
        down = pl.ds(f, step)
        copies.append(
            [
                pltpu.make_async_copy(w_gate.at[e, :, down], gate_held.at[n], sems.at[n, 0]),
                pltpu.make_async_copy(w_up.at[e, :, down], up_held.at[n], sems.at[n, 1]),
                pltpu.make_async_copy(w_down.at[e, down, :], down_held.at[n], sems.at[n, 2]),
            ]
        )
    for piece in copies:
        for copy in piece[:2]:
            copy.start()
    for piece in copies:
        piece[2].start()
    slot = lax.broadcasted_iota(jnp.int32, (rows, 1), 0)
    values = arrived[...]
    hidden = []
    for n, (e, f) in enumerate(pieces):
        copies[n][0].wait()
        copies[n][1].wait()
        gate = nn_dot(values, gate_held[n])
        upward = nn_dot(values, up_held[n])
        part = gate / (1.0 + jnp.exp(-gate)) * upward
        mine = lax.rem(slot, experts * MOST) // MOST == e
        hidden.append(jnp.where(mine, part, 0.0).astype(BF16))
    total = None
    for n in range(len(pieces)):
        copies[n][2].wait()
        term = nn_dot(hidden[n], down_held[n])
        total = term if total is None else total + term
    out[...] = total.astype(BF16)


def run_experts(arrived, w_gate, w_up, w_down):
    rows, width = arrived.shape
    experts, _, depth = w_gate.shape
    step = 256
    pieces = experts * depth // step
    vmem = pl.BlockSpec(memory_space=pltpu.VMEM)
    hbm = pl.BlockSpec(memory_space=pltpu.HBM)
    weights = [pltpu.with_memory_space_constraint(w, pltpu.HBM) for w in (w_gate, w_up, w_down)]
    return pl.pallas_call(
        functools.partial(experts_body, step),
        in_specs=[vmem] + [hbm] * 3,
        out_specs=vmem,
        out_shape=jax.ShapeDtypeStruct((rows, width), BF16),
        scratch_shapes=[
            pltpu.VMEM((pieces, width, step), BF16),
            pltpu.VMEM((pieces, width, step), BF16),
            pltpu.VMEM((pieces, step, width), BF16),
            pltpu.SemaphoreType.DMA((pieces, 3)),
        ],
        compiler_params=pltpu.CompilerParams(vmem_limit_bytes=44 * MIB),
        cost_estimate=pl.CostEstimate(
            flops=6 * rows * width * experts * depth,
            bytes_accessed=6 * width * experts * depth,
            transcendentals=rows * experts * depth,
        ),
        name="experts",
    )(arrived, *weights)


def mix_body(returned, coarse, fine, middle, out):
    values = returned[...]
    mixed = nn_dot(coarse[...], values) + nn_dot(fine[...], values)
    out[...] = (middle[...].astype(F32) + mixed).astype(BF16)


def mix(returned, coarse, fine, middle):
    vmem = pl.BlockSpec(memory_space=pltpu.VMEM)
    return pl.pallas_call(
        mix_body,
        in_specs=[vmem] * 4,
        out_specs=vmem,
        out_shape=jax.ShapeDtypeStruct(middle.shape, BF16),
        compiler_params=pltpu.CompilerParams(vmem_limit_bytes=16 * MIB),
        name="mix",
    )(returned, coarse, fine, middle)


def on_device(
    queries,
    new_key,
    new_value,
    key_cache,
    value_cache,
    cache_len,
    out_weight,
    residual,
    norm_gain,
    expert_ids,
    route_weight,
    w_gate,
    w_up,
    w_down,
):
    devices = lax.axis_size("ctx")
    chips = devices // CORES
    index = lax.axis_index("ctx")
    chip, core = index // CORES, index % CORES
    home_rows, width = residual.shape
    top = expert_ids.shape[1]
    heads_here = out_weight.shape[0] // HD
    cache_here = key_cache.shape[0]
    same_core = [[CORES * j + c for j in range(chips)] for c in range(CORES)]
    swap = [(i, i ^ 1) for i in range(devices)]

    across = [(i, i ^ CORES) for i in range(devices)]
    along = [
        [CORES * (2 * ring + side) + c for ring in range(chips // 2)]
        for side in range(2)
        for c in range(CORES)
    ]
    rings = chips // 2
    side_rows = rings * home_rows

    by_owner = queries.reshape(home_rows, chips, CORES, heads_here * HD)
    query_chunks = []
    for chunk in range(CORES):
        part = by_owner[:, :, chunk].reshape(1, home_rows, chips * heads_here * HD)
        if chunk:
            part, _ = lax.optimization_barrier((part, query_chunks[0][0]))
        mine = lax.all_to_all(
            jnp.broadcast_to(part, (rings, *part.shape[1:])),
            "ctx",
            split_axis=0,
            concat_axis=0,
            axis_index_groups=along,
            tiled=True,
        ).reshape(side_rows, part.shape[2])
        query_chunks.append((mine, lax.ppermute(mine, "ctx", across)))
    key_other = lax.ppermute(key_cache, "ctx", swap)
    value_turned = value_cache.T
    value_other = lax.ppermute(value_turned, "ctx", swap)
    weight_swapped = lax.ppermute(out_weight, "ctx", swap)

    place = jnp.stack([chip, index * cache_here, (index ^ 1) * cache_here, core, chip % 2]).astype(jnp.int32)

    def in_lanes(by_row):
        sides = by_row.reshape(rings, 2, CORES, home_rows)
        sides = lax.dynamic_index_in_dim(sides, core, axis=2, keepdims=False)
        sides = jnp.swapaxes(sides, 0, 1).reshape(2, 1, side_rows)
        return jnp.tile(sides, (1, HD // side_rows, 1)).reshape(1, 2 * HD)

    lens = in_lanes(cache_len)
    numbers = jnp.arange(chips * home_rows, dtype=jnp.int32).reshape(chips, 1, home_rows)
    row_ids = in_lanes(jnp.broadcast_to(numbers, (chips, CORES, home_rows)))

    flat_ids = expert_ids.reshape(-1)
    picks = jnp.arange(flat_ids.shape[0])
    earlier = (flat_ids[:, None] == flat_ids[None, :]) & (picks[None, :] < picks[:, None])
    target = (flat_ids * MOST + jnp.sum(earlier, axis=1, dtype=jnp.int32)).reshape(home_rows, top)
    experts = w_gate.shape[0]
    slots = experts * devices * MOST
    takes = target[:, :, None] == jnp.arange(slots, dtype=jnp.int32)
    chooser = jnp.any(takes, axis=1).T.astype(BF16)
    spread = jnp.sum(jnp.where(takes, route_weight[:, :, None], 0.0), axis=1)
    coarse = spread.astype(BF16)
    fine = (spread - coarse.astype(F32)).astype(BF16)

    gathered = []
    for chunk, (own_q, other_q) in enumerate(query_chunks):
        sums = attention(
            place,
            own_q,
            other_q,
            (key_cache, key_other),
            (value_turned, value_other),
            new_key,
            new_value,
            lens,
            row_ids,
            chips,
            key_cache.shape[1] // HD,
        )
        if chunk + 1 < len(query_chunks):
            own_next, other_next = query_chunks[chunk + 1]
            sums, other_next = lax.optimization_barrier((sums, other_next))
            query_chunks[chunk + 1] = (own_next, other_next)
        if chunk:
            sums, gathered[-1] = lax.optimization_barrier((sums, gathered[-1]))
        gathered.append(
            lax.all_to_all(
                sums, "ctx", split_axis=0, concat_axis=0, axis_index_groups=same_core, tiled=True
            )
        )
    late_weight, _ = lax.optimization_barrier((out_weight, query_chunks[-1][1]))
    weight_across = lax.ppermute(late_weight, "ctx", across)
    weights = (out_weight, weight_swapped, weight_across, lax.ppermute(weight_across, "ctx", swap))
    share = project(place, gathered, weights, side_rows)
    shares = lax.all_to_all(
        share.reshape(rings, home_rows, width),
        "ctx",
        split_axis=0,
        concat_axis=0,
        axis_index_groups=along,
        tiled=True,
    )
    middle, outgoing = norm_and_dispatch(shares, residual, norm_gain.reshape(1, width), chooser)
    arrived = lax.all_to_all(
        outgoing.reshape(devices, experts * MOST, width), "ctx", split_axis=0, concat_axis=0, tiled=True
    )
    produced = run_experts(arrived.reshape(slots, width), w_gate, w_up, w_down)
    returned = lax.all_to_all(
        produced.reshape(devices, experts * MOST, width), "ctx", split_axis=0, concat_axis=0, tiled=True
    )
    return mix(returned.reshape(slots, width), coarse, fine, middle)


def solution(mesh):
    placed = (
        P(("groups", "ctx"), None),
        P(("groups", "ctx"), None),
        P(("groups", "ctx"), None),
        P(("groups", "ctx"), None),
        P(("groups", "ctx"), None),
        P("groups"),
        P("ctx", None),
        P(("groups", "ctx"), None),
        P(),
        P(("groups", "ctx"), None),
        P(("groups", "ctx"), None),
        P("ctx", None, None),
        P("ctx", None, None),
        P("ctx", None, None),
    )
    return jax.shard_map(
        on_device, mesh=mesh, in_specs=placed, out_specs=P(("groups", "ctx"), None), check_vma=False
    )
```

time: 159 us -> 164 us (1.031)
  starting transfers between devices: 23.3 us -> 32.2 us
  waiting for transfers between devices: 75.3 us -> 71.5 us
    all_to_all x2, waiting for transfers between devices: 29.1 us -> 15.7 us  [on_device(): lax.all_to_all(sums, 'ctx', split_axis=0, concat_axis=0, axis_index_group...]
    all_to_all x1 -> x3, starting transfers between devices: 3.64 us -> 13.3 us  [the longest x2 9.85 us: on_device(): lax.all_to_all(jnp.broadcast_to(part, (rings, *part.shape[1:])), 'ctx', s...]
    all_to_all x1 -> x3, waiting for transfers between devices: 13.7 us -> 21.1 us  [the longest x2 13 us: on_device(): lax.all_to_all(jnp.broadcast_to(part, (rings, *part.shape[1:])), 'ctx', s...]
    ppermute x4 -> x3, starting transfers between devices: 5.92 us -> 0.65 us  [the longest x1 0.58 us: on_device(): weight_across = lax.ppermute(late_weight, 'ctx', across)]
    all_to_all x2, starting transfers between devices: 7.31 us -> 10.5 us  [on_device(): lax.all_to_all(sums, 'ctx', split_axis=0, concat_axis=0, axis_index_group...]
    ppermute x4 -> x3, waiting for transfers between devices: 18.2 us -> 20.4 us  [the longest x1 20.4 us: on_device(): weight_across = lax.ppermute(late_weight, 'ctx', across)]
    pallas_call x2, Pallas kernels: 22.3 us -> 20.4 us  [attention(): pl.pallas_call(functools.partial(attention_body, shape), grid_spec=pltpu....]
  transfers between devices with their start and end apart: 12 -> 13, of which waited for: 7 -> 6; matrix products, arithmetic and copies ran while one was open for 4% -> 4% of each run, Pallas kernels for 7% -> 12%
where the time goes in v7:
time: 164 us; the launch traced here: 163 us
  waiting for transfers between devices  71.5 us (44%)
  Pallas kernels  33.2 us (20%)
  starting transfers between devices  32.2 us (20%)
  blocking collectives  18 us (11%)
  local copies, waits for them, and re-layouts  7.8 us (5%)
    ppermute x1, waiting for transfers between devices, on_device(): weight_across = lax.ppermute(late_weight, 'ctx', across)  20.4 us
    pallas_call x2, Pallas kernels, attention(): pl.pallas_call(functools.partial(attention_body, shape), grid_spec=pltpu....  20.4 us
    all_to_all x1, blocking collectives, on_device(): lax.all_to_all(outgoing.reshape(devices, experts * MOST, width), 'ctx', s...  18 us
    all_to_all x2, waiting for transfers between devices, on_device(): lax.all_to_all(sums, 'ctx', split_axis=0, concat_axis=0, axis_index_group...  15.7 us
    all_to_all x1, waiting for transfers between devices, on_device(): lax.all_to_all(produced.reshape(devices, experts * MOST, width), 'ctx', s...  14.3 us
    all_to_all x2, waiting for transfers between devices, on_device(): lax.all_to_all(jnp.broadcast_to(part, (rings, *part.shape[1:])), 'ctx', s...  13 us
    all_to_all x2, starting transfers between devices, on_device(): lax.all_to_all(sums, 'ctx', split_axis=0, concat_axis=0, axis_index_group...  10.5 us
    all_to_all x2, starting transfers between devices, on_device(): lax.all_to_all(jnp.broadcast_to(part, (rings, *part.shape[1:])), 'ctx', s...  9.85 us
  transfers between devices with their start and end apart: 13, of which 6 were waited for; matrix products, arithmetic and copies ran while one was open for 4% of the time, Pallas kernels for 12%

profile of v7, /device:TPU:0, one launch (start us, length us, event | category | flops | bytes accessed | tf_op | source)
XLA Modules:
  0.0 163.4 jit_solution(7566308198180493028)
XLA Ops:
  0.0 0.5 collective-permute-start.1
  0.5 1.5 copy.29
  1.9 0.1 collective-permute-start.2
  2.1 1.0 reshape.82
  3.1 0.6 slice_reduce_fusion
  3.6 0.7 broadcast_in_dim.34
  4.4 6.3 %all-to-all-start = ((bf16[4,16,2048]{2,1,0:T(8,128)(2,1)}), bf16[4,16,2048]{2,1,0:T(8,128)(2,1)S(1)}, u32[]{:S(2)}, u32[]{:S(2)}) async-start(bf16[4,16,2048]{2,1,0:T(8,128)(2,1)} %broadcast_in_dim.34), calls=%async_computation | async-start | bytes 524288 | tf_op jit(solution)/shard_map/all_to_all | solution.py:358
  10.7 0.8 reshape.85
  11.5 8.3 %all-to-all-done = bf16[4,16,2048]{2,1,0:T(8,128)(2,1)S(1)} async-done(((bf16[4,16,2048]{2,1,0:T(8,128)(2,1)}), bf16[4,16,2048]{2,1,0:T(8,128)(2,1)S(1)}, u32[]{:S(2)}, u32[]{:S(2)}) %all-to-all-start) | async-done | bytes 262176 | tf_op jit(solution)/shard_map/all_to_all | solution.py:358
  19.8 0.7 broadcast_in_dim.36
  20.5 3.5 %all-to-all-start.1 = ((bf16[4,16,2048]{2,1,0:T(8,128)(2,1)}), bf16[4,16,2048]{2,1,0:T(8,128)(2,1)S(1)}, u32[]{:S(2)}, u32[]{:S(2)}) async-start(bf16[4,16,2048]{2,1,0:T(8,128)(2,1)} %broadcast_in_dim.36), calls=%async_computation.1 | async-start | bytes 524288 | tf_op jit(solution)/shard_map/all_to_all | solution.py:358
  24.1 1.6 collective-permute-start
  25.7 0.1 tile.20
  25.8 0.1 tile.22.lens
  25.9 0.1 iota.71
  25.9 0.1 iota.72
  26.0 0.1 iota.64
  26.1 0.1 tile.24.row_ids
  26.2 0.1 stack.23.place
  26.3 4.7 %all-to-all-done.1 = bf16[4,16,2048]{2,1,0:T(8,128)(2,1)S(1)} async-done(((bf16[4,16,2048]{2,1,0:T(8,128)(2,1)}), bf16[4,16,2048]{2,1,0:T(8,128)(2,1)S(1)}, u32[]{:S(2)}, u32[]{:S(2)}) %all-to-all-start.1) | async-done | bytes 262176 | tf_op jit(solution)/shard_map/all_to_all | solution.py:358
  30.9 1.5 collective-permute-start.3
  32.5 0.7 copy-done.2
  33.2 0.7 copy-done.4
  33.9 10.2 %attention.2 = bf16[8,272,128]{2,1,0:T(8,128)(2,1)} custom-call(s32[5]{0:T(128)S(1)} %stack.23.place, bf16[64,2048]{1,0:T(8,128)(2,1)S(1)} %bitcast.31, bf16[64,2048]{1,0:T(8,128)(2,1)S(1)} %collective-permute-done.other_q, bf16[1024,512]{1,0:T(8,128)(2,1)} %key_own.3, bf16[1024,512]{1,0:T(8,128)(2,1)} %collective-permute-done.1.key_other, ...), custom_call_target="tpu_custom_call" | custom-call | flops 3221225472 | bytes 8388608 | tf_op jit(solution)/shard_map/attention/pallas_call | solution.py:113
  44.1 0.6 collective-permute-start.5
  44.7 5.9 %all-to-all-start.2 = ((bf16[8,272,128]{2,1,0:T(8,128)(2,1)}), bf16[8,272,128]{2,1,0:T(8,128)(2,1)S(1)}, u32[]{:S(2)}, u32[]{:S(2)}) async-start(bf16[8,272,128]{2,1,0:T(8,128)(2,1)} %attention.2), calls=%async_computation.2 | async-start | bytes 1114112 | tf_op jit(solution)/shard_map/all_to_all | solution.py:418
  50.6 0.1 collective-permute-start.4
  50.7 20.4 %collective-permute-done.5.refs_4_ = bf16[256,2048]{1,0:T(8,128)(2,1)} collective-permute-done((bf16[256,2048]{1,0:T(8,128)(2,1)S(1)}, bf16[256,2048]{1,0:T(8,128)(2,1)}, u32[]{:S(2)}, u32[]{:S(2)}) %collective-permute-start.5) | collective-permute-done | bytes 1048608 | tf_op jit(solution)/shard_map/ppermute | solution.py:423
  71.1 10.2 %attention.3 = bf16[8,272,128]{2,1,0:T(8,128)(2,1)} custom-call(s32[5]{0:T(128)S(1)} %stack.23.place, bf16[64,2048]{1,0:T(8,128)(2,1)S(1)} %bitcast.33, bf16[64,2048]{1,0:T(8,128)(2,1)S(1)} %collective-permute-done.3.other_q, bf16[1024,512]{1,0:T(8,128)(2,1)} %key_own.3, bf16[1024,512]{1,0:T(8,128)(2,1)} %collective-permute-done.1.key_other, ...), custom_call_target="tpu_custom_call" | custom-call | flops 3221225472 | bytes 8388608 | tf_op jit(solution)/shard_map/attention/pallas_call | solution.py:113
  81.3 4.6 %all-to-all-start.3 = ((bf16[8,272,128]{2,1,0:T(8,128)(2,1)}), bf16[8,272,128]{2,1,0:T(8,128)(2,1)S(1)}, u32[]{:S(2)}, u32[]{:S(2)}) async-start(bf16[8,272,128]{2,1,0:T(8,128)(2,1)} %attention.3), calls=%async_computation.3 | async-start | bytes 1114112 | tf_op jit(solution)/shard_map/all_to_all | solution.py:418
  86.0 0.1 copy.31
  86.0 0.1 eq.31
  86.1 15.7 %all-to-all-done.3.refs_1_ = bf16[8,272,128]{2,1,0:T(8,128)(2,1)S(1)} async-done(((bf16[8,272,128]{2,1,0:T(8,128)(2,1)}), bf16[8,272,128]{2,1,0:T(8,128)(2,1)S(1)}, u32[]{:S(2)}, u32[]{:S(2)}) %all-to-all-start.3) | async-done | bytes 557088 | tf_op jit(solution)/shard_map/all_to_all | solution.py:418
  101.8 3.7 %project.1 = bf16[64,2048]{1,0:T(8,128)(2,1)} custom-call(s32[5]{0:T(128)S(1)} %stack.23.place, bf16[8,272,128]{2,1,0:T(8,128)(2,1)S(1)} %all-to-all-done.2.refs_0_, bf16[8,272,128]{2,1,0:T(8,128)(2,1)S(1)} %all-to-all-done.3.refs_1_, bf16[256,2048]{1,0:T(8,128)(2,1)S(1)} %copy-done, bf16[256,2048]{1,0:T(8,128)(2,1)} %collective-permute-done.4.refs_3_, ...), custom_call_target="tpu_custom_call" | custom-call | flops 268435456 | bytes 6291456 | tf_op jit(solution)/shard_map/project/pallas_call | solution.py:186
  105.5 3.4 %all-to-all-start.4 = ((bf16[4,16,2048]{2,1,0:T(8,128)(2,1)}), bf16[4,16,2048]{2,1,0:T(8,128)(2,1)S(1)}, u32[]{:S(2)}, u32[]{:S(2)}) async-start(bf16[4,16,2048]{2,1,0:T(8,128)(2,1)} %bitcast.11), calls=%async_computation.4 | async-start | bytes 524288 | tf_op jit(solution)/shard_map/all_to_all | solution.py:426
  108.9 0.2 convert_reduce_fusion
  109.1 0.1 reduce_sum.21
  109.2 0.1 fusion
  109.3 0.1 copy.33
  109.5 8.2 %all-to-all-done.4.parts = bf16[4,16,2048]{2,1,0:T(8,128)(2,1)S(1)} async-done(((bf16[4,16,2048]{2,1,0:T(8,128)(2,1)}), bf16[4,16,2048]{2,1,0:T(8,128)(2,1)S(1)}, u32[]{:S(2)}, u32[]{:S(2)}) %all-to-all-start.4) | async-done | bytes 262176 | tf_op jit(solution)/shard_map/all_to_all | solution.py:426
  117.7 0.4 norm_and_dispatch.1
  118.1 18.0 %all_to_all.35 = bf16[16,8,2048]{2,1,0:T(8,128)(2,1)S(1)} all-to-all(bf16[16,8,2048]{2,1,0:T(8,128)(2,1)S(1)} %bitcast.29), channel_id=1, replica_groups=mesh['groups'=2,'ctx'=16] {'ctx'}, dimensions={0} | all-to-all | bytes 1048576 | tf_op jit(solution)/shard_map/all_to_all | solution.py:435
  136.0 7.9 %experts.1 = bf16[128,2048]{1,0:T(8,128)(2,1)} custom-call(bf16[128,2048]{1,0:T(8,128)(2,1)S(1)} %bitcast.24, bf16[2,2048,768]{2,1,0:T(8,128)(2,1)} %w_gate.1, bf16[2,2048,768]{2,1,0:T(8,128)(2,1)} %w_up.1, bf16[2,768,2048]{2,1,0:T(8,128)(2,1)} %w_down.1), custom_call_target="tpu_custom_call" | custom-call | flops 2415919104 | bytes 18874368 | tf_op jit(solution)/shard_map/experts/pallas_call | solution.py:277
  143.9 4.1 %all-to-all-start.6 = ((bf16[16,8,2048]{2,1,0:T(8,128)(2,1)}), bf16[16,8,2048]{2,1,0:T(8,128)(2,1)S(1)}, u32[]{:S(2)}, u32[]{:S(2)}) async-start(bf16[16,8,2048]{2,1,0:T(8,128)(2,1)} %bitcast.15), calls=%async_computation.6 | async-start | bytes 1048576 | tf_op jit(solution)/shard_map/all_to_all | solution.py:439
  148.0 0.1 copy.34
  148.1 0.1 select_reduce_fusion
  148.2 14.3 %all-to-all-done.6 = bf16[16,8,2048]{2,1,0:T(8,128)(2,1)S(1)} async-done(((bf16[16,8,2048]{2,1,0:T(8,128)(2,1)}), bf16[16,8,2048]{2,1,0:T(8,128)(2,1)S(1)}, u32[]{:S(2)}, u32[]{:S(2)}) %all-to-all-start.6) | async-done | bytes 524320 | tf_op jit(solution)/shard_map/all_to_all | solution.py:439
  162.5 0.9 mix.1
  (37 shorter events, 0.2 us)
Async XLA Ops:
  0.0 32.5 %collective-permute-start.1 = (bf16[1024,512]{1,0:T(8,128)(2,1)}, bf16[1024,512]{1,0:T(8,128)(2,1)}, u32[]{:S(2)}, u32[]{:S(2)}) collective-permute-start(bf16[1024,512]{1,0:T(8,128)(2,1)} %key_own.3), channel_id=1, source_target_pairs={{0,1},{1,0},{2,3},{3,2},{4,5},{5,4},{6,7},{7,6},{8,9},{9,8},{10,11... | collective-permute-start | bytes 3145736 | tf_op jit(solution)/shard_map/ppermute | solution.py:367
  1.9 30.5 %collective-permute-start.2 = (bf16[512,1024]{1,0:T(8,128)(2,1)S(1)}, bf16[512,1024]{1,0:T(8,128)(2,1)}, u32[]{:S(2)}, u32[]{:S(2)}) collective-permute-start(bf16[512,1024]{1,0:T(8,128)(2,1)S(1)} %bitcast.26), channel_id=1, source_target_pairs={{0,1},{1,0},{2,3},{3,2},{4,5},{5,4},{6,7},{7,6},{8,9},{9,8},{10,11... | collective-permute-start | bytes 3145736 | tf_op jit(solution)/shard_map/ppermute | solution.py:369
  4.4 15.4 %all-to-all-start = ((bf16[4,16,2048]{2,1,0:T(8,128)(2,1)}), bf16[4,16,2048]{2,1,0:T(8,128)(2,1)S(1)}, u32[]{:S(2)}, u32[]{:S(2)}) async-start(bf16[4,16,2048]{2,1,0:T(8,128)(2,1)} %broadcast_in_dim.34), calls=%async_computation | async-start | bytes 524288 | tf_op jit(solution)/shard_map/all_to_all | solution.py:358
  20.5 23.6 %copy-start = (bf16[256,2048]{1,0:T(8,128)(2,1)S(1)}, bf16[256,2048]{1,0:T(8,128)(2,1)}, u32[]{:S(2)}) copy-start(bf16[256,2048]{1,0:T(8,128)(2,1)} %refs_2_.1) | copy-start | bytes 3145732
  20.5 10.4 %all-to-all-start.1 = ((bf16[4,16,2048]{2,1,0:T(8,128)(2,1)}), bf16[4,16,2048]{2,1,0:T(8,128)(2,1)S(1)}, u32[]{:S(2)}, u32[]{:S(2)}) async-start(bf16[4,16,2048]{2,1,0:T(8,128)(2,1)} %broadcast_in_dim.36), calls=%async_computation.1 | async-start | bytes 524288 | tf_op jit(solution)/shard_map/all_to_all | solution.py:358
  24.1 8.4 %collective-permute-start = (bf16[64,2048]{1,0:T(8,128)(2,1)S(1)}, bf16[64,2048]{1,0:T(8,128)(2,1)S(1)}, u32[]{:S(2)}, u32[]{:S(2)}) collective-permute-start(bf16[64,2048]{1,0:T(8,128)(2,1)S(1)} %bitcast.30), channel_id=1, source_target_pairs={{0,2},{1,3},{2,0},{3,1},{4,6},{5,7},{6,4},{7,5},{8,10},{9,11},{10,... | collective-permute-start | bytes 786440 | tf_op jit(solution)/shard_map/ppermute | solution.py:366
  30.9 13.2 %collective-permute-start.3 = (bf16[64,2048]{1,0:T(8,128)(2,1)S(1)}, bf16[64,2048]{1,0:T(8,128)(2,1)S(1)}, u32[]{:S(2)}, u32[]{:S(2)}) collective-permute-start(bf16[64,2048]{1,0:T(8,128)(2,1)S(1)} %bitcast.32), channel_id=1, source_target_pairs={{0,2},{1,3},{2,0},{3,1},{4,6},{5,7},{6,4},{7,5},{8,10},{9,11},{10,... | collective-permute-start | bytes 786440 | tf_op jit(solution)/shard_map/ppermute | solution.py:366
  32.5 0.7 copy-start.2
  33.2 0.7 copy-start.4
  33.9 37.2 %copy-start.3 = (bf16[16,512]{1,0:T(8,128)(2,1)S(1)}, bf16[16,512]{1,0:T(8,128)(2,1)}, u32[]{:S(2)}) copy-start(bf16[16,512]{1,0:T(8,128)(2,1)} %key_fresh.3) | copy-start | bytes 49156
  33.9 37.2 %copy-start.5 = (bf16[16,512]{1,0:T(8,128)(2,1)S(1)}, bf16[16,512]{1,0:T(8,128)(2,1)}, u32[]{:S(2)}) copy-start(bf16[16,512]{1,0:T(8,128)(2,1)} %value_fresh.3) | copy-start | bytes 49156
  44.1 27.0 %collective-permute-start.5 = (bf16[256,2048]{1,0:T(8,128)(2,1)S(1)}, bf16[256,2048]{1,0:T(8,128)(2,1)}, u32[]{:S(2)}, u32[]{:S(2)}) collective-permute-start(bf16[256,2048]{1,0:T(8,128)(2,1)S(1)} %copy-done), channel_id=1, source_target_pairs={{0,2},{1,3},{2,0},{3,1},{4,6},{5,7},{6,4},{7,5},{8,10},{9,11},{10,... | collective-permute-start | bytes 3145736 | tf_op jit(solution)/shard_map/ppermute | solution.py:423
  44.7 36.6 %all-to-all-start.2 = ((bf16[8,272,128]{2,1,0:T(8,128)(2,1)}), bf16[8,272,128]{2,1,0:T(8,128)(2,1)S(1)}, u32[]{:S(2)}, u32[]{:S(2)}) async-start(bf16[8,272,128]{2,1,0:T(8,128)(2,1)} %attention.2), calls=%async_computation.2 | async-start | bytes 1114112 | tf_op jit(solution)/shard_map/all_to_all | solution.py:418
  50.6 35.4 %copy-start.6 = (s32[16,8]{0,1:T(8,128)S(1)}, s32[16,8]{0,1:T(8,128)}, u32[]{:S(2)}) copy-start(s32[16,8]{0,1:T(8,128)} %param.23) | copy-start | bytes 1540
  50.6 35.5 %collective-permute-start.4 = (bf16[256,2048]{1,0:T(8,128)(2,1)S(1)}, bf16[256,2048]{1,0:T(8,128)(2,1)}, u32[]{:S(2)}, u32[]{:S(2)}) collective-permute-start(bf16[256,2048]{1,0:T(8,128)(2,1)S(1)} %copy-done), channel_id=1, source_target_pairs={{0,1},{1,0},{2,3},{3,2},{4,5},{5,4},{6,7},{7,6},{8,9},{9,8},{10,11... | collective-permute-start | bytes 3145736 | tf_op jit(solution)/shard_map/ppermute | solution.py:370
  71.1 30.7 %collective-permute-start.6 = (bf16[256,2048]{1,0:T(8,128)(2,1)}, bf16[256,2048]{1,0:T(8,128)(2,1)}, u32[]{:S(2)}, u32[]{:S(2)}) collective-permute-start(bf16[256,2048]{1,0:T(8,128)(2,1)} %collective-permute-done.5.refs_4_), channel_id=1, source_target_pairs={{0,1},{1,0},{2,3},{3,2},{4,5},{5,4},{6,7},{7,6},{8,9},{9,8},{10,11... | collective-permute-start | bytes 3145736 | tf_op jit(solution)/shard_map/ppermute | solution.py:424
  81.3 27.8 %copy-start.7 = (bf16[2048]{0:T(1024)(128)(2,1)S(1)}, bf16[2048]{0:T(1024)(128)(2,1)}, u32[]{:S(2)}) copy-start(bf16[2048]{0:T(1024)(128)(2,1)} %param.22) | copy-start | bytes 12292
  81.3 36.3 %copy-start.1 = (bf16[16,2048]{1,0:T(8,128)(2,1)S(1)}, bf16[16,2048]{1,0:T(8,128)(2,1)}, u32[]{:S(2)}) copy-start(bf16[16,2048]{1,0:T(8,128)(2,1)} %residual.1) | copy-start | bytes 196612
  81.3 20.5 %all-to-all-start.3 = ((bf16[8,272,128]{2,1,0:T(8,128)(2,1)}), bf16[8,272,128]{2,1,0:T(8,128)(2,1)S(1)}, u32[]{:S(2)}, u32[]{:S(2)}) async-start(bf16[8,272,128]{2,1,0:T(8,128)(2,1)} %attention.3), calls=%async_computation.3 | async-start | bytes 1114112 | tf_op jit(solution)/shard_map/all_to_all | solution.py:418
  105.5 12.1 %all-to-all-start.4 = ((bf16[4,16,2048]{2,1,0:T(8,128)(2,1)}), bf16[4,16,2048]{2,1,0:T(8,128)(2,1)S(1)}, u32[]{:S(2)}, u32[]{:S(2)}) async-start(bf16[4,16,2048]{2,1,0:T(8,128)(2,1)} %bitcast.11), calls=%async_computation.4 | async-start | bytes 524288 | tf_op jit(solution)/shard_map/all_to_all | solution.py:426
  136.0 12.0 %copy-start.8 = (f32[16,8]{0,1:T(8,128)S(1)}, f32[16,8]{0,1:T(8,128)}, u32[]{:S(2)}) copy-start(f32[16,8]{0,1:T(8,128)} %param.24) | copy-start | bytes 1540
  143.9 18.6 %all-to-all-start.6 = ((bf16[16,8,2048]{2,1,0:T(8,128)(2,1)}), bf16[16,8,2048]{2,1,0:T(8,128)(2,1)S(1)}, u32[]{:S(2)}, u32[]{:S(2)}) async-start(bf16[16,8,2048]{2,1,0:T(8,128)(2,1)} %bitcast.15), calls=%async_computation.6 | async-start | bytes 1048576 | tf_op jit(solution)/shard_map/all_to_all | solution.py:439

commit v8 on v7

--- a/solution.py
+++ b/solution.py
@@ -28,10 +28,12 @@
     return lax.dot_general(a, b, (((1,), (0,)), ((), ())), preferred_element_type=F32)
 
 
-def attention_body(shape, place, own_q, other_q, key_own, key_other, value_own, value_other, key_fresh, value_fresh, lens, row_ids, out, *scratch):
+def attention_body(shape, place, *refs):
     rings, ring_heads, home_rows, side_rows, cache_here, step = shape
-    q_rows, q_turned, hidden, scores, probs = scratch
-    chip, start_own, start_other, side_here = place[0], place[1], place[2], place[4]
+    *query_refs, key_own, key_other, value_own, value_other, key_fresh, value_fresh = refs[:-8]
+    lens, row_ids, out, q_rows, q_turned, hidden, scores, probs = refs[-8:]
+    chip, start_own, start_other, side_here, ring_here = place[0], place[1], place[2], place[4], place[5]
+    near = side_rows // home_rows
     pack = HD // side_rows
     groups = ring_heads // pack
 
@@ -46,8 +48,10 @@
         token = chip * home_rows + lax.broadcasted_iota(jnp.int32, (home_rows, lanes), 0)
         hidden[2 * cache_here :, :] = jnp.where(token == row_ids[...], 0.0, MASKED)
 
-    for piece, side in ((own_q, side_here), (other_q, 1 - side_here)):
-        q_rows[side] = piece[...]
+    for k, piece in enumerate(query_refs):
+        side = side_here if k < near else 1 - side_here
+        spot = lax.rem(ring_here, near) ^ (k % near)
+        q_rows[side, pl.ds(pl.multiple_of(spot * home_rows, home_rows), home_rows), :] = piece[...]
 
     factor = LOG2E / math.sqrt(HD)
     spots = [(r, s, k) for r in range(rings) for s in range(2) for k in range(groups)]
@@ -95,12 +99,12 @@
         out[owner, groups * HD :, :] = jnp.concatenate(filled, axis=0).astype(BF16)
 
 
-def attention(place, own_q, other_q, keys, values, new_key, new_value, lens, row_ids, chips, kv_heads):
-    side_rows = own_q.shape[0]
+def attention(place, query_blocks, keys, values, new_key, new_value, lens, row_ids, chips, kv_heads):
     home_rows = new_key.shape[0]
+    side_rows = home_rows * len(query_blocks) // 2
     cache_here = keys[0].shape[0]
     rings = chips // 2 // kv_heads
-    columns = own_q.shape[1] // kv_heads
+    columns = query_blocks[0][0].shape[1] // kv_heads
     ring_heads = columns // HD // rings
     wide = 2 * side_rows * columns // HD
     height = ring_heads * side_rows + STATS
@@ -115,7 +119,10 @@
         grid_spec=pltpu.PrefetchScalarGridSpec(
             num_scalar_prefetch=1,
             grid=(kv_heads,),
-            in_specs=[pl.BlockSpec((side_rows, columns), kv)] * 2
+            in_specs=[
+                pl.BlockSpec((home_rows, columns), functools.partial(lambda n, g, place: (n, g), n))
+                for _, n in query_blocks
+            ]
             + [pl.BlockSpec((cache_here, HD), kv)] * 2
             + [pl.BlockSpec((HD, cache_here), lambda g, place: (g, 0))] * 2
             + [pl.BlockSpec((home_rows, HD), kv)] * 2
@@ -137,8 +144,7 @@
         name="attention",
     )(
         place,
-        own_q,
-        other_q,
+        *[block for block, _ in query_blocks],
         pltpu.with_memory_space_constraint(keys[0], pltpu.HBM),
         keys[1],
         *values,
@@ -152,28 +158,29 @@
 def project_body(side_rows, place, *refs):
     *chunks, same_own, same_other, across_own, across_other, out, turned = refs
     core, side = place[3], place[4]
+    chips, height, _ = chunks[0].shape
+    base = height - STATS
+    groups = base // HD
     pack = HD // side_rows
-    for chunk, parts in enumerate(chunks):
-        chips, height, _ = parts.shape
-        base = height - STATS
-        groups = base // HD
-        owner_heads = groups * pack // 2
-        stats = parts[:, base:, :].astype(F32)
-        peaks = stats[:, :groups]
-        share = jnp.exp2(peaks - jnp.max(peaks, axis=0, keepdims=True))
-        totals = stats[:, groups : 2 * groups] + stats[:, 2 * groups : 3 * groups]
-        denom = jnp.sum(share * totals, axis=0)
+    heads_here = groups * pack // 4
+    half = chips // 2 // 2
+    for near in range(2):
+        sources = [chunks[s // 2 // half ^ near].at[s] for s in range(chips)]
+        stats = [part[base:, :].astype(F32) for part in sources]
+        peaks = [stat[:groups] for stat in stats]
+        top = functools.reduce(jnp.maximum, peaks)
+        share = [jnp.exp2(peak - top) for peak in peaks]
+        denom = sum(w * (t[groups : 2 * groups] + t[2 * groups : 3 * groups]) for w, t in zip(share, stats))
         for k in range(groups):
-            numer = None
-            for s in range(chips):
-                term = parts[s, k * HD : (k + 1) * HD, :].astype(F32) * share[s, k : k + 1, :]
-                numer = term if numer is None else numer + term
+            numer = sum(
+                part[k * HD : (k + 1) * HD, :].astype(F32) * w[k : k + 1, :] for part, w in zip(sources, share)
+            )
             attended = (numer / denom[k : k + 1, :]).T.astype(BF16)
             for j in range(pack):
-                owner, h = divmod(k * pack + j, owner_heads)
-                turned[owner, chunk, :, h * HD : (h + 1) * HD] = attended[
-                    j * side_rows : (j + 1) * side_rows
-                ]
+                owner, h = divmod(k * pack + j, heads_here)
+                turned[owner // CORES, owner % CORES, near * side_rows : (near + 1) * side_rows, h * HD : (h + 1) * HD] = (
+                    attended[j * side_rows : (j + 1) * side_rows]
+                )
     product = nn_dot(turned[side, core], same_own[...]) + nn_dot(turned[side, 1 - core], same_other[...])
     product = product + nn_dot(turned[1 - side, core], across_own[...])
     product = product + nn_dot(turned[1 - side, 1 - core], across_other[...])
@@ -182,16 +189,17 @@
 
 def project(place, chunks, weights, side_rows):
     depth, width = weights[0].shape
+    rows = 2 * side_rows
     vmem = pl.BlockSpec(memory_space=pltpu.VMEM)
     return pl.pallas_call(
         functools.partial(project_body, side_rows),
         in_specs=[pl.BlockSpec(memory_space=pltpu.SMEM)] + [vmem] * (len(chunks) + len(weights)),
         out_specs=vmem,
-        out_shape=jax.ShapeDtypeStruct((side_rows, width), BF16),
-        scratch_shapes=[pltpu.VMEM((2, CORES, side_rows, depth), BF16)],
+        out_shape=jax.ShapeDtypeStruct((rows, width), BF16),
+        scratch_shapes=[pltpu.VMEM((2, CORES, rows, depth), BF16)],
         compiler_params=pltpu.CompilerParams(vmem_limit_bytes=32 * MIB),
         cost_estimate=pl.CostEstimate(
-            flops=8 * side_rows * width * depth, bytes_accessed=6 * MIB, transcendentals=0
+            flops=8 * rows * width * depth, bytes_accessed=6 * MIB, transcendentals=0
         ),
         name="project",
     )(place, *chunks, *weights)
@@ -347,35 +355,36 @@
         for c in range(CORES)
     ]
     rings = chips // 2
-    side_rows = rings * home_rows
-
-    by_owner = queries.reshape(home_rows, chips, CORES, heads_here * HD)
-    query_chunks = []
-    for chunk in range(CORES):
-        part = by_owner[:, :, chunk].reshape(1, home_rows, chips * heads_here * HD)
-        if chunk:
-            part, _ = lax.optimization_barrier((part, query_chunks[0][0]))
-        mine = lax.all_to_all(
-            jnp.broadcast_to(part, (rings, *part.shape[1:])),
-            "ctx",
-            split_axis=0,
-            concat_axis=0,
-            axis_index_groups=along,
-            tiled=True,
-        ).reshape(side_rows, part.shape[2])
-        query_chunks.append((mine, lax.ppermute(mine, "ctx", across)))
+    half = rings // 2
+    side_rows = half * home_rows
+
+    def across_y(block):
+        return lax.ppermute(block, "ctx", across)
+
+    neighbour = across_y(queries)
+    by_ring = [queries] + [
+        lax.ppermute(queries, "ctx", [(i, i ^ (2 * CORES * k)) for i in range(devices)])
+        for k in range(1, rings)
+    ]
+    near_blocks = [(block, 0) for block in by_ring[:half]]
+    near_blocks += [(neighbour, 0)] + [(across_y(block), 0) for block in by_ring[1:half]]
+    far = jnp.concatenate(by_ring[half:], axis=0)
+    far_across = across_y(far)
+    far_blocks = [(far, k) for k in range(half)] + [(far_across, k) for k in range(half)]
     key_other = lax.ppermute(key_cache, "ctx", swap)
     value_turned = value_cache.T
     value_other = lax.ppermute(value_turned, "ctx", swap)
     weight_swapped = lax.ppermute(out_weight, "ctx", swap)
 
-    place = jnp.stack([chip, index * cache_here, (index ^ 1) * cache_here, core, chip % 2]).astype(jnp.int32)
+    place = jnp.stack([chip, index * cache_here, (index ^ 1) * cache_here, core, chip % 2, chip // 2]).astype(jnp.int32)
 
     def in_lanes(by_row):
-        sides = by_row.reshape(rings, 2, CORES, home_rows)
-        sides = lax.dynamic_index_in_dim(sides, core, axis=2, keepdims=False)
-        sides = jnp.swapaxes(sides, 0, 1).reshape(2, 1, side_rows)
-        return jnp.tile(sides, (1, HD // side_rows, 1)).reshape(1, 2 * HD)
+        sides = by_row.reshape(2, half, 2, CORES, home_rows)
+        sides = lax.dynamic_index_in_dim(sides, core, axis=3, keepdims=False)
+        sides = jnp.swapaxes(sides, 1, 2).reshape(2, 2, 1, side_rows)
+        lanes = jnp.tile(sides, (1, 1, HD // side_rows, 1)).reshape(2, 1, 2 * HD)
+        here = chip // CORES // half
+        return [lax.dynamic_index_in_dim(lanes, here ^ n, axis=0, keepdims=False) for n in range(2)]
 
     lens = in_lanes(cache_len)
     numbers = jnp.arange(chips * home_rows, dtype=jnp.int32).reshape(chips, 1, home_rows)
@@ -394,33 +403,30 @@
     fine = (spread - coarse.astype(F32)).astype(BF16)
 
     gathered = []
-    for chunk, (own_q, other_q) in enumerate(query_chunks):
+    for chunk, blocks in enumerate((near_blocks, far_blocks)):
         sums = attention(
             place,
-            own_q,
-            other_q,
+            blocks,
             (key_cache, key_other),
             (value_turned, value_other),
             new_key,
             new_value,
-            lens,
-            row_ids,
+            lens[chunk],
+            row_ids[chunk],
             chips,
             key_cache.shape[1] // HD,
         )
-        if chunk + 1 < len(query_chunks):
-            own_next, other_next = query_chunks[chunk + 1]
-            sums, other_next = lax.optimization_barrier((sums, other_next))
-            query_chunks[chunk + 1] = (own_next, other_next)
         if chunk:
             sums, gathered[-1] = lax.optimization_barrier((sums, gathered[-1]))
+        else:
+            sums, place, late_weight = lax.optimization_barrier((sums, place, out_weight))
         gathered.append(
             lax.all_to_all(
                 sums, "ctx", split_axis=0, concat_axis=0, axis_index_groups=same_core, tiled=True
             )
         )
-    late_weight, _ = lax.optimization_barrier((out_weight, query_chunks[-1][1]))
     weight_across = lax.ppermute(late_weight, "ctx", across)
+    weight_across, _ = lax.optimization_barrier((weight_across, sums))
     weights = (out_weight, weight_swapped, weight_across, lax.ppermute(weight_across, "ctx", swap))
     share = project(place, gathered, weights, side_rows)
     shares = lax.all_to_all(

time: 164 us -> 158 us (0.963)
  waiting for transfers between devices: 71.5 us -> 65.4 us
  local copies, waits for them, and re-layouts: 7.8 us -> 5.87 us
    ppermute x2 -> x6, waiting for transfers between devices: 0.01 us -> 27.3 us  [the longest x3 27.3 us: across_y(): return lax.ppermute(block, 'ctx', across)]
    ppermute x1, waiting for transfers between devices: 20.4 us -> 0.01 us  [on_device(): weight_across = lax.ppermute(late_weight, 'ctx', across)]
    all_to_all x2 -> x0, waiting for transfers between devices: 13 us -> none  [on_device(): lax.all_to_all(jnp.broadcast_to(part, (rings, *part.shape[1:])), 'ctx', s...]
    ppermute x2 -> x6, starting transfers between devices: 3.1 us -> 14.7 us  [the longest x3 8.8 us: on_device(): lax.ppermute(queries, 'ctx', [(i, i ^ 2 * CORES * k) for i in range(devic...]
    all_to_all x2 -> x0, starting transfers between devices: 9.85 us -> none  [on_device(): lax.all_to_all(jnp.broadcast_to(part, (rings, *part.shape[1:])), 'ctx', s...]
    unnamed x22 -> x24, local copies, waits for them, and re-layouts: 3.1 us -> 4.02 us
  transfers between devices with their start and end apart: 13 -> 15, of which waited for: 6 -> 4; matrix products, arithmetic and copies ran while one was open for 4% -> 2% of each run, Pallas kernels for 12% -> 13%
where the time goes in v8:
time: 158 us; the launch traced here: 157 us
  waiting for transfers between devices  65.4 us (41%)
  starting transfers between devices  33.5 us (21%)
  Pallas kernels  33.3 us (21%)
  blocking collectives  18 us (11%)
  local copies, waits for them, and re-layouts  5.87 us (4%)
    ppermute x3, waiting for transfers between devices, across_y(): return lax.ppermute(block, 'ctx', across)  27.3 us
    pallas_call x2, Pallas kernels, attention(): pl.pallas_call(functools.partial(attention_body, shape), grid_spec=pltpu....  20.5 us
    all_to_all x1, blocking collectives, on_device(): lax.all_to_all(outgoing.reshape(devices, experts * MOST, width), 'ctx', s...  18 us
    all_to_all x2, waiting for transfers between devices, on_device(): lax.all_to_all(sums, 'ctx', split_axis=0, concat_axis=0, axis_index_group...  15.7 us
    all_to_all x1, waiting for transfers between devices, on_device(): lax.all_to_all(produced.reshape(devices, experts * MOST, width), 'ctx', s...  14.3 us
    all_to_all x2, starting transfers between devices, on_device(): lax.all_to_all(sums, 'ctx', split_axis=0, concat_axis=0, axis_index_group...  9.32 us
    ppermute x3, starting transfers between devices, on_device(): lax.ppermute(queries, 'ctx', [(i, i ^ 2 * CORES * k) for i in range(devic...  8.8 us
    all_to_all x1, waiting for transfers between devices, on_device(): lax.all_to_all(share.reshape(rings, home_rows, width), 'ctx', split_axis=...  8.15 us
  transfers between devices with their start and end apart: 15, of which 4 were waited for; matrix products, arithmetic and copies ran while one was open for 2% of the time, Pallas kernels for 13%

profile of v8, /device:TPU:0, one launch (start us, length us, event | category | flops | bytes accessed | tf_op | source)
XLA Modules:
  0.0 156.8 jit_solution(15633073383807995273)
XLA Ops:
  0.0 1.5 copy.25
  1.5 0.0 copy-start
  1.5 0.5 collective-permute-start.4
  2.0 0.1 collective-permute-start.3
  2.1 3.0 %collective-permute-start = (bf16[16,4096]{1,0:T(8,128)(2,1)}, bf16[16,4096]{1,0:T(8,128)(2,1)S(1)}, u32[]{:S(2)}, u32[]{:S(2)}) collective-permute-start(bf16[16,4096]{1,0:T(8,128)(2,1)} %refs_0_.1), channel_id=1, source_target_pairs={{0,4},{1,5},{2,6},{3,7},{4,0},{5,1},{6,2},{7,3},{8,12},{9,13},{10,... | collective-permute-start | bytes 393224 | tf_op jit(solution)/shard_map/ppermute | solution.py:366
  5.1 1.5 collective-permute-start.1
  6.6 2.6 %collective-permute-start.5 = (bf16[16,4096]{1,0:T(8,128)(2,1)}, bf16[16,4096]{1,0:T(8,128)(2,1)S(1)}, u32[]{:S(2)}, u32[]{:S(2)}) collective-permute-start(bf16[16,4096]{1,0:T(8,128)(2,1)} %refs_0_.1), channel_id=1, source_target_pairs={{0,8},{1,9},{2,10},{3,11},{4,12},{5,13},{6,14},{7,15},{8,0},{9,1},... | collective-permute-start | bytes 393224 | tf_op jit(solution)/shard_map/ppermute | solution.py:366
  9.2 0.8 reshape.76
  10.0 0.1 iota.91
  10.1 0.1 iota.92
  10.2 0.1 iota.80
  10.2 2.3 %collective-permute-start.2 = (bf16[16,4096]{1,0:T(8,128)(2,1)S(1)}, bf16[16,4096]{1,0:T(8,128)(2,1)S(1)}, u32[]{:S(2)}, u32[]{:S(2)}) collective-permute-start(bf16[16,4096]{1,0:T(8,128)(2,1)S(1)} %collective-permute-done.refs_1_), channel_id=1, source_target_pairs={{0,2},{1,3},{2,0},{3,1},{4,6},{5,7},{6,4},{7,5},{8,10},{9,11},{10,... | collective-permute-start | bytes 393224 | tf_op jit(solution)/shard_map/ppermute | solution.py:362
  12.6 0.1 tile.22
  12.7 0.1 tile.24
  12.8 0.1 tile.26
  12.9 0.1 stack.27.place
  13.0 3.2 %collective-permute-start.6 = (bf16[16,4096]{1,0:T(8,128)(2,1)}, bf16[16,4096]{1,0:T(8,128)(2,1)S(1)}, u32[]{:S(2)}, u32[]{:S(2)}) collective-permute-start(bf16[16,4096]{1,0:T(8,128)(2,1)} %refs_0_.1), channel_id=1, source_target_pairs={{0,12},{1,13},{2,14},{3,15},{4,8},{5,9},{6,10},{7,11},{8,4},{9,5},... | collective-permute-start | bytes 393224 | tf_op jit(solution)/shard_map/ppermute | solution.py:366
  16.2 0.9 copy-done.2
  17.1 0.7 copy-done.3
  17.9 0.7 copy-done.5
  18.6 10.2 %attention.2 = bf16[8,272,128]{2,1,0:T(8,128)(2,1)} custom-call(s32[6]{0:T(128)S(1)} %stack.27.place, bf16[16,4096]{1,0:T(8,128)(2,1)S(1)} %copy-done.2, bf16[16,4096]{1,0:T(8,128)(2,1)S(1)} %collective-permute-done.refs_1_, bf16[16,4096]{1,0:T(8,128)(2,1)S(1)} %collective-permute-done.1.refs_2_, bf16[16,4096]{1,0:T(8,128)(2,1)S(1)} %collective-permute-done.2.refs_3_, ...), custom_call_target="tpu_custom_call" | custom-call | flops 3221225472 | bytes 8388608 | tf_op jit(solution)/shard_map/attention/pallas_call | solution.py:117
  28.8 1.3 collective-permute-start.9
  30.1 4.4 %all-to-all-start = ((bf16[8,272,128]{2,1,0:T(8,128)(2,1)}), bf16[8,272,128]{2,1,0:T(8,128)(2,1)S(1)}, u32[]{:S(2)}, u32[]{:S(2)}) async-start(bf16[8,272,128]{2,1,0:T(8,128)(2,1)} %attention.2), calls=%async_computation | async-start | bytes 1114112 | tf_op jit(solution)/shard_map/all_to_all | solution.py:424
  34.6 2.1 %collective-permute-start.7 = (bf16[32,4096]{1,0:T(8,128)(2,1)S(1)}, bf16[32,4096]{1,0:T(8,128)(2,1)S(1)}, u32[]{:S(2)}, u32[]{:S(2)}) collective-permute-start(bf16[32,4096]{1,0:T(8,128)(2,1)S(1)} %constant_dynamic-update-slice_fusion.refs_0_.refs_1_), channel_id=1, source_target_pairs={{0,2},{1,3},{2,0},{3,1},{4,6},{5,7},{6,4},{7,5},{8,10},{9,11},{10,... | collective-permute-start | bytes 786440 | tf_op jit(solution)/shard_map/ppermute | solution.py:362
  36.7 0.1 tile.27
  36.7 0.1 tile.28
  36.8 27.3 %collective-permute-done.7.refs_2_.refs_3_ = bf16[32,4096]{1,0:T(8,128)(2,1)S(1)} collective-permute-done((bf16[32,4096]{1,0:T(8,128)(2,1)S(1)}, bf16[32,4096]{1,0:T(8,128)(2,1)S(1)}, u32[]{:S(2)}, u32[]{:S(2)}) %collective-permute-start.7) | collective-permute-done | bytes 262176 | tf_op jit(solution)/shard_map/ppermute | solution.py:362
  64.2 10.2 %attention.3 = bf16[8,272,128]{2,1,0:T(8,128)(2,1)} custom-call(s32[6]{0:T(128)S(1)} %stack.27.place, bf16[32,4096]{1,0:T(8,128)(2,1)S(1)} %constant_dynamic-update-slice_fusion.refs_0_.refs_1_, bf16[32,4096]{1,0:T(8,128)(2,1)S(1)} %constant_dynamic-update-slice_fusion.refs_0_.refs_1_, bf16[32,4096]{1,0:T(8,128)(2,1)S(1)} %collective-permute-done.7.refs_2_.refs_3_, ...), custom_call_target="tpu_custom_call" | custom-call | flops 3221225472 | bytes 8388608 | tf_op jit(solution)/shard_map/attention/pallas_call | solution.py:117
  74.4 0.1 collective-permute-start.10
  74.5 4.9 %all-to-all-start.1 = ((bf16[8,272,128]{2,1,0:T(8,128)(2,1)}), bf16[8,272,128]{2,1,0:T(8,128)(2,1)S(1)}, u32[]{:S(2)}, u32[]{:S(2)}) async-start(bf16[8,272,128]{2,1,0:T(8,128)(2,1)} %attention.3), calls=%async_computation.1 | async-start | bytes 1114112 | tf_op jit(solution)/shard_map/all_to_all | solution.py:424
  79.4 0.1 copy.27
  79.5 0.1 eq.31
  79.6 15.7 %all-to-all-done.1.refs_1_ = bf16[8,272,128]{2,1,0:T(8,128)(2,1)S(1)} async-done(((bf16[8,272,128]{2,1,0:T(8,128)(2,1)}), bf16[8,272,128]{2,1,0:T(8,128)(2,1)S(1)}, u32[]{:S(2)}, u32[]{:S(2)}) %all-to-all-start.1) | async-done | bytes 557088 | tf_op jit(solution)/shard_map/all_to_all | solution.py:424
  95.2 3.7 %project.1 = bf16[64,2048]{1,0:T(8,128)(2,1)} custom-call(s32[6]{0:T(128)S(1)} %stack.27.place, bf16[8,272,128]{2,1,0:T(8,128)(2,1)S(1)} %all-to-all-done.refs_0_, bf16[8,272,128]{2,1,0:T(8,128)(2,1)S(1)} %all-to-all-done.1.refs_1_, bf16[256,2048]{1,0:T(8,128)(2,1)S(1)} %copy-done, bf16[256,2048]{1,0:T(8,128)(2,1)} %collective-permute-done.8.refs_3_, ...), custom_call_target="tpu_custom_call" | custom-call | flops 268435456 | bytes 6291456 | tf_op jit(solution)/shard_map/project/pallas_call | solution.py:194
  98.9 3.4 %all-to-all-start.2 = ((bf16[4,16,2048]{2,1,0:T(8,128)(2,1)}), bf16[4,16,2048]{2,1,0:T(8,128)(2,1)S(1)}, u32[]{:S(2)}, u32[]{:S(2)}) async-start(bf16[4,16,2048]{2,1,0:T(8,128)(2,1)} %bitcast.11), calls=%async_computation.2 | async-start | bytes 524288 | tf_op jit(solution)/shard_map/all_to_all | solution.py:432
  102.3 0.2 convert_reduce_fusion
  102.5 0.1 reduce_sum.21
  102.6 0.1 fusion
  102.7 0.1 copy.29
  102.9 8.2 %all-to-all-done.2.parts = bf16[4,16,2048]{2,1,0:T(8,128)(2,1)S(1)} async-done(((bf16[4,16,2048]{2,1,0:T(8,128)(2,1)}), bf16[4,16,2048]{2,1,0:T(8,128)(2,1)S(1)}, u32[]{:S(2)}, u32[]{:S(2)}) %all-to-all-start.2) | async-done | bytes 262176 | tf_op jit(solution)/shard_map/all_to_all | solution.py:432
  111.0 0.4 norm_and_dispatch.1
  111.5 18.0 %all_to_all.25 = bf16[16,8,2048]{2,1,0:T(8,128)(2,1)S(1)} all-to-all(bf16[16,8,2048]{2,1,0:T(8,128)(2,1)S(1)} %bitcast.33), channel_id=1, replica_groups=mesh['groups'=2,'ctx'=16] {'ctx'}, dimensions={0} | all-to-all | bytes 1048576 | tf_op jit(solution)/shard_map/all_to_all | solution.py:441
  129.4 7.9 %experts.1 = bf16[128,2048]{1,0:T(8,128)(2,1)} custom-call(bf16[128,2048]{1,0:T(8,128)(2,1)S(1)} %bitcast.28, bf16[2,2048,768]{2,1,0:T(8,128)(2,1)} %w_gate.1, bf16[2,2048,768]{2,1,0:T(8,128)(2,1)} %w_up.1, bf16[2,768,2048]{2,1,0:T(8,128)(2,1)} %w_down.1), custom_call_target="tpu_custom_call" | custom-call | flops 2415919104 | bytes 18874368 | tf_op jit(solution)/shard_map/experts/pallas_call | solution.py:285
  137.3 4.1 %all-to-all-start.4 = ((bf16[16,8,2048]{2,1,0:T(8,128)(2,1)}), bf16[16,8,2048]{2,1,0:T(8,128)(2,1)S(1)}, u32[]{:S(2)}, u32[]{:S(2)}) async-start(bf16[16,8,2048]{2,1,0:T(8,128)(2,1)} %bitcast.15), calls=%async_computation.4 | async-start | bytes 1048576 | tf_op jit(solution)/shard_map/all_to_all | solution.py:445
  141.4 0.1 copy.30
  141.5 0.1 select_reduce_fusion
  141.6 14.3 %all-to-all-done.4 = bf16[16,8,2048]{2,1,0:T(8,128)(2,1)S(1)} async-done(((bf16[16,8,2048]{2,1,0:T(8,128)(2,1)}), bf16[16,8,2048]{2,1,0:T(8,128)(2,1)S(1)}, u32[]{:S(2)}, u32[]{:S(2)}) %all-to-all-start.4) | async-done | bytes 524320 | tf_op jit(solution)/shard_map/all_to_all | solution.py:445
  155.9 0.9 mix.1
  (43 shorter events, 0.2 us)
Async XLA Ops:
  1.5 27.3 %copy-start = (bf16[256,2048]{1,0:T(8,128)(2,1)S(1)}, bf16[256,2048]{1,0:T(8,128)(2,1)}, u32[]{:S(2)}) copy-start(bf16[256,2048]{1,0:T(8,128)(2,1)} %refs_2_.1) | copy-start | bytes 3145732
  1.5 14.7 %collective-permute-start.4 = (bf16[512,1024]{1,0:T(8,128)(2,1)S(1)}, bf16[512,1024]{1,0:T(8,128)(2,1)}, u32[]{:S(2)}, u32[]{:S(2)}) collective-permute-start(bf16[512,1024]{1,0:T(8,128)(2,1)S(1)} %bitcast.30), channel_id=1, source_target_pairs={{0,1},{1,0},{2,3},{3,2},{4,5},{5,4},{6,7},{7,6},{8,9},{9,8},{10,11... | collective-permute-start | bytes 3145736 | tf_op jit(solution)/shard_map/ppermute | solution.py:376
  2.0 14.2 %collective-permute-start.3 = (bf16[1024,512]{1,0:T(8,128)(2,1)}, bf16[1024,512]{1,0:T(8,128)(2,1)}, u32[]{:S(2)}, u32[]{:S(2)}) collective-permute-start(bf16[1024,512]{1,0:T(8,128)(2,1)} %refs_4_.3), channel_id=1, source_target_pairs={{0,1},{1,0},{2,3},{3,2},{4,5},{5,4},{6,7},{7,6},{8,9},{9,8},{10,11... | collective-permute-start | bytes 3145736 | tf_op jit(solution)/shard_map/ppermute | solution.py:374
  2.1 8.1 %collective-permute-start = (bf16[16,4096]{1,0:T(8,128)(2,1)}, bf16[16,4096]{1,0:T(8,128)(2,1)S(1)}, u32[]{:S(2)}, u32[]{:S(2)}) collective-permute-start(bf16[16,4096]{1,0:T(8,128)(2,1)} %refs_0_.1), channel_id=1, source_target_pairs={{0,4},{1,5},{2,6},{3,7},{4,0},{5,1},{6,2},{7,3},{8,12},{9,13},{10,... | collective-permute-start | bytes 393224 | tf_op jit(solution)/shard_map/ppermute | solution.py:366
  5.1 7.9 %collective-permute-start.1 = (bf16[16,4096]{1,0:T(8,128)(2,1)}, bf16[16,4096]{1,0:T(8,128)(2,1)S(1)}, u32[]{:S(2)}, u32[]{:S(2)}) collective-permute-start(bf16[16,4096]{1,0:T(8,128)(2,1)} %refs_0_.1), channel_id=1, source_target_pairs={{0,2},{1,3},{2,0},{3,1},{4,6},{5,7},{6,4},{7,5},{8,10},{9,11},{10,... | collective-permute-start | bytes 393224 | tf_op jit(solution)/shard_map/ppermute | solution.py:362
  6.6 23.5 %collective-permute-start.5 = (bf16[16,4096]{1,0:T(8,128)(2,1)}, bf16[16,4096]{1,0:T(8,128)(2,1)S(1)}, u32[]{:S(2)}, u32[]{:S(2)}) collective-permute-start(bf16[16,4096]{1,0:T(8,128)(2,1)} %refs_0_.1), channel_id=1, source_target_pairs={{0,8},{1,9},{2,10},{3,11},{4,12},{5,13},{6,14},{7,15},{8,0},{9,1},... | collective-permute-start | bytes 393224 | tf_op jit(solution)/shard_map/ppermute | solution.py:366
  10.2 6.0 %collective-permute-start.2 = (bf16[16,4096]{1,0:T(8,128)(2,1)S(1)}, bf16[16,4096]{1,0:T(8,128)(2,1)S(1)}, u32[]{:S(2)}, u32[]{:S(2)}) collective-permute-start(bf16[16,4096]{1,0:T(8,128)(2,1)S(1)} %collective-permute-done.refs_1_), channel_id=1, source_target_pairs={{0,2},{1,3},{2,0},{3,1},{4,6},{5,7},{6,4},{7,5},{8,10},{9,11},{10,... | collective-permute-start | bytes 393224 | tf_op jit(solution)/shard_map/ppermute | solution.py:362
  13.0 21.6 %collective-permute-start.6 = (bf16[16,4096]{1,0:T(8,128)(2,1)}, bf16[16,4096]{1,0:T(8,128)(2,1)S(1)}, u32[]{:S(2)}, u32[]{:S(2)}) collective-permute-start(bf16[16,4096]{1,0:T(8,128)(2,1)} %refs_0_.1), channel_id=1, source_target_pairs={{0,12},{1,13},{2,14},{3,15},{4,8},{5,9},{6,10},{7,11},{8,4},{9,5},... | collective-permute-start | bytes 393224 | tf_op jit(solution)/shard_map/ppermute | solution.py:366
  16.2 0.9 copy-start.2
  17.1 0.7 copy-start.3
  17.9 0.7 copy-start.5
  18.6 45.6 %copy-start.4 = (bf16[16,512]{1,0:T(8,128)(2,1)S(1)}, bf16[16,512]{1,0:T(8,128)(2,1)}, u32[]{:S(2)}) copy-start(bf16[16,512]{1,0:T(8,128)(2,1)} %refs_8_.3) | copy-start | bytes 49156
  18.6 45.6 %copy-start.6 = (bf16[16,512]{1,0:T(8,128)(2,1)S(1)}, bf16[16,512]{1,0:T(8,128)(2,1)}, u32[]{:S(2)}) copy-start(bf16[16,512]{1,0:T(8,128)(2,1)} %refs_9_.3) | copy-start | bytes 49156
  28.8 45.6 %collective-permute-start.9 = (bf16[256,2048]{1,0:T(8,128)(2,1)S(1)}, bf16[256,2048]{1,0:T(8,128)(2,1)}, u32[]{:S(2)}, u32[]{:S(2)}) collective-permute-start(bf16[256,2048]{1,0:T(8,128)(2,1)S(1)} %copy-done), channel_id=1, source_target_pairs={{0,2},{1,3},{2,0},{3,1},{4,6},{5,7},{6,4},{7,5},{8,10},{9,11},{10,... | collective-permute-start | bytes 3145736 | tf_op jit(solution)/shard_map/ppermute | solution.py:428
  30.1 44.3 %all-to-all-start = ((bf16[8,272,128]{2,1,0:T(8,128)(2,1)}), bf16[8,272,128]{2,1,0:T(8,128)(2,1)S(1)}, u32[]{:S(2)}, u32[]{:S(2)}) async-start(bf16[8,272,128]{2,1,0:T(8,128)(2,1)} %attention.2), calls=%async_computation | async-start | bytes 1114112 | tf_op jit(solution)/shard_map/all_to_all | solution.py:424
  34.6 29.6 %collective-permute-start.7 = (bf16[32,4096]{1,0:T(8,128)(2,1)S(1)}, bf16[32,4096]{1,0:T(8,128)(2,1)S(1)}, u32[]{:S(2)}, u32[]{:S(2)}) collective-permute-start(bf16[32,4096]{1,0:T(8,128)(2,1)S(1)} %constant_dynamic-update-slice_fusion.refs_0_.refs_1_), channel_id=1, source_target_pairs={{0,2},{1,3},{2,0},{3,1},{4,6},{5,7},{6,4},{7,5},{8,10},{9,11},{10,... | collective-permute-start | bytes 786440 | tf_op jit(solution)/shard_map/ppermute | solution.py:362
  36.7 42.9 %collective-permute-start.8 = (bf16[256,2048]{1,0:T(8,128)(2,1)S(1)}, bf16[256,2048]{1,0:T(8,128)(2,1)}, u32[]{:S(2)}, u32[]{:S(2)}) collective-permute-start(bf16[256,2048]{1,0:T(8,128)(2,1)S(1)} %copy-done), channel_id=1, source_target_pairs={{0,1},{1,0},{2,3},{3,2},{4,5},{5,4},{6,7},{7,6},{8,9},{9,8},{10,11... | collective-permute-start | bytes 3145736 | tf_op jit(solution)/shard_map/ppermute | solution.py:377
  64.1 15.2 %copy-start.7 = (s32[16,8]{0,1:T(8,128)S(1)}, s32[16,8]{0,1:T(8,128)}, u32[]{:S(2)}) copy-start(s32[16,8]{0,1:T(8,128)} %param.23) | copy-start | bytes 1540
  74.4 28.5 %copy-start.8 = (bf16[2048]{0:T(1024)(128)(2,1)S(1)}, bf16[2048]{0:T(1024)(128)(2,1)}, u32[]{:S(2)}) copy-start(bf16[2048]{0:T(1024)(128)(2,1)} %param.22) | copy-start | bytes 12292
  74.4 36.7 %copy-start.1 = (bf16[16,2048]{1,0:T(8,128)(2,1)S(1)}, bf16[16,2048]{1,0:T(8,128)(2,1)}, u32[]{:S(2)}) copy-start(bf16[16,2048]{1,0:T(8,128)(2,1)} %residual.1) | copy-start | bytes 196612
  74.4 20.8 %collective-permute-start.10 = (bf16[256,2048]{1,0:T(8,128)(2,1)}, bf16[256,2048]{1,0:T(8,128)(2,1)}, u32[]{:S(2)}, u32[]{:S(2)}) collective-permute-start(bf16[256,2048]{1,0:T(8,128)(2,1)} %collective-permute-done.9.refs_4_), channel_id=1, source_target_pairs={{0,1},{1,0},{2,3},{3,2},{4,5},{5,4},{6,7},{7,6},{8,9},{9,8},{10,11... | collective-permute-start | bytes 3145736 | tf_op jit(solution)/shard_map/ppermute | solution.py:430
  74.5 20.7 %all-to-all-start.1 = ((bf16[8,272,128]{2,1,0:T(8,128)(2,1)}), bf16[8,272,128]{2,1,0:T(8,128)(2,1)S(1)}, u32[]{:S(2)}, u32[]{:S(2)}) async-start(bf16[8,272,128]{2,1,0:T(8,128)(2,1)} %attention.3), calls=%async_computation.1 | async-start | bytes 1114112 | tf_op jit(solution)/shard_map/all_to_all | solution.py:424
  98.9 12.1 %all-to-all-start.2 = ((bf16[4,16,2048]{2,1,0:T(8,128)(2,1)}), bf16[4,16,2048]{2,1,0:T(8,128)(2,1)S(1)}, u32[]{:S(2)}, u32[]{:S(2)}) async-start(bf16[4,16,2048]{2,1,0:T(8,128)(2,1)} %bitcast.11), calls=%async_computation.2 | async-start | bytes 524288 | tf_op jit(solution)/shard_map/all_to_all | solution.py:432
  129.4 12.0 %copy-start.9 = (f32[16,8]{0,1:T(8,128)S(1)}, f32[16,8]{0,1:T(8,128)}, u32[]{:S(2)}) copy-start(f32[16,8]{0,1:T(8,128)} %param.24) | copy-start | bytes 1540
  137.3 18.6 %all-to-all-start.4 = ((bf16[16,8,2048]{2,1,0:T(8,128)(2,1)}), bf16[16,8,2048]{2,1,0:T(8,128)(2,1)S(1)}, u32[]{:S(2)}, u32[]{:S(2)}) async-start(bf16[16,8,2048]{2,1,0:T(8,128)(2,1)} %bitcast.15), calls=%async_computation.4 | async-start | bytes 1048576 | tf_op jit(solution)/shard_map/all_to_all | solution.py:445

commit v9 on v8

--- a/solution.py
+++ b/solution.py
@@ -148,8 +148,8 @@
         pltpu.with_memory_space_constraint(keys[0], pltpu.HBM),
         keys[1],
         *values,
-        new_key,
-        new_value,
+        pltpu.with_memory_space_constraint(new_key, pltpu.HBM),
+        pltpu.with_memory_space_constraint(new_value, pltpu.HBM),
         lens,
         row_ids,
     )
@@ -366,29 +366,34 @@
         lax.ppermute(queries, "ctx", [(i, i ^ (2 * CORES * k)) for i in range(devices)])
         for k in range(1, rings)
     ]
-    near_blocks = [(block, 0) for block in by_ring[:half]]
+    near_blocks = [(pltpu.with_memory_space_constraint(queries, pltpu.HBM), 0)]
+    near_blocks += [(block, 0) for block in by_ring[1:half]]
     near_blocks += [(neighbour, 0)] + [(across_y(block), 0) for block in by_ring[1:half]]
     far = jnp.concatenate(by_ring[half:], axis=0)
     far_across = across_y(far)
     far_blocks = [(far, k) for k in range(half)] + [(far_across, k) for k in range(half)]
-    key_other = lax.ppermute(key_cache, "ctx", swap)
-    value_turned = value_cache.T
+    late_keys, late_values, _ = lax.optimization_barrier((key_cache, value_cache, neighbour))
+    key_other = lax.ppermute(late_keys, "ctx", swap)
+    value_turned = late_values.T
     value_other = lax.ppermute(value_turned, "ctx", swap)
     weight_swapped = lax.ppermute(out_weight, "ctx", swap)
 
     place = jnp.stack([chip, index * cache_here, (index ^ 1) * cache_here, core, chip % 2, chip // 2]).astype(jnp.int32)
 
-    def in_lanes(by_row):
-        sides = by_row.reshape(2, half, 2, CORES, home_rows)
-        sides = lax.dynamic_index_in_dim(sides, core, axis=3, keepdims=False)
-        sides = jnp.swapaxes(sides, 1, 2).reshape(2, 2, 1, side_rows)
-        lanes = jnp.tile(sides, (1, 1, HD // side_rows, 1)).reshape(2, 1, 2 * HD)
-        here = chip // CORES // half
-        return [lax.dynamic_index_in_dim(lanes, here ^ n, axis=0, keepdims=False) for n in range(2)]
-
-    lens = in_lanes(cache_len)
-    numbers = jnp.arange(chips * home_rows, dtype=jnp.int32).reshape(chips, 1, home_rows)
-    row_ids = in_lanes(jnp.broadcast_to(numbers, (chips, CORES, home_rows)))
+    def in_lanes(by_chip, n):
+        here = lax.dynamic_slice_in_dim(by_chip, (chip // CORES // half ^ n) * chips // 2, chips // 2, 0)
+        sides = [
+            jnp.concatenate([here[2 * ring + side : 2 * ring + side + 1] for ring in range(half)], axis=1)
+            for side in range(2)
+        ]
+        return jnp.concatenate([lanes for lanes in sides for _ in range(HD // side_rows)], axis=1)
+
+    len_by_chip = lax.dynamic_slice_in_dim(
+        cache_len.reshape(chips, CORES * home_rows), core * home_rows, home_rows, 1
+    )
+    number_by_chip = jnp.arange(chips * home_rows, dtype=jnp.int32).reshape(chips, home_rows)
+    lens = [in_lanes(len_by_chip, n) for n in range(2)]
+    row_ids = [in_lanes(number_by_chip, n) for n in range(2)]
 
     flat_ids = expert_ids.reshape(-1)
     picks = jnp.arange(flat_ids.shape[0])
@@ -419,7 +424,7 @@
         if chunk:
             sums, gathered[-1] = lax.optimization_barrier((sums, gathered[-1]))
         else:
-            sums, place, late_weight = lax.optimization_barrier((sums, place, out_weight))
+            sums, place, late_weight, _ = lax.optimization_barrier((sums, place, out_weight, far_across))
         gathered.append(
             lax.all_to_all(
                 sums, "ctx", split_axis=0, concat_axis=0, axis_index_groups=same_core, tiled=True

time: 158 us -> 141 us (0.89)
  waiting for transfers between devices: 65.4 us -> 55.2 us
  starting transfers between devices: 33.5 us -> 30.2 us
  local copies, waits for them, and re-layouts: 5.87 us -> 3.34 us
    ppermute x3, waiting for transfers between devices: 27.3 us -> 0.01 us  [across_y(): return lax.ppermute(block, 'ctx', across)]
    all_to_all x2, waiting for transfers between devices: 15.7 us -> 27.7 us  [on_device(): lax.all_to_all(sums, 'ctx', split_axis=0, concat_axis=0, axis_index_group...]
    ppermute x3, waiting for transfers between devices: 0.01 us -> 4.95 us  [on_device(): lax.ppermute(queries, 'ctx', [(i, i ^ 2 * CORES * k) for i in range(devic...]
    unnamed x24 -> x13, local copies, waits for them, and re-layouts: 4.02 us -> 0.18 us
    ppermute x3, starting transfers between devices: 8.8 us -> 5.83 us  [on_device(): lax.ppermute(queries, 'ctx', [(i, i ^ 2 * CORES * k) for i in range(devic...]
    ppermute x3, starting transfers between devices: 5.89 us -> 3.87 us  [across_y(): return lax.ppermute(block, 'ctx', across)]
    all_to_all x2, starting transfers between devices: 9.32 us -> 11.2 us  [on_device(): lax.all_to_all(sums, 'ctx', split_axis=0, concat_axis=0, axis_index_group...]
  transfers between devices with their start and end apart: 15 -> 15, of which waited for: 4 -> 5; matrix products, arithmetic and copies ran while one was open for 2% -> 3% of each run, Pallas kernels for 13% -> 15%
where the time goes in v9:
time: 141 us
  waiting for transfers between devices  55.2 us (39%)
  Pallas kernels  33.4 us (24%)
  starting transfers between devices  30.2 us (21%)
  blocking collectives  18 us (13%)
  local copies, waits for them, and re-layouts  3.34 us (2%)
    all_to_all x2, waiting for transfers between devices, on_device(): lax.all_to_all(sums, 'ctx', split_axis=0, concat_axis=0, axis_index_group...  27.7 us
    pallas_call x2, Pallas kernels, attention(): pl.pallas_call(functools.partial(attention_body, shape), grid_spec=pltpu....  20.5 us
    all_to_all x1, blocking collectives, on_device(): lax.all_to_all(outgoing.reshape(devices, experts * MOST, width), 'ctx', s...  18 us
    all_to_all x1, waiting for transfers between devices, on_device(): lax.all_to_all(produced.reshape(devices, experts * MOST, width), 'ctx', s...  14.3 us
    all_to_all x2, starting transfers between devices, on_device(): lax.all_to_all(sums, 'ctx', split_axis=0, concat_axis=0, axis_index_group...  11.2 us
    all_to_all x1, waiting for transfers between devices, on_device(): lax.all_to_all(share.reshape(rings, home_rows, width), 'ctx', split_axis=...  8.19 us
    pallas_call x1, Pallas kernels, run_experts(): pl.pallas_call(functools.partial(experts_body, step), in_specs=[vmem] + [...  7.87 us
    ppermute x3, starting transfers between devices, on_device(): lax.ppermute(queries, 'ctx', [(i, i ^ 2 * CORES * k) for i in range(devic...  5.83 us
  transfers between devices with their start and end apart: 15, of which 5 were waited for; matrix products, arithmetic and copies ran while one was open for 3% of the time, Pallas kernels for 15%

profile of v9, /device:TPU:0, one launch (start us, length us, event | category | flops | bytes accessed | tf_op | source)
XLA Modules:
  0.0 140.7 jit_solution(947368766780939853)
XLA Ops:
  0.0 3.0 %collective-permute-start = (bf16[16,4096]{1,0:T(8,128)(2,1)}, bf16[16,4096]{1,0:T(8,128)(2,1)S(1)}, u32[]{:S(2)}, u32[]{:S(2)}) collective-permute-start(bf16[16,4096]{1,0:T(8,128)(2,1)} %refs_0_.1), channel_id=1, source_target_pairs={{0,4},{1,5},{2,6},{3,7},{4,0},{5,1},{6,2},{7,3},{8,12},{9,13},{10,... | collective-permute-start | bytes 393224 | tf_op jit(solution)/shard_map/ppermute | solution.py:366
  3.0 1.5 %collective-permute-start.1 = (bf16[16,4096]{1,0:T(8,128)(2,1)}, bf16[16,4096]{1,0:T(8,128)(2,1)S(1)}, u32[]{:S(2)}, u32[]{:S(2)}) collective-permute-start(bf16[16,4096]{1,0:T(8,128)(2,1)} %refs_0_.1), channel_id=1, source_target_pairs={{0,2},{1,3},{2,0},{3,1},{4,6},{5,7},{6,4},{7,5},{8,10},{9,11},{10,... | collective-permute-start | bytes 393224 | tf_op jit(solution)/shard_map/ppermute | solution.py:362
  4.5 2.6 %collective-permute-start.5 = (bf16[16,4096]{1,0:T(8,128)(2,1)}, bf16[16,4096]{1,0:T(8,128)(2,1)S(1)}, u32[]{:S(2)}, u32[]{:S(2)}) collective-permute-start(bf16[16,4096]{1,0:T(8,128)(2,1)} %refs_0_.1), channel_id=1, source_target_pairs={{0,8},{1,9},{2,10},{3,11},{4,12},{5,13},{6,14},{7,15},{8,0},{9,1},... | collective-permute-start | bytes 393224 | tf_op jit(solution)/shard_map/ppermute | solution.py:366
  7.1 0.2 collective-permute-start.6
  7.4 0.8 reshape.42
  8.1 0.1 fusion.2
  8.2 0.1 concatenate.27.refs_10_
  8.4 0.1 collective-permute-start.3
  8.4 1.5 %copy.23 = bf16[1024,512]{0,1:T(8,128)(2,1)S(1)} copy(bf16[1024,512]{1,0:T(8,128)(2,1)} %param.18) | data formatting | bytes 2097152 | tf_op jit(solution)/shard_map/optimization_barrier | solution.py:375
  9.9 0.0 copy-start
  9.9 0.6 collective-permute-start.4
  10.5 0.1 concatenate.28.refs_11_
  10.6 0.1 stack.27.place
  10.7 0.0 collective-permute-done.refs_1_
  10.7 1.3 collective-permute-start.2
  12.0 4.9 %collective-permute-done.5 = bf16[16,4096]{1,0:T(8,128)(2,1)S(1)} collective-permute-done((bf16[16,4096]{1,0:T(8,128)(2,1)}, bf16[16,4096]{1,0:T(8,128)(2,1)S(1)}, u32[]{:S(2)}, u32[]{:S(2)}) %collective-permute-start.5) | collective-permute-done | bytes 131104 | tf_op jit(solution)/shard_map/ppermute | solution.py:366
  17.0 0.0 collective-permute-done.6
  17.0 1.0 collective-permute-start.7
  18.0 0.0 collective-permute-done.2.refs_3_
  18.0 0.0 collective-permute-done.3.refs_5_
  18.0 0.0 collective-permute-done.4.refs_7_
  18.0 10.2 %attention.2 = bf16[8,272,128]{2,1,0:T(8,128)(2,1)} custom-call(s32[6]{0:T(128)S(1)} %stack.27.place, bf16[16,4096]{1,0:T(8,128)(2,1)} %refs_0_.1, bf16[16,4096]{1,0:T(8,128)(2,1)S(1)} %collective-permute-done.refs_1_, bf16[16,4096]{1,0:T(8,128)(2,1)S(1)} %collective-permute-done.1.refs_2_, bf16[16,4096]{1,0:T(8,128)(2,1)S(1)} %collective-permute-done.2.refs_3_, ...), custom_call_target="tpu_custom_call" | custom-call | flops 3221225472 | bytes 8388608 | tf_op jit(solution)/shard_map/attention/pallas_call | solution.py:117
  28.3 1.2 collective-permute-start.9
  29.5 4.6 %all-to-all-start = ((bf16[8,272,128]{2,1,0:T(8,128)(2,1)}), bf16[8,272,128]{2,1,0:T(8,128)(2,1)S(1)}, u32[]{:S(2)}, u32[]{:S(2)}) async-start(bf16[8,272,128]{2,1,0:T(8,128)(2,1)} %attention.2), calls=%async_computation | async-start | bytes 1114112 | tf_op jit(solution)/shard_map/all_to_all | solution.py:429
  34.1 0.1 concatenate.30.refs_10_
  34.2 0.1 concatenate.31.refs_11_
  34.3 0.0 copy-start.2
  34.3 10.3 %attention.3 = bf16[8,272,128]{2,1,0:T(8,128)(2,1)} custom-call(s32[6]{0:T(128)S(1)} %stack.27.place, bf16[32,4096]{1,0:T(8,128)(2,1)S(1)} %constant_dynamic-update-slice_fusion.refs_0_.refs_1_, bf16[32,4096]{1,0:T(8,128)(2,1)S(1)} %constant_dynamic-update-slice_fusion.refs_0_.refs_1_, bf16[32,4096]{1,0:T(8,128)(2,1)S(1)} %collective-permute-done.7.refs_2_.refs_3_, ...), custom_call_target="tpu_custom_call" | custom-call | flops 3221225472 | bytes 8388608 | tf_op jit(solution)/shard_map/attention/pallas_call | solution.py:117
  44.6 12.1 %all-to-all-done.refs_0_ = bf16[8,272,128]{2,1,0:T(8,128)(2,1)S(1)} async-done(((bf16[8,272,128]{2,1,0:T(8,128)(2,1)}), bf16[8,272,128]{2,1,0:T(8,128)(2,1)S(1)}, u32[]{:S(2)}, u32[]{:S(2)}) %all-to-all-start) | async-done | bytes 557088 | tf_op jit(solution)/shard_map/all_to_all | solution.py:429
  56.7 6.6 %all-to-all-start.1 = ((bf16[8,272,128]{2,1,0:T(8,128)(2,1)}), bf16[8,272,128]{2,1,0:T(8,128)(2,1)S(1)}, u32[]{:S(2)}, u32[]{:S(2)}) async-start(bf16[8,272,128]{2,1,0:T(8,128)(2,1)} %attention.3), calls=%async_computation.1 | async-start | bytes 1114112 | tf_op jit(solution)/shard_map/all_to_all | solution.py:429
  63.3 0.1 copy.24
  63.4 0.1 eq.31
  63.5 15.7 %all-to-all-done.1.refs_1_ = bf16[8,272,128]{2,1,0:T(8,128)(2,1)S(1)} async-done(((bf16[8,272,128]{2,1,0:T(8,128)(2,1)}), bf16[8,272,128]{2,1,0:T(8,128)(2,1)S(1)}, u32[]{:S(2)}, u32[]{:S(2)}) %all-to-all-start.1) | async-done | bytes 557088 | tf_op jit(solution)/shard_map/all_to_all | solution.py:429
  79.1 3.7 %project.1 = bf16[64,2048]{1,0:T(8,128)(2,1)} custom-call(s32[6]{0:T(128)S(1)} %stack.27.place, bf16[8,272,128]{2,1,0:T(8,128)(2,1)S(1)} %all-to-all-done.refs_0_, bf16[8,272,128]{2,1,0:T(8,128)(2,1)S(1)} %all-to-all-done.1.refs_1_, bf16[256,2048]{1,0:T(8,128)(2,1)S(1)} %copy-done, bf16[256,2048]{1,0:T(8,128)(2,1)} %collective-permute-done.8.refs_3_, ...), custom_call_target="tpu_custom_call" | custom-call | flops 268435456 | bytes 6291456 | tf_op jit(solution)/shard_map/project/pallas_call | solution.py:194
  82.8 3.4 %all-to-all-start.2 = ((bf16[4,16,2048]{2,1,0:T(8,128)(2,1)}), bf16[4,16,2048]{2,1,0:T(8,128)(2,1)S(1)}, u32[]{:S(2)}, u32[]{:S(2)}) async-start(bf16[4,16,2048]{2,1,0:T(8,128)(2,1)} %bitcast.7), calls=%async_computation.2 | async-start | bytes 524288 | tf_op jit(solution)/shard_map/all_to_all | solution.py:437
  86.3 0.2 convert_reduce_fusion
  86.5 0.1 reduce_sum.21
  86.5 0.1 fusion
  86.7 0.1 copy.26
  86.8 8.2 %all-to-all-done.2.parts = bf16[4,16,2048]{2,1,0:T(8,128)(2,1)S(1)} async-done(((bf16[4,16,2048]{2,1,0:T(8,128)(2,1)}), bf16[4,16,2048]{2,1,0:T(8,128)(2,1)S(1)}, u32[]{:S(2)}, u32[]{:S(2)}) %all-to-all-start.2) | async-done | bytes 262176 | tf_op jit(solution)/shard_map/all_to_all | solution.py:437
  95.0 0.4 norm_and_dispatch.1
  95.4 18.0 %all_to_all.25 = bf16[16,8,2048]{2,1,0:T(8,128)(2,1)S(1)} all-to-all(bf16[16,8,2048]{2,1,0:T(8,128)(2,1)S(1)} %bitcast.18), channel_id=1, replica_groups=mesh['groups'=2,'ctx'=16] {'ctx'}, dimensions={0} | all-to-all | bytes 1048576 | tf_op jit(solution)/shard_map/all_to_all | solution.py:446
  113.4 7.9 %experts.1 = bf16[128,2048]{1,0:T(8,128)(2,1)} custom-call(bf16[128,2048]{1,0:T(8,128)(2,1)S(1)} %bitcast.13, bf16[2,2048,768]{2,1,0:T(8,128)(2,1)} %w_gate.1, bf16[2,2048,768]{2,1,0:T(8,128)(2,1)} %w_up.1, bf16[2,768,2048]{2,1,0:T(8,128)(2,1)} %w_down.1), custom_call_target="tpu_custom_call" | custom-call | flops 2415919104 | bytes 18874368 | tf_op jit(solution)/shard_map/experts/pallas_call | solution.py:285
  121.2 4.1 %all-to-all-start.4 = ((bf16[16,8,2048]{2,1,0:T(8,128)(2,1)}), bf16[16,8,2048]{2,1,0:T(8,128)(2,1)S(1)}, u32[]{:S(2)}, u32[]{:S(2)}) async-start(bf16[16,8,2048]{2,1,0:T(8,128)(2,1)} %bitcast.11), calls=%async_computation.4 | async-start | bytes 1048576 | tf_op jit(solution)/shard_map/all_to_all | solution.py:450
  125.4 0.1 copy.27
  125.4 0.1 select_reduce_fusion
  125.6 14.3 %all-to-all-done.4 = bf16[16,8,2048]{2,1,0:T(8,128)(2,1)S(1)} async-done(((bf16[16,8,2048]{2,1,0:T(8,128)(2,1)}), bf16[16,8,2048]{2,1,0:T(8,128)(2,1)S(1)}, u32[]{:S(2)}, u32[]{:S(2)}) %all-to-all-start.4) | async-done | bytes 524320 | tf_op jit(solution)/shard_map/all_to_all | solution.py:450
  139.8 0.9 mix.1
  (25 shorter events, 0.1 us)
Async XLA Ops:
  0.0 10.7 %collective-permute-start = (bf16[16,4096]{1,0:T(8,128)(2,1)}, bf16[16,4096]{1,0:T(8,128)(2,1)S(1)}, u32[]{:S(2)}, u32[]{:S(2)}) collective-permute-start(bf16[16,4096]{1,0:T(8,128)(2,1)} %refs_0_.1), channel_id=1, source_target_pairs={{0,4},{1,5},{2,6},{3,7},{4,0},{5,1},{6,2},{7,3},{8,12},{9,13},{10,... | collective-permute-start | bytes 393224 | tf_op jit(solution)/shard_map/ppermute | solution.py:366
  3.0 5.3 %collective-permute-start.1 = (bf16[16,4096]{1,0:T(8,128)(2,1)}, bf16[16,4096]{1,0:T(8,128)(2,1)S(1)}, u32[]{:S(2)}, u32[]{:S(2)}) collective-permute-start(bf16[16,4096]{1,0:T(8,128)(2,1)} %refs_0_.1), channel_id=1, source_target_pairs={{0,2},{1,3},{2,0},{3,1},{4,6},{5,7},{6,4},{7,5},{8,10},{9,11},{10,... | collective-permute-start | bytes 393224 | tf_op jit(solution)/shard_map/ppermute | solution.py:362
  4.5 12.4 %collective-permute-start.5 = (bf16[16,4096]{1,0:T(8,128)(2,1)}, bf16[16,4096]{1,0:T(8,128)(2,1)S(1)}, u32[]{:S(2)}, u32[]{:S(2)}) collective-permute-start(bf16[16,4096]{1,0:T(8,128)(2,1)} %refs_0_.1), channel_id=1, source_target_pairs={{0,8},{1,9},{2,10},{3,11},{4,12},{5,13},{6,14},{7,15},{8,0},{9,1},... | collective-permute-start | bytes 393224 | tf_op jit(solution)/shard_map/ppermute | solution.py:366
  7.1 9.9 %collective-permute-start.6 = (bf16[16,4096]{1,0:T(8,128)(2,1)}, bf16[16,4096]{1,0:T(8,128)(2,1)S(1)}, u32[]{:S(2)}, u32[]{:S(2)}) collective-permute-start(bf16[16,4096]{1,0:T(8,128)(2,1)} %refs_0_.1), channel_id=1, source_target_pairs={{0,12},{1,13},{2,14},{3,15},{4,8},{5,9},{6,10},{7,11},{8,4},{9,5},... | collective-permute-start | bytes 393224 | tf_op jit(solution)/shard_map/ppermute | solution.py:366
  8.4 9.7 %collective-permute-start.3 = (bf16[1024,512]{1,0:T(8,128)(2,1)}, bf16[1024,512]{1,0:T(8,128)(2,1)}, u32[]{:S(2)}, u32[]{:S(2)}) collective-permute-start(bf16[1024,512]{1,0:T(8,128)(2,1)} %refs_4_.3), channel_id=1, source_target_pairs={{0,1},{1,0},{2,3},{3,2},{4,5},{5,4},{6,7},{7,6},{8,9},{9,8},{10,11... | collective-permute-start | bytes 3145736 | tf_op jit(solution)/shard_map/ppermute | solution.py:376
  9.9 18.4 %copy-start = (bf16[256,2048]{1,0:T(8,128)(2,1)S(1)}, bf16[256,2048]{1,0:T(8,128)(2,1)}, u32[]{:S(2)}) copy-start(bf16[256,2048]{1,0:T(8,128)(2,1)} %refs_2_.1) | copy-start | bytes 3145732
  9.9 8.1 %collective-permute-start.4 = (bf16[512,1024]{1,0:T(8,128)(2,1)S(1)}, bf16[512,1024]{1,0:T(8,128)(2,1)}, u32[]{:S(2)}, u32[]{:S(2)}) collective-permute-start(bf16[512,1024]{1,0:T(8,128)(2,1)S(1)} %bitcast.15), channel_id=1, source_target_pairs={{0,1},{1,0},{2,3},{3,2},{4,5},{5,4},{6,7},{7,6},{8,9},{9,8},{10,11... | collective-permute-start | bytes 3145736 | tf_op jit(solution)/shard_map/ppermute | solution.py:378
  10.7 7.3 %collective-permute-start.2 = (bf16[16,4096]{1,0:T(8,128)(2,1)S(1)}, bf16[16,4096]{1,0:T(8,128)(2,1)S(1)}, u32[]{:S(2)}, u32[]{:S(2)}) collective-permute-start(bf16[16,4096]{1,0:T(8,128)(2,1)S(1)} %collective-permute-done.refs_1_), channel_id=1, source_target_pairs={{0,2},{1,3},{2,0},{3,1},{4,6},{5,7},{6,4},{7,5},{8,10},{9,11},{10,... | collective-permute-start | bytes 393224 | tf_op jit(solution)/shard_map/ppermute | solution.py:362
  17.0 11.3 %collective-permute-start.7 = (bf16[32,4096]{1,0:T(8,128)(2,1)S(1)}, bf16[32,4096]{1,0:T(8,128)(2,1)S(1)}, u32[]{:S(2)}, u32[]{:S(2)}) collective-permute-start(bf16[32,4096]{1,0:T(8,128)(2,1)S(1)} %constant_dynamic-update-slice_fusion.refs_0_.refs_1_), channel_id=1, source_target_pairs={{0,2},{1,3},{2,0},{3,1},{4,6},{5,7},{6,4},{7,5},{8,10},{9,11},{10,... | collective-permute-start | bytes 786440 | tf_op jit(solution)/shard_map/ppermute | solution.py:362
  28.3 28.4 %collective-permute-start.9 = (bf16[256,2048]{1,0:T(8,128)(2,1)S(1)}, bf16[256,2048]{1,0:T(8,128)(2,1)}, u32[]{:S(2)}, u32[]{:S(2)}) collective-permute-start(bf16[256,2048]{1,0:T(8,128)(2,1)S(1)} %copy-done), channel_id=1, source_target_pairs={{0,2},{1,3},{2,0},{3,1},{4,6},{5,7},{6,4},{7,5},{8,10},{9,11},{10,... | collective-permute-start | bytes 3145736 | tf_op jit(solution)/shard_map/ppermute | solution.py:433
  29.5 27.2 %all-to-all-start = ((bf16[8,272,128]{2,1,0:T(8,128)(2,1)}), bf16[8,272,128]{2,1,0:T(8,128)(2,1)S(1)}, u32[]{:S(2)}, u32[]{:S(2)}) async-start(bf16[8,272,128]{2,1,0:T(8,128)(2,1)} %attention.2), calls=%async_computation | async-start | bytes 1114112 | tf_op jit(solution)/shard_map/all_to_all | solution.py:429
  34.1 29.3 %collective-permute-start.8 = (bf16[256,2048]{1,0:T(8,128)(2,1)S(1)}, bf16[256,2048]{1,0:T(8,128)(2,1)}, u32[]{:S(2)}, u32[]{:S(2)}) collective-permute-start(bf16[256,2048]{1,0:T(8,128)(2,1)S(1)} %copy-done), channel_id=1, source_target_pairs={{0,1},{1,0},{2,3},{3,2},{4,5},{5,4},{6,7},{7,6},{8,9},{9,8},{10,11... | collective-permute-start | bytes 3145736 | tf_op jit(solution)/shard_map/ppermute | solution.py:379
  34.3 29.0 %copy-start.2 = (s32[16,8]{0,1:T(8,128)S(1)}, s32[16,8]{0,1:T(8,128)}, u32[]{:S(2)}) copy-start(s32[16,8]{0,1:T(8,128)} %param.23) | copy-start | bytes 1540
  44.6 41.8 %copy-start.3 = (bf16[2048]{0:T(1024)(128)(2,1)S(1)}, bf16[2048]{0:T(1024)(128)(2,1)}, u32[]{:S(2)}) copy-start(bf16[2048]{0:T(1024)(128)(2,1)} %param.22) | copy-start | bytes 12292
  44.6 50.4 %copy-start.1 = (bf16[16,2048]{1,0:T(8,128)(2,1)S(1)}, bf16[16,2048]{1,0:T(8,128)(2,1)}, u32[]{:S(2)}) copy-start(bf16[16,2048]{1,0:T(8,128)(2,1)} %residual.1) | copy-start | bytes 196612
  56.7 22.4 %collective-permute-start.10 = (bf16[256,2048]{1,0:T(8,128)(2,1)}, bf16[256,2048]{1,0:T(8,128)(2,1)}, u32[]{:S(2)}, u32[]{:S(2)}) collective-permute-start(bf16[256,2048]{1,0:T(8,128)(2,1)} %collective-permute-done.9.refs_4_), channel_id=1, source_target_pairs={{0,1},{1,0},{2,3},{3,2},{4,5},{5,4},{6,7},{7,6},{8,9},{9,8},{10,11... | collective-permute-start | bytes 3145736 | tf_op jit(solution)/shard_map/ppermute | solution.py:435
  56.7 22.4 %all-to-all-start.1 = ((bf16[8,272,128]{2,1,0:T(8,128)(2,1)}), bf16[8,272,128]{2,1,0:T(8,128)(2,1)S(1)}, u32[]{:S(2)}, u32[]{:S(2)}) async-start(bf16[8,272,128]{2,1,0:T(8,128)(2,1)} %attention.3), calls=%async_computation.1 | async-start | bytes 1114112 | tf_op jit(solution)/shard_map/all_to_all | solution.py:429
  82.8 12.1 %all-to-all-start.2 = ((bf16[4,16,2048]{2,1,0:T(8,128)(2,1)}), bf16[4,16,2048]{2,1,0:T(8,128)(2,1)S(1)}, u32[]{:S(2)}, u32[]{:S(2)}) async-start(bf16[4,16,2048]{2,1,0:T(8,128)(2,1)} %bitcast.7), calls=%async_computation.2 | async-start | bytes 524288 | tf_op jit(solution)/shard_map/all_to_all | solution.py:437
  113.3 12.0 %copy-start.4 = (f32[16,8]{0,1:T(8,128)S(1)}, f32[16,8]{0,1:T(8,128)}, u32[]{:S(2)}) copy-start(f32[16,8]{0,1:T(8,128)} %param.24) | copy-start | bytes 1540
  121.2 18.6 %all-to-all-start.4 = ((bf16[16,8,2048]{2,1,0:T(8,128)(2,1)}), bf16[16,8,2048]{2,1,0:T(8,128)(2,1)S(1)}, u32[]{:S(2)}, u32[]{:S(2)}) async-start(bf16[16,8,2048]{2,1,0:T(8,128)(2,1)} %bitcast.11), calls=%async_computation.4 | async-start | bytes 1048576 | tf_op jit(solution)/shard_map/all_to_all | solution.py:450

commit v10 on v9

--- a/solution.py
+++ b/solution.py
@@ -29,13 +29,13 @@
 
 
 def attention_body(shape, place, *refs):
-    rings, ring_heads, home_rows, side_rows, cache_here, step = shape
+    owners, owner_heads, home_rows, rows, cache_here, step = shape
     *query_refs, key_own, key_other, value_own, value_other, key_fresh, value_fresh = refs[:-8]
     lens, row_ids, out, q_rows, q_turned, hidden, scores, probs = refs[-8:]
     chip, start_own, start_other, side_here, ring_here = place[0], place[1], place[2], place[4], place[5]
-    near = side_rows // home_rows
-    pack = HD // side_rows
-    groups = ring_heads // pack
+    near = rows // home_rows // 2
+    pack = HD // rows
+    groups = owner_heads // pack
 
     @pl.when(pl.program_id(0) == 0)
     def _():
@@ -50,25 +50,23 @@
 
     for k, piece in enumerate(query_refs):
         side = side_here if k < near else 1 - side_here
-        spot = lax.rem(ring_here, near) ^ (k % near)
-        q_rows[side, pl.ds(pl.multiple_of(spot * home_rows, home_rows), home_rows), :] = piece[...]
+        spot = 2 * (lax.rem(ring_here, near) ^ (k % near)) + side
+        q_rows[pl.ds(pl.multiple_of(spot * home_rows, home_rows), home_rows), :] = piece[...]
 
     factor = LOG2E / math.sqrt(HD)
-    spots = [(r, s, k) for r in range(rings) for s in range(2) for k in range(groups)]
-    for n, (r, s, k) in enumerate(spots):
-        first = r * ring_heads + k * pack
+    for n in range(owners * groups):
         block = jnp.concatenate(
-            [q_rows[s, :, h * HD : (h + 1) * HD] for h in range(first, first + pack)], axis=0
+            [q_rows[:, h * HD : (h + 1) * HD] for h in range(n * pack, (n + 1) * pack)], axis=0
         )
         scaled = block.T.astype(F32) * factor
         coarse = scaled.astype(BF16)
         q_turned[:HD, n * HD : (n + 1) * HD] = coarse
         q_turned[HD:, n * HD : (n + 1) * HD] = (scaled - coarse.astype(F32)).astype(BF16)
-    wide = len(spots) * HD
+    wide = owners * groups * HD
 
     def score(keys, at):
         s = nn_dot(jnp.concatenate([keys, keys], axis=1), q_turned[...])
-        return s + jnp.concatenate([hidden[at, s * HD : (s + 1) * HD] for _, s, _ in spots], axis=1)
+        return s + jnp.concatenate([hidden[at, :]] * (owners * groups), axis=1)
 
     s_new = score(key_fresh[...], slice(2 * cache_here, 2 * cache_here + home_rows))
     run = jnp.max(s_new.reshape(home_rows // 8, 8, wide), axis=0)
@@ -90,7 +88,7 @@
     denom = sums[HD : HD + 1] + jnp.sum(p_new.astype(F32), axis=0, keepdims=True)
     high = denom.astype(BF16).astype(F32)
     low = denom - high
-    for owner in range(2 * rings):
+    for owner in range(owners):
         lanes = [slice((owner * groups + k) * HD, (owner * groups + k + 1) * HD) for k in range(groups)]
         for k, cols in enumerate(lanes):
             out[owner, k * HD : (k + 1) * HD, :] = numer[:, cols].astype(BF16)
@@ -101,18 +99,18 @@
 
 def attention(place, query_blocks, keys, values, new_key, new_value, lens, row_ids, chips, kv_heads):
     home_rows = new_key.shape[0]
-    side_rows = home_rows * len(query_blocks) // 2
+    rows = home_rows * len(query_blocks)
     cache_here = keys[0].shape[0]
-    rings = chips // 2 // kv_heads
+    owners = chips // kv_heads
     columns = query_blocks[0][0].shape[1] // kv_heads
-    ring_heads = columns // HD // rings
-    wide = 2 * side_rows * columns // HD
-    height = ring_heads * side_rows + STATS
+    owner_heads = columns // HD // owners
+    wide = rows * columns // HD
+    height = owner_heads * rows + STATS
     step = 512
     positions = 2 * cache_here + home_rows
     kv = lambda g, place: (0, g)
     whole = lambda g, place: (0, 0)
-    shape = (rings, ring_heads, home_rows, side_rows, cache_here, step)
+    shape = (owners, owner_heads, home_rows, rows, cache_here, step)
     work = wide * kv_heads * 2 * cache_here
     return pl.pallas_call(
         functools.partial(attention_body, shape),
@@ -127,11 +125,11 @@
             + [pl.BlockSpec((HD, cache_here), lambda g, place: (g, 0))] * 2
             + [pl.BlockSpec((home_rows, HD), kv)] * 2
             + [pl.BlockSpec(lens.shape, whole)] * 2,
-            out_specs=pl.BlockSpec((2 * rings, height, HD), lambda g, place: (g, 0, 0)),
+            out_specs=pl.BlockSpec((owners, height, HD), lambda g, place: (g, 0, 0)),
             scratch_shapes=[
-                pltpu.VMEM((2, side_rows, columns), BF16),
+                pltpu.VMEM((rows, columns), BF16),
                 pltpu.VMEM((2 * HD, wide), BF16),
-                pltpu.VMEM((positions, 2 * HD), F32),
+                pltpu.VMEM((positions, HD), F32),
                 pltpu.VMEM((2 * cache_here, wide), F32),
                 pltpu.VMEM((2 * cache_here, wide), BF16),
             ],
@@ -155,14 +153,14 @@
     )
 
 
-def project_body(side_rows, place, *refs):
-    *chunks, same_own, same_other, across_own, across_other, out, turned = refs
-    core, side = place[3], place[4]
+def project_body(rows, place, *refs):
+    *chunks, weight_own, weight_other, out, turned = refs
+    core = place[3]
     chips, height, _ = chunks[0].shape
     base = height - STATS
     groups = base // HD
-    pack = HD // side_rows
-    heads_here = groups * pack // 4
+    pack = HD // rows
+    heads_here = groups * pack // CORES
     half = chips // 2 // 2
     for near in range(2):
         sources = [chunks[s // 2 // half ^ near].at[s] for s in range(chips)]
@@ -177,32 +175,29 @@
             )
             attended = (numer / denom[k : k + 1, :]).T.astype(BF16)
             for j in range(pack):
-                owner, h = divmod(k * pack + j, heads_here)
-                turned[owner // CORES, owner % CORES, near * side_rows : (near + 1) * side_rows, h * HD : (h + 1) * HD] = (
-                    attended[j * side_rows : (j + 1) * side_rows]
-                )
-    product = nn_dot(turned[side, core], same_own[...]) + nn_dot(turned[side, 1 - core], same_other[...])
-    product = product + nn_dot(turned[1 - side, core], across_own[...])
-    product = product + nn_dot(turned[1 - side, 1 - core], across_other[...])
+                part, h = divmod(k * pack + j, heads_here)
+                turned[part, near * rows : (near + 1) * rows, h * HD : (h + 1) * HD] = attended[
+                    j * rows : (j + 1) * rows
+                ]
+    product = nn_dot(turned[core], weight_own[...]) + nn_dot(turned[1 - core], weight_other[...])
     out[...] = product.astype(BF16)
 
 
-def project(place, chunks, weights, side_rows):
-    depth, width = weights[0].shape
-    rows = 2 * side_rows
+def project(place, chunks, weight_own, weight_other, rows):
+    depth, width = weight_own.shape
     vmem = pl.BlockSpec(memory_space=pltpu.VMEM)
     return pl.pallas_call(
-        functools.partial(project_body, side_rows),
-        in_specs=[pl.BlockSpec(memory_space=pltpu.SMEM)] + [vmem] * (len(chunks) + len(weights)),
+        functools.partial(project_body, rows),
+        in_specs=[pl.BlockSpec(memory_space=pltpu.SMEM)] + [vmem] * (len(chunks) + 2),
         out_specs=vmem,
-        out_shape=jax.ShapeDtypeStruct((rows, width), BF16),
-        scratch_shapes=[pltpu.VMEM((2, CORES, rows, depth), BF16)],
+        out_shape=jax.ShapeDtypeStruct((2 * rows, width), BF16),
+        scratch_shapes=[pltpu.VMEM((CORES, 2 * rows, depth), BF16)],
         compiler_params=pltpu.CompilerParams(vmem_limit_bytes=32 * MIB),
         cost_estimate=pl.CostEstimate(
-            flops=8 * rows * width * depth, bytes_accessed=6 * MIB, transcendentals=0
+            flops=8 * rows * width * depth, bytes_accessed=4 * MIB, transcendentals=0
         ),
         name="project",
-    )(place, *chunks, *weights)
+    )(place, *chunks, weight_own, weight_other)
 
 
 def norm_body(parts, residual, gain, chooser, middle_out, sent):
@@ -349,14 +344,9 @@
     swap = [(i, i ^ 1) for i in range(devices)]
 
     across = [(i, i ^ CORES) for i in range(devices)]
-    along = [
-        [CORES * (2 * ring + side) + c for ring in range(chips // 2)]
-        for side in range(2)
-        for c in range(CORES)
-    ]
     rings = chips // 2
     half = rings // 2
-    side_rows = half * home_rows
+    chunk_rows = 2 * half * home_rows
 
     def across_y(block):
         return lax.ppermute(block, "ctx", across)
@@ -376,17 +366,12 @@
     key_other = lax.ppermute(late_keys, "ctx", swap)
     value_turned = late_values.T
     value_other = lax.ppermute(value_turned, "ctx", swap)
-    weight_swapped = lax.ppermute(out_weight, "ctx", swap)
-
     place = jnp.stack([chip, index * cache_here, (index ^ 1) * cache_here, core, chip % 2, chip // 2]).astype(jnp.int32)
 
     def in_lanes(by_chip, n):
-        here = lax.dynamic_slice_in_dim(by_chip, (chip // CORES // half ^ n) * chips // 2, chips // 2, 0)
-        sides = [
-            jnp.concatenate([here[2 * ring + side : 2 * ring + side + 1] for ring in range(half)], axis=1)
-            for side in range(2)
-        ]
-        return jnp.concatenate([lanes for lanes in sides for _ in range(HD // side_rows)], axis=1)
+        first = (chip // CORES // half ^ n) * chips // 2
+        here = lax.dynamic_slice_in_dim(by_chip, first, chips // 2, 0).reshape(1, chunk_rows)
+        return jnp.tile(here, (1, HD // chunk_rows))
 
     len_by_chip = lax.dynamic_slice_in_dim(
         cache_len.reshape(chips, CORES * home_rows), core * home_rows, home_rows, 1
@@ -430,16 +415,14 @@
                 sums, "ctx", split_axis=0, concat_axis=0, axis_index_groups=same_core, tiled=True
             )
         )
-    weight_across = lax.ppermute(late_weight, "ctx", across)
-    weight_across, _ = lax.optimization_barrier((weight_across, sums))
-    weights = (out_weight, weight_swapped, weight_across, lax.ppermute(weight_across, "ctx", swap))
-    share = project(place, gathered, weights, side_rows)
+    weight_other = lax.ppermute(late_weight, "ctx", swap)
+    share = project(place, gathered, out_weight, weight_other, chunk_rows)
     shares = lax.all_to_all(
-        share.reshape(rings, home_rows, width),
+        share.reshape(chips, home_rows, width),
         "ctx",
         split_axis=0,
         concat_axis=0,
-        axis_index_groups=along,
+        axis_index_groups=same_core,
         tiled=True,
     )
     middle, outgoing = norm_and_dispatch(shares, residual, norm_gain.reshape(1, width), chooser)

time: 141 us -> 132 us (0.936)
  starting transfers between devices: 30.2 us -> 25.6 us
  waiting for transfers between devices: 55.2 us -> 52.4 us
  Pallas kernels: 33.4 us -> 31.7 us
    all_to_all x2, waiting for transfers between devices: 27.7 us -> 18.2 us  [on_device(): lax.all_to_all(sums, 'ctx', split_axis=0, concat_axis=0, axis_index_group...]
    all_to_all x1, waiting for transfers between devices: 8.19 us -> 13.6 us  [on_device(): lax.all_to_all(share.reshape(chips, home_rows, width), 'ctx', split_axis=...]
    all_to_all x2, starting transfers between devices: 11.2 us -> 8.86 us  [on_device(): lax.all_to_all(sums, 'ctx', split_axis=0, concat_axis=0, axis_index_group...]
    ppermute x3, starting transfers between devices: 5.83 us -> 4.39 us  [on_device(): lax.ppermute(queries, 'ctx', [(i, i ^ 2 * CORES * k) for i in range(devic...]
  transfers between devices with their start and end apart: 15 -> 13, of which waited for: 5 -> 5; matrix products, arithmetic and copies ran while one was open for 3% -> 3% of each run, Pallas kernels for 15% -> 15%
where the time goes in v10:
time: 132 us
  waiting for transfers between devices  52.4 us (40%)
  Pallas kernels  31.7 us (24%)
  starting transfers between devices  25.6 us (19%)
  blocking collectives  18 us (14%)
  local copies, waits for them, and re-layouts  3.58 us (3%)
    pallas_call x2, Pallas kernels, attention(): pl.pallas_call(functools.partial(attention_body, shape), grid_spec=pltpu....  19.8 us
    all_to_all x2, waiting for transfers between devices, on_device(): lax.all_to_all(sums, 'ctx', split_axis=0, concat_axis=0, axis_index_group...  18.2 us
    all_to_all x1, blocking collectives, on_device(): lax.all_to_all(outgoing.reshape(devices, experts * MOST, width), 'ctx', s...  18 us
    all_to_all x1, waiting for transfers between devices, on_device(): lax.all_to_all(produced.reshape(devices, experts * MOST, width), 'ctx', s...  14.3 us
    all_to_all x1, waiting for transfers between devices, on_device(): lax.all_to_all(share.reshape(chips, home_rows, width), 'ctx', split_axis=...  13.6 us
    all_to_all x2, starting transfers between devices, on_device(): lax.all_to_all(sums, 'ctx', split_axis=0, concat_axis=0, axis_index_group...  8.86 us
    pallas_call x1, Pallas kernels, run_experts(): pl.pallas_call(functools.partial(experts_body, step), in_specs=[vmem] + [...  7.86 us
    ppermute x3, waiting for transfers between devices, on_device(): lax.ppermute(queries, 'ctx', [(i, i ^ 2 * CORES * k) for i in range(devic...  6.34 us
  transfers between devices with their start and end apart: 13, of which 5 were waited for; matrix products, arithmetic and copies ran while one was open for 3% of the time, Pallas kernels for 15%

profile of v10, /device:TPU:0, one launch (start us, length us, event | category | flops | bytes accessed | tf_op | source)
XLA Modules:
  0.0 131.9 jit_solution(2664997016458287033)
XLA Ops:
  0.0 3.0 %collective-permute-start.1 = (bf16[16,4096]{1,0:T(8,128)(2,1)}, bf16[16,4096]{1,0:T(8,128)(2,1)S(1)}, u32[]{:S(2)}, u32[]{:S(2)}) collective-permute-start(bf16[16,4096]{1,0:T(8,128)(2,1)} %refs_0_.1), channel_id=1, source_target_pairs={{0,2},{1,3},{2,0},{3,1},{4,6},{5,7},{6,4},{7,5},{8,10},{9,11},{10,... | collective-permute-start | bytes 393224 | tf_op jit(solution)/shard_map/ppermute | solution.py:352
  3.0 1.6 %collective-permute-start = (bf16[16,4096]{1,0:T(8,128)(2,1)}, bf16[16,4096]{1,0:T(8,128)(2,1)S(1)}, u32[]{:S(2)}, u32[]{:S(2)}) collective-permute-start(bf16[16,4096]{1,0:T(8,128)(2,1)} %refs_0_.1), channel_id=1, source_target_pairs={{0,4},{1,5},{2,6},{3,7},{4,0},{5,1},{6,2},{7,3},{8,12},{9,13},{10,... | collective-permute-start | bytes 393224 | tf_op jit(solution)/shard_map/ppermute | solution.py:356
  4.5 2.6 %collective-permute-start.5 = (bf16[16,4096]{1,0:T(8,128)(2,1)}, bf16[16,4096]{1,0:T(8,128)(2,1)S(1)}, u32[]{:S(2)}, u32[]{:S(2)}) collective-permute-start(bf16[16,4096]{1,0:T(8,128)(2,1)} %refs_0_.1), channel_id=1, source_target_pairs={{0,8},{1,9},{2,10},{3,11},{4,12},{5,13},{6,14},{7,15},{8,0},{9,1},... | collective-permute-start | bytes 393224 | tf_op jit(solution)/shard_map/ppermute | solution.py:356
  7.1 0.2 collective-permute-start.6
  7.4 0.8 reshape.66
  8.1 0.1 collective-permute-start.3
  8.2 1.5 %copy.23 = bf16[1024,512]{0,1:T(8,128)(2,1)S(1)} copy(bf16[1024,512]{1,0:T(8,128)(2,1)} %param.18) | data formatting | bytes 2097152 | tf_op jit(solution)/shard_map/optimization_barrier | solution.py:365
  9.7 0.6 collective-permute-start.4
  10.2 0.1 fusion.2
  10.3 0.1 tile.40
  10.4 0.1 tile.42.refs_10_
  10.5 0.1 tile.43
  10.6 0.1 tile.45.refs_11_
  10.7 0.1 stack.27.place
  10.8 0.3 collective-permute-start.2
  11.1 6.3 %collective-permute-done.5 = bf16[16,4096]{1,0:T(8,128)(2,1)S(1)} collective-permute-done((bf16[16,4096]{1,0:T(8,128)(2,1)}, bf16[16,4096]{1,0:T(8,128)(2,1)S(1)}, u32[]{:S(2)}, u32[]{:S(2)}) %collective-permute-start.5) | collective-permute-done | bytes 131104 | tf_op jit(solution)/shard_map/ppermute | solution.py:356
  17.5 0.0 copy-start
  17.5 0.6 collective-permute-start.7
  18.0 0.0 collective-permute-done.2.refs_3_
  18.0 0.0 collective-permute-done.3.refs_5_
  18.1 9.9 %attention.2 = bf16[8,272,128]{2,1,0:T(8,128)(2,1)} custom-call(s32[6]{0:T(128)S(1)} %stack.27.place, bf16[16,4096]{1,0:T(8,128)(2,1)} %refs_0_.1, bf16[16,4096]{1,0:T(8,128)(2,1)S(1)} %collective-permute-done.refs_1_, bf16[16,4096]{1,0:T(8,128)(2,1)S(1)} %collective-permute-done.1.refs_2_, bf16[16,4096]{1,0:T(8,128)(2,1)S(1)} %collective-permute-done.2.refs_3_, ...), custom_call_target="tpu_custom_call" | custom-call | flops 3221225472 | bytes 8388608 | tf_op jit(solution)/shard_map/attention/pallas_call | solution.py:115
  27.9 5.2 %all-to-all-start = ((bf16[8,272,128]{2,1,0:T(8,128)(2,1)}), bf16[8,272,128]{2,1,0:T(8,128)(2,1)S(1)}, u32[]{:S(2)}, u32[]{:S(2)}) async-start(bf16[8,272,128]{2,1,0:T(8,128)(2,1)} %attention.2), calls=%async_computation | async-start | bytes 1114112 | tf_op jit(solution)/shard_map/all_to_all | solution.py:414
  33.1 0.1 tile.46
  33.2 0.1 tile.48.refs_10_
  33.3 0.1 tile.49
  33.4 0.1 tile.51.refs_11_
  33.5 0.1 collective-permute-start.8
  33.6 9.9 %attention.3 = bf16[8,272,128]{2,1,0:T(8,128)(2,1)} custom-call(s32[6]{0:T(128)S(1)} %stack.27.place, bf16[32,4096]{1,0:T(8,128)(2,1)S(1)} %constant_dynamic-update-slice_fusion.refs_0_.refs_1_, bf16[32,4096]{1,0:T(8,128)(2,1)S(1)} %constant_dynamic-update-slice_fusion.refs_0_.refs_1_, bf16[32,4096]{1,0:T(8,128)(2,1)S(1)} %collective-permute-done.7.refs_2_.refs_3_, ...), custom_call_target="tpu_custom_call" | custom-call | flops 3221225472 | bytes 8388608 | tf_op jit(solution)/shard_map/attention/pallas_call | solution.py:115
  43.5 3.5 %all-to-all-done.refs_0_ = bf16[8,272,128]{2,1,0:T(8,128)(2,1)S(1)} async-done(((bf16[8,272,128]{2,1,0:T(8,128)(2,1)}), bf16[8,272,128]{2,1,0:T(8,128)(2,1)S(1)}, u32[]{:S(2)}, u32[]{:S(2)}) %all-to-all-start) | async-done | bytes 557088 | tf_op jit(solution)/shard_map/all_to_all | solution.py:414
  46.9 3.7 %all-to-all-start.1 = ((bf16[8,272,128]{2,1,0:T(8,128)(2,1)}), bf16[8,272,128]{2,1,0:T(8,128)(2,1)S(1)}, u32[]{:S(2)}, u32[]{:S(2)}) async-start(bf16[8,272,128]{2,1,0:T(8,128)(2,1)} %attention.3), calls=%async_computation.1 | async-start | bytes 1114112 | tf_op jit(solution)/shard_map/all_to_all | solution.py:414
  50.6 14.7 %all-to-all-done.1.refs_1_ = bf16[8,272,128]{2,1,0:T(8,128)(2,1)S(1)} async-done(((bf16[8,272,128]{2,1,0:T(8,128)(2,1)}), bf16[8,272,128]{2,1,0:T(8,128)(2,1)S(1)}, u32[]{:S(2)}, u32[]{:S(2)}) %all-to-all-start.1) | async-done | bytes 557088 | tf_op jit(solution)/shard_map/all_to_all | solution.py:414
  65.4 2.8 %project.1 = bf16[128,2048]{1,0:T(8,128)(2,1)} custom-call(s32[6]{0:T(128)S(1)} %stack.27.place, bf16[8,272,128]{2,1,0:T(8,128)(2,1)S(1)} %all-to-all-done.refs_0_, bf16[8,272,128]{2,1,0:T(8,128)(2,1)S(1)} %all-to-all-done.1.refs_1_, bf16[256,2048]{1,0:T(8,128)(2,1)S(1)} %copy-done, bf16[256,2048]{1,0:T(8,128)(2,1)} %collective-permute-done.8.refs_3_), custom_call_target="tpu_custom_call" | custom-call | flops 268435456 | bytes 4194304 | tf_op jit(solution)/shard_map/project/pallas_call | solution.py:189
  68.1 3.6 %all-to-all-start.2 = ((bf16[8,16,2048]{2,1,0:T(8,128)(2,1)}), bf16[8,16,2048]{2,1,0:T(8,128)(2,1)S(1)}, u32[]{:S(2)}, u32[]{:S(2)}) async-start(bf16[8,16,2048]{2,1,0:T(8,128)(2,1)} %bitcast.7), calls=%async_computation.2 | async-start | bytes 1048576 | tf_op jit(solution)/shard_map/all_to_all | solution.py:420
  71.8 0.1 copy.24
  71.8 0.1 eq.31
  71.9 0.2 convert_reduce_fusion
  72.1 0.1 reduce_sum.21
  72.2 0.1 fusion
  72.3 0.1 copy.26
  72.5 13.6 %all-to-all-done.2.parts = bf16[8,16,2048]{2,1,0:T(8,128)(2,1)S(1)} async-done(((bf16[8,16,2048]{2,1,0:T(8,128)(2,1)}), bf16[8,16,2048]{2,1,0:T(8,128)(2,1)S(1)}, u32[]{:S(2)}, u32[]{:S(2)}) %all-to-all-start.2) | async-done | bytes 524320 | tf_op jit(solution)/shard_map/all_to_all | solution.py:420
  86.1 0.4 norm_and_dispatch.1
  86.5 18.0 %all_to_all.25 = bf16[16,8,2048]{2,1,0:T(8,128)(2,1)S(1)} all-to-all(bf16[16,8,2048]{2,1,0:T(8,128)(2,1)S(1)} %bitcast.18), channel_id=1, replica_groups=mesh['groups'=2,'ctx'=16] {'ctx'}, dimensions={0} | all-to-all | bytes 1048576 | tf_op jit(solution)/shard_map/all_to_all | solution.py:429
  104.5 7.9 %experts.1 = bf16[128,2048]{1,0:T(8,128)(2,1)} custom-call(bf16[128,2048]{1,0:T(8,128)(2,1)S(1)} %bitcast.13, bf16[2,2048,768]{2,1,0:T(8,128)(2,1)} %w_gate.1, bf16[2,2048,768]{2,1,0:T(8,128)(2,1)} %w_up.1, bf16[2,768,2048]{2,1,0:T(8,128)(2,1)} %w_down.1), custom_call_target="tpu_custom_call" | custom-call | flops 2415919104 | bytes 18874368 | tf_op jit(solution)/shard_map/experts/pallas_call | solution.py:280
  112.4 4.1 %all-to-all-start.4 = ((bf16[16,8,2048]{2,1,0:T(8,128)(2,1)}), bf16[16,8,2048]{2,1,0:T(8,128)(2,1)S(1)}, u32[]{:S(2)}, u32[]{:S(2)}) async-start(bf16[16,8,2048]{2,1,0:T(8,128)(2,1)} %bitcast.11), calls=%async_computation.4 | async-start | bytes 1048576 | tf_op jit(solution)/shard_map/all_to_all | solution.py:433
  116.5 0.1 copy.27
  116.6 0.1 select_reduce_fusion
  116.7 14.3 %all-to-all-done.4 = bf16[16,8,2048]{2,1,0:T(8,128)(2,1)S(1)} async-done(((bf16[16,8,2048]{2,1,0:T(8,128)(2,1)}), bf16[16,8,2048]{2,1,0:T(8,128)(2,1)S(1)}, u32[]{:S(2)}, u32[]{:S(2)}) %all-to-all-start.4) | async-done | bytes 524320 | tf_op jit(solution)/shard_map/all_to_all | solution.py:433
  131.0 0.9 mix.1
  (27 shorter events, 0.1 us)
Async XLA Ops:
  0.0 8.1 %collective-permute-start.1 = (bf16[16,4096]{1,0:T(8,128)(2,1)}, bf16[16,4096]{1,0:T(8,128)(2,1)S(1)}, u32[]{:S(2)}, u32[]{:S(2)}) collective-permute-start(bf16[16,4096]{1,0:T(8,128)(2,1)} %refs_0_.1), channel_id=1, source_target_pairs={{0,2},{1,3},{2,0},{3,1},{4,6},{5,7},{6,4},{7,5},{8,10},{9,11},{10,... | collective-permute-start | bytes 393224 | tf_op jit(solution)/shard_map/ppermute | solution.py:352
  3.0 7.8 %collective-permute-start = (bf16[16,4096]{1,0:T(8,128)(2,1)}, bf16[16,4096]{1,0:T(8,128)(2,1)S(1)}, u32[]{:S(2)}, u32[]{:S(2)}) collective-permute-start(bf16[16,4096]{1,0:T(8,128)(2,1)} %refs_0_.1), channel_id=1, source_target_pairs={{0,4},{1,5},{2,6},{3,7},{4,0},{5,1},{6,2},{7,3},{8,12},{9,13},{10,... | collective-permute-start | bytes 393224 | tf_op jit(solution)/shard_map/ppermute | solution.py:356
  4.5 12.9 %collective-permute-start.5 = (bf16[16,4096]{1,0:T(8,128)(2,1)}, bf16[16,4096]{1,0:T(8,128)(2,1)S(1)}, u32[]{:S(2)}, u32[]{:S(2)}) collective-permute-start(bf16[16,4096]{1,0:T(8,128)(2,1)} %refs_0_.1), channel_id=1, source_target_pairs={{0,8},{1,9},{2,10},{3,11},{4,12},{5,13},{6,14},{7,15},{8,0},{9,1},... | collective-permute-start | bytes 393224 | tf_op jit(solution)/shard_map/ppermute | solution.py:356
  7.1 10.3 %collective-permute-start.6 = (bf16[16,4096]{1,0:T(8,128)(2,1)}, bf16[16,4096]{1,0:T(8,128)(2,1)S(1)}, u32[]{:S(2)}, u32[]{:S(2)}) collective-permute-start(bf16[16,4096]{1,0:T(8,128)(2,1)} %refs_0_.1), channel_id=1, source_target_pairs={{0,12},{1,13},{2,14},{3,15},{4,8},{5,9},{6,10},{7,11},{8,4},{9,5},... | collective-permute-start | bytes 393224 | tf_op jit(solution)/shard_map/ppermute | solution.py:356
  8.1 9.9 %collective-permute-start.3 = (bf16[1024,512]{1,0:T(8,128)(2,1)}, bf16[1024,512]{1,0:T(8,128)(2,1)}, u32[]{:S(2)}, u32[]{:S(2)}) collective-permute-start(bf16[1024,512]{1,0:T(8,128)(2,1)} %refs_4_.3), channel_id=1, source_target_pairs={{0,1},{1,0},{2,3},{3,2},{4,5},{5,4},{6,7},{7,6},{8,9},{9,8},{10,11... | collective-permute-start | bytes 3145736 | tf_op jit(solution)/shard_map/ppermute | solution.py:366
  9.7 8.4 %collective-permute-start.4 = (bf16[512,1024]{1,0:T(8,128)(2,1)S(1)}, bf16[512,1024]{1,0:T(8,128)(2,1)}, u32[]{:S(2)}, u32[]{:S(2)}) collective-permute-start(bf16[512,1024]{1,0:T(8,128)(2,1)S(1)} %bitcast.15), channel_id=1, source_target_pairs={{0,1},{1,0},{2,3},{3,2},{4,5},{5,4},{6,7},{7,6},{8,9},{9,8},{10,11... | collective-permute-start | bytes 3145736 | tf_op jit(solution)/shard_map/ppermute | solution.py:368
  10.8 7.3 %collective-permute-start.2 = (bf16[16,4096]{1,0:T(8,128)(2,1)S(1)}, bf16[16,4096]{1,0:T(8,128)(2,1)S(1)}, u32[]{:S(2)}, u32[]{:S(2)}) collective-permute-start(bf16[16,4096]{1,0:T(8,128)(2,1)S(1)} %collective-permute-done.refs_1_), channel_id=1, source_target_pairs={{0,2},{1,3},{2,0},{3,1},{4,6},{5,7},{6,4},{7,5},{8,10},{9,11},{10,... | collective-permute-start | bytes 393224 | tf_op jit(solution)/shard_map/ppermute | solution.py:352
  17.5 16.0 %copy-start = (bf16[256,2048]{1,0:T(8,128)(2,1)S(1)}, bf16[256,2048]{1,0:T(8,128)(2,1)}, u32[]{:S(2)}) copy-start(bf16[256,2048]{1,0:T(8,128)(2,1)} %refs_2_.1) | copy-start | bytes 3145732
  17.5 10.5 %collective-permute-start.7 = (bf16[32,4096]{1,0:T(8,128)(2,1)S(1)}, bf16[32,4096]{1,0:T(8,128)(2,1)S(1)}, u32[]{:S(2)}, u32[]{:S(2)}) collective-permute-start(bf16[32,4096]{1,0:T(8,128)(2,1)S(1)} %constant_dynamic-update-slice_fusion.refs_0_.refs_1_), channel_id=1, source_target_pairs={{0,2},{1,3},{2,0},{3,1},{4,6},{5,7},{6,4},{7,5},{8,10},{9,11},{10,... | collective-permute-start | bytes 786440 | tf_op jit(solution)/shard_map/ppermute | solution.py:352
  27.9 19.0 %all-to-all-start = ((bf16[8,272,128]{2,1,0:T(8,128)(2,1)}), bf16[8,272,128]{2,1,0:T(8,128)(2,1)S(1)}, u32[]{:S(2)}, u32[]{:S(2)}) async-start(bf16[8,272,128]{2,1,0:T(8,128)(2,1)} %attention.2), calls=%async_computation | async-start | bytes 1114112 | tf_op jit(solution)/shard_map/all_to_all | solution.py:414
  33.5 38.3 %copy-start.2 = (bf16[2048]{0:T(1024)(128)(2,1)S(1)}, bf16[2048]{0:T(1024)(128)(2,1)}, u32[]{:S(2)}) copy-start(bf16[2048]{0:T(1024)(128)(2,1)} %param.22) | copy-start | bytes 12292
  33.5 38.3 %copy-start.3 = (s32[16,8]{0,1:T(8,128)S(1)}, s32[16,8]{0,1:T(8,128)}, u32[]{:S(2)}) copy-start(s32[16,8]{0,1:T(8,128)} %param.23) | copy-start | bytes 1540
  33.5 52.6 %copy-start.1 = (bf16[16,2048]{1,0:T(8,128)(2,1)S(1)}, bf16[16,2048]{1,0:T(8,128)(2,1)}, u32[]{:S(2)}) copy-start(bf16[16,2048]{1,0:T(8,128)(2,1)} %residual.1) | copy-start | bytes 196612
  33.5 17.1 %collective-permute-start.8 = (bf16[256,2048]{1,0:T(8,128)(2,1)S(1)}, bf16[256,2048]{1,0:T(8,128)(2,1)}, u32[]{:S(2)}, u32[]{:S(2)}) collective-permute-start(bf16[256,2048]{1,0:T(8,128)(2,1)S(1)} %copy-done), channel_id=1, source_target_pairs={{0,1},{1,0},{2,3},{3,2},{4,5},{5,4},{6,7},{7,6},{8,9},{9,8},{10,11... | collective-permute-start | bytes 3145736 | tf_op jit(solution)/shard_map/ppermute | solution.py:418
  46.9 18.4 %all-to-all-start.1 = ((bf16[8,272,128]{2,1,0:T(8,128)(2,1)}), bf16[8,272,128]{2,1,0:T(8,128)(2,1)S(1)}, u32[]{:S(2)}, u32[]{:S(2)}) async-start(bf16[8,272,128]{2,1,0:T(8,128)(2,1)} %attention.3), calls=%async_computation.1 | async-start | bytes 1114112 | tf_op jit(solution)/shard_map/all_to_all | solution.py:414
  68.1 18.0 %all-to-all-start.2 = ((bf16[8,16,2048]{2,1,0:T(8,128)(2,1)}), bf16[8,16,2048]{2,1,0:T(8,128)(2,1)S(1)}, u32[]{:S(2)}, u32[]{:S(2)}) async-start(bf16[8,16,2048]{2,1,0:T(8,128)(2,1)} %bitcast.7), calls=%async_computation.2 | async-start | bytes 1048576 | tf_op jit(solution)/shard_map/all_to_all | solution.py:420
  104.5 12.0 %copy-start.4 = (f32[16,8]{0,1:T(8,128)S(1)}, f32[16,8]{0,1:T(8,128)}, u32[]{:S(2)}) copy-start(f32[16,8]{0,1:T(8,128)} %param.24) | copy-start | bytes 1540
  112.4 18.6 %all-to-all-start.4 = ((bf16[16,8,2048]{2,1,0:T(8,128)(2,1)}), bf16[16,8,2048]{2,1,0:T(8,128)(2,1)S(1)}, u32[]{:S(2)}, u32[]{:S(2)}) async-start(bf16[16,8,2048]{2,1,0:T(8,128)(2,1)} %bitcast.11), calls=%async_computation.4 | async-start | bytes 1048576 | tf_op jit(solution)/shard_map/all_to_all | solution.py:433

commit v11 on v10

--- a/solution.py
+++ b/solution.py
@@ -28,10 +28,11 @@
     return lax.dot_general(a, b, (((1,), (0,)), ((), ())), preferred_element_type=F32)
 
 
-def attention_body(shape, place, *refs):
+def attention_body(shape, chips, place, *refs):
     owners, owner_heads, home_rows, rows, cache_here, step = shape
-    *query_refs, key_own, key_other, value_own, value_other, key_fresh, value_fresh = refs[:-8]
-    lens, row_ids, out, q_rows, q_turned, hidden, scores, probs = refs[-8:]
+    q_rows, q_turned, hidden, scores, probs, held = refs[-6:]
+    outs = refs[-6 - chips : -6]
+    *query_refs, key_own, key_other, value_own, value_other, key_fresh, value_fresh, lens, row_ids = refs[: -6 - chips]
     chip, start_own, start_other, side_here, ring_here = place[0], place[1], place[2], place[4], place[5]
     near = rows // home_rows // 2
     pack = HD // rows
@@ -64,23 +65,25 @@
         q_turned[HD:, n * HD : (n + 1) * HD] = (scaled - coarse.astype(F32)).astype(BF16)
     wide = owners * groups * HD
 
-    def score(keys, at):
-        s = nn_dot(jnp.concatenate([keys, keys], axis=1), q_turned[...])
+    def score(keys):
+        return nn_dot(jnp.concatenate([keys, keys], axis=1), q_turned[...])
+
+    def masked(s, at):
         return s + jnp.concatenate([hidden[at, :]] * (owners * groups), axis=1)
 
-    s_new = score(key_fresh[...], slice(2 * cache_here, 2 * cache_here + home_rows))
+    s_new = masked(score(key_fresh[...]), slice(2 * cache_here, 2 * cache_here + home_rows))
     run = jnp.max(s_new.reshape(home_rows // 8, 8, wide), axis=0)
-    pieces = [(part, i) for part in range(2) for i in range(0, cache_here, step)]
-    for part, i in pieces:
-        at = slice(part * cache_here + i, part * cache_here + i + step)
-        s = score((key_own, key_other)[part][i : i + step, :], at)
-        scores[at, :] = s
-        run = jnp.maximum(run, jnp.max(s.reshape(step // 8, 8, wide), axis=0))
+    for part, keys in enumerate((key_own, key_other)):
+        for i in range(0, cache_here, step):
+            scores[part * cache_here + i : part * cache_here + i + step, :] = score(keys[i : i + step, :])
+    fine_step = 64
+    pieces = [slice(i, i + fine_step) for i in range(0, 2 * cache_here, fine_step)]
+    for at in pieces:
+        run = jnp.maximum(run, jnp.max(masked(scores[at, :], at).reshape(fine_step // 8, 8, wide), axis=0))
     peak = jnp.maximum(jnp.max(run, axis=0, keepdims=True), FLOOR).astype(BF16).astype(F32)
     p_new = jnp.exp2((s_new - peak).astype(BF16))
-    for part, i in pieces:
-        at = slice(part * cache_here + i, part * cache_here + i + step)
-        probs[at, :] = jnp.exp2((scores[at, :] - peak).astype(BF16))
+    for at in pieces:
+        probs[at, :] = jnp.exp2((masked(scores[at, :], at) - peak).astype(BF16))
     ones = jnp.ones((STATS, cache_here), BF16)
     sums = nn_dot(jnp.concatenate([value_own[...], ones], axis=0), probs[:cache_here, :])
     sums = sums + nn_dot(jnp.concatenate([value_other[...], ones], axis=0), probs[cache_here:, :])
@@ -89,12 +92,18 @@
     high = denom.astype(BF16).astype(F32)
     low = denom - high
     for owner in range(owners):
+        distance = (pl.program_id(0) * owners + owner) ^ chip
         lanes = [slice((owner * groups + k) * HD, (owner * groups + k + 1) * HD) for k in range(groups)]
         for k, cols in enumerate(lanes):
-            out[owner, k * HD : (k + 1) * HD, :] = numer[:, cols].astype(BF16)
+            held[distance, k * HD : (k + 1) * HD, :] = numer[:, cols].astype(BF16)
         filled = [kind[:, cols] for kind in (peak, high, low) for cols in lanes]
         filled += [jnp.zeros_like(filled[0])] * (STATS - len(filled))
-        out[owner, groups * HD :, :] = jnp.concatenate(filled, axis=0).astype(BF16)
+        held[distance, groups * HD :, :] = jnp.concatenate(filled, axis=0).astype(BF16)
+
+    @pl.when(pl.program_id(0) == pl.num_programs(0) - 1)
+    def _():
+        for k, out in enumerate(outs):
+            out[...] = held[k]
 
 
 def attention(place, query_blocks, keys, values, new_key, new_value, lens, row_ids, chips, kv_heads):
@@ -113,7 +122,7 @@
     shape = (owners, owner_heads, home_rows, rows, cache_here, step)
     work = wide * kv_heads * 2 * cache_here
     return pl.pallas_call(
-        functools.partial(attention_body, shape),
+        functools.partial(attention_body, shape, chips),
         grid_spec=pltpu.PrefetchScalarGridSpec(
             num_scalar_prefetch=1,
             grid=(kv_heads,),
@@ -125,16 +134,17 @@
             + [pl.BlockSpec((HD, cache_here), lambda g, place: (g, 0))] * 2
             + [pl.BlockSpec((home_rows, HD), kv)] * 2
             + [pl.BlockSpec(lens.shape, whole)] * 2,
-            out_specs=pl.BlockSpec((owners, height, HD), lambda g, place: (g, 0, 0)),
+            out_specs=[pl.BlockSpec((height, HD), whole)] * chips,
             scratch_shapes=[
                 pltpu.VMEM((rows, columns), BF16),
                 pltpu.VMEM((2 * HD, wide), BF16),
                 pltpu.VMEM((positions, HD), F32),
                 pltpu.VMEM((2 * cache_here, wide), F32),
                 pltpu.VMEM((2 * cache_here, wide), BF16),
+                pltpu.VMEM((chips, height, HD), BF16),
             ],
         ),
-        out_shape=jax.ShapeDtypeStruct((chips, height, HD), BF16),
+        out_shape=[jax.ShapeDtypeStruct((height, HD), BF16)] * chips,
         compiler_params=pltpu.CompilerParams(vmem_limit_bytes=32 * MIB),
         cost_estimate=pl.CostEstimate(
             flops=6 * work * HD, bytes_accessed=8 * MIB, transcendentals=work
@@ -153,57 +163,64 @@
     )
 
 
-def project_body(rows, place, *refs):
-    *chunks, weight_own, weight_other, out, turned = refs
-    core = place[3]
-    chips, height, _ = chunks[0].shape
-    base = height - STATS
+def project_body(rows, chips, place, *refs):
+    chunks = refs[:chips], refs[chips : 2 * chips]
+    weight_own, weight_other = refs[2 * chips : 2 * chips + 2]
+    *outs, turned, product = refs[2 * chips + 2 :]
+    chip, core, ring = place[0], place[3], place[5]
+    base = chunks[0][0].shape[0] - STATS
     groups = base // HD
     pack = HD // rows
     heads_here = groups * pack // CORES
     half = chips // 2 // 2
     for near in range(2):
-        sources = [chunks[s // 2 // half ^ near].at[s] for s in range(chips)]
-        stats = [part[base:, :].astype(F32) for part in sources]
+        sources = [chunks[near ^ (k // 2 // half)][k] for k in range(chips)]
+        stats = [source[base:, :].astype(F32) for source in sources]
         peaks = [stat[:groups] for stat in stats]
         top = functools.reduce(jnp.maximum, peaks)
         share = [jnp.exp2(peak - top) for peak in peaks]
         denom = sum(w * (t[groups : 2 * groups] + t[2 * groups : 3 * groups]) for w, t in zip(share, stats))
+        first = pl.multiple_of((ring // half ^ near) * rows, rows)
         for k in range(groups):
             numer = sum(
-                part[k * HD : (k + 1) * HD, :].astype(F32) * w[k : k + 1, :] for part, w in zip(sources, share)
+                source[k * HD : (k + 1) * HD, :].astype(F32) * w[k : k + 1, :]
+                for source, w in zip(sources, share)
             )
             attended = (numer / denom[k : k + 1, :]).T.astype(BF16)
             for j in range(pack):
                 part, h = divmod(k * pack + j, heads_here)
-                turned[part, near * rows : (near + 1) * rows, h * HD : (h + 1) * HD] = attended[
-                    j * rows : (j + 1) * rows
-                ]
-    product = nn_dot(turned[core], weight_own[...]) + nn_dot(turned[1 - core], weight_other[...])
-    out[...] = product.astype(BF16)
+                turned[part, pl.ds(first, rows), h * HD : (h + 1) * HD] = attended[j * rows : (j + 1) * rows]
+    total = nn_dot(turned[core], weight_own[...]) + nn_dot(turned[1 - core], weight_other[...])
+    product[...] = total.astype(BF16)
+    for k, out in enumerate(outs):
+        home_rows = out.shape[0]
+        out[...] = product[pl.ds(pl.multiple_of((chip ^ k) * home_rows, home_rows), home_rows), :]
 
 
 def project(place, chunks, weight_own, weight_other, rows):
+    chips = len(chunks[0])
     depth, width = weight_own.shape
     vmem = pl.BlockSpec(memory_space=pltpu.VMEM)
     return pl.pallas_call(
-        functools.partial(project_body, rows),
-        in_specs=[pl.BlockSpec(memory_space=pltpu.SMEM)] + [vmem] * (len(chunks) + 2),
-        out_specs=vmem,
-        out_shape=jax.ShapeDtypeStruct((2 * rows, width), BF16),
-        scratch_shapes=[pltpu.VMEM((CORES, 2 * rows, depth), BF16)],
+        functools.partial(project_body, rows, chips),
+        in_specs=[pl.BlockSpec(memory_space=pltpu.SMEM)] + [vmem] * (2 * chips + 2),
+        out_specs=[vmem] * chips,
+        out_shape=[jax.ShapeDtypeStruct((2 * rows // chips, width), BF16)] * chips,
+        scratch_shapes=[
+            pltpu.VMEM((CORES, 2 * rows, depth), BF16),
+            pltpu.VMEM((2 * rows, width), BF16),
+        ],
         compiler_params=pltpu.CompilerParams(vmem_limit_bytes=32 * MIB),
         cost_estimate=pl.CostEstimate(
             flops=8 * rows * width * depth, bytes_accessed=4 * MIB, transcendentals=0
         ),
         name="project",
-    )(place, *chunks, weight_own, weight_other)
-
-
-def norm_body(parts, residual, gain, chooser, middle_out, sent):
-    total = parts[0].astype(F32)
-    for s in range(1, parts.shape[0]):
-        total = total + parts[s].astype(F32)
+    )(place, *chunks[0], *chunks[1], weight_own, weight_other)
+
+
+def norm_body(*refs):
+    *parts, residual, gain, chooser, middle_out, sent = refs
+    total = sum(part[...].astype(F32) for part in parts)
     middle = (residual[...].astype(F32) + total).astype(BF16)
     middle_out[...] = middle
     middle = middle.astype(F32)
@@ -217,7 +234,7 @@
     rows, width = residual.shape
     return pl.pallas_call(
         norm_body,
-        in_specs=[vmem] * 4,
+        in_specs=[vmem] * (len(parts) + 3),
         out_specs=[vmem] * 2,
         out_shape=[
             jax.ShapeDtypeStruct((rows, width), BF16),
@@ -228,7 +245,7 @@
             flops=2 * chooser.shape[0] * rows * width, bytes_accessed=2 * MIB, transcendentals=0
         ),
         name="norm_and_dispatch",
-    )(parts, residual, gain, chooser)
+    )(*parts, residual, gain, chooser)
 
 
 def experts_body(step, arrived, w_gate, w_up, w_down, out, gate_held, up_held, down_held, sems):
@@ -340,7 +357,14 @@
     top = expert_ids.shape[1]
     heads_here = out_weight.shape[0] // HD
     cache_here = key_cache.shape[0]
-    same_core = [[CORES * j + c for j in range(chips)] for c in range(CORES)]
+
+    def to_peers(blocks):
+        return blocks[:1] + [
+            lax.ppermute(block, "ctx", [(i, i ^ (CORES * k)) for i in range(devices)])
+            for k, block in enumerate(blocks)
+            if k
+        ]
+
     swap = [(i, i ^ 1) for i in range(devices)]
 
     across = [(i, i ^ CORES) for i in range(devices)]
@@ -410,21 +434,9 @@
             sums, gathered[-1] = lax.optimization_barrier((sums, gathered[-1]))
         else:
             sums, place, late_weight, _ = lax.optimization_barrier((sums, place, out_weight, far_across))
-        gathered.append(
-            lax.all_to_all(
-                sums, "ctx", split_axis=0, concat_axis=0, axis_index_groups=same_core, tiled=True
-            )
-        )
+        gathered.append(to_peers(list(sums)))
     weight_other = lax.ppermute(late_weight, "ctx", swap)
-    share = project(place, gathered, out_weight, weight_other, chunk_rows)
-    shares = lax.all_to_all(
-        share.reshape(chips, home_rows, width),
-        "ctx",
-        split_axis=0,
-        concat_axis=0,
-        axis_index_groups=same_core,
-        tiled=True,
-    )
+    shares = to_peers(list(project(place, gathered, out_weight, weight_other, chunk_rows)))
     middle, outgoing = norm_and_dispatch(shares, residual, norm_gain.reshape(1, width), chooser)
     arrived = lax.all_to_all(
         outgoing.reshape(devices, experts * MOST, width), "ctx", split_axis=0, concat_axis=0, tiled=True

time: 132 us -> 155 us (1.17)
  starting transfers between devices: 25.6 us -> 50.2 us
  waiting for transfers between devices: 52.4 us -> 32.8 us
  local copies, waits for them, and re-layouts: 3.58 us -> 21 us
    ppermute x0 -> x21, starting transfers between devices: none -> 36.5 us  [to_peers(): lax.ppermute(block, 'ctx', [(i, i ^ CORES * k) for i in range(devices)])]
    all_to_all x3 -> x0, waiting for transfers between devices: 31.8 us -> none  [the longest x2 18.2 us: on_device(): lax.all_to_all(sums, 'ctx', split_axis=0, concat_axis=0, axis_index_group...]
    unnamed x13 -> x61, local copies, waits for them, and re-layouts: 0.17 us -> 17.6 us
    ppermute x0 -> x21, waiting for transfers between devices: none -> 13.5 us  [to_peers(): lax.ppermute(block, 'ctx', [(i, i ^ CORES * k) for i in range(devices)])]
    all_to_all x3 -> x0, starting transfers between devices: 12.5 us -> none  [the longest x2 8.86 us: on_device(): lax.all_to_all(sums, 'ctx', split_axis=0, concat_axis=0, axis_index_group...]
  transfers between devices with their start and end apart: 13 -> 31, of which waited for: 5 -> 7; matrix products, arithmetic and copies ran while one was open for 3% -> 3% of each run, Pallas kernels for 15% -> 13%
where the time goes in v11:
time: 155 us
  starting transfers between devices  50.2 us (32%)
  waiting for transfers between devices  32.8 us (21%)
  Pallas kernels  31.3 us (20%)
  local copies, waits for them, and re-layouts  21 us (14%)
  blocking collectives  18.9 us (12%)
    ppermute x21, starting transfers between devices, to_peers(): lax.ppermute(block, 'ctx', [(i, i ^ CORES * k) for i in range(devices)])  36.5 us
    pallas_call x2, Pallas kernels, attention(): pl.pallas_call(functools.partial(attention_body, shape, chips), grid_spec...  20.1 us
    all_to_all x1, blocking collectives, on_device(): lax.all_to_all(outgoing.reshape(devices, experts * MOST, width), 'ctx', s...  18.9 us
    unnamed x61, local copies, waits for them, and re-layouts  17.6 us
    all_to_all x1, waiting for transfers between devices, on_device(): lax.all_to_all(produced.reshape(devices, experts * MOST, width), 'ctx', s...  14.3 us
    ppermute x21, waiting for transfers between devices, to_peers(): lax.ppermute(block, 'ctx', [(i, i ^ CORES * k) for i in range(devices)])  13.5 us
    pallas_call x1, Pallas kernels, run_experts(): pl.pallas_call(functools.partial(experts_body, step), in_specs=[vmem] + [...  7.88 us
    ppermute x3, waiting for transfers between devices, on_device(): lax.ppermute(queries, 'ctx', [(i, i ^ 2 * CORES * k) for i in range(devic...  4.96 us
  transfers between devices with their start and end apart: 31, of which 7 were waited for; matrix products, arithmetic and copies ran while one was open for 3% of the time, Pallas kernels for 13%

profile of v11, /device:TPU:0, one launch (start us, length us, event | category | flops | bytes accessed | tf_op | source)
XLA Modules:
  0.0 154.8 jit_solution(12768272801018615176)
XLA Ops:
  0.0 3.0 %collective-permute-start.1 = (bf16[16,4096]{1,0:T(8,128)(2,1)}, bf16[16,4096]{1,0:T(8,128)(2,1)S(1)}, u32[]{:S(2)}, u32[]{:S(2)}) collective-permute-start(bf16[16,4096]{1,0:T(8,128)(2,1)} %refs_0_.1), channel_id=1, source_target_pairs={{0,2},{1,3},{2,0},{3,1},{4,6},{5,7},{6,4},{7,5},{8,10},{9,11},{10,... | collective-permute-start | bytes 393224 | tf_op jit(solution)/shard_map/ppermute | solution.py:376
  3.0 1.6 %collective-permute-start = (bf16[16,4096]{1,0:T(8,128)(2,1)}, bf16[16,4096]{1,0:T(8,128)(2,1)}, u32[]{:S(2)}, u32[]{:S(2)}) collective-permute-start(bf16[16,4096]{1,0:T(8,128)(2,1)} %refs_0_.1), channel_id=1, source_target_pairs={{0,4},{1,5},{2,6},{3,7},{4,0},{5,1},{6,2},{7,3},{8,12},{9,13},{10,... | collective-permute-start | bytes 393224 | tf_op jit(solution)/shard_map/ppermute | solution.py:380
  4.5 2.6 %collective-permute-start.5 = (bf16[16,4096]{1,0:T(8,128)(2,1)}, bf16[16,4096]{1,0:T(8,128)(2,1)S(1)}, u32[]{:S(2)}, u32[]{:S(2)}) collective-permute-start(bf16[16,4096]{1,0:T(8,128)(2,1)} %refs_0_.1), channel_id=1, source_target_pairs={{0,8},{1,9},{2,10},{3,11},{4,12},{5,13},{6,14},{7,15},{8,0},{9,1},... | collective-permute-start | bytes 393224 | tf_op jit(solution)/shard_map/ppermute | solution.py:380
  7.4 0.7 copy-done.16
  8.0 1.5 copy.23
  10.3 0.8 reshape.63
  11.4 1.1 collective-permute-start.2
  12.5 5.0 %collective-permute-done.5 = bf16[16,4096]{1,0:T(8,128)(2,1)S(1)} collective-permute-done((bf16[16,4096]{1,0:T(8,128)(2,1)}, bf16[16,4096]{1,0:T(8,128)(2,1)S(1)}, u32[]{:S(2)}, u32[]{:S(2)}) %collective-permute-start.5) | collective-permute-done | bytes 131104 | tf_op jit(solution)/shard_map/ppermute | solution.py:380
  18.1 1.0 copy-done.17
  19.1 10.0 %attention.2 = (bf16[272,128]{1,0:T(8,128)(2,1)S(1)}, bf16[272,128]{1,0:T(8,128)(2,1)S(1)}, bf16[272,128]{1,0:T(8,128)(2,1)S(1)}, bf16[272,128]{1,0:T(8,128)(2,1...) custom-call(s32[6]{0:T(128)S(1)} %stack.27.place, ...), custom_call_target="tpu_custom_call" | custom-call | flops 3221225472 | bytes 8388608 | tf_op jit(solution)/shard_map/attention/pallas_call | solution.py:124
  31.6 0.7 copy-done.14
  32.4 3.0 %collective-permute-start.10 = (bf16[272,128]{1,0:T(8,128)(2,1)}, bf16[272,128]{1,0:T(8,128)(2,1)S(1)}, u32[]{:S(2)}, u32[]{:S(2)}) collective-permute-start(bf16[272,128]{1,0:T(8,128)(2,1)} %get-tuple-element.81), channel_id=1, source_target_pairs={{0,6},{1,7},{2,4},{3,5},{4,2},{5,3},{6,0},{7,1},{8,14},{9,15},{10,... | collective-permute-start | bytes 208904 | tf_op jit(solution)/shard_map/ppermute | solution.py:363
  35.4 1.7 %collective-permute-start.11 = (bf16[272,128]{1,0:T(8,128)(2,1)}, bf16[272,128]{1,0:T(8,128)(2,1)S(1)}, u32[]{:S(2)}, u32[]{:S(2)}) collective-permute-start(bf16[272,128]{1,0:T(8,128)(2,1)} %get-tuple-element.82), channel_id=1, source_target_pairs={{0,8},{1,9},{2,10},{3,11},{4,12},{5,13},{6,14},{7,15},{8,0},{9,1},... | collective-permute-start | bytes 208904 | tf_op jit(solution)/shard_map/ppermute | solution.py:363
  37.0 1.2 collective-permute-start.12
  38.6 2.4 %collective-permute-start.13 = (bf16[272,128]{1,0:T(8,128)(2,1)}, bf16[272,128]{1,0:T(8,128)(2,1)S(1)}, u32[]{:S(2)}, u32[]{:S(2)}) collective-permute-start(bf16[272,128]{1,0:T(8,128)(2,1)} %copy-done.21), channel_id=1, source_target_pairs={{0,12},{1,13},{2,14},{3,15},{4,8},{5,9},{6,10},{7,11},{8,4},{9,5},... | collective-permute-start | bytes 208904 | tf_op jit(solution)/shard_map/ppermute | solution.py:363
  41.0 2.3 %collective-permute-start.14 = (bf16[272,128]{1,0:T(8,128)(2,1)}, bf16[272,128]{1,0:T(8,128)(2,1)S(1)}, u32[]{:S(2)}, u32[]{:S(2)}) collective-permute-start(bf16[272,128]{1,0:T(8,128)(2,1)} %copy-done.20), channel_id=1, source_target_pairs={{0,14},{1,15},{2,12},{3,13},{4,10},{5,11},{6,8},{7,9},{8,6},{9,7},... | collective-permute-start | bytes 208904 | tf_op jit(solution)/shard_map/ppermute | solution.py:363
  43.4 2.1 %collective-permute-done.11.refs_4_ = bf16[272,128]{1,0:T(8,128)(2,1)S(1)} collective-permute-done((bf16[272,128]{1,0:T(8,128)(2,1)}, bf16[272,128]{1,0:T(8,128)(2,1)S(1)}, u32[]{:S(2)}, u32[]{:S(2)}) %collective-permute-start.11) | collective-permute-done | bytes 69664 | tf_op jit(solution)/shard_map/ppermute | solution.py:363
  45.5 2.1 %collective-permute-done.12.refs_5_ = bf16[272,128]{1,0:T(8,128)(2,1)S(1)} collective-permute-done((bf16[272,128]{1,0:T(8,128)(2,1)}, bf16[272,128]{1,0:T(8,128)(2,1)S(1)}, u32[]{:S(2)}, u32[]{:S(2)}) %collective-permute-start.12) | collective-permute-done | bytes 69664 | tf_op jit(solution)/shard_map/ppermute | solution.py:363
  48.1 0.9 copy-done.11
  49.1 1.2 copy-done.13
  50.3 0.9 copy-done.15
  51.3 10.1 %attention.3 = (bf16[272,128]{1,0:T(8,128)(2,1)S(1)}, bf16[272,128]{1,0:T(8,128)(2,1)}, bf16[272,128]{1,0:T(8,128)(2,1)}, bf16[272,128]{1,0:T(8,128)(2,1)}, bf16...) custom-call(s32[6]{0:T(128)S(1)} %stack.27.place, ...), custom_call_target="tpu_custom_call" | custom-call | flops 3221225472 | bytes 8388608 | tf_op jit(solution)/shard_map/attention/pallas_call | solution.py:124
  66.4 1.8 %collective-permute-start.15 = (bf16[272,128]{1,0:T(8,128)(2,1)}, bf16[272,128]{1,0:T(8,128)(2,1)S(1)}, u32[]{:S(2)}, u32[]{:S(2)}) collective-permute-start(bf16[272,128]{1,0:T(8,128)(2,1)} %get-tuple-element.95), channel_id=1, source_target_pairs={{0,2},{1,3},{2,0},{3,1},{4,6},{5,7},{6,4},{7,5},{8,10},{9,11},{10,... | collective-permute-start | bytes 208904 | tf_op jit(solution)/shard_map/ppermute | solution.py:363
  68.2 2.0 %collective-permute-start.16 = (bf16[272,128]{1,0:T(8,128)(2,1)}, bf16[272,128]{1,0:T(8,128)(2,1)S(1)}, u32[]{:S(2)}, u32[]{:S(2)}) collective-permute-start(bf16[272,128]{1,0:T(8,128)(2,1)} %get-tuple-element.96), channel_id=1, source_target_pairs={{0,4},{1,5},{2,6},{3,7},{4,0},{5,1},{6,2},{7,3},{8,12},{9,13},{10,... | collective-permute-start | bytes 208904 | tf_op jit(solution)/shard_map/ppermute | solution.py:363
  70.4 3.4 %collective-permute-start.18 = (bf16[272,128]{1,0:T(8,128)(2,1)}, bf16[272,128]{1,0:T(8,128)(2,1)S(1)}, u32[]{:S(2)}, u32[]{:S(2)}) collective-permute-start(bf16[272,128]{1,0:T(8,128)(2,1)} %copy-done.25), channel_id=1, source_target_pairs={{0,8},{1,9},{2,10},{3,11},{4,12},{5,13},{6,14},{7,15},{8,0},{9,1},... | collective-permute-start | bytes 208904 | tf_op jit(solution)/shard_map/ppermute | solution.py:363
  73.7 2.1 %collective-permute-start.19 = (bf16[272,128]{1,0:T(8,128)(2,1)}, bf16[272,128]{1,0:T(8,128)(2,1)S(1)}, u32[]{:S(2)}, u32[]{:S(2)}) collective-permute-start(bf16[272,128]{1,0:T(8,128)(2,1)} %copy-done.24), channel_id=1, source_target_pairs={{0,10},{1,11},{2,8},{3,9},{4,14},{5,15},{6,12},{7,13},{8,2},{9,3},... | collective-permute-start | bytes 208904 | tf_op jit(solution)/shard_map/ppermute | solution.py:363
  75.8 1.0 collective-permute-start.20
  76.8 3.2 %collective-permute-start.21 = (bf16[272,128]{1,0:T(8,128)(2,1)}, bf16[272,128]{1,0:T(8,128)(2,1)S(1)}, u32[]{:S(2)}, u32[]{:S(2)}) collective-permute-start(bf16[272,128]{1,0:T(8,128)(2,1)} %copy-done.22), channel_id=1, source_target_pairs={{0,14},{1,15},{2,12},{3,13},{4,10},{5,11},{6,8},{7,9},{8,6},{9,7},... | collective-permute-start | bytes 208904 | tf_op jit(solution)/shard_map/ppermute | solution.py:363
  80.3 3.9 %collective-permute-done.19.refs_13_ = bf16[272,128]{1,0:T(8,128)(2,1)S(1)} collective-permute-done((bf16[272,128]{1,0:T(8,128)(2,1)}, bf16[272,128]{1,0:T(8,128)(2,1)S(1)}, u32[]{:S(2)}, u32[]{:S(2)}) %collective-permute-start.19) | collective-permute-done | bytes 69664 | tf_op jit(solution)/shard_map/ppermute | solution.py:363
  84.2 0.9 copy-done.2
  85.1 0.9 copy-done.4
  86.0 0.9 copy-done.6
  86.9 0.9 copy-done.8
  87.7 2.0 %project.1 = (bf16[16,2048]{1,0:T(8,128)(2,1)S(1)}, bf16[16,2048]{1,0:T(8,128)(2,1)S(1)}, bf16[16,2048]{1,0:T(8,128)(2,1)S(1)}, bf16[16,2048]{1,0:T(8,128)(2,1)S...) custom-call(s32[6]{0:T(128)S(1)} %stack.27.place, ...), custom_call_target="tpu_custom_call" | custom-call | flops 268435456 | bytes 4194304 | tf_op jit(solution)/shard_map/project/pallas_call | solution.py:204
  89.7 0.6 collective-permute-start.23
  90.4 3.1 %collective-permute-start.24 = (bf16[16,2048]{1,0:T(8,128)(2,1)S(1)}, bf16[16,2048]{1,0:T(8,128)(2,1)S(1)}, u32[]{:S(2)}, u32[]{:S(2)}) collective-permute-start(bf16[16,2048]{1,0:T(8,128)(2,1)S(1)} %get-tuple-element.105), channel_id=1, source_target_pairs={{0,4},{1,5},{2,6},{3,7},{4,0},{5,1},{6,2},{7,3},{8,12},{9,13},{10,... | collective-permute-start | bytes 196616 | tf_op jit(solution)/shard_map/ppermute | solution.py:363
  93.9 2.4 %collective-permute-start.26 = (bf16[16,2048]{1,0:T(8,128)(2,1)}, bf16[16,2048]{1,0:T(8,128)(2,1)S(1)}, u32[]{:S(2)}, u32[]{:S(2)}) collective-permute-start(bf16[16,2048]{1,0:T(8,128)(2,1)} %get-tuple-element.107), channel_id=1, source_target_pairs={{0,8},{1,9},{2,10},{3,11},{4,12},{5,13},{6,14},{7,15},{8,0},{9,1},... | collective-permute-start | bytes 196616 | tf_op jit(solution)/shard_map/ppermute | solution.py:363
  96.3 1.0 collective-permute-start.27
  97.3 2.0 %collective-permute-start.28 = (bf16[16,2048]{1,0:T(8,128)(2,1)}, bf16[16,2048]{1,0:T(8,128)(2,1)S(1)}, u32[]{:S(2)}, u32[]{:S(2)}) collective-permute-start(bf16[16,2048]{1,0:T(8,128)(2,1)} %get-tuple-element.109), channel_id=1, source_target_pairs={{0,12},{1,13},{2,14},{3,15},{4,8},{5,9},{6,10},{7,11},{8,4},{9,5},... | collective-permute-start | bytes 196616 | tf_op jit(solution)/shard_map/ppermute | solution.py:363
  99.3 2.3 %collective-permute-start.29 = (bf16[16,2048]{1,0:T(8,128)(2,1)}, bf16[16,2048]{1,0:T(8,128)(2,1)S(1)}, u32[]{:S(2)}, u32[]{:S(2)}) collective-permute-start(bf16[16,2048]{1,0:T(8,128)(2,1)} %get-tuple-element.110), channel_id=1, source_target_pairs={{0,14},{1,15},{2,12},{3,13},{4,10},{5,11},{6,8},{7,9},{8,6},{9,7},... | collective-permute-start | bytes 196616 | tf_op jit(solution)/shard_map/ppermute | solution.py:363
  101.9 2.0 %collective-permute-done.26.refs_4_ = bf16[16,2048]{1,0:T(8,128)(2,1)S(1)} collective-permute-done((bf16[16,2048]{1,0:T(8,128)(2,1)}, bf16[16,2048]{1,0:T(8,128)(2,1)S(1)}, u32[]{:S(2)}, u32[]{:S(2)}) %collective-permute-start.26) | collective-permute-done | bytes 65568 | tf_op jit(solution)/shard_map/ppermute | solution.py:363
  103.9 3.3 %collective-permute-done.27.refs_5_ = bf16[16,2048]{1,0:T(8,128)(2,1)S(1)} collective-permute-done((bf16[16,2048]{1,0:T(8,128)(2,1)}, bf16[16,2048]{1,0:T(8,128)(2,1)S(1)}, u32[]{:S(2)}, u32[]{:S(2)}) %collective-permute-start.27) | collective-permute-done | bytes 65568 | tf_op jit(solution)/shard_map/ppermute | solution.py:363
  107.3 0.8 copy-done.9
  108.6 18.9 %all_to_all.10 = bf16[16,8,2048]{2,1,0:T(8,128)(2,1)S(1)} all-to-all(bf16[16,8,2048]{2,1,0:T(8,128)(2,1)S(1)} %bitcast.17), channel_id=1, replica_groups=mesh['groups'=2,'ctx'=16] {'ctx'}, dimensions={0} | all-to-all | bytes 1048576 | tf_op jit(solution)/shard_map/all_to_all | solution.py:441
  127.4 7.9 %experts.1 = bf16[128,2048]{1,0:T(8,128)(2,1)} custom-call(bf16[128,2048]{1,0:T(8,128)(2,1)S(1)} %bitcast.12, bf16[2,2048,768]{2,1,0:T(8,128)(2,1)} %w_gate.1, bf16[2,2048,768]{2,1,0:T(8,128)(2,1)} %w_up.1, bf16[2,768,2048]{2,1,0:T(8,128)(2,1)} %w_down.1), custom_call_target="tpu_custom_call" | custom-call | flops 2415919104 | bytes 18874368 | tf_op jit(solution)/shard_map/experts/pallas_call | solution.py:297
  135.3 4.1 %all-to-all-start.1 = ((bf16[16,8,2048]{2,1,0:T(8,128)(2,1)}), bf16[16,8,2048]{2,1,0:T(8,128)(2,1)S(1)}, u32[]{:S(2)}, u32[]{:S(2)}) async-start(bf16[16,8,2048]{2,1,0:T(8,128)(2,1)} %bitcast.10), calls=%async_computation.1 | async-start | bytes 1048576 | tf_op jit(solution)/shard_map/all_to_all | solution.py:445
  139.6 14.3 %all-to-all-done.1 = bf16[16,8,2048]{2,1,0:T(8,128)(2,1)S(1)} async-done(((bf16[16,8,2048]{2,1,0:T(8,128)(2,1)}), bf16[16,8,2048]{2,1,0:T(8,128)(2,1)S(1)}, u32[]{:S(2)}, u32[]{:S(2)}) %all-to-all-start.1) | async-done | bytes 524320 | tf_op jit(solution)/shard_map/all_to_all | solution.py:445
  153.9 0.9 mix.1
  (111 shorter events, 12.2 us)
Async XLA Ops:
  0.0 7.4 %collective-permute-start.1 = (bf16[16,4096]{1,0:T(8,128)(2,1)}, bf16[16,4096]{1,0:T(8,128)(2,1)S(1)}, u32[]{:S(2)}, u32[]{:S(2)}) collective-permute-start(bf16[16,4096]{1,0:T(8,128)(2,1)} %refs_0_.1), channel_id=1, source_target_pairs={{0,2},{1,3},{2,0},{3,1},{4,6},{5,7},{6,4},{7,5},{8,10},{9,11},{10,... | collective-permute-start | bytes 393224 | tf_op jit(solution)/shard_map/ppermute | solution.py:376
  3.0 8.4 %collective-permute-start = (bf16[16,4096]{1,0:T(8,128)(2,1)}, bf16[16,4096]{1,0:T(8,128)(2,1)}, u32[]{:S(2)}, u32[]{:S(2)}) collective-permute-start(bf16[16,4096]{1,0:T(8,128)(2,1)} %refs_0_.1), channel_id=1, source_target_pairs={{0,4},{1,5},{2,6},{3,7},{4,0},{5,1},{6,2},{7,3},{8,12},{9,13},{10,... | collective-permute-start | bytes 393224 | tf_op jit(solution)/shard_map/ppermute | solution.py:380
  4.5 12.9 %collective-permute-start.5 = (bf16[16,4096]{1,0:T(8,128)(2,1)}, bf16[16,4096]{1,0:T(8,128)(2,1)S(1)}, u32[]{:S(2)}, u32[]{:S(2)}) collective-permute-start(bf16[16,4096]{1,0:T(8,128)(2,1)} %refs_0_.1), channel_id=1, source_target_pairs={{0,8},{1,9},{2,10},{3,11},{4,12},{5,13},{6,14},{7,15},{8,0},{9,1},... | collective-permute-start | bytes 393224 | tf_op jit(solution)/shard_map/ppermute | solution.py:380
  7.1 10.3 %collective-permute-start.6 = (bf16[16,4096]{1,0:T(8,128)(2,1)}, bf16[16,4096]{1,0:T(8,128)(2,1)S(1)}, u32[]{:S(2)}, u32[]{:S(2)}) collective-permute-start(bf16[16,4096]{1,0:T(8,128)(2,1)} %refs_0_.1), channel_id=1, source_target_pairs={{0,12},{1,13},{2,14},{3,15},{4,8},{5,9},{6,10},{7,11},{8,4},{9,5},... | collective-permute-start | bytes 393224 | tf_op jit(solution)/shard_map/ppermute | solution.py:380
  7.4 0.7 copy-start.16
  9.5 22.9 %copy-start = (bf16[256,2048]{1,0:T(8,128)(2,1)S(1)}, bf16[256,2048]{1,0:T(8,128)(2,1)}, u32[]{:S(2)}) copy-start(bf16[256,2048]{1,0:T(8,128)(2,1)} %refs_16_.1) | copy-start | bytes 3145732
  9.5 8.5 %collective-permute-start.4 = (bf16[512,1024]{1,0:T(8,128)(2,1)S(1)}, bf16[512,1024]{1,0:T(8,128)(2,1)S(1)}, u32[]{:S(2)}, u32[]{:S(2)}) collective-permute-start(bf16[512,1024]{1,0:T(8,128)(2,1)S(1)} %bitcast.14), channel_id=1, source_target_pairs={{0,1},{1,0},{2,3},{3,2},{4,5},{5,4},{6,7},{7,6},{8,9},{9,8},{10,11... | collective-permute-start | bytes 3145736 | tf_op jit(solution)/shard_map/ppermute | solution.py:392
  9.6 8.5 %collective-permute-start.3 = (bf16[1024,512]{1,0:T(8,128)(2,1)}, bf16[1024,512]{1,0:T(8,128)(2,1)}, u32[]{:S(2)}, u32[]{:S(2)}) collective-permute-start(bf16[1024,512]{1,0:T(8,128)(2,1)} %refs_4_.3), channel_id=1, source_target_pairs={{0,1},{1,0},{2,3},{3,2},{4,5},{5,4},{6,7},{7,6},{8,9},{9,8},{10,11... | collective-permute-start | bytes 3145736 | tf_op jit(solution)/shard_map/ppermute | solution.py:390
  11.4 6.7 %collective-permute-start.2 = (bf16[16,4096]{1,0:T(8,128)(2,1)}, bf16[16,4096]{1,0:T(8,128)(2,1)S(1)}, u32[]{:S(2)}, u32[]{:S(2)}) collective-permute-start(bf16[16,4096]{1,0:T(8,128)(2,1)} %collective-permute-done.refs_1_), channel_id=1, source_target_pairs={{0,2},{1,3},{2,0},{3,1},{4,6},{5,7},{6,4},{7,5},{8,10},{9,11},{10,... | collective-permute-start | bytes 393224 | tf_op jit(solution)/shard_map/ppermute | solution.py:376
  17.5 17.9 %copy-start.10 = (bf16[32,4096]{1,0:T(8,128)(2,1)}, bf16[32,4096]{1,0:T(8,128)(2,1)S(1)}, u32[]{:S(2)}) copy-start(bf16[32,4096]{1,0:T(8,128)(2,1)S(1)} %constant_dynamic-update-slice_fusion.refs_0_.refs_1_) | copy-start | bytes 786436
  17.5 14.2 %collective-permute-start.7 = (bf16[32,4096]{1,0:T(8,128)(2,1)S(1)}, bf16[32,4096]{1,0:T(8,128)(2,1)S(1)}, u32[]{:S(2)}, u32[]{:S(2)}) collective-permute-start(bf16[32,4096]{1,0:T(8,128)(2,1)S(1)} %constant_dynamic-update-slice_fusion.refs_0_.refs_1_), channel_id=1, source_target_pairs={{0,2},{1,3},{2,0},{3,1},{4,6},{5,7},{6,4},{7,5},{8,10},{9,11},{10,... | collective-permute-start | bytes 786440 | tf_op jit(solution)/shard_map/ppermute | solution.py:376
  18.0 14.3 %copy-start.12 = (bf16[512,1024]{1,0:T(8,128)(2,1)}, bf16[512,1024]{1,0:T(8,128)(2,1)S(1)}, u32[]{:S(2)}) copy-start(bf16[512,1024]{1,0:T(8,128)(2,1)S(1)} %collective-permute-done.4.refs_7_) | copy-start | bytes 3145732
  18.1 1.0 copy-start.17
  31.6 38.6 %copy-start.26 = (s32[16,8]{0,1:T(8,128)S(1)}, s32[16,8]{0,1:T(8,128)}, u32[]{:S(2)}) copy-start(s32[16,8]{0,1:T(8,128)} %param.23) | copy-start | bytes 1540
  31.6 0.7 copy-start.14
  32.4 51.8 %collective-permute-start.22 = (bf16[256,2048]{1,0:T(8,128)(2,1)S(1)}, bf16[256,2048]{1,0:T(8,128)(2,1)S(1)}, u32[]{:S(2)}, u32[]{:S(2)}) collective-permute-start(bf16[256,2048]{1,0:T(8,128)(2,1)S(1)} %copy-done), channel_id=1, source_target_pairs={{0,1},{1,0},{2,3},{3,2},{4,5},{5,4},{6,7},{7,6},{8,9},{9,8},{10,11... | collective-permute-start | bytes 3145736 | tf_op jit(solution)/shard_map/ppermute | solution.py:438
  32.4 8.6 %collective-permute-start.10 = (bf16[272,128]{1,0:T(8,128)(2,1)}, bf16[272,128]{1,0:T(8,128)(2,1)S(1)}, u32[]{:S(2)}, u32[]{:S(2)}) collective-permute-start(bf16[272,128]{1,0:T(8,128)(2,1)} %get-tuple-element.81), channel_id=1, source_target_pairs={{0,6},{1,7},{2,4},{3,5},{4,2},{5,3},{6,0},{7,1},{8,14},{9,15},{10,... | collective-permute-start | bytes 208904 | tf_op jit(solution)/shard_map/ppermute | solution.py:363
  35.4 10.1 %collective-permute-start.11 = (bf16[272,128]{1,0:T(8,128)(2,1)}, bf16[272,128]{1,0:T(8,128)(2,1)S(1)}, u32[]{:S(2)}, u32[]{:S(2)}) collective-permute-start(bf16[272,128]{1,0:T(8,128)(2,1)} %get-tuple-element.82), channel_id=1, source_target_pairs={{0,8},{1,9},{2,10},{3,11},{4,12},{5,13},{6,14},{7,15},{8,0},{9,1},... | collective-permute-start | bytes 208904 | tf_op jit(solution)/shard_map/ppermute | solution.py:363
  37.0 10.5 %collective-permute-start.12 = (bf16[272,128]{1,0:T(8,128)(2,1)}, bf16[272,128]{1,0:T(8,128)(2,1)S(1)}, u32[]{:S(2)}, u32[]{:S(2)}) collective-permute-start(bf16[272,128]{1,0:T(8,128)(2,1)} %get-tuple-element.83), channel_id=1, source_target_pairs={{0,10},{1,11},{2,8},{3,9},{4,14},{5,15},{6,12},{7,13},{8,2},{9,3},... | collective-permute-start | bytes 208904 | tf_op jit(solution)/shard_map/ppermute | solution.py:363
  38.4 63.5 %copy-start.27 = (bf16[2048]{0:T(1024)(128)(2,1)S(1)}, bf16[2048]{0:T(1024)(128)(2,1)}, u32[]{:S(2)}) copy-start(bf16[2048]{0:T(1024)(128)(2,1)} %param.22) | copy-start | bytes 12292
  38.6 25.9 %collective-permute-start.13 = (bf16[272,128]{1,0:T(8,128)(2,1)}, bf16[272,128]{1,0:T(8,128)(2,1)S(1)}, u32[]{:S(2)}, u32[]{:S(2)}) collective-permute-start(bf16[272,128]{1,0:T(8,128)(2,1)} %copy-done.21), channel_id=1, source_target_pairs={{0,12},{1,13},{2,14},{3,15},{4,8},{5,9},{6,10},{7,11},{8,4},{9,5},... | collective-permute-start | bytes 208904 | tf_op jit(solution)/shard_map/ppermute | solution.py:363
  41.0 23.5 %collective-permute-start.14 = (bf16[272,128]{1,0:T(8,128)(2,1)}, bf16[272,128]{1,0:T(8,128)(2,1)S(1)}, u32[]{:S(2)}, u32[]{:S(2)}) collective-permute-start(bf16[272,128]{1,0:T(8,128)(2,1)} %copy-done.20), channel_id=1, source_target_pairs={{0,14},{1,15},{2,12},{3,13},{4,10},{5,11},{6,8},{7,9},{8,6},{9,7},... | collective-permute-start | bytes 208904 | tf_op jit(solution)/shard_map/ppermute | solution.py:363
  45.5 19.6 %collective-permute-start.8 = (bf16[272,128]{1,0:T(8,128)(2,1)}, bf16[272,128]{1,0:T(8,128)(2,1)S(1)}, u32[]{:S(2)}, u32[]{:S(2)}) collective-permute-start(bf16[272,128]{1,0:T(8,128)(2,1)} %copy-done.19), channel_id=1, source_target_pairs={{0,2},{1,3},{2,0},{3,1},{4,6},{5,7},{6,4},{7,5},{8,10},{9,11},{10,... | collective-permute-start | bytes 208904 | tf_op jit(solution)/shard_map/ppermute | solution.py:363
  47.5 18.2 %collective-permute-start.9 = (bf16[272,128]{1,0:T(8,128)(2,1)}, bf16[272,128]{1,0:T(8,128)(2,1)S(1)}, u32[]{:S(2)}, u32[]{:S(2)}) collective-permute-start(bf16[272,128]{1,0:T(8,128)(2,1)} %copy-done.18), channel_id=1, source_target_pairs={{0,4},{1,5},{2,6},{3,7},{4,0},{5,1},{6,2},{7,3},{8,12},{9,13},{10,... | collective-permute-start | bytes 208904 | tf_op jit(solution)/shard_map/ppermute | solution.py:363
  48.1 0.9 copy-start.11
  49.1 1.2 copy-start.13
  50.3 0.9 copy-start.15
  66.4 7.4 %collective-permute-start.15 = (bf16[272,128]{1,0:T(8,128)(2,1)}, bf16[272,128]{1,0:T(8,128)(2,1)S(1)}, u32[]{:S(2)}, u32[]{:S(2)}) collective-permute-start(bf16[272,128]{1,0:T(8,128)(2,1)} %get-tuple-element.95), channel_id=1, source_target_pairs={{0,2},{1,3},{2,0},{3,1},{4,6},{5,7},{6,4},{7,5},{8,10},{9,11},{10,... | collective-permute-start | bytes 208904 | tf_op jit(solution)/shard_map/ppermute | solution.py:363
  68.2 7.6 %collective-permute-start.16 = (bf16[272,128]{1,0:T(8,128)(2,1)}, bf16[272,128]{1,0:T(8,128)(2,1)S(1)}, u32[]{:S(2)}, u32[]{:S(2)}) collective-permute-start(bf16[272,128]{1,0:T(8,128)(2,1)} %get-tuple-element.96), channel_id=1, source_target_pairs={{0,4},{1,5},{2,6},{3,7},{4,0},{5,1},{6,2},{7,3},{8,12},{9,13},{10,... | collective-permute-start | bytes 208904 | tf_op jit(solution)/shard_map/ppermute | solution.py:363
  70.2 6.6 %collective-permute-start.17 = (bf16[272,128]{1,0:T(8,128)(2,1)}, bf16[272,128]{1,0:T(8,128)(2,1)S(1)}, u32[]{:S(2)}, u32[]{:S(2)}) collective-permute-start(bf16[272,128]{1,0:T(8,128)(2,1)} %get-tuple-element.97), channel_id=1, source_target_pairs={{0,6},{1,7},{2,4},{3,5},{4,2},{5,3},{6,0},{7,1},{8,14},{9,15},{10,... | collective-permute-start | bytes 208904 | tf_op jit(solution)/shard_map/ppermute | solution.py:363
  70.4 9.9 %collective-permute-start.18 = (bf16[272,128]{1,0:T(8,128)(2,1)}, bf16[272,128]{1,0:T(8,128)(2,1)S(1)}, u32[]{:S(2)}, u32[]{:S(2)}) collective-permute-start(bf16[272,128]{1,0:T(8,128)(2,1)} %copy-done.25), channel_id=1, source_target_pairs={{0,8},{1,9},{2,10},{3,11},{4,12},{5,13},{6,14},{7,15},{8,0},{9,1},... | collective-permute-start | bytes 208904 | tf_op jit(solution)/shard_map/ppermute | solution.py:363
  73.7 10.5 %collective-permute-start.19 = (bf16[272,128]{1,0:T(8,128)(2,1)}, bf16[272,128]{1,0:T(8,128)(2,1)S(1)}, u32[]{:S(2)}, u32[]{:S(2)}) collective-permute-start(bf16[272,128]{1,0:T(8,128)(2,1)} %copy-done.24), channel_id=1, source_target_pairs={{0,10},{1,11},{2,8},{3,9},{4,14},{5,15},{6,12},{7,13},{8,2},{9,3},... | collective-permute-start | bytes 208904 | tf_op jit(solution)/shard_map/ppermute | solution.py:363
  75.8 8.4 %collective-permute-start.20 = (bf16[272,128]{1,0:T(8,128)(2,1)}, bf16[272,128]{1,0:T(8,128)(2,1)S(1)}, u32[]{:S(2)}, u32[]{:S(2)}) collective-permute-start(bf16[272,128]{1,0:T(8,128)(2,1)} %copy-done.23), channel_id=1, source_target_pairs={{0,12},{1,13},{2,14},{3,15},{4,8},{5,9},{6,10},{7,11},{8,4},{9,5},... | collective-permute-start | bytes 208904 | tf_op jit(solution)/shard_map/ppermute | solution.py:363
  76.8 7.4 %collective-permute-start.21 = (bf16[272,128]{1,0:T(8,128)(2,1)}, bf16[272,128]{1,0:T(8,128)(2,1)S(1)}, u32[]{:S(2)}, u32[]{:S(2)}) collective-permute-start(bf16[272,128]{1,0:T(8,128)(2,1)} %copy-done.22), channel_id=1, source_target_pairs={{0,14},{1,15},{2,12},{3,13},{4,10},{5,11},{6,8},{7,9},{8,6},{9,7},... | collective-permute-start | bytes 208904 | tf_op jit(solution)/shard_map/ppermute | solution.py:363
  84.2 0.9 copy-start.2
  85.1 0.9 copy-start.4
  86.0 0.9 copy-start.6
  86.9 0.9 copy-start.8
  89.7 7.6 %collective-permute-start.23 = (bf16[16,2048]{1,0:T(8,128)(2,1)S(1)}, bf16[16,2048]{1,0:T(8,128)(2,1)S(1)}, u32[]{:S(2)}, u32[]{:S(2)}) collective-permute-start(bf16[16,2048]{1,0:T(8,128)(2,1)S(1)} %get-tuple-element.104), channel_id=1, source_target_pairs={{0,2},{1,3},{2,0},{3,1},{4,6},{5,7},{6,4},{7,5},{8,10},{9,11},{10,... | collective-permute-start | bytes 196616 | tf_op jit(solution)/shard_map/ppermute | solution.py:363
  90.4 8.9 %collective-permute-start.24 = (bf16[16,2048]{1,0:T(8,128)(2,1)S(1)}, bf16[16,2048]{1,0:T(8,128)(2,1)S(1)}, u32[]{:S(2)}, u32[]{:S(2)}) collective-permute-start(bf16[16,2048]{1,0:T(8,128)(2,1)S(1)} %get-tuple-element.105), channel_id=1, source_target_pairs={{0,4},{1,5},{2,6},{3,7},{4,0},{5,1},{6,2},{7,3},{8,12},{9,13},{10,... | collective-permute-start | bytes 196616 | tf_op jit(solution)/shard_map/ppermute | solution.py:363
  93.5 8.4 %collective-permute-start.25 = (bf16[16,2048]{1,0:T(8,128)(2,1)S(1)}, bf16[16,2048]{1,0:T(8,128)(2,1)S(1)}, u32[]{:S(2)}, u32[]{:S(2)}) collective-permute-start(bf16[16,2048]{1,0:T(8,128)(2,1)S(1)} %get-tuple-element.106), channel_id=1, source_target_pairs={{0,6},{1,7},{2,4},{3,5},{4,2},{5,3},{6,0},{7,1},{8,14},{9,15},{10,... | collective-permute-start | bytes 196616 | tf_op jit(solution)/shard_map/ppermute | solution.py:363
  93.9 10.0 %collective-permute-start.26 = (bf16[16,2048]{1,0:T(8,128)(2,1)}, bf16[16,2048]{1,0:T(8,128)(2,1)S(1)}, u32[]{:S(2)}, u32[]{:S(2)}) collective-permute-start(bf16[16,2048]{1,0:T(8,128)(2,1)} %get-tuple-element.107), channel_id=1, source_target_pairs={{0,8},{1,9},{2,10},{3,11},{4,12},{5,13},{6,14},{7,15},{8,0},{9,1},... | collective-permute-start | bytes 196616 | tf_op jit(solution)/shard_map/ppermute | solution.py:363
  96.3 11.0 %collective-permute-start.27 = (bf16[16,2048]{1,0:T(8,128)(2,1)}, bf16[16,2048]{1,0:T(8,128)(2,1)S(1)}, u32[]{:S(2)}, u32[]{:S(2)}) collective-permute-start(bf16[16,2048]{1,0:T(8,128)(2,1)} %get-tuple-element.108), channel_id=1, source_target_pairs={{0,10},{1,11},{2,8},{3,9},{4,14},{5,15},{6,12},{7,13},{8,2},{9,3},... | collective-permute-start | bytes 196616 | tf_op jit(solution)/shard_map/ppermute | solution.py:363
  97.3 9.9 %collective-permute-start.28 = (bf16[16,2048]{1,0:T(8,128)(2,1)}, bf16[16,2048]{1,0:T(8,128)(2,1)S(1)}, u32[]{:S(2)}, u32[]{:S(2)}) collective-permute-start(bf16[16,2048]{1,0:T(8,128)(2,1)} %get-tuple-element.109), channel_id=1, source_target_pairs={{0,12},{1,13},{2,14},{3,15},{4,8},{5,9},{6,10},{7,11},{8,4},{9,5},... | collective-permute-start | bytes 196616 | tf_op jit(solution)/shard_map/ppermute | solution.py:363
  99.3 8.0 %collective-permute-start.29 = (bf16[16,2048]{1,0:T(8,128)(2,1)}, bf16[16,2048]{1,0:T(8,128)(2,1)S(1)}, u32[]{:S(2)}, u32[]{:S(2)}) collective-permute-start(bf16[16,2048]{1,0:T(8,128)(2,1)} %get-tuple-element.110), channel_id=1, source_target_pairs={{0,14},{1,15},{2,12},{3,13},{4,10},{5,11},{6,8},{7,9},{8,6},{9,7},... | collective-permute-start | bytes 196616 | tf_op jit(solution)/shard_map/ppermute | solution.py:363
  107.3 0.8 copy-start.9
  127.4 12.0 %copy-start.28 = (f32[16,8]{0,1:T(8,128)S(1)}, f32[16,8]{0,1:T(8,128)}, u32[]{:S(2)}) copy-start(f32[16,8]{0,1:T(8,128)} %param.24) | copy-start | bytes 1540
  135.3 18.6 %all-to-all-start.1 = ((bf16[16,8,2048]{2,1,0:T(8,128)(2,1)}), bf16[16,8,2048]{2,1,0:T(8,128)(2,1)S(1)}, u32[]{:S(2)}, u32[]{:S(2)}) async-start(bf16[16,8,2048]{2,1,0:T(8,128)(2,1)} %bitcast.10), calls=%async_computation.1 | async-start | bytes 1048576 | tf_op jit(solution)/shard_map/all_to_all | solution.py:445
  (12 other events, 7.5 us)

commit v12 on v10

--- a/solution.py
+++ b/solution.py
@@ -34,8 +34,9 @@
     lens, row_ids, out, q_rows, q_turned, hidden, scores, probs = refs[-8:]
     chip, start_own, start_other, side_here, ring_here = place[0], place[1], place[2], place[4], place[5]
     near = rows // home_rows // 2
-    pack = HD // rows
-    groups = owner_heads // pack
+    block_rows = HD // owner_heads
+    blocks = rows // block_rows
+    spots = [(owner, block) for owner in range(owners) for block in range(blocks)]
 
     @pl.when(pl.program_id(0) == 0)
     def _():
@@ -54,19 +55,21 @@
         q_rows[pl.ds(pl.multiple_of(spot * home_rows, home_rows), home_rows), :] = piece[...]
 
     factor = LOG2E / math.sqrt(HD)
-    for n in range(owners * groups):
-        block = jnp.concatenate(
-            [q_rows[:, h * HD : (h + 1) * HD] for h in range(n * pack, (n + 1) * pack)], axis=0
+    for n, (owner, block) in enumerate(spots):
+        here = slice(block * block_rows, (block + 1) * block_rows)
+        first = owner * owner_heads
+        stacked = jnp.concatenate(
+            [q_rows[here, h * HD : (h + 1) * HD] for h in range(first, first + owner_heads)], axis=0
         )
-        scaled = block.T.astype(F32) * factor
+        scaled = stacked.T.astype(F32) * factor
         coarse = scaled.astype(BF16)
         q_turned[:HD, n * HD : (n + 1) * HD] = coarse
         q_turned[HD:, n * HD : (n + 1) * HD] = (scaled - coarse.astype(F32)).astype(BF16)
-    wide = owners * groups * HD
+    wide = len(spots) * HD
 
     def score(keys, at):
         s = nn_dot(jnp.concatenate([keys, keys], axis=1), q_turned[...])
-        return s + jnp.concatenate([hidden[at, :]] * (owners * groups), axis=1)
+        return s + jnp.concatenate([hidden[at, :]] * owners, axis=1)
 
     s_new = score(key_fresh[...], slice(2 * cache_here, 2 * cache_here + home_rows))
     run = jnp.max(s_new.reshape(home_rows // 8, 8, wide), axis=0)
@@ -89,12 +92,12 @@
     high = denom.astype(BF16).astype(F32)
     low = denom - high
     for owner in range(owners):
-        lanes = [slice((owner * groups + k) * HD, (owner * groups + k + 1) * HD) for k in range(groups)]
+        lanes = [slice(n * HD, (n + 1) * HD) for n in range(owner * blocks, (owner + 1) * blocks)]
         for k, cols in enumerate(lanes):
             out[owner, k * HD : (k + 1) * HD, :] = numer[:, cols].astype(BF16)
         filled = [kind[:, cols] for kind in (peak, high, low) for cols in lanes]
         filled += [jnp.zeros_like(filled[0])] * (STATS - len(filled))
-        out[owner, groups * HD :, :] = jnp.concatenate(filled, axis=0).astype(BF16)
+        out[owner, blocks * HD :, :] = jnp.concatenate(filled, axis=0).astype(BF16)
 
 
 def attention(place, query_blocks, keys, values, new_key, new_value, lens, row_ids, chips, kv_heads):
@@ -129,7 +132,7 @@
             scratch_shapes=[
                 pltpu.VMEM((rows, columns), BF16),
                 pltpu.VMEM((2 * HD, wide), BF16),
-                pltpu.VMEM((positions, HD), F32),
+                pltpu.VMEM((positions, wide // owners), F32),
                 pltpu.VMEM((2 * cache_here, wide), F32),
                 pltpu.VMEM((2 * cache_here, wide), BF16),
             ],
@@ -153,48 +156,50 @@
     )
 
 
-def project_body(rows, place, *refs):
-    *chunks, weight_own, weight_other, out, turned = refs
+def project_body(chunks_n, blocks_n, place, *refs):
+    chunks = refs[:chunks_n]
+    weight_own, weight_other, out, turned = refs[chunks_n:]
     core = place[3]
-    chips, height, _ = chunks[0].shape
-    base = height - STATS
-    groups = base // HD
-    pack = HD // rows
-    heads_here = groups * pack // CORES
-    half = chips // 2 // 2
-    for near in range(2):
-        sources = [chunks[s // 2 // half ^ near].at[s] for s in range(chips)]
-        stats = [part[base:, :].astype(F32) for part in sources]
-        peaks = [stat[:groups] for stat in stats]
-        top = functools.reduce(jnp.maximum, peaks)
-        share = [jnp.exp2(peak - top) for peak in peaks]
-        denom = sum(w * (t[groups : 2 * groups] + t[2 * groups : 3 * groups]) for w, t in zip(share, stats))
-        for k in range(groups):
-            numer = sum(
-                part[k * HD : (k + 1) * HD, :].astype(F32) * w[k : k + 1, :] for part, w in zip(sources, share)
-            )
-            attended = (numer / denom[k : k + 1, :]).T.astype(BF16)
-            for j in range(pack):
-                part, h = divmod(k * pack + j, heads_here)
-                turned[part, near * rows : (near + 1) * rows, h * HD : (h + 1) * HD] = attended[
-                    j * rows : (j + 1) * rows
-                ]
+    chips = chunks[0].shape[0]
+    heads_here = weight_own.shape[0] // HD
+    rows = HD // (CORES * heads_here)
+    block_chips = chips // blocks_n
+    for block in range(blocks_n):
+        sources, stats = [], []
+        for s in range(chips):
+            chunk = (s // block_chips ^ block).bit_length()
+            held = chunks[chunk].at[s]
+            wide = (held.shape[0] - STATS) // HD
+            spot = block % wide
+            sources.append(held.at[spot * HD : (spot + 1) * HD])
+            stat = held[wide * HD :, :].astype(F32)
+            stats.append([stat[kind * wide + spot : kind * wide + spot + 1] for kind in range(3)])
+        top = functools.reduce(jnp.maximum, [peak for peak, _, _ in stats])
+        share = [jnp.exp2(peak - top) for peak, _, _ in stats]
+        denom = sum(w * (high + low) for w, (_, high, low) in zip(share, stats))
+        numer = sum(source[...].astype(F32) * w for source, w in zip(sources, share))
+        attended = (numer / denom).T.astype(BF16)
+        for h in range(CORES * heads_here):
+            part, column = divmod(h, heads_here)
+            turned[part, block * rows : (block + 1) * rows, column * HD : (column + 1) * HD] = attended[
+                h * rows : (h + 1) * rows
+            ]
     product = nn_dot(turned[core], weight_own[...]) + nn_dot(turned[1 - core], weight_other[...])
     out[...] = product.astype(BF16)
 
 
-def project(place, chunks, weight_own, weight_other, rows):
+def project(place, chunks, weight_own, weight_other, rows, blocks):
     depth, width = weight_own.shape
     vmem = pl.BlockSpec(memory_space=pltpu.VMEM)
     return pl.pallas_call(
-        functools.partial(project_body, rows),
+        functools.partial(project_body, len(chunks), blocks),
         in_specs=[pl.BlockSpec(memory_space=pltpu.SMEM)] + [vmem] * (len(chunks) + 2),
         out_specs=vmem,
-        out_shape=jax.ShapeDtypeStruct((2 * rows, width), BF16),
-        scratch_shapes=[pltpu.VMEM((CORES, 2 * rows, depth), BF16)],
+        out_shape=jax.ShapeDtypeStruct((rows, width), BF16),
+        scratch_shapes=[pltpu.VMEM((CORES, rows, depth), BF16)],
         compiler_params=pltpu.CompilerParams(vmem_limit_bytes=32 * MIB),
         cost_estimate=pl.CostEstimate(
-            flops=8 * rows * width * depth, bytes_accessed=4 * MIB, transcendentals=0
+            flops=4 * rows * width * depth, bytes_accessed=4 * MIB, transcendentals=0
         ),
         name="project",
     )(place, *chunks, weight_own, weight_other)
@@ -345,40 +350,43 @@
 
     across = [(i, i ^ CORES) for i in range(devices)]
     rings = chips // 2
-    half = rings // 2
-    chunk_rows = 2 * half * home_rows
-
-    def across_y(block):
-        return lax.ppermute(block, "ctx", across)
-
-    neighbour = across_y(queries)
+    block_rings = max(1, HD // (CORES * heads_here * 2 * home_rows))
+    steps = [(0, block_rings)]
+    while sum(steps[-1]) < rings:
+        steps.append((sum(steps[-1]), sum(steps[-1])))
+
     by_ring = [queries] + [
         lax.ppermute(queries, "ctx", [(i, i ^ (2 * CORES * k)) for i in range(devices)])
         for k in range(1, rings)
     ]
-    near_blocks = [(pltpu.with_memory_space_constraint(queries, pltpu.HBM), 0)]
-    near_blocks += [(block, 0) for block in by_ring[1:half]]
-    near_blocks += [(neighbour, 0)] + [(across_y(block), 0) for block in by_ring[1:half]]
-    far = jnp.concatenate(by_ring[half:], axis=0)
-    far_across = across_y(far)
-    far_blocks = [(far, k) for k in range(half)] + [(far_across, k) for k in range(half)]
-    late_keys, late_values, _ = lax.optimization_barrier((key_cache, value_cache, neighbour))
-    key_other = lax.ppermute(late_keys, "ctx", swap)
-    value_turned = late_values.T
+    query_chunks = []
+
+    def gather_chunk(first, count):
+        mine = by_ring[first] if count == 1 else jnp.concatenate(by_ring[first : first + count], axis=0)
+        query_chunks.append((mine, lax.ppermute(mine, "ctx", across)))
+
+    for step in steps[:2]:
+        gather_chunk(*step)
+    key_other = lax.ppermute(key_cache, "ctx", swap)
+    value_turned = value_cache.T
     value_other = lax.ppermute(value_turned, "ctx", swap)
-    place = jnp.stack([chip, index * cache_here, (index ^ 1) * cache_here, core, chip % 2, chip // 2]).astype(jnp.int32)
-
-    def in_lanes(by_chip, n):
-        first = (chip // CORES // half ^ n) * chips // 2
-        here = lax.dynamic_slice_in_dim(by_chip, first, chips // 2, 0).reshape(1, chunk_rows)
-        return jnp.tile(here, (1, HD // chunk_rows))
+
+    place = jnp.stack(
+        [chip, index * cache_here, (index ^ 1) * cache_here, core, chip % 2, chip // 2]
+    ).astype(jnp.int32)
+
+    def in_lanes(by_chip, first, count):
+        base = (chip // 2 // count ^ first // count) * 2 * count
+        here = lax.dynamic_slice_in_dim(by_chip, base, 2 * count, 0)
+        here = here.reshape(count // block_rings, 2 * block_rings * home_rows)
+        return jnp.tile(here, (1, CORES * heads_here)).reshape(1, count // block_rings * HD)
 
     len_by_chip = lax.dynamic_slice_in_dim(
         cache_len.reshape(chips, CORES * home_rows), core * home_rows, home_rows, 1
     )
     number_by_chip = jnp.arange(chips * home_rows, dtype=jnp.int32).reshape(chips, home_rows)
-    lens = [in_lanes(len_by_chip, n) for n in range(2)]
-    row_ids = [in_lanes(number_by_chip, n) for n in range(2)]
+    lens = [in_lanes(len_by_chip, *step) for step in steps]
+    row_ids = [in_lanes(number_by_chip, *step) for step in steps]
 
     flat_ids = expert_ids.reshape(-1)
     picks = jnp.arange(flat_ids.shape[0])
@@ -393,30 +401,41 @@
     fine = (spread - coarse.astype(F32)).astype(BF16)
 
     gathered = []
-    for chunk, blocks in enumerate((near_blocks, far_blocks)):
+    for n, (_, count) in enumerate(steps):
+        mine, mine_across = query_chunks[n]
+        if count == 1 and n == 0:
+            mine = pltpu.with_memory_space_constraint(mine, pltpu.HBM)
         sums = attention(
             place,
-            blocks,
+            [(block, k) for block in (mine, mine_across) for k in range(count)],
             (key_cache, key_other),
             (value_turned, value_other),
             new_key,
             new_value,
-            lens[chunk],
-            row_ids[chunk],
+            lens[n],
+            row_ids[n],
             chips,
             key_cache.shape[1] // HD,
         )
-        if chunk:
+        if n:
             sums, gathered[-1] = lax.optimization_barrier((sums, gathered[-1]))
-        else:
-            sums, place, late_weight, _ = lax.optimization_barrier((sums, place, out_weight, far_across))
+        if n == 0:
+            sums, by_ring = lax.optimization_barrier((sums, by_ring))
+            for step in steps[2:]:
+                gather_chunk(*step)
+        if n + 1 < len(query_chunks):
+            sums, place, _ = lax.optimization_barrier((sums, place, query_chunks[n + 1][1]))
+        if n == 0:
+            sums, late_weight = lax.optimization_barrier((sums, out_weight))
         gathered.append(
             lax.all_to_all(
                 sums, "ctx", split_axis=0, concat_axis=0, axis_index_groups=same_core, tiled=True
             )
         )
     weight_other = lax.ppermute(late_weight, "ctx", swap)
-    share = project(place, gathered, out_weight, weight_other, chunk_rows)
+    share = project(
+        place, gathered, out_weight, weight_other, chips * home_rows, rings // block_rings
+    )
     shares = lax.all_to_all(
         share.reshape(chips, home_rows, width),
         "ctx",

time: 132 us -> 141 us (1.068)
  starting transfers between devices: 25.6 us -> 36 us
  waiting for transfers between devices: 52.4 us -> 44.1 us
  Pallas kernels: 31.7 us -> 37.2 us
    ppermute x3, waiting for transfers between devices: 6.34 us -> 0.01 us  [on_device(): lax.ppermute(queries, 'ctx', [(i, i ^ 2 * CORES * k) for i in range(devic...]
    all_to_all x2 -> x3, starting transfers between devices: 8.86 us -> 14.6 us  [on_device(): lax.all_to_all(sums, 'ctx', split_axis=0, concat_axis=0, axis_index_group...]
    pallas_call x2 -> x3, Pallas kernels: 19.8 us -> 25.2 us  [attention(): pl.pallas_call(functools.partial(attention_body, shape), grid_spec=pltpu....]
    ppermute x4, starting transfers between devices: 3.92 us -> 7.03 us  [the longest x3 6.57 us: gather_chunk(): query_chunks.append((mine, lax.ppermute(mine, 'ctx', across)))]
    all_to_all x2 -> x3, waiting for transfers between devices: 18.2 us -> 15.8 us  [on_device(): lax.all_to_all(sums, 'ctx', split_axis=0, concat_axis=0, axis_index_group...]
    ppermute x3, starting transfers between devices: 4.39 us -> 6.49 us  [on_device(): lax.ppermute(queries, 'ctx', [(i, i ^ 2 * CORES * k) for i in range(devic...]
    optimization_barrier x1 -> x0, local copies, waits for them, and re-layouts: 1.49 us -> none  [on_device(): lax.optimization_barrier((key_cache, value_cache, neighbour))]
    unnamed x13 -> x14, local copies, waits for them, and re-layouts: 0.17 us -> 1.66 us
  transfers between devices with their start and end apart: 13 -> 14, of which waited for: 5 -> 3; matrix products, arithmetic and copies ran while one was open for 3% -> 3% of each run, Pallas kernels for 15% -> 18%
where the time goes in v12:
time: 141 us; the launch traced here: 140 us
  waiting for transfers between devices  44.1 us (31%)
  Pallas kernels  37.2 us (26%)
  starting transfers between devices  36 us (26%)
  blocking collectives  18 us (13%)
  local copies, waits for them, and re-layouts  4 us (3%)
    pallas_call x3, Pallas kernels, attention(): pl.pallas_call(functools.partial(attention_body, shape), grid_spec=pltpu....  25.2 us
    all_to_all x1, blocking collectives, on_device(): lax.all_to_all(outgoing.reshape(devices, experts * MOST, width), 'ctx', s...  18 us
    all_to_all x3, waiting for transfers between devices, on_device(): lax.all_to_all(sums, 'ctx', split_axis=0, concat_axis=0, axis_index_group...  15.8 us
    all_to_all x3, starting transfers between devices, on_device(): lax.all_to_all(sums, 'ctx', split_axis=0, concat_axis=0, axis_index_group...  14.6 us
    all_to_all x1, waiting for transfers between devices, on_device(): lax.all_to_all(produced.reshape(devices, experts * MOST, width), 'ctx', s...  14.3 us
    all_to_all x1, waiting for transfers between devices, on_device(): lax.all_to_all(share.reshape(chips, home_rows, width), 'ctx', split_axis=...  14 us
    pallas_call x1, Pallas kernels, run_experts(): pl.pallas_call(functools.partial(experts_body, step), in_specs=[vmem] + [...  7.87 us
    ppermute x3, starting transfers between devices, gather_chunk(): query_chunks.append((mine, lax.ppermute(mine, 'ctx', across)))  6.57 us
  transfers between devices with their start and end apart: 14, of which 3 were waited for; matrix products, arithmetic and copies ran while one was open for 3% of the time, Pallas kernels for 18%

profile of v12, /device:TPU:0, one launch (start us, length us, event | category | flops | bytes accessed | tf_op | source)
XLA Modules:
  0.0 139.9 jit_solution(15486283524980778737)
XLA Ops:
  0.0 0.5 collective-permute-start.1
  0.5 1.5 %copy.23 = bf16[1024,512]{0,1:T(8,128)(2,1)S(1)} copy(bf16[1024,512]{1,0:T(8,128)(2,1)} %param.18) | data formatting | bytes 2097152 | tf_op args[4]
  1.9 0.1 collective-permute-start.2
  2.1 3.0 %collective-permute-start = (bf16[16,4096]{1,0:T(8,128)(2,1)}, bf16[16,4096]{1,0:T(8,128)(2,1)S(1)}, u32[]{:S(2)}, u32[]{:S(2)}) collective-permute-start(bf16[16,4096]{1,0:T(8,128)(2,1)} %refs_0_.1), channel_id=1, source_target_pairs={{0,2},{1,3},{2,0},{3,1},{4,6},{5,7},{6,4},{7,5},{8,10},{9,11},{10,... | collective-permute-start | bytes 393224 | tf_op jit(solution)/shard_map/ppermute | solution.py:366
  5.0 1.6 %collective-permute-start.3 = (bf16[16,4096]{1,0:T(8,128)(2,1)}, bf16[16,4096]{1,0:T(8,128)(2,1)S(1)}, u32[]{:S(2)}, u32[]{:S(2)}) collective-permute-start(bf16[16,4096]{1,0:T(8,128)(2,1)} %refs_0_.1), channel_id=1, source_target_pairs={{0,4},{1,5},{2,6},{3,7},{4,0},{5,1},{6,2},{7,3},{8,12},{9,13},{10,... | collective-permute-start | bytes 393224 | tf_op jit(solution)/shard_map/ppermute | solution.py:359
  6.6 2.6 %collective-permute-start.4 = (bf16[16,4096]{1,0:T(8,128)(2,1)}, bf16[16,4096]{1,0:T(8,128)(2,1)S(1)}, u32[]{:S(2)}, u32[]{:S(2)}) collective-permute-start(bf16[16,4096]{1,0:T(8,128)(2,1)} %refs_0_.1), channel_id=1, source_target_pairs={{0,8},{1,9},{2,10},{3,11},{4,12},{5,13},{6,14},{7,15},{8,0},{9,1},... | collective-permute-start | bytes 393224 | tf_op jit(solution)/shard_map/ppermute | solution.py:359
  9.2 0.8 reshape.82
  10.0 0.1 fusion.2
  10.0 0.1 tile.58
  10.1 0.1 tile.60.refs_8_
  10.2 0.1 tile.61
  10.3 0.1 tile.63.refs_9_
  10.4 0.1 stack.27.place
  10.5 2.3 %collective-permute-start.5 = (bf16[16,4096]{1,0:T(8,128)(2,1)}, bf16[16,4096]{1,0:T(8,128)(2,1)S(1)}, u32[]{:S(2)}, u32[]{:S(2)}) collective-permute-start(bf16[16,4096]{1,0:T(8,128)(2,1)} %refs_0_.1), channel_id=1, source_target_pairs={{0,12},{1,13},{2,14},{3,15},{4,8},{5,9},{6,10},{7,11},{8,4},{9,5},... | collective-permute-start | bytes 393224 | tf_op jit(solution)/shard_map/ppermute | solution.py:359
  12.8 1.5 %collective-permute-start.6 = (bf16[16,4096]{1,0:T(8,128)(2,1)S(1)}, bf16[16,4096]{1,0:T(8,128)(2,1)S(1)}, u32[]{:S(2)}, u32[]{:S(2)}) collective-permute-start(bf16[16,4096]{1,0:T(8,128)(2,1)S(1)} %collective-permute-done.3.refs_0_), channel_id=1, source_target_pairs={{0,2},{1,3},{2,0},{3,1},{4,6},{5,7},{6,4},{7,5},{8,10},{9,11},{10,... | collective-permute-start | bytes 393224 | tf_op jit(solution)/shard_map/ppermute | solution.py:366
  14.3 7.6 %attention.3 = bf16[8,144,128]{2,1,0:T(8,128)(2,1)} custom-call(s32[6]{0:T(128)S(1)} %stack.27.place, bf16[16,4096]{1,0:T(8,128)(2,1)} %refs_0_.1, bf16[16,4096]{1,0:T(8,128)(2,1)S(1)} %collective-permute-done.refs_1_, bf16[1024,512]{1,0:T(8,128)(2,1)} %refs_4_.1, bf16[1024,512]{1,0:T(8,128)(2,1)} %collective-permute-done.1.refs_3_.refs_5_, ...), custom_call_target="tpu_custom_call" | custom-call | flops 1610612736 | bytes 8388608 | tf_op jit(solution)/shard_map/attention/pallas_call | solution.py:118
  22.0 4.0 %all-to-all-start = ((bf16[8,144,128]{2,1,0:T(8,128)(2,1)}), bf16[8,144,128]{2,1,0:T(8,128)(2,1)S(1)}, u32[]{:S(2)}, u32[]{:S(2)}) async-start(bf16[8,144,128]{2,1,0:T(8,128)(2,1)} %attention.3), calls=%async_computation | async-start | bytes 589824 | tf_op jit(solution)/shard_map/all_to_all | solution.py:431
  26.0 2.1 %collective-permute-start.7 = (bf16[32,4096]{1,0:T(8,128)(2,1)S(1)}, bf16[32,4096]{1,0:T(8,128)(2,1)S(1)}, u32[]{:S(2)}, u32[]{:S(2)}) collective-permute-start(bf16[32,4096]{1,0:T(8,128)(2,1)S(1)} %constant_dynamic-update-slice_fusion.refs_0_.refs_1_), channel_id=1, source_target_pairs={{0,2},{1,3},{2,0},{3,1},{4,6},{5,7},{6,4},{7,5},{8,10},{9,11},{10,... | collective-permute-start | bytes 786440 | tf_op jit(solution)/shard_map/ppermute | solution.py:366
  28.1 0.1 tile.64
  28.2 0.1 tile.66.refs_8_
  28.3 0.1 tile.67
  28.4 0.1 tile.69.refs_9_
  28.5 7.6 %attention.4 = bf16[8,144,128]{2,1,0:T(8,128)(2,1)} custom-call(s32[6]{0:T(128)S(1)} %stack.27.place, bf16[16,4096]{1,0:T(8,128)(2,1)S(1)} %collective-permute-done.3.refs_0_, bf16[16,4096]{1,0:T(8,128)(2,1)S(1)} %collective-permute-done.6.refs_1_, bf16[1024,512]{1,0:T(8,128)(2,1)} %refs_4_.1, bf16[1024,512]{1,0:T(8,128)(2,1)} %collective-permute-done.1.refs_3_.refs_5_, ...), custom_call_target="tpu_custom_call" | custom-call | flops 1610612736 | bytes 8388608 | tf_op jit(solution)/shard_map/attention/pallas_call | solution.py:118
  36.1 4.6 %all-to-all-start.1 = ((bf16[8,144,128]{2,1,0:T(8,128)(2,1)}), bf16[8,144,128]{2,1,0:T(8,128)(2,1)S(1)}, u32[]{:S(2)}, u32[]{:S(2)}) async-start(bf16[8,144,128]{2,1,0:T(8,128)(2,1)} %attention.4), calls=%async_computation.1 | async-start | bytes 589824 | tf_op jit(solution)/shard_map/all_to_all | solution.py:431
  40.6 0.1 dynamic_slice.23
  40.7 0.1 tile.70
  40.8 0.1 tile.72.refs_10_
  40.9 0.1 tile.73
  41.0 0.1 tile.75.refs_11_
  41.2 10.0 %attention.5 = bf16[8,272,128]{2,1,0:T(8,128)(2,1)} custom-call(s32[6]{0:T(128)S(1)} %stack.27.place, bf16[32,4096]{1,0:T(8,128)(2,1)S(1)} %constant_dynamic-update-slice_fusion.refs_0_.refs_1_, bf16[32,4096]{1,0:T(8,128)(2,1)S(1)} %constant_dynamic-update-slice_fusion.refs_0_.refs_1_, bf16[32,4096]{1,0:T(8,128)(2,1)S(1)} %collective-permute-done.7.refs_2_.refs_3_, ...), custom_call_target="tpu_custom_call" | custom-call | flops 3221225472 | bytes 8388608 | tf_op jit(solution)/shard_map/attention/pallas_call | solution.py:118
  51.2 6.0 %all-to-all-start.2 = ((bf16[8,272,128]{2,1,0:T(8,128)(2,1)}), bf16[8,272,128]{2,1,0:T(8,128)(2,1)S(1)}, u32[]{:S(2)}, u32[]{:S(2)}) async-start(bf16[8,272,128]{2,1,0:T(8,128)(2,1)} %attention.5), calls=%async_computation.2 | async-start | bytes 1114112 | tf_op jit(solution)/shard_map/all_to_all | solution.py:431
  57.2 15.8 %all-to-all-done.2.refs_2_ = bf16[8,272,128]{2,1,0:T(8,128)(2,1)S(1)} async-done(((bf16[8,272,128]{2,1,0:T(8,128)(2,1)}), bf16[8,272,128]{2,1,0:T(8,128)(2,1)S(1)}, u32[]{:S(2)}, u32[]{:S(2)}) %all-to-all-start.2) | async-done | bytes 557088 | tf_op jit(solution)/shard_map/all_to_all | solution.py:431
  73.0 2.8 %project.1 = bf16[128,2048]{1,0:T(8,128)(2,1)} custom-call(s32[6]{0:T(128)S(1)} %stack.27.place, bf16[8,144,128]{2,1,0:T(8,128)(2,1)S(1)} %all-to-all-done.refs_0_, bf16[8,144,128]{2,1,0:T(8,128)(2,1)S(1)} %all-to-all-done.1.refs_1_, bf16[8,272,128]{2,1,0:T(8,128)(2,1)S(1)} %all-to-all-done.2.refs_2_, bf16[256,2048]{1,0:T(8,128)(2,1)S(1)} %copy-done, ...), custom_call_target="tpu_custom_call" | custom-call | flops 268435456 | bytes 4194304 | tf_op jit(solution)/shard_map/project/pallas_call | solution.py:194
  75.8 3.6 %all-to-all-start.3 = ((bf16[8,16,2048]{2,1,0:T(8,128)(2,1)}), bf16[8,16,2048]{2,1,0:T(8,128)(2,1)S(1)}, u32[]{:S(2)}, u32[]{:S(2)}) async-start(bf16[8,16,2048]{2,1,0:T(8,128)(2,1)} %bitcast.7), calls=%async_computation.3 | async-start | bytes 1048576 | tf_op jit(solution)/shard_map/all_to_all | solution.py:439
  79.5 0.1 copy.24
  79.5 0.1 eq.31
  79.6 0.2 convert_reduce_fusion
  79.8 0.1 reduce_sum.21
  79.9 0.1 fusion
  80.0 0.1 copy.26
  80.2 14.0 %all-to-all-done.3.parts = bf16[8,16,2048]{2,1,0:T(8,128)(2,1)S(1)} async-done(((bf16[8,16,2048]{2,1,0:T(8,128)(2,1)}), bf16[8,16,2048]{2,1,0:T(8,128)(2,1)S(1)}, u32[]{:S(2)}, u32[]{:S(2)}) %all-to-all-start.3) | async-done | bytes 524320 | tf_op jit(solution)/shard_map/all_to_all | solution.py:439
  94.1 0.4 norm_and_dispatch.1
  94.6 18.0 %all_to_all.30 = bf16[16,8,2048]{2,1,0:T(8,128)(2,1)S(1)} all-to-all(bf16[16,8,2048]{2,1,0:T(8,128)(2,1)S(1)} %bitcast.19), channel_id=1, replica_groups=mesh['groups'=2,'ctx'=16] {'ctx'}, dimensions={0} | all-to-all | bytes 1048576 | tf_op jit(solution)/shard_map/all_to_all | solution.py:448
  112.6 7.9 %experts.1 = bf16[128,2048]{1,0:T(8,128)(2,1)} custom-call(bf16[128,2048]{1,0:T(8,128)(2,1)S(1)} %bitcast.13, bf16[2,2048,768]{2,1,0:T(8,128)(2,1)} %w_gate.1, bf16[2,2048,768]{2,1,0:T(8,128)(2,1)} %w_up.1, bf16[2,768,2048]{2,1,0:T(8,128)(2,1)} %w_down.1), custom_call_target="tpu_custom_call" | custom-call | flops 2415919104 | bytes 18874368 | tf_op jit(solution)/shard_map/experts/pallas_call | solution.py:285
  120.5 4.1 %all-to-all-start.5 = ((bf16[16,8,2048]{2,1,0:T(8,128)(2,1)}), bf16[16,8,2048]{2,1,0:T(8,128)(2,1)S(1)}, u32[]{:S(2)}, u32[]{:S(2)}) async-start(bf16[16,8,2048]{2,1,0:T(8,128)(2,1)} %bitcast.11), calls=%async_computation.5 | async-start | bytes 1048576 | tf_op jit(solution)/shard_map/all_to_all | solution.py:452
  124.7 0.1 select_reduce_fusion
  124.8 14.3 %all-to-all-done.5 = bf16[16,8,2048]{2,1,0:T(8,128)(2,1)S(1)} async-done(((bf16[16,8,2048]{2,1,0:T(8,128)(2,1)}), bf16[16,8,2048]{2,1,0:T(8,128)(2,1)S(1)}, u32[]{:S(2)}, u32[]{:S(2)}) %all-to-all-start.5) | async-done | bytes 524320 | tf_op jit(solution)/shard_map/all_to_all | solution.py:452
  139.0 0.9 mix.1
  (38 shorter events, 0.3 us)
Async XLA Ops:
  0.0 14.3 %collective-permute-start.1 = (bf16[1024,512]{1,0:T(8,128)(2,1)}, bf16[1024,512]{1,0:T(8,128)(2,1)}, u32[]{:S(2)}, u32[]{:S(2)}) collective-permute-start(bf16[1024,512]{1,0:T(8,128)(2,1)} %refs_4_.1), channel_id=1, source_target_pairs={{0,1},{1,0},{2,3},{3,2},{4,5},{5,4},{6,7},{7,6},{8,9},{9,8},{10,11... | collective-permute-start | bytes 3145736 | tf_op jit(solution)/shard_map/ppermute | solution.py:370
  1.9 12.4 %collective-permute-start.2 = (bf16[512,1024]{1,0:T(8,128)(2,1)S(1)}, bf16[512,1024]{1,0:T(8,128)(2,1)}, u32[]{:S(2)}, u32[]{:S(2)}) collective-permute-start(bf16[512,1024]{1,0:T(8,128)(2,1)S(1)} %bitcast.15), channel_id=1, source_target_pairs={{0,1},{1,0},{2,3},{3,2},{4,5},{5,4},{6,7},{7,6},{8,9},{9,8},{10,11... | collective-permute-start | bytes 3145736 | tf_op jit(solution)/shard_map/ppermute | solution.py:372
  2.1 8.4 %collective-permute-start = (bf16[16,4096]{1,0:T(8,128)(2,1)}, bf16[16,4096]{1,0:T(8,128)(2,1)S(1)}, u32[]{:S(2)}, u32[]{:S(2)}) collective-permute-start(bf16[16,4096]{1,0:T(8,128)(2,1)} %refs_0_.1), channel_id=1, source_target_pairs={{0,2},{1,3},{2,0},{3,1},{4,6},{5,7},{6,4},{7,5},{8,10},{9,11},{10,... | collective-permute-start | bytes 393224 | tf_op jit(solution)/shard_map/ppermute | solution.py:366
  5.0 7.8 %collective-permute-start.3 = (bf16[16,4096]{1,0:T(8,128)(2,1)}, bf16[16,4096]{1,0:T(8,128)(2,1)S(1)}, u32[]{:S(2)}, u32[]{:S(2)}) collective-permute-start(bf16[16,4096]{1,0:T(8,128)(2,1)} %refs_0_.1), channel_id=1, source_target_pairs={{0,4},{1,5},{2,6},{3,7},{4,0},{5,1},{6,2},{7,3},{8,12},{9,13},{10,... | collective-permute-start | bytes 393224 | tf_op jit(solution)/shard_map/ppermute | solution.py:359
  6.6 15.3 %collective-permute-start.4 = (bf16[16,4096]{1,0:T(8,128)(2,1)}, bf16[16,4096]{1,0:T(8,128)(2,1)S(1)}, u32[]{:S(2)}, u32[]{:S(2)}) collective-permute-start(bf16[16,4096]{1,0:T(8,128)(2,1)} %refs_0_.1), channel_id=1, source_target_pairs={{0,8},{1,9},{2,10},{3,11},{4,12},{5,13},{6,14},{7,15},{8,0},{9,1},... | collective-permute-start | bytes 393224 | tf_op jit(solution)/shard_map/ppermute | solution.py:359
  10.5 30.6 %copy-start = (bf16[256,2048]{1,0:T(8,128)(2,1)S(1)}, bf16[256,2048]{1,0:T(8,128)(2,1)}, u32[]{:S(2)}) copy-start(bf16[256,2048]{1,0:T(8,128)(2,1)} %refs_3_.1) | copy-start | bytes 3145732
  10.5 11.5 %collective-permute-start.5 = (bf16[16,4096]{1,0:T(8,128)(2,1)}, bf16[16,4096]{1,0:T(8,128)(2,1)S(1)}, u32[]{:S(2)}, u32[]{:S(2)}) collective-permute-start(bf16[16,4096]{1,0:T(8,128)(2,1)} %refs_0_.1), channel_id=1, source_target_pairs={{0,12},{1,13},{2,14},{3,15},{4,8},{5,9},{6,10},{7,11},{8,4},{9,5},... | collective-permute-start | bytes 393224 | tf_op jit(solution)/shard_map/ppermute | solution.py:359
  12.8 9.1 %collective-permute-start.6 = (bf16[16,4096]{1,0:T(8,128)(2,1)S(1)}, bf16[16,4096]{1,0:T(8,128)(2,1)S(1)}, u32[]{:S(2)}, u32[]{:S(2)}) collective-permute-start(bf16[16,4096]{1,0:T(8,128)(2,1)S(1)} %collective-permute-done.3.refs_0_), channel_id=1, source_target_pairs={{0,2},{1,3},{2,0},{3,1},{4,6},{5,7},{6,4},{7,5},{8,10},{9,11},{10,... | collective-permute-start | bytes 393224 | tf_op jit(solution)/shard_map/ppermute | solution.py:366
  22.0 14.1 %all-to-all-start = ((bf16[8,144,128]{2,1,0:T(8,128)(2,1)}), bf16[8,144,128]{2,1,0:T(8,128)(2,1)S(1)}, u32[]{:S(2)}, u32[]{:S(2)}) async-start(bf16[8,144,128]{2,1,0:T(8,128)(2,1)} %attention.3), calls=%async_computation | async-start | bytes 589824 | tf_op jit(solution)/shard_map/all_to_all | solution.py:431
  26.0 10.1 %collective-permute-start.7 = (bf16[32,4096]{1,0:T(8,128)(2,1)S(1)}, bf16[32,4096]{1,0:T(8,128)(2,1)S(1)}, u32[]{:S(2)}, u32[]{:S(2)}) collective-permute-start(bf16[32,4096]{1,0:T(8,128)(2,1)S(1)} %constant_dynamic-update-slice_fusion.refs_0_.refs_1_), channel_id=1, source_target_pairs={{0,2},{1,3},{2,0},{3,1},{4,6},{5,7},{6,4},{7,5},{8,10},{9,11},{10,... | collective-permute-start | bytes 786440 | tf_op jit(solution)/shard_map/ppermute | solution.py:366
  36.1 15.1 %all-to-all-start.1 = ((bf16[8,144,128]{2,1,0:T(8,128)(2,1)}), bf16[8,144,128]{2,1,0:T(8,128)(2,1)S(1)}, u32[]{:S(2)}, u32[]{:S(2)}) async-start(bf16[8,144,128]{2,1,0:T(8,128)(2,1)} %attention.4), calls=%async_computation.1 | async-start | bytes 589824 | tf_op jit(solution)/shard_map/all_to_all | solution.py:431
  41.1 38.4 %copy-start.2 = (bf16[2048]{0:T(1024)(128)(2,1)S(1)}, bf16[2048]{0:T(1024)(128)(2,1)}, u32[]{:S(2)}) copy-start(bf16[2048]{0:T(1024)(128)(2,1)} %param.22) | copy-start | bytes 12292
  41.1 38.4 %copy-start.3 = (s32[16,8]{0,1:T(8,128)S(1)}, s32[16,8]{0,1:T(8,128)}, u32[]{:S(2)}) copy-start(s32[16,8]{0,1:T(8,128)} %param.23) | copy-start | bytes 1540
  41.1 53.0 %copy-start.1 = (bf16[16,2048]{1,0:T(8,128)(2,1)S(1)}, bf16[16,2048]{1,0:T(8,128)(2,1)}, u32[]{:S(2)}) copy-start(bf16[16,2048]{1,0:T(8,128)(2,1)} %residual.1) | copy-start | bytes 196612
  41.1 16.1 %collective-permute-start.8 = (bf16[256,2048]{1,0:T(8,128)(2,1)S(1)}, bf16[256,2048]{1,0:T(8,128)(2,1)}, u32[]{:S(2)}, u32[]{:S(2)}) collective-permute-start(bf16[256,2048]{1,0:T(8,128)(2,1)S(1)} %copy-done), channel_id=1, source_target_pairs={{0,1},{1,0},{2,3},{3,2},{4,5},{5,4},{6,7},{7,6},{8,9},{9,8},{10,11... | collective-permute-start | bytes 3145736 | tf_op jit(solution)/shard_map/ppermute | solution.py:435
  51.2 21.8 %all-to-all-start.2 = ((bf16[8,272,128]{2,1,0:T(8,128)(2,1)}), bf16[8,272,128]{2,1,0:T(8,128)(2,1)S(1)}, u32[]{:S(2)}, u32[]{:S(2)}) async-start(bf16[8,272,128]{2,1,0:T(8,128)(2,1)} %attention.5), calls=%async_computation.2 | async-start | bytes 1114112 | tf_op jit(solution)/shard_map/all_to_all | solution.py:431
  75.8 18.3 %all-to-all-start.3 = ((bf16[8,16,2048]{2,1,0:T(8,128)(2,1)}), bf16[8,16,2048]{2,1,0:T(8,128)(2,1)S(1)}, u32[]{:S(2)}, u32[]{:S(2)}) async-start(bf16[8,16,2048]{2,1,0:T(8,128)(2,1)} %bitcast.7), calls=%async_computation.3 | async-start | bytes 1048576 | tf_op jit(solution)/shard_map/all_to_all | solution.py:439
  112.6 12.0 %copy-start.4 = (f32[16,8]{0,1:T(8,128)S(1)}, f32[16,8]{0,1:T(8,128)}, u32[]{:S(2)}) copy-start(f32[16,8]{0,1:T(8,128)} %param.24) | copy-start | bytes 1540
  120.5 18.6 %all-to-all-start.5 = ((bf16[16,8,2048]{2,1,0:T(8,128)(2,1)}), bf16[16,8,2048]{2,1,0:T(8,128)(2,1)S(1)}, u32[]{:S(2)}, u32[]{:S(2)}) async-start(bf16[16,8,2048]{2,1,0:T(8,128)(2,1)} %bitcast.11), calls=%async_computation.5 | async-start | bytes 1048576 | tf_op jit(solution)/shard_map/all_to_all | solution.py:452

commit v13 on v10

--- a/solution.py
+++ b/solution.py
@@ -29,7 +29,7 @@
 
 
 def attention_body(shape, place, *refs):
-    owners, owner_heads, home_rows, rows, cache_here, step = shape
+    key_heads, owners, owner_heads, home_rows, rows, cache_here, step = shape
     *query_refs, key_own, key_other, value_own, value_other, key_fresh, value_fresh = refs[:-8]
     lens, row_ids, out, q_rows, q_turned, hidden, scores, probs = refs[-8:]
     chip, start_own, start_other, side_here, ring_here = place[0], place[1], place[2], place[4], place[5]
@@ -54,7 +54,8 @@
         q_rows[pl.ds(pl.multiple_of(spot * home_rows, home_rows), home_rows), :] = piece[...]
 
     factor = LOG2E / math.sqrt(HD)
-    for n in range(owners * groups):
+    wide = owners * groups * HD
+    for n in range(key_heads * owners * groups):
         block = jnp.concatenate(
             [q_rows[:, h * HD : (h + 1) * HD] for h in range(n * pack, (n + 1) * pack)], axis=0
         )
@@ -62,70 +63,93 @@
         coarse = scaled.astype(BF16)
         q_turned[:HD, n * HD : (n + 1) * HD] = coarse
         q_turned[HD:, n * HD : (n + 1) * HD] = (scaled - coarse.astype(F32)).astype(BF16)
-    wide = owners * groups * HD
-
-    def score(keys, at):
-        s = nn_dot(jnp.concatenate([keys, keys], axis=1), q_turned[...])
+
+    each = range(key_heads)
+    heads = [slice(g * HD, (g + 1) * HD) for g in each]
+    across = [slice(g * wide, (g + 1) * wide) for g in each]
+
+    def score(g, keys, at):
+        s = nn_dot(jnp.concatenate([keys, keys], axis=1), q_turned[:, across[g]])
         return s + jnp.concatenate([hidden[at, :]] * (owners * groups), axis=1)
 
-    s_new = score(key_fresh[...], slice(2 * cache_here, 2 * cache_here + home_rows))
-    run = jnp.max(s_new.reshape(home_rows // 8, 8, wide), axis=0)
+    def most(s):
+        return jnp.max(s.reshape(s.shape[0] // 8, 8, wide), axis=0)
+
+    fresh_at = slice(2 * cache_here, 2 * cache_here + home_rows)
+    s_new = [score(g, key_fresh[:, heads[g]], fresh_at) for g in each]
+    run = [most(s) for s in s_new]
     pieces = [(part, i) for part in range(2) for i in range(0, cache_here, step)]
     for part, i in pieces:
         at = slice(part * cache_here + i, part * cache_here + i + step)
-        s = score((key_own, key_other)[part][i : i + step, :], at)
-        scores[at, :] = s
-        run = jnp.maximum(run, jnp.max(s.reshape(step // 8, 8, wide), axis=0))
-    peak = jnp.maximum(jnp.max(run, axis=0, keepdims=True), FLOOR).astype(BF16).astype(F32)
-    p_new = jnp.exp2((s_new - peak).astype(BF16))
+        for g in each:
+            s = score(g, (key_own, key_other)[part][i : i + step, heads[g]], at)
+            scores[at, across[g]] = s
+            run[g] = jnp.maximum(run[g], most(s))
+    peak = [
+        jnp.maximum(jnp.max(r, axis=0, keepdims=True), FLOOR).astype(BF16).astype(F32) for r in run
+    ]
     for part, i in pieces:
         at = slice(part * cache_here + i, part * cache_here + i + step)
-        probs[at, :] = jnp.exp2((scores[at, :] - peak).astype(BF16))
+        for g in each:
+            probs[at, across[g]] = jnp.exp2((scores[at, across[g]] - peak[g]).astype(BF16))
     ones = jnp.ones((STATS, cache_here), BF16)
-    sums = nn_dot(jnp.concatenate([value_own[...], ones], axis=0), probs[:cache_here, :])
-    sums = sums + nn_dot(jnp.concatenate([value_other[...], ones], axis=0), probs[cache_here:, :])
-    numer = sums[:HD] + nn_dot(value_fresh[...].astype(F32).T.astype(BF16), p_new)
-    denom = sums[HD : HD + 1] + jnp.sum(p_new.astype(F32), axis=0, keepdims=True)
-    high = denom.astype(BF16).astype(F32)
-    low = denom - high
-    for owner in range(owners):
-        lanes = [slice((owner * groups + k) * HD, (owner * groups + k + 1) * HD) for k in range(groups)]
-        for k, cols in enumerate(lanes):
-            out[owner, k * HD : (k + 1) * HD, :] = numer[:, cols].astype(BF16)
-        filled = [kind[:, cols] for kind in (peak, high, low) for cols in lanes]
-        filled += [jnp.zeros_like(filled[0])] * (STATS - len(filled))
-        out[owner, groups * HD :, :] = jnp.concatenate(filled, axis=0).astype(BF16)
+    sums = [
+        nn_dot(jnp.concatenate([value_own[heads[g], :], ones], axis=0), probs[:cache_here, across[g]])
+        for g in each
+    ]
+    sums = [
+        sums[g]
+        + nn_dot(jnp.concatenate([value_other[heads[g], :], ones], axis=0), probs[cache_here:, across[g]])
+        for g in each
+    ]
+    for g in each:
+        p_new = jnp.exp2((s_new[g] - peak[g]).astype(BF16))
+        values = value_fresh[:, heads[g]].astype(F32).T.astype(BF16)
+        numer = sums[g][:HD] + nn_dot(values, p_new)
+        denom = sums[g][HD : HD + 1] + jnp.sum(p_new.astype(F32), axis=0, keepdims=True)
+        high = denom.astype(BF16).astype(F32)
+        low = denom - high
+        for owner in range(owners):
+            spot = g * owners + owner
+            lanes = [slice((owner * groups + k) * HD, (owner * groups + k + 1) * HD) for k in range(groups)]
+            for k, cols in enumerate(lanes):
+                out[spot, k * HD : (k + 1) * HD, :] = numer[:, cols].astype(BF16)
+            filled = [kind[:, cols] for kind in (peak[g], high, low) for cols in lanes]
+            filled += [jnp.zeros_like(filled[0])] * (STATS - len(filled))
+            out[spot, groups * HD :, :] = jnp.concatenate(filled, axis=0).astype(BF16)
 
 
 def attention(place, query_blocks, keys, values, new_key, new_value, lens, row_ids, chips, kv_heads):
     home_rows = new_key.shape[0]
     rows = home_rows * len(query_blocks)
     cache_here = keys[0].shape[0]
+    together = 2
+    steps = kv_heads // together
     owners = chips // kv_heads
-    columns = query_blocks[0][0].shape[1] // kv_heads
-    owner_heads = columns // HD // owners
+    columns = query_blocks[0][0].shape[1] // steps
+    owner_heads = columns // HD // owners // together
     wide = rows * columns // HD
     height = owner_heads * rows + STATS
     step = 512
     positions = 2 * cache_here + home_rows
     kv = lambda g, place: (0, g)
     whole = lambda g, place: (0, 0)
-    shape = (owners, owner_heads, home_rows, rows, cache_here, step)
-    work = wide * kv_heads * 2 * cache_here
+    shape = (together, owners, owner_heads, home_rows, rows, cache_here, step)
+    work = wide * steps * 2 * cache_here
     return pl.pallas_call(
         functools.partial(attention_body, shape),
         grid_spec=pltpu.PrefetchScalarGridSpec(
             num_scalar_prefetch=1,
-            grid=(kv_heads,),
+            grid=(steps,),
             in_specs=[
                 pl.BlockSpec((home_rows, columns), functools.partial(lambda n, g, place: (n, g), n))
                 for _, n in query_blocks
             ]
-            + [pl.BlockSpec((cache_here, HD), kv)] * 2
-            + [pl.BlockSpec((HD, cache_here), lambda g, place: (g, 0))] * 2
-            + [pl.BlockSpec((home_rows, HD), kv)] * 2
+            + [pl.BlockSpec((cache_here, together * HD), kv)] * 2
+            + [pl.BlockSpec((together * HD, cache_here), lambda g, place: (g, 0))] * 2
+            + [pl.BlockSpec((home_rows, together * HD), kv)] * 2
             + [pl.BlockSpec(lens.shape, whole)] * 2,
-            out_specs=pl.BlockSpec((owners, height, HD), lambda g, place: (g, 0, 0)),
+            out_specs=pl.BlockSpec((together * owners, height, HD), lambda g, place: (g, 0, 0)),
             scratch_shapes=[
                 pltpu.VMEM((rows, columns), BF16),
                 pltpu.VMEM((2 * HD, wide), BF16),
@@ -135,7 +159,7 @@
             ],
         ),
         out_shape=jax.ShapeDtypeStruct((chips, height, HD), BF16),
-        compiler_params=pltpu.CompilerParams(vmem_limit_bytes=32 * MIB),
+        compiler_params=pltpu.CompilerParams(vmem_limit_bytes=40 * MIB),
         cost_estimate=pl.CostEstimate(
             flops=6 * work * HD, bytes_accessed=8 * MIB, transcendentals=work
         ),

time: 132 us -> 131 us (level)
  Pallas kernels: 31.7 us -> 30.2 us
    pallas_call x2, Pallas kernels: 19.8 us -> 18.3 us  [attention(): pl.pallas_call(functools.partial(attention_body, shape), grid_spec=pltpu....]
  transfers between devices with their start and end apart: 13 -> 13, of which waited for: 5 -> 5; matrix products, arithmetic and copies ran while one was open for 3% -> 3% of each run, Pallas kernels for 15% -> 14%
where the time goes in v13:
time: 131 us
  waiting for transfers between devices  52.6 us (40%)
  Pallas kernels  30.2 us (23%)
  starting transfers between devices  25.5 us (19%)
  blocking collectives  18 us (14%)
  local copies, waits for them, and re-layouts  3.58 us (3%)
    all_to_all x2, waiting for transfers between devices, on_device(): lax.all_to_all(sums, 'ctx', split_axis=0, concat_axis=0, axis_index_group...  18.7 us
    pallas_call x2, Pallas kernels, attention(): pl.pallas_call(functools.partial(attention_body, shape), grid_spec=pltpu....  18.3 us
    all_to_all x1, blocking collectives, on_device(): lax.all_to_all(outgoing.reshape(devices, experts * MOST, width), 'ctx', s...  18 us
    all_to_all x1, waiting for transfers between devices, on_device(): lax.all_to_all(produced.reshape(devices, experts * MOST, width), 'ctx', s...  14.3 us
    all_to_all x1, waiting for transfers between devices, on_device(): lax.all_to_all(share.reshape(chips, home_rows, width), 'ctx', split_axis=...  13.4 us
    all_to_all x2, starting transfers between devices, on_device(): lax.all_to_all(sums, 'ctx', split_axis=0, concat_axis=0, axis_index_group...  8.85 us
    pallas_call x1, Pallas kernels, run_experts(): pl.pallas_call(functools.partial(experts_body, step), in_specs=[vmem] + [...  7.86 us
    ppermute x3, waiting for transfers between devices, on_device(): lax.ppermute(queries, 'ctx', [(i, i ^ 2 * CORES * k) for i in range(devic...  6.34 us
  transfers between devices with their start and end apart: 13, of which 5 were waited for; matrix products, arithmetic and copies ran while one was open for 3% of the time, Pallas kernels for 14%

profile of v13, /device:TPU:0, one launch (start us, length us, event | category | flops | bytes accessed | tf_op | source)
XLA Modules:
  0.0 130.6 jit_solution(3359488877205657053)
XLA Ops:
  0.0 3.0 %collective-permute-start.1 = (bf16[16,4096]{1,0:T(8,128)(2,1)}, bf16[16,4096]{1,0:T(8,128)(2,1)S(1)}, u32[]{:S(2)}, u32[]{:S(2)}) collective-permute-start(bf16[16,4096]{1,0:T(8,128)(2,1)} %refs_0_.1), channel_id=1, source_target_pairs={{0,2},{1,3},{2,0},{3,1},{4,6},{5,7},{6,4},{7,5},{8,10},{9,11},{10,... | collective-permute-start | bytes 393224 | tf_op jit(solution)/shard_map/ppermute | solution.py:376
  3.0 1.6 %collective-permute-start = (bf16[16,4096]{1,0:T(8,128)(2,1)}, bf16[16,4096]{1,0:T(8,128)(2,1)S(1)}, u32[]{:S(2)}, u32[]{:S(2)}) collective-permute-start(bf16[16,4096]{1,0:T(8,128)(2,1)} %refs_0_.1), channel_id=1, source_target_pairs={{0,4},{1,5},{2,6},{3,7},{4,0},{5,1},{6,2},{7,3},{8,12},{9,13},{10,... | collective-permute-start | bytes 393224 | tf_op jit(solution)/shard_map/ppermute | solution.py:380
  4.5 2.6 %collective-permute-start.5 = (bf16[16,4096]{1,0:T(8,128)(2,1)}, bf16[16,4096]{1,0:T(8,128)(2,1)S(1)}, u32[]{:S(2)}, u32[]{:S(2)}) collective-permute-start(bf16[16,4096]{1,0:T(8,128)(2,1)} %refs_0_.1), channel_id=1, source_target_pairs={{0,8},{1,9},{2,10},{3,11},{4,12},{5,13},{6,14},{7,15},{8,0},{9,1},... | collective-permute-start | bytes 393224 | tf_op jit(solution)/shard_map/ppermute | solution.py:380
  7.1 0.2 collective-permute-start.6
  7.4 0.8 reshape.66
  8.1 0.1 collective-permute-start.3
  8.2 1.5 %copy.23 = bf16[1024,512]{0,1:T(8,128)(2,1)S(1)} copy(bf16[1024,512]{1,0:T(8,128)(2,1)} %param.18) | data formatting | bytes 2097152 | tf_op jit(solution)/shard_map/optimization_barrier | solution.py:389
  9.7 0.6 collective-permute-start.4
  10.2 0.1 fusion.2
  10.3 0.1 tile.40
  10.4 0.1 tile.42.refs_10_
  10.5 0.1 tile.43
  10.6 0.1 tile.45.refs_11_
  10.7 0.1 stack.27.place
  10.8 0.3 collective-permute-start.2
  11.1 6.3 %collective-permute-done.5 = bf16[16,4096]{1,0:T(8,128)(2,1)S(1)} collective-permute-done((bf16[16,4096]{1,0:T(8,128)(2,1)}, bf16[16,4096]{1,0:T(8,128)(2,1)S(1)}, u32[]{:S(2)}, u32[]{:S(2)}) %collective-permute-start.5) | collective-permute-done | bytes 131104 | tf_op jit(solution)/shard_map/ppermute | solution.py:380
  17.4 0.0 collective-permute-done.6
  17.5 0.0 copy-start
  17.5 0.6 collective-permute-start.7
  18.0 0.0 collective-permute-done.2.refs_3_
  18.1 9.2 %attention.2 = bf16[8,272,128]{2,1,0:T(8,128)(2,1)} custom-call(s32[6]{0:T(128)S(1)} %stack.27.place, bf16[16,4096]{1,0:T(8,128)(2,1)} %refs_0_.1, bf16[16,4096]{1,0:T(8,128)(2,1)S(1)} %collective-permute-done.refs_1_, bf16[16,4096]{1,0:T(8,128)(2,1)S(1)} %collective-permute-done.1.refs_2_, bf16[16,4096]{1,0:T(8,128)(2,1)S(1)} %collective-permute-done.2.refs_3_, ...), custom_call_target="tpu_custom_call" | custom-call | flops 3221225472 | bytes 8388608 | tf_op jit(solution)/shard_map/attention/pallas_call | solution.py:139
  27.2 5.2 %all-to-all-start = ((bf16[8,272,128]{2,1,0:T(8,128)(2,1)}), bf16[8,272,128]{2,1,0:T(8,128)(2,1)S(1)}, u32[]{:S(2)}, u32[]{:S(2)}) async-start(bf16[8,272,128]{2,1,0:T(8,128)(2,1)} %attention.2), calls=%async_computation | async-start | bytes 1114112 | tf_op jit(solution)/shard_map/all_to_all | solution.py:438
  32.4 0.1 tile.46
  32.5 0.1 tile.48.refs_10_
  32.6 0.1 tile.49
  32.6 0.1 tile.51.refs_11_
  32.7 0.1 collective-permute-start.8
  32.8 9.1 %attention.3 = bf16[8,272,128]{2,1,0:T(8,128)(2,1)} custom-call(s32[6]{0:T(128)S(1)} %stack.27.place, bf16[32,4096]{1,0:T(8,128)(2,1)S(1)} %constant_dynamic-update-slice_fusion.refs_0_.refs_1_, bf16[32,4096]{1,0:T(8,128)(2,1)S(1)} %constant_dynamic-update-slice_fusion.refs_0_.refs_1_, bf16[32,4096]{1,0:T(8,128)(2,1)S(1)} %collective-permute-done.7.refs_2_.refs_3_, ...), custom_call_target="tpu_custom_call" | custom-call | flops 3221225472 | bytes 8388608 | tf_op jit(solution)/shard_map/attention/pallas_call | solution.py:139
  42.0 4.2 %all-to-all-done.refs_0_ = bf16[8,272,128]{2,1,0:T(8,128)(2,1)S(1)} async-done(((bf16[8,272,128]{2,1,0:T(8,128)(2,1)}), bf16[8,272,128]{2,1,0:T(8,128)(2,1)S(1)}, u32[]{:S(2)}, u32[]{:S(2)}) %all-to-all-start) | async-done | bytes 557088 | tf_op jit(solution)/shard_map/all_to_all | solution.py:438
  46.2 3.7 %all-to-all-start.1 = ((bf16[8,272,128]{2,1,0:T(8,128)(2,1)}), bf16[8,272,128]{2,1,0:T(8,128)(2,1)S(1)}, u32[]{:S(2)}, u32[]{:S(2)}) async-start(bf16[8,272,128]{2,1,0:T(8,128)(2,1)} %attention.3), calls=%async_computation.1 | async-start | bytes 1114112 | tf_op jit(solution)/shard_map/all_to_all | solution.py:438
  49.9 14.4 %all-to-all-done.1.refs_1_ = bf16[8,272,128]{2,1,0:T(8,128)(2,1)S(1)} async-done(((bf16[8,272,128]{2,1,0:T(8,128)(2,1)}), bf16[8,272,128]{2,1,0:T(8,128)(2,1)S(1)}, u32[]{:S(2)}, u32[]{:S(2)}) %all-to-all-start.1) | async-done | bytes 557088 | tf_op jit(solution)/shard_map/all_to_all | solution.py:438
  64.3 2.8 %project.1 = bf16[128,2048]{1,0:T(8,128)(2,1)} custom-call(s32[6]{0:T(128)S(1)} %stack.27.place, bf16[8,272,128]{2,1,0:T(8,128)(2,1)S(1)} %all-to-all-done.refs_0_, bf16[8,272,128]{2,1,0:T(8,128)(2,1)S(1)} %all-to-all-done.1.refs_1_, bf16[256,2048]{1,0:T(8,128)(2,1)S(1)} %copy-done, bf16[256,2048]{1,0:T(8,128)(2,1)} %collective-permute-done.8.refs_3_), custom_call_target="tpu_custom_call" | custom-call | flops 268435456 | bytes 4194304 | tf_op jit(solution)/shard_map/project/pallas_call | solution.py:213
  67.1 3.6 %all-to-all-start.2 = ((bf16[8,16,2048]{2,1,0:T(8,128)(2,1)}), bf16[8,16,2048]{2,1,0:T(8,128)(2,1)S(1)}, u32[]{:S(2)}, u32[]{:S(2)}) async-start(bf16[8,16,2048]{2,1,0:T(8,128)(2,1)} %bitcast.7), calls=%async_computation.2 | async-start | bytes 1048576 | tf_op jit(solution)/shard_map/all_to_all | solution.py:444
  70.7 0.1 copy.24
  70.8 0.1 eq.31
  70.9 0.2 convert_reduce_fusion
  71.1 0.1 reduce_sum.21
  71.2 0.1 fusion
  71.3 0.1 copy.26
  71.4 13.4 %all-to-all-done.2.parts = bf16[8,16,2048]{2,1,0:T(8,128)(2,1)S(1)} async-done(((bf16[8,16,2048]{2,1,0:T(8,128)(2,1)}), bf16[8,16,2048]{2,1,0:T(8,128)(2,1)S(1)}, u32[]{:S(2)}, u32[]{:S(2)}) %all-to-all-start.2) | async-done | bytes 524320 | tf_op jit(solution)/shard_map/all_to_all | solution.py:444
  84.8 0.4 norm_and_dispatch.1
  85.2 18.0 %all_to_all.25 = bf16[16,8,2048]{2,1,0:T(8,128)(2,1)S(1)} all-to-all(bf16[16,8,2048]{2,1,0:T(8,128)(2,1)S(1)} %bitcast.18), channel_id=1, replica_groups=mesh['groups'=2,'ctx'=16] {'ctx'}, dimensions={0} | all-to-all | bytes 1048576 | tf_op jit(solution)/shard_map/all_to_all | solution.py:453
  103.2 7.9 %experts.1 = bf16[128,2048]{1,0:T(8,128)(2,1)} custom-call(bf16[128,2048]{1,0:T(8,128)(2,1)S(1)} %bitcast.13, bf16[2,2048,768]{2,1,0:T(8,128)(2,1)} %w_gate.1, bf16[2,2048,768]{2,1,0:T(8,128)(2,1)} %w_up.1, bf16[2,768,2048]{2,1,0:T(8,128)(2,1)} %w_down.1), custom_call_target="tpu_custom_call" | custom-call | flops 2415919104 | bytes 18874368 | tf_op jit(solution)/shard_map/experts/pallas_call | solution.py:304
  111.1 4.1 %all-to-all-start.4 = ((bf16[16,8,2048]{2,1,0:T(8,128)(2,1)}), bf16[16,8,2048]{2,1,0:T(8,128)(2,1)S(1)}, u32[]{:S(2)}, u32[]{:S(2)}) async-start(bf16[16,8,2048]{2,1,0:T(8,128)(2,1)} %bitcast.11), calls=%async_computation.4 | async-start | bytes 1048576 | tf_op jit(solution)/shard_map/all_to_all | solution.py:457
  115.2 0.1 copy.27
  115.3 0.1 select_reduce_fusion
  115.4 14.3 %all-to-all-done.4 = bf16[16,8,2048]{2,1,0:T(8,128)(2,1)S(1)} async-done(((bf16[16,8,2048]{2,1,0:T(8,128)(2,1)}), bf16[16,8,2048]{2,1,0:T(8,128)(2,1)S(1)}, u32[]{:S(2)}, u32[]{:S(2)}) %all-to-all-start.4) | async-done | bytes 524320 | tf_op jit(solution)/shard_map/all_to_all | solution.py:457
  129.7 0.9 mix.1
  (27 shorter events, 0.1 us)
Async XLA Ops:
  0.0 8.1 %collective-permute-start.1 = (bf16[16,4096]{1,0:T(8,128)(2,1)}, bf16[16,4096]{1,0:T(8,128)(2,1)S(1)}, u32[]{:S(2)}, u32[]{:S(2)}) collective-permute-start(bf16[16,4096]{1,0:T(8,128)(2,1)} %refs_0_.1), channel_id=1, source_target_pairs={{0,2},{1,3},{2,0},{3,1},{4,6},{5,7},{6,4},{7,5},{8,10},{9,11},{10,... | collective-permute-start | bytes 393224 | tf_op jit(solution)/shard_map/ppermute | solution.py:376
  3.0 7.8 %collective-permute-start = (bf16[16,4096]{1,0:T(8,128)(2,1)}, bf16[16,4096]{1,0:T(8,128)(2,1)S(1)}, u32[]{:S(2)}, u32[]{:S(2)}) collective-permute-start(bf16[16,4096]{1,0:T(8,128)(2,1)} %refs_0_.1), channel_id=1, source_target_pairs={{0,4},{1,5},{2,6},{3,7},{4,0},{5,1},{6,2},{7,3},{8,12},{9,13},{10,... | collective-permute-start | bytes 393224 | tf_op jit(solution)/shard_map/ppermute | solution.py:380
  4.5 12.9 %collective-permute-start.5 = (bf16[16,4096]{1,0:T(8,128)(2,1)}, bf16[16,4096]{1,0:T(8,128)(2,1)S(1)}, u32[]{:S(2)}, u32[]{:S(2)}) collective-permute-start(bf16[16,4096]{1,0:T(8,128)(2,1)} %refs_0_.1), channel_id=1, source_target_pairs={{0,8},{1,9},{2,10},{3,11},{4,12},{5,13},{6,14},{7,15},{8,0},{9,1},... | collective-permute-start | bytes 393224 | tf_op jit(solution)/shard_map/ppermute | solution.py:380
  7.1 10.3 %collective-permute-start.6 = (bf16[16,4096]{1,0:T(8,128)(2,1)}, bf16[16,4096]{1,0:T(8,128)(2,1)S(1)}, u32[]{:S(2)}, u32[]{:S(2)}) collective-permute-start(bf16[16,4096]{1,0:T(8,128)(2,1)} %refs_0_.1), channel_id=1, source_target_pairs={{0,12},{1,13},{2,14},{3,15},{4,8},{5,9},{6,10},{7,11},{8,4},{9,5},... | collective-permute-start | bytes 393224 | tf_op jit(solution)/shard_map/ppermute | solution.py:380
  8.1 9.9 %collective-permute-start.3 = (bf16[1024,512]{1,0:T(8,128)(2,1)}, bf16[1024,512]{1,0:T(8,128)(2,1)}, u32[]{:S(2)}, u32[]{:S(2)}) collective-permute-start(bf16[1024,512]{1,0:T(8,128)(2,1)} %refs_4_.3), channel_id=1, source_target_pairs={{0,1},{1,0},{2,3},{3,2},{4,5},{5,4},{6,7},{7,6},{8,9},{9,8},{10,11... | collective-permute-start | bytes 3145736 | tf_op jit(solution)/shard_map/ppermute | solution.py:390
  9.7 8.4 %collective-permute-start.4 = (bf16[512,1024]{1,0:T(8,128)(2,1)S(1)}, bf16[512,1024]{1,0:T(8,128)(2,1)}, u32[]{:S(2)}, u32[]{:S(2)}) collective-permute-start(bf16[512,1024]{1,0:T(8,128)(2,1)S(1)} %bitcast.15), channel_id=1, source_target_pairs={{0,1},{1,0},{2,3},{3,2},{4,5},{5,4},{6,7},{7,6},{8,9},{9,8},{10,11... | collective-permute-start | bytes 3145736 | tf_op jit(solution)/shard_map/ppermute | solution.py:392
  10.8 7.3 %collective-permute-start.2 = (bf16[16,4096]{1,0:T(8,128)(2,1)S(1)}, bf16[16,4096]{1,0:T(8,128)(2,1)S(1)}, u32[]{:S(2)}, u32[]{:S(2)}) collective-permute-start(bf16[16,4096]{1,0:T(8,128)(2,1)S(1)} %collective-permute-done.refs_1_), channel_id=1, source_target_pairs={{0,2},{1,3},{2,0},{3,1},{4,6},{5,7},{6,4},{7,5},{8,10},{9,11},{10,... | collective-permute-start | bytes 393224 | tf_op jit(solution)/shard_map/ppermute | solution.py:376
  17.5 15.3 %copy-start = (bf16[256,2048]{1,0:T(8,128)(2,1)S(1)}, bf16[256,2048]{1,0:T(8,128)(2,1)}, u32[]{:S(2)}) copy-start(bf16[256,2048]{1,0:T(8,128)(2,1)} %refs_2_.1) | copy-start | bytes 3145732
  17.5 9.7 %collective-permute-start.7 = (bf16[32,4096]{1,0:T(8,128)(2,1)S(1)}, bf16[32,4096]{1,0:T(8,128)(2,1)S(1)}, u32[]{:S(2)}, u32[]{:S(2)}) collective-permute-start(bf16[32,4096]{1,0:T(8,128)(2,1)S(1)} %constant_dynamic-update-slice_fusion.refs_0_.refs_1_), channel_id=1, source_target_pairs={{0,2},{1,3},{2,0},{3,1},{4,6},{5,7},{6,4},{7,5},{8,10},{9,11},{10,... | collective-permute-start | bytes 786440 | tf_op jit(solution)/shard_map/ppermute | solution.py:376
  27.2 19.0 %all-to-all-start = ((bf16[8,272,128]{2,1,0:T(8,128)(2,1)}), bf16[8,272,128]{2,1,0:T(8,128)(2,1)S(1)}, u32[]{:S(2)}, u32[]{:S(2)}) async-start(bf16[8,272,128]{2,1,0:T(8,128)(2,1)} %attention.2), calls=%async_computation | async-start | bytes 1114112 | tf_op jit(solution)/shard_map/all_to_all | solution.py:438
  32.7 38.0 %copy-start.2 = (bf16[2048]{0:T(1024)(128)(2,1)S(1)}, bf16[2048]{0:T(1024)(128)(2,1)}, u32[]{:S(2)}) copy-start(bf16[2048]{0:T(1024)(128)(2,1)} %param.22) | copy-start | bytes 12292
  32.7 38.0 %copy-start.3 = (s32[16,8]{0,1:T(8,128)S(1)}, s32[16,8]{0,1:T(8,128)}, u32[]{:S(2)}) copy-start(s32[16,8]{0,1:T(8,128)} %param.23) | copy-start | bytes 1540
  32.7 52.1 %copy-start.1 = (bf16[16,2048]{1,0:T(8,128)(2,1)S(1)}, bf16[16,2048]{1,0:T(8,128)(2,1)}, u32[]{:S(2)}) copy-start(bf16[16,2048]{1,0:T(8,128)(2,1)} %residual.1) | copy-start | bytes 196612
  32.7 17.1 %collective-permute-start.8 = (bf16[256,2048]{1,0:T(8,128)(2,1)S(1)}, bf16[256,2048]{1,0:T(8,128)(2,1)}, u32[]{:S(2)}, u32[]{:S(2)}) collective-permute-start(bf16[256,2048]{1,0:T(8,128)(2,1)S(1)} %copy-done), channel_id=1, source_target_pairs={{0,1},{1,0},{2,3},{3,2},{4,5},{5,4},{6,7},{7,6},{8,9},{9,8},{10,11... | collective-permute-start | bytes 3145736 | tf_op jit(solution)/shard_map/ppermute | solution.py:442
  46.2 18.1 %all-to-all-start.1 = ((bf16[8,272,128]{2,1,0:T(8,128)(2,1)}), bf16[8,272,128]{2,1,0:T(8,128)(2,1)S(1)}, u32[]{:S(2)}, u32[]{:S(2)}) async-start(bf16[8,272,128]{2,1,0:T(8,128)(2,1)} %attention.3), calls=%async_computation.1 | async-start | bytes 1114112 | tf_op jit(solution)/shard_map/all_to_all | solution.py:438
  67.1 17.7 %all-to-all-start.2 = ((bf16[8,16,2048]{2,1,0:T(8,128)(2,1)}), bf16[8,16,2048]{2,1,0:T(8,128)(2,1)S(1)}, u32[]{:S(2)}, u32[]{:S(2)}) async-start(bf16[8,16,2048]{2,1,0:T(8,128)(2,1)} %bitcast.7), calls=%async_computation.2 | async-start | bytes 1048576 | tf_op jit(solution)/shard_map/all_to_all | solution.py:444
  103.2 12.0 %copy-start.4 = (f32[16,8]{0,1:T(8,128)S(1)}, f32[16,8]{0,1:T(8,128)}, u32[]{:S(2)}) copy-start(f32[16,8]{0,1:T(8,128)} %param.24) | copy-start | bytes 1540
  111.1 18.6 %all-to-all-start.4 = ((bf16[16,8,2048]{2,1,0:T(8,128)(2,1)}), bf16[16,8,2048]{2,1,0:T(8,128)(2,1)S(1)}, u32[]{:S(2)}, u32[]{:S(2)}) async-start(bf16[16,8,2048]{2,1,0:T(8,128)(2,1)} %bitcast.11), calls=%async_computation.4 | async-start | bytes 1048576 | tf_op jit(solution)/shard_map/all_to_all | solution.py:457

commit v14 on v13

--- a/solution.py
+++ b/solution.py
@@ -30,12 +30,26 @@
 
 def attention_body(shape, place, *refs):
     key_heads, owners, owner_heads, home_rows, rows, cache_here, step = shape
-    *query_refs, key_own, key_other, value_own, value_other, key_fresh, value_fresh = refs[:-8]
-    lens, row_ids, out, q_rows, q_turned, hidden, scores, probs = refs[-8:]
+    *query_refs, key_own, key_other, value_own, value_other, key_fresh, value_fresh = refs[:-11]
+    lens, row_ids, out, q_rows, q_turned, hidden, scores, probs, keys_held, values_held, sems = refs[-11:]
     chip, start_own, start_other, side_here, ring_here = place[0], place[1], place[2], place[4], place[5]
     near = rows // home_rows // 2
     pack = HD // rows
     groups = owner_heads // pack
+    parts = [slice(part * cache_here, (part + 1) * cache_here) for part in range(2)]
+    key_copies = [
+        pltpu.make_async_copy(source, keys_held.at[parts[n], :], sems.at[n])
+        for n, source in enumerate((key_own, key_other))
+    ]
+    value_copies = [
+        pltpu.make_async_copy(source, values_held.at[n], sems.at[2 + n])
+        for n, source in enumerate((value_own, value_other))
+    ]
+
+    @pl.when(pl.program_id(0) == 0)
+    def _():
+        for copy in key_copies + value_copies:
+            copy.start()
 
     @pl.when(pl.program_id(0) == 0)
     def _():
@@ -64,8 +78,16 @@
         q_turned[:HD, n * HD : (n + 1) * HD] = coarse
         q_turned[HD:, n * HD : (n + 1) * HD] = (scaled - coarse.astype(F32)).astype(BF16)
 
+    @pl.when(pl.program_id(0) == 0)
+    def _():
+        for copy in key_copies:
+            copy.wait()
+
     each = range(key_heads)
     heads = [slice(g * HD, (g + 1) * HD) for g in each]
+    held = [
+        pl.ds(pl.multiple_of((pl.program_id(0) * key_heads + g) * HD, HD), HD) for g in each
+    ]
     across = [slice(g * wide, (g + 1) * wide) for g in each]
 
     def score(g, keys, at):
@@ -82,7 +104,7 @@
     for part, i in pieces:
         at = slice(part * cache_here + i, part * cache_here + i + step)
         for g in each:
-            s = score(g, (key_own, key_other)[part][i : i + step, heads[g]], at)
+            s = score(g, keys_held[at, held[g]], at)
             scores[at, across[g]] = s
             run[g] = jnp.maximum(run[g], most(s))
     peak = [
@@ -92,14 +114,19 @@
         at = slice(part * cache_here + i, part * cache_here + i + step)
         for g in each:
             probs[at, across[g]] = jnp.exp2((scores[at, across[g]] - peak[g]).astype(BF16))
+    @pl.when(pl.program_id(0) == 0)
+    def _():
+        for copy in value_copies:
+            copy.wait()
+
     ones = jnp.ones((STATS, cache_here), BF16)
     sums = [
-        nn_dot(jnp.concatenate([value_own[heads[g], :], ones], axis=0), probs[:cache_here, across[g]])
+        nn_dot(jnp.concatenate([values_held[0, held[g], :], ones], axis=0), probs[parts[0], across[g]])
         for g in each
     ]
     sums = [
         sums[g]
-        + nn_dot(jnp.concatenate([value_other[heads[g], :], ones], axis=0), probs[cache_here:, across[g]])
+        + nn_dot(jnp.concatenate([values_held[1, held[g], :], ones], axis=0), probs[parts[1], across[g]])
         for g in each
     ]
     for g in each:
@@ -145,8 +172,7 @@
                 pl.BlockSpec((home_rows, columns), functools.partial(lambda n, g, place: (n, g), n))
                 for _, n in query_blocks
             ]
-            + [pl.BlockSpec((cache_here, together * HD), kv)] * 2
-            + [pl.BlockSpec((together * HD, cache_here), lambda g, place: (g, 0))] * 2
+            + [pl.BlockSpec(memory_space=pl.ANY)] * 4
             + [pl.BlockSpec((home_rows, together * HD), kv)] * 2
             + [pl.BlockSpec(lens.shape, whole)] * 2,
             out_specs=pl.BlockSpec((together * owners, height, HD), lambda g, place: (g, 0, 0)),
@@ -156,6 +182,9 @@
                 pltpu.VMEM((positions, HD), F32),
                 pltpu.VMEM((2 * cache_here, wide), F32),
                 pltpu.VMEM((2 * cache_here, wide), BF16),
+                pltpu.VMEM((2 * cache_here, kv_heads * HD), BF16),
+                pltpu.VMEM((2, kv_heads * HD, cache_here), BF16),
+                pltpu.SemaphoreType.DMA((4,)),
             ],
         ),
         out_shape=jax.ShapeDtypeStruct((chips, height, HD), BF16),

time: 131 us -> 136 us (1.038)
  Pallas kernels: 30.2 us -> 34.4 us
    pallas_call x2, Pallas kernels: 18.3 us -> 22.5 us  [attention(): pl.pallas_call(functools.partial(attention_body, shape), grid_spec=pltpu....]
  transfers between devices with their start and end apart: 13 -> 13, of which waited for: 5 -> 5; matrix products, arithmetic and copies ran while one was open for 3% -> 3% of each run, Pallas kernels for 14% -> 17%
where the time goes in v14:
time: 136 us; the launch traced here: 135 us
  waiting for transfers between devices  52.6 us (39%)
  Pallas kernels  34.4 us (25%)
  starting transfers between devices  25.7 us (19%)
  blocking collectives  18 us (13%)
  local copies, waits for them, and re-layouts  3.58 us (3%)
    pallas_call x2, Pallas kernels, attention(): pl.pallas_call(functools.partial(attention_body, shape), grid_spec=pltpu....  22.5 us
    all_to_all x1, blocking collectives, on_device(): lax.all_to_all(outgoing.reshape(devices, experts * MOST, width), 'ctx', s...  18 us
    all_to_all x2, waiting for transfers between devices, on_device(): lax.all_to_all(sums, 'ctx', split_axis=0, concat_axis=0, axis_index_group...  18 us
    all_to_all x1, waiting for transfers between devices, on_device(): lax.all_to_all(produced.reshape(devices, experts * MOST, width), 'ctx', s...  14.3 us
    all_to_all x1, waiting for transfers between devices, on_device(): lax.all_to_all(share.reshape(chips, home_rows, width), 'ctx', split_axis=...  14 us
    all_to_all x2, starting transfers between devices, on_device(): lax.all_to_all(sums, 'ctx', split_axis=0, concat_axis=0, axis_index_group...  9.03 us
    pallas_call x1, Pallas kernels, run_experts(): pl.pallas_call(functools.partial(experts_body, step), in_specs=[vmem] + [...  7.86 us
    ppermute x3, waiting for transfers between devices, on_device(): lax.ppermute(queries, 'ctx', [(i, i ^ 2 * CORES * k) for i in range(devic...  6.34 us
  transfers between devices with their start and end apart: 13, of which 5 were waited for; matrix products, arithmetic and copies ran while one was open for 3% of the time, Pallas kernels for 17%

profile of v14, /device:TPU:0, one launch (start us, length us, event | category | flops | bytes accessed | tf_op | source)
XLA Modules:
  0.0 135.0 jit_solution(11960750701187122141)
XLA Ops:
  0.0 3.0 %collective-permute-start.1 = (bf16[16,4096]{1,0:T(8,128)(2,1)}, bf16[16,4096]{1,0:T(8,128)(2,1)S(1)}, u32[]{:S(2)}, u32[]{:S(2)}) collective-permute-start(bf16[16,4096]{1,0:T(8,128)(2,1)} %refs_0_.1), channel_id=1, source_target_pairs={{0,2},{1,3},{2,0},{3,1},{4,6},{5,7},{6,4},{7,5},{8,10},{9,11},{10,... | collective-permute-start | bytes 393224 | tf_op jit(solution)/shard_map/ppermute | solution.py:405
  3.0 1.6 %collective-permute-start = (bf16[16,4096]{1,0:T(8,128)(2,1)}, bf16[16,4096]{1,0:T(8,128)(2,1)S(1)}, u32[]{:S(2)}, u32[]{:S(2)}) collective-permute-start(bf16[16,4096]{1,0:T(8,128)(2,1)} %refs_0_.1), channel_id=1, source_target_pairs={{0,4},{1,5},{2,6},{3,7},{4,0},{5,1},{6,2},{7,3},{8,12},{9,13},{10,... | collective-permute-start | bytes 393224 | tf_op jit(solution)/shard_map/ppermute | solution.py:409
  4.5 2.6 %collective-permute-start.5 = (bf16[16,4096]{1,0:T(8,128)(2,1)}, bf16[16,4096]{1,0:T(8,128)(2,1)S(1)}, u32[]{:S(2)}, u32[]{:S(2)}) collective-permute-start(bf16[16,4096]{1,0:T(8,128)(2,1)} %refs_0_.1), channel_id=1, source_target_pairs={{0,8},{1,9},{2,10},{3,11},{4,12},{5,13},{6,14},{7,15},{8,0},{9,1},... | collective-permute-start | bytes 393224 | tf_op jit(solution)/shard_map/ppermute | solution.py:409
  7.1 0.2 collective-permute-start.6
  7.4 0.8 reshape.66
  8.1 0.0 collective-permute-done.1.refs_2_
  8.1 0.1 collective-permute-start.3
  8.2 1.5 %copy.23 = bf16[1024,512]{0,1:T(8,128)(2,1)S(1)} copy(bf16[1024,512]{1,0:T(8,128)(2,1)} %param.18) | data formatting | bytes 2097152 | tf_op jit(solution)/shard_map/optimization_barrier | solution.py:418
  9.7 0.6 collective-permute-start.4
  10.2 0.1 fusion.2
  10.3 0.1 tile.40
  10.4 0.1 tile.42.refs_10_
  10.5 0.1 tile.43
  10.6 0.1 tile.45.refs_11_
  10.7 0.1 stack.27.place
  10.8 0.0 collective-permute-done.refs_1_
  10.8 0.3 collective-permute-start.2
  11.1 6.3 %collective-permute-done.5 = bf16[16,4096]{1,0:T(8,128)(2,1)S(1)} collective-permute-done((bf16[16,4096]{1,0:T(8,128)(2,1)}, bf16[16,4096]{1,0:T(8,128)(2,1)S(1)}, u32[]{:S(2)}, u32[]{:S(2)}) %collective-permute-start.5) | collective-permute-done | bytes 131104 | tf_op jit(solution)/shard_map/ppermute | solution.py:409
  17.5 0.0 copy-start
  17.5 0.6 collective-permute-start.7
  18.1 11.3 %attention.2 = bf16[8,272,128]{2,1,0:T(8,128)(2,1)} custom-call(s32[6]{0:T(128)S(1)} %stack.27.place, bf16[16,4096]{1,0:T(8,128)(2,1)} %refs_0_.1, bf16[16,4096]{1,0:T(8,128)(2,1)S(1)} %collective-permute-done.refs_1_, bf16[16,4096]{1,0:T(8,128)(2,1)S(1)} %collective-permute-done.1.refs_2_, bf16[16,4096]{1,0:T(8,128)(2,1)S(1)} %collective-permute-done.2.refs_3_, ...), custom_call_target="tpu_custom_call" | custom-call | flops 3221225472 | bytes 8388608 | tf_op jit(solution)/shard_map/attention/pallas_call | solution.py:166
  29.4 5.2 %all-to-all-start = ((bf16[8,272,128]{2,1,0:T(8,128)(2,1)}), bf16[8,272,128]{2,1,0:T(8,128)(2,1)S(1)}, u32[]{:S(2)}, u32[]{:S(2)}) async-start(bf16[8,272,128]{2,1,0:T(8,128)(2,1)} %attention.2), calls=%async_computation | async-start | bytes 1114112 | tf_op jit(solution)/shard_map/all_to_all | solution.py:467
  34.6 0.1 tile.46
  34.6 0.1 tile.48.refs_10_
  34.7 0.1 tile.49
  34.8 0.1 tile.51.refs_11_
  34.9 0.1 collective-permute-start.8
  35.0 11.2 %attention.3 = bf16[8,272,128]{2,1,0:T(8,128)(2,1)} custom-call(s32[6]{0:T(128)S(1)} %stack.27.place, bf16[32,4096]{1,0:T(8,128)(2,1)S(1)} %constant_dynamic-update-slice_fusion.refs_0_.refs_1_, bf16[32,4096]{1,0:T(8,128)(2,1)S(1)} %constant_dynamic-update-slice_fusion.refs_0_.refs_1_, bf16[32,4096]{1,0:T(8,128)(2,1)S(1)} %collective-permute-done.7.refs_2_.refs_3_, ...), custom_call_target="tpu_custom_call" | custom-call | flops 3221225472 | bytes 8388608 | tf_op jit(solution)/shard_map/attention/pallas_call | solution.py:166
  46.2 2.2 %all-to-all-done.refs_0_ = bf16[8,272,128]{2,1,0:T(8,128)(2,1)S(1)} async-done(((bf16[8,272,128]{2,1,0:T(8,128)(2,1)}), bf16[8,272,128]{2,1,0:T(8,128)(2,1)S(1)}, u32[]{:S(2)}, u32[]{:S(2)}) %all-to-all-start) | async-done | bytes 557088 | tf_op jit(solution)/shard_map/all_to_all | solution.py:467
  48.4 3.9 %all-to-all-start.1 = ((bf16[8,272,128]{2,1,0:T(8,128)(2,1)}), bf16[8,272,128]{2,1,0:T(8,128)(2,1)S(1)}, u32[]{:S(2)}, u32[]{:S(2)}) async-start(bf16[8,272,128]{2,1,0:T(8,128)(2,1)} %attention.3), calls=%async_computation.1 | async-start | bytes 1114112 | tf_op jit(solution)/shard_map/all_to_all | solution.py:467
  52.2 15.8 %all-to-all-done.1.refs_1_ = bf16[8,272,128]{2,1,0:T(8,128)(2,1)S(1)} async-done(((bf16[8,272,128]{2,1,0:T(8,128)(2,1)}), bf16[8,272,128]{2,1,0:T(8,128)(2,1)S(1)}, u32[]{:S(2)}, u32[]{:S(2)}) %all-to-all-start.1) | async-done | bytes 557088 | tf_op jit(solution)/shard_map/all_to_all | solution.py:467
  68.1 2.8 %project.1 = bf16[128,2048]{1,0:T(8,128)(2,1)} custom-call(s32[6]{0:T(128)S(1)} %stack.27.place, bf16[8,272,128]{2,1,0:T(8,128)(2,1)S(1)} %all-to-all-done.refs_0_, bf16[8,272,128]{2,1,0:T(8,128)(2,1)S(1)} %all-to-all-done.1.refs_1_, bf16[256,2048]{1,0:T(8,128)(2,1)S(1)} %copy-done, bf16[256,2048]{1,0:T(8,128)(2,1)} %collective-permute-done.8.refs_3_), custom_call_target="tpu_custom_call" | custom-call | flops 268435456 | bytes 4194304 | tf_op jit(solution)/shard_map/project/pallas_call | solution.py:242
  70.8 3.6 %all-to-all-start.2 = ((bf16[8,16,2048]{2,1,0:T(8,128)(2,1)}), bf16[8,16,2048]{2,1,0:T(8,128)(2,1)S(1)}, u32[]{:S(2)}, u32[]{:S(2)}) async-start(bf16[8,16,2048]{2,1,0:T(8,128)(2,1)} %bitcast.7), calls=%async_computation.2 | async-start | bytes 1048576 | tf_op jit(solution)/shard_map/all_to_all | solution.py:473
  74.5 0.1 copy.24
  74.6 0.1 eq.31
  74.6 0.2 convert_reduce_fusion
  74.8 0.1 reduce_sum.21
  74.9 0.1 fusion
  75.1 0.1 copy.26
  75.2 14.0 %all-to-all-done.2.parts = bf16[8,16,2048]{2,1,0:T(8,128)(2,1)S(1)} async-done(((bf16[8,16,2048]{2,1,0:T(8,128)(2,1)}), bf16[8,16,2048]{2,1,0:T(8,128)(2,1)S(1)}, u32[]{:S(2)}, u32[]{:S(2)}) %all-to-all-start.2) | async-done | bytes 524320 | tf_op jit(solution)/shard_map/all_to_all | solution.py:473
  89.2 0.4 norm_and_dispatch.1
  89.6 18.0 %all_to_all.25 = bf16[16,8,2048]{2,1,0:T(8,128)(2,1)S(1)} all-to-all(bf16[16,8,2048]{2,1,0:T(8,128)(2,1)S(1)} %bitcast.18), channel_id=1, replica_groups=mesh['groups'=2,'ctx'=16] {'ctx'}, dimensions={0} | all-to-all | bytes 1048576 | tf_op jit(solution)/shard_map/all_to_all | solution.py:482
  107.6 7.9 %experts.1 = bf16[128,2048]{1,0:T(8,128)(2,1)} custom-call(bf16[128,2048]{1,0:T(8,128)(2,1)S(1)} %bitcast.13, bf16[2,2048,768]{2,1,0:T(8,128)(2,1)} %w_gate.1, bf16[2,2048,768]{2,1,0:T(8,128)(2,1)} %w_up.1, bf16[2,768,2048]{2,1,0:T(8,128)(2,1)} %w_down.1), custom_call_target="tpu_custom_call" | custom-call | flops 2415919104 | bytes 18874368 | tf_op jit(solution)/shard_map/experts/pallas_call | solution.py:333
  115.5 4.1 %all-to-all-start.4 = ((bf16[16,8,2048]{2,1,0:T(8,128)(2,1)}), bf16[16,8,2048]{2,1,0:T(8,128)(2,1)S(1)}, u32[]{:S(2)}, u32[]{:S(2)}) async-start(bf16[16,8,2048]{2,1,0:T(8,128)(2,1)} %bitcast.11), calls=%async_computation.4 | async-start | bytes 1048576 | tf_op jit(solution)/shard_map/all_to_all | solution.py:486
  119.6 0.1 copy.27
  119.7 0.1 select_reduce_fusion
  119.8 14.3 %all-to-all-done.4 = bf16[16,8,2048]{2,1,0:T(8,128)(2,1)S(1)} async-done(((bf16[16,8,2048]{2,1,0:T(8,128)(2,1)}), bf16[16,8,2048]{2,1,0:T(8,128)(2,1)S(1)}, u32[]{:S(2)}, u32[]{:S(2)}) %all-to-all-start.4) | async-done | bytes 524320 | tf_op jit(solution)/shard_map/all_to_all | solution.py:486
  134.1 0.9 mix.1
  (27 shorter events, 0.1 us)
Async XLA Ops:
  0.0 8.1 %collective-permute-start.1 = (bf16[16,4096]{1,0:T(8,128)(2,1)}, bf16[16,4096]{1,0:T(8,128)(2,1)S(1)}, u32[]{:S(2)}, u32[]{:S(2)}) collective-permute-start(bf16[16,4096]{1,0:T(8,128)(2,1)} %refs_0_.1), channel_id=1, source_target_pairs={{0,2},{1,3},{2,0},{3,1},{4,6},{5,7},{6,4},{7,5},{8,10},{9,11},{10,... | collective-permute-start | bytes 393224 | tf_op jit(solution)/shard_map/ppermute | solution.py:405
  3.0 7.8 %collective-permute-start = (bf16[16,4096]{1,0:T(8,128)(2,1)}, bf16[16,4096]{1,0:T(8,128)(2,1)S(1)}, u32[]{:S(2)}, u32[]{:S(2)}) collective-permute-start(bf16[16,4096]{1,0:T(8,128)(2,1)} %refs_0_.1), channel_id=1, source_target_pairs={{0,4},{1,5},{2,6},{3,7},{4,0},{5,1},{6,2},{7,3},{8,12},{9,13},{10,... | collective-permute-start | bytes 393224 | tf_op jit(solution)/shard_map/ppermute | solution.py:409
  4.5 12.9 %collective-permute-start.5 = (bf16[16,4096]{1,0:T(8,128)(2,1)}, bf16[16,4096]{1,0:T(8,128)(2,1)S(1)}, u32[]{:S(2)}, u32[]{:S(2)}) collective-permute-start(bf16[16,4096]{1,0:T(8,128)(2,1)} %refs_0_.1), channel_id=1, source_target_pairs={{0,8},{1,9},{2,10},{3,11},{4,12},{5,13},{6,14},{7,15},{8,0},{9,1},... | collective-permute-start | bytes 393224 | tf_op jit(solution)/shard_map/ppermute | solution.py:409
  7.1 10.3 %collective-permute-start.6 = (bf16[16,4096]{1,0:T(8,128)(2,1)}, bf16[16,4096]{1,0:T(8,128)(2,1)S(1)}, u32[]{:S(2)}, u32[]{:S(2)}) collective-permute-start(bf16[16,4096]{1,0:T(8,128)(2,1)} %refs_0_.1), channel_id=1, source_target_pairs={{0,12},{1,13},{2,14},{3,15},{4,8},{5,9},{6,10},{7,11},{8,4},{9,5},... | collective-permute-start | bytes 393224 | tf_op jit(solution)/shard_map/ppermute | solution.py:409
  8.1 9.9 %collective-permute-start.3 = (bf16[1024,512]{1,0:T(8,128)(2,1)}, bf16[1024,512]{1,0:T(8,128)(2,1)}, u32[]{:S(2)}, u32[]{:S(2)}) collective-permute-start(bf16[1024,512]{1,0:T(8,128)(2,1)} %refs_4_.3), channel_id=1, source_target_pairs={{0,1},{1,0},{2,3},{3,2},{4,5},{5,4},{6,7},{7,6},{8,9},{9,8},{10,11... | collective-permute-start | bytes 3145736 | tf_op jit(solution)/shard_map/ppermute | solution.py:419
  9.7 8.4 %collective-permute-start.4 = (bf16[512,1024]{1,0:T(8,128)(2,1)S(1)}, bf16[512,1024]{1,0:T(8,128)(2,1)}, u32[]{:S(2)}, u32[]{:S(2)}) collective-permute-start(bf16[512,1024]{1,0:T(8,128)(2,1)S(1)} %bitcast.15), channel_id=1, source_target_pairs={{0,1},{1,0},{2,3},{3,2},{4,5},{5,4},{6,7},{7,6},{8,9},{9,8},{10,11... | collective-permute-start | bytes 3145736 | tf_op jit(solution)/shard_map/ppermute | solution.py:421
  10.8 7.3 %collective-permute-start.2 = (bf16[16,4096]{1,0:T(8,128)(2,1)S(1)}, bf16[16,4096]{1,0:T(8,128)(2,1)S(1)}, u32[]{:S(2)}, u32[]{:S(2)}) collective-permute-start(bf16[16,4096]{1,0:T(8,128)(2,1)S(1)} %collective-permute-done.refs_1_), channel_id=1, source_target_pairs={{0,2},{1,3},{2,0},{3,1},{4,6},{5,7},{6,4},{7,5},{8,10},{9,11},{10,... | collective-permute-start | bytes 393224 | tf_op jit(solution)/shard_map/ppermute | solution.py:405
  17.5 17.4 %copy-start = (bf16[256,2048]{1,0:T(8,128)(2,1)S(1)}, bf16[256,2048]{1,0:T(8,128)(2,1)}, u32[]{:S(2)}) copy-start(bf16[256,2048]{1,0:T(8,128)(2,1)} %refs_2_.1) | copy-start | bytes 3145732
  17.5 11.9 %collective-permute-start.7 = (bf16[32,4096]{1,0:T(8,128)(2,1)S(1)}, bf16[32,4096]{1,0:T(8,128)(2,1)S(1)}, u32[]{:S(2)}, u32[]{:S(2)}) collective-permute-start(bf16[32,4096]{1,0:T(8,128)(2,1)S(1)} %constant_dynamic-update-slice_fusion.refs_0_.refs_1_), channel_id=1, source_target_pairs={{0,2},{1,3},{2,0},{3,1},{4,6},{5,7},{6,4},{7,5},{8,10},{9,11},{10,... | collective-permute-start | bytes 786440 | tf_op jit(solution)/shard_map/ppermute | solution.py:405
  29.4 19.0 %all-to-all-start = ((bf16[8,272,128]{2,1,0:T(8,128)(2,1)}), bf16[8,272,128]{2,1,0:T(8,128)(2,1)S(1)}, u32[]{:S(2)}, u32[]{:S(2)}) async-start(bf16[8,272,128]{2,1,0:T(8,128)(2,1)} %attention.2), calls=%async_computation | async-start | bytes 1114112 | tf_op jit(solution)/shard_map/all_to_all | solution.py:467
  34.9 39.6 %copy-start.2 = (bf16[2048]{0:T(1024)(128)(2,1)S(1)}, bf16[2048]{0:T(1024)(128)(2,1)}, u32[]{:S(2)}) copy-start(bf16[2048]{0:T(1024)(128)(2,1)} %param.22) | copy-start | bytes 12292
  34.9 39.6 %copy-start.3 = (s32[16,8]{0,1:T(8,128)S(1)}, s32[16,8]{0,1:T(8,128)}, u32[]{:S(2)}) copy-start(s32[16,8]{0,1:T(8,128)} %param.23) | copy-start | bytes 1540
  34.9 54.3 %copy-start.1 = (bf16[16,2048]{1,0:T(8,128)(2,1)S(1)}, bf16[16,2048]{1,0:T(8,128)(2,1)}, u32[]{:S(2)}) copy-start(bf16[16,2048]{1,0:T(8,128)(2,1)} %residual.1) | copy-start | bytes 196612
  34.9 17.3 %collective-permute-start.8 = (bf16[256,2048]{1,0:T(8,128)(2,1)S(1)}, bf16[256,2048]{1,0:T(8,128)(2,1)}, u32[]{:S(2)}, u32[]{:S(2)}) collective-permute-start(bf16[256,2048]{1,0:T(8,128)(2,1)S(1)} %copy-done), channel_id=1, source_target_pairs={{0,1},{1,0},{2,3},{3,2},{4,5},{5,4},{6,7},{7,6},{8,9},{9,8},{10,11... | collective-permute-start | bytes 3145736 | tf_op jit(solution)/shard_map/ppermute | solution.py:471
  48.4 19.7 %all-to-all-start.1 = ((bf16[8,272,128]{2,1,0:T(8,128)(2,1)}), bf16[8,272,128]{2,1,0:T(8,128)(2,1)S(1)}, u32[]{:S(2)}, u32[]{:S(2)}) async-start(bf16[8,272,128]{2,1,0:T(8,128)(2,1)} %attention.3), calls=%async_computation.1 | async-start | bytes 1114112 | tf_op jit(solution)/shard_map/all_to_all | solution.py:467
  70.8 18.3 %all-to-all-start.2 = ((bf16[8,16,2048]{2,1,0:T(8,128)(2,1)}), bf16[8,16,2048]{2,1,0:T(8,128)(2,1)S(1)}, u32[]{:S(2)}, u32[]{:S(2)}) async-start(bf16[8,16,2048]{2,1,0:T(8,128)(2,1)} %bitcast.7), calls=%async_computation.2 | async-start | bytes 1048576 | tf_op jit(solution)/shard_map/all_to_all | solution.py:473
  107.6 12.0 %copy-start.4 = (f32[16,8]{0,1:T(8,128)S(1)}, f32[16,8]{0,1:T(8,128)}, u32[]{:S(2)}) copy-start(f32[16,8]{0,1:T(8,128)} %param.24) | copy-start | bytes 1540
  115.5 18.6 %all-to-all-start.4 = ((bf16[16,8,2048]{2,1,0:T(8,128)(2,1)}), bf16[16,8,2048]{2,1,0:T(8,128)(2,1)S(1)}, u32[]{:S(2)}, u32[]{:S(2)}) async-start(bf16[16,8,2048]{2,1,0:T(8,128)(2,1)} %bitcast.11), calls=%async_computation.4 | async-start | bytes 1048576 | tf_op jit(solution)/shard_map/all_to_all | solution.py:486

commit v15 on v13

--- a/solution.py
+++ b/solution.py
@@ -94,12 +94,12 @@
             probs[at, across[g]] = jnp.exp2((scores[at, across[g]] - peak[g]).astype(BF16))
     ones = jnp.ones((STATS, cache_here), BF16)
     sums = [
-        nn_dot(jnp.concatenate([value_own[heads[g], :], ones], axis=0), probs[:cache_here, across[g]])
+        nn_dot(jnp.concatenate([value_own[:, heads[g]].T, ones], axis=0), probs[:cache_here, across[g]])
         for g in each
     ]
     sums = [
         sums[g]
-        + nn_dot(jnp.concatenate([value_other[heads[g], :], ones], axis=0), probs[cache_here:, across[g]])
+        + nn_dot(jnp.concatenate([value_other[:, heads[g]].T, ones], axis=0), probs[cache_here:, across[g]])
         for g in each
     ]
     for g in each:
@@ -145,8 +145,7 @@
                 pl.BlockSpec((home_rows, columns), functools.partial(lambda n, g, place: (n, g), n))
                 for _, n in query_blocks
             ]
-            + [pl.BlockSpec((cache_here, together * HD), kv)] * 2
-            + [pl.BlockSpec((together * HD, cache_here), lambda g, place: (g, 0))] * 2
+            + [pl.BlockSpec((cache_here, together * HD), kv)] * 4
             + [pl.BlockSpec((home_rows, together * HD), kv)] * 2
             + [pl.BlockSpec(lens.shape, whole)] * 2,
             out_specs=pl.BlockSpec((together * owners, height, HD), lambda g, place: (g, 0, 0)),
@@ -169,7 +168,8 @@
         *[block for block, _ in query_blocks],
         pltpu.with_memory_space_constraint(keys[0], pltpu.HBM),
         keys[1],
-        *values,
+        pltpu.with_memory_space_constraint(values[0], pltpu.HBM),
+        values[1],
         pltpu.with_memory_space_constraint(new_key, pltpu.HBM),
         pltpu.with_memory_space_constraint(new_value, pltpu.HBM),
         lens,
@@ -383,13 +383,9 @@
     near_blocks = [(pltpu.with_memory_space_constraint(queries, pltpu.HBM), 0)]
     near_blocks += [(block, 0) for block in by_ring[1:half]]
     near_blocks += [(neighbour, 0)] + [(across_y(block), 0) for block in by_ring[1:half]]
-    far = jnp.concatenate(by_ring[half:], axis=0)
-    far_across = across_y(far)
-    far_blocks = [(far, k) for k in range(half)] + [(far_across, k) for k in range(half)]
-    late_keys, late_values, _ = lax.optimization_barrier((key_cache, value_cache, neighbour))
-    key_other = lax.ppermute(late_keys, "ctx", swap)
-    value_turned = late_values.T
-    value_other = lax.ppermute(value_turned, "ctx", swap)
+    key_other = lax.ppermute(key_cache, "ctx", swap)
+    value_other = lax.ppermute(value_cache, "ctx", swap)
+
     place = jnp.stack([chip, index * cache_here, (index ^ 1) * cache_here, core, chip % 2, chip // 2]).astype(jnp.int32)
 
     def in_lanes(by_chip, n):
@@ -416,29 +412,32 @@
     coarse = spread.astype(BF16)
     fine = (spread - coarse.astype(F32)).astype(BF16)
 
-    gathered = []
-    for chunk, blocks in enumerate((near_blocks, far_blocks)):
-        sums = attention(
+    def attend(blocks, n, place):
+        return attention(
             place,
             blocks,
             (key_cache, key_other),
-            (value_turned, value_other),
+            (value_cache, value_other),
             new_key,
             new_value,
-            lens[chunk],
-            row_ids[chunk],
+            lens[n],
+            row_ids[n],
             chips,
             key_cache.shape[1] // HD,
         )
-        if chunk:
-            sums, gathered[-1] = lax.optimization_barrier((sums, gathered[-1]))
-        else:
-            sums, place, late_weight, _ = lax.optimization_barrier((sums, place, out_weight, far_across))
-        gathered.append(
-            lax.all_to_all(
-                sums, "ctx", split_axis=0, concat_axis=0, axis_index_groups=same_core, tiled=True
-            )
+
+    def to_owners(sums):
+        return lax.all_to_all(
+            sums, "ctx", split_axis=0, concat_axis=0, axis_index_groups=same_core, tiled=True
         )
+
+    sums = attend(near_blocks, 0, place)
+    sums, late_place, late_weight, far = lax.optimization_barrier((sums, place, out_weight, by_ring[half:]))
+    far_blocks = [(block, 0) for block in far] + [(across_y(block), 0) for block in far]
+    gathered = [to_owners(sums)]
+    sums = attend(far_blocks, 1, late_place)
+    sums, gathered[0] = lax.optimization_barrier((sums, gathered[0]))
+    gathered.append(to_owners(sums))
     weight_other = lax.ppermute(late_weight, "ctx", swap)
     share = project(place, gathered, out_weight, weight_other, chunk_rows)
     shares = lax.all_to_all(

time: 131 us -> 137 us (1.046)
  starting transfers between devices: 25.5 us -> 32.4 us
  local copies, waits for them, and re-layouts: 3.58 us -> 6.59 us
  waiting for transfers between devices: 52.6 us -> 50.3 us
    ppermute x3 -> x4, waiting for transfers between devices: 0.01 us -> 9.19 us  [across_y(): return lax.ppermute(block, 'ctx', across)]
    ppermute x3, waiting for transfers between devices: 6.34 us -> 0.01 us  [on_device(): lax.ppermute(queries, 'ctx', [(i, i ^ 2 * CORES * k) for i in range(devic...]
    all_to_all x2, waiting for transfers between devices: 18.7 us -> 13.8 us  [to_owners(): lax.all_to_all(sums, 'ctx', split_axis=0, concat_axis=0, axis_index_group...]
    ppermute x3, starting transfers between devices: 4.39 us -> 8.96 us  [on_device(): lax.ppermute(queries, 'ctx', [(i, i ^ 2 * CORES * k) for i in range(devic...]
    unnamed x13 -> x22, local copies, waits for them, and re-layouts: 0.17 us -> 3.43 us
    ppermute x3 -> x4, starting transfers between devices: 3.86 us -> 5.93 us  [across_y(): return lax.ppermute(block, 'ctx', across)]
    optimization_barrier x1 -> x0, local copies, waits for them, and re-layouts: 1.49 us -> none  [on_device(): lax.optimization_barrier((key_cache, value_cache, neighbour))]
  transfers between devices with their start and end apart: 13 -> 14, of which waited for: 5 -> 5; matrix products, arithmetic and copies ran while one was open for 3% -> 3% of each run, Pallas kernels for 14% -> 13%
where the time goes in v15:
time: 137 us
  waiting for transfers between devices  50.3 us (37%)
  starting transfers between devices  32.4 us (24%)
  Pallas kernels  28.9 us (21%)
  blocking collectives  18 us (13%)
  local copies, waits for them, and re-layouts  6.59 us (5%)
    all_to_all x1, blocking collectives, on_device(): lax.all_to_all(outgoing.reshape(devices, experts * MOST, width), 'ctx', s...  18 us
    pallas_call x2, Pallas kernels, attention(): pl.pallas_call(functools.partial(attention_body, shape), grid_spec=pltpu....  17.6 us
    all_to_all x1, waiting for transfers between devices, on_device(): lax.all_to_all(produced.reshape(devices, experts * MOST, width), 'ctx', s...  14.3 us
    all_to_all x2, waiting for transfers between devices, to_owners(): lax.all_to_all(sums, 'ctx', split_axis=0, concat_axis=0, axis_index_group...  13.8 us
    all_to_all x1, waiting for transfers between devices, on_device(): lax.all_to_all(share.reshape(chips, home_rows, width), 'ctx', split_axis=...  13 us
    ppermute x4, waiting for transfers between devices, across_y(): return lax.ppermute(block, 'ctx', across)  9.19 us
    all_to_all x2, starting transfers between devices, to_owners(): lax.all_to_all(sums, 'ctx', split_axis=0, concat_axis=0, axis_index_group...  9.17 us
    ppermute x3, starting transfers between devices, on_device(): lax.ppermute(queries, 'ctx', [(i, i ^ 2 * CORES * k) for i in range(devic...  8.96 us
  transfers between devices with their start and end apart: 14, of which 5 were waited for; matrix products, arithmetic and copies ran while one was open for 3% of the time, Pallas kernels for 13%

profile of v15, /device:TPU:0, one launch (start us, length us, event | category | flops | bytes accessed | tf_op | source)
XLA Modules:
  0.0 136.8 jit_solution(656959950915372662)
XLA Ops:
  0.0 0.5 collective-permute-start.3
  0.5 0.1 collective-permute-start.4
  0.5 3.0 %collective-permute-start = (bf16[16,4096]{1,0:T(8,128)(2,1)}, bf16[16,4096]{1,0:T(8,128)(2,1)S(1)}, u32[]{:S(2)}, u32[]{:S(2)}) collective-permute-start(bf16[16,4096]{1,0:T(8,128)(2,1)} %refs_0_.1), channel_id=1, source_target_pairs={{0,4},{1,5},{2,6},{3,7},{4,0},{5,1},{6,2},{7,3},{8,12},{9,13},{10,... | collective-permute-start | bytes 393224 | tf_op jit(solution)/shard_map/ppermute | solution.py:380
  3.5 1.5 %collective-permute-start.1 = (bf16[16,4096]{1,0:T(8,128)(2,1)}, bf16[16,4096]{1,0:T(8,128)(2,1)S(1)}, u32[]{:S(2)}, u32[]{:S(2)}) collective-permute-start(bf16[16,4096]{1,0:T(8,128)(2,1)} %refs_0_.1), channel_id=1, source_target_pairs={{0,2},{1,3},{2,0},{3,1},{4,6},{5,7},{6,4},{7,5},{8,10},{9,11},{10,... | collective-permute-start | bytes 393224 | tf_op jit(solution)/shard_map/ppermute | solution.py:376
  5.1 2.6 %collective-permute-start.5 = (bf16[16,4096]{1,0:T(8,128)(2,1)}, bf16[16,4096]{1,0:T(8,128)(2,1)S(1)}, u32[]{:S(2)}, u32[]{:S(2)}) collective-permute-start(bf16[16,4096]{1,0:T(8,128)(2,1)} %refs_0_.1), channel_id=1, source_target_pairs={{0,8},{1,9},{2,10},{3,11},{4,12},{5,13},{6,14},{7,15},{8,0},{9,1},... | collective-permute-start | bytes 393224 | tf_op jit(solution)/shard_map/ppermute | solution.py:380
  7.6 0.8 reshape.66
  8.4 2.3 %collective-permute-start.2 = (bf16[16,4096]{1,0:T(8,128)(2,1)S(1)}, bf16[16,4096]{1,0:T(8,128)(2,1)}, u32[]{:S(2)}, u32[]{:S(2)}) collective-permute-start(bf16[16,4096]{1,0:T(8,128)(2,1)S(1)} %collective-permute-done.refs_1_), channel_id=1, source_target_pairs={{0,2},{1,3},{2,0},{3,1},{4,6},{5,7},{6,4},{7,5},{8,10},{9,11},{10,... | collective-permute-start | bytes 393224 | tf_op jit(solution)/shard_map/ppermute | solution.py:376
  10.8 0.1 fusion.2
  10.8 0.1 tile.40
  10.9 0.1 tile.42.refs_10_
  11.0 0.6 constant_dynamic-slice_fusion
  11.6 0.1 tile.43
  11.7 0.1 tile.45.refs_11_
  11.8 0.1 stack.27.place
  11.9 3.3 %collective-permute-start.6 = (bf16[16,4096]{1,0:T(8,128)(2,1)}, bf16[16,4096]{1,0:T(8,128)(2,1)}, u32[]{:S(2)}, u32[]{:S(2)}) collective-permute-start(bf16[16,4096]{1,0:T(8,128)(2,1)} %refs_0_.1), channel_id=1, source_target_pairs={{0,12},{1,13},{2,14},{3,15},{4,8},{5,9},{6,10},{7,11},{8,4},{9,5},... | collective-permute-start | bytes 393224 | tf_op jit(solution)/shard_map/ppermute | solution.py:380
  15.2 9.2 %attention.2 = bf16[8,272,128]{2,1,0:T(8,128)(2,1)} custom-call(s32[6]{0:T(128)S(1)} %stack.27.place, bf16[16,4096]{1,0:T(8,128)(2,1)} %refs_0_.1, bf16[16,4096]{1,0:T(8,128)(2,1)S(1)} %collective-permute-done.refs_1_, bf16[16,4096]{1,0:T(8,128)(2,1)S(1)} %collective-permute-done.1.refs_2_, bf16[16,4096]{1,0:T(8,128)(2,1)} %collective-permute-done.2.refs_3_, ...), custom_call_target="tpu_custom_call" | custom-call | flops 3221225472 | bytes 8388608 | tf_op jit(solution)/shard_map/attention/pallas_call | solution.py:139
  24.5 4.6 %all-to-all-start = ((bf16[8,272,128]{2,1,0:T(8,128)(2,1)}), bf16[8,272,128]{2,1,0:T(8,128)(2,1)S(1)}, u32[]{:S(2)}, u32[]{:S(2)}) async-start(bf16[8,272,128]{2,1,0:T(8,128)(2,1)} %attention.2), calls=%async_computation | async-start | bytes 1114112 | tf_op jit(solution)/shard_map/all_to_all | solution.py:430
  29.1 2.0 %collective-permute-start.7 = (bf16[16,4096]{1,0:T(8,128)(2,1)S(1)}, bf16[16,4096]{1,0:T(8,128)(2,1)S(1)}, u32[]{:S(2)}, u32[]{:S(2)}) collective-permute-start(bf16[16,4096]{1,0:T(8,128)(2,1)S(1)} %collective-permute-done.5.refs_0_), channel_id=1, source_target_pairs={{0,2},{1,3},{2,0},{3,1},{4,6},{5,7},{6,4},{7,5},{8,10},{9,11},{10,... | collective-permute-start | bytes 393224 | tf_op jit(solution)/shard_map/ppermute | solution.py:376
  31.2 0.0 collective-permute-start.8
  31.2 0.1 tile.46
  31.3 0.1 tile.48.refs_10_
  31.4 0.8 tile.49
  32.1 0.1 tile.51.refs_11_
  32.2 7.0 %collective-permute-done.7.refs_2_ = bf16[16,4096]{1,0:T(8,128)(2,1)S(1)} collective-permute-done((bf16[16,4096]{1,0:T(8,128)(2,1)S(1)}, bf16[16,4096]{1,0:T(8,128)(2,1)S(1)}, u32[]{:S(2)}, u32[]{:S(2)}) %collective-permute-start.7) | collective-permute-done | bytes 131104 | tf_op jit(solution)/shard_map/ppermute | solution.py:376
  39.2 2.2 %collective-permute-done.8.refs_3_ = bf16[16,4096]{1,0:T(8,128)(2,1)S(1)} collective-permute-done((bf16[16,4096]{1,0:T(8,128)(2,1)}, bf16[16,4096]{1,0:T(8,128)(2,1)S(1)}, u32[]{:S(2)}, u32[]{:S(2)}) %collective-permute-start.8) | collective-permute-done | bytes 131104 | tf_op jit(solution)/shard_map/ppermute | solution.py:376
  41.4 1.2 copy-done.4
  42.7 1.2 copy-done.6
  43.9 8.4 %attention.3 = bf16[8,272,128]{2,1,0:T(8,128)(2,1)S(1)} custom-call(s32[6]{0:T(128)S(1)} %stack.27.place, bf16[16,4096]{1,0:T(8,128)(2,1)S(1)} %collective-permute-done.5.refs_0_, bf16[16,4096]{1,0:T(8,128)(2,1)} %collective-permute-done.6.refs_1_, bf16[16,4096]{1,0:T(8,128)(2,1)S(1)} %collective-permute-done.7.refs_2_, ...), custom_call_target="tpu_custom_call" | custom-call | flops 3221225472 | bytes 8388608 | tf_op jit(solution)/shard_map/attention/pallas_call | solution.py:139
  52.3 0.8 copy-done.1
  53.1 4.5 %all-to-all-start.1 = ((bf16[8,272,128]{2,1,0:T(8,128)(2,1)}), bf16[8,272,128]{2,1,0:T(8,128)(2,1)S(1)}, u32[]{:S(2)}, u32[]{:S(2)}) async-start(bf16[8,272,128]{2,1,0:T(8,128)(2,1)} %copy-done.1), calls=%async_computation.1 | async-start | bytes 1114112 | tf_op jit(solution)/shard_map/all_to_all | solution.py:430
  57.7 13.8 %all-to-all-done.1.refs_1_ = bf16[8,272,128]{2,1,0:T(8,128)(2,1)S(1)} async-done(((bf16[8,272,128]{2,1,0:T(8,128)(2,1)}), bf16[8,272,128]{2,1,0:T(8,128)(2,1)S(1)}, u32[]{:S(2)}, u32[]{:S(2)}) %all-to-all-start.1) | async-done | bytes 557088 | tf_op jit(solution)/shard_map/all_to_all | solution.py:430
  71.5 2.1 %project.1 = bf16[128,2048]{1,0:T(8,128)(2,1)} custom-call(s32[6]{0:T(128)S(1)} %stack.27.place, bf16[8,272,128]{2,1,0:T(8,128)(2,1)S(1)} %all-to-all-done.refs_0_, bf16[8,272,128]{2,1,0:T(8,128)(2,1)S(1)} %all-to-all-done.1.refs_1_, bf16[256,2048]{1,0:T(8,128)(2,1)S(1)} %copy-done, bf16[256,2048]{1,0:T(8,128)(2,1)S(1)} %collective-permute-done.9.refs_3_), custom_call_target="tpu_custom_call" | custom-call | flops 268435456 | bytes 4194304 | tf_op jit(solution)/shard_map/project/pallas_call | solution.py:213
  73.5 3.7 %all-to-all-start.2 = ((bf16[8,16,2048]{2,1,0:T(8,128)(2,1)}), bf16[8,16,2048]{2,1,0:T(8,128)(2,1)S(1)}, u32[]{:S(2)}, u32[]{:S(2)}) async-start(bf16[8,16,2048]{2,1,0:T(8,128)(2,1)} %bitcast.6), calls=%async_computation.2 | async-start | bytes 1048576 | tf_op jit(solution)/shard_map/all_to_all | solution.py:443
  77.2 0.1 copy.21
  77.3 0.1 eq.31
  77.4 0.2 convert_reduce_fusion
  77.6 0.1 reduce_sum.21
  77.7 0.1 fusion
  77.8 0.1 copy.23
  77.9 13.0 %all-to-all-done.2.parts = bf16[8,16,2048]{2,1,0:T(8,128)(2,1)S(1)} async-done(((bf16[8,16,2048]{2,1,0:T(8,128)(2,1)}), bf16[8,16,2048]{2,1,0:T(8,128)(2,1)S(1)}, u32[]{:S(2)}, u32[]{:S(2)}) %all-to-all-start.2) | async-done | bytes 524320 | tf_op jit(solution)/shard_map/all_to_all | solution.py:443
  91.0 0.4 norm_and_dispatch.1
  91.4 18.0 %all_to_all.25 = bf16[16,8,2048]{2,1,0:T(8,128)(2,1)S(1)} all-to-all(bf16[16,8,2048]{2,1,0:T(8,128)(2,1)S(1)} %bitcast.14), channel_id=1, replica_groups=mesh['groups'=2,'ctx'=16] {'ctx'}, dimensions={0} | all-to-all | bytes 1048576 | tf_op jit(solution)/shard_map/all_to_all | solution.py:452
  109.4 7.9 %experts.1 = bf16[128,2048]{1,0:T(8,128)(2,1)} custom-call(bf16[128,2048]{1,0:T(8,128)(2,1)S(1)} %bitcast.12, bf16[2,2048,768]{2,1,0:T(8,128)(2,1)} %w_gate.1, bf16[2,2048,768]{2,1,0:T(8,128)(2,1)} %w_up.1, bf16[2,768,2048]{2,1,0:T(8,128)(2,1)} %w_down.1), custom_call_target="tpu_custom_call" | custom-call | flops 2415919104 | bytes 18874368 | tf_op jit(solution)/shard_map/experts/pallas_call | solution.py:304
  117.3 4.1 %all-to-all-start.4 = ((bf16[16,8,2048]{2,1,0:T(8,128)(2,1)}), bf16[16,8,2048]{2,1,0:T(8,128)(2,1)S(1)}, u32[]{:S(2)}, u32[]{:S(2)}) async-start(bf16[16,8,2048]{2,1,0:T(8,128)(2,1)} %bitcast.10), calls=%async_computation.4 | async-start | bytes 1048576 | tf_op jit(solution)/shard_map/all_to_all | solution.py:456
  121.4 0.1 copy.24
  121.5 0.1 select_reduce_fusion
  121.6 14.3 %all-to-all-done.4 = bf16[16,8,2048]{2,1,0:T(8,128)(2,1)S(1)} async-done(((bf16[16,8,2048]{2,1,0:T(8,128)(2,1)}), bf16[16,8,2048]{2,1,0:T(8,128)(2,1)S(1)}, u32[]{:S(2)}, u32[]{:S(2)}) %all-to-all-start.4) | async-done | bytes 524320 | tf_op jit(solution)/shard_map/all_to_all | solution.py:456
  135.9 0.9 mix.1
  (36 shorter events, 0.1 us)
Async XLA Ops:
  0.0 15.2 %collective-permute-start.3 = (bf16[1024,512]{1,0:T(8,128)(2,1)}, bf16[1024,512]{1,0:T(8,128)(2,1)S(1)}, u32[]{:S(2)}, u32[]{:S(2)}) collective-permute-start(bf16[1024,512]{1,0:T(8,128)(2,1)} %refs_4_.3), channel_id=1, source_target_pairs={{0,1},{1,0},{2,3},{3,2},{4,5},{5,4},{6,7},{7,6},{8,9},{9,8},{10,11... | collective-permute-start | bytes 3145736 | tf_op jit(solution)/shard_map/ppermute | solution.py:386
  0.5 14.8 %collective-permute-start.4 = (bf16[1024,512]{1,0:T(8,128)(2,1)}, bf16[1024,512]{1,0:T(8,128)(2,1)S(1)}, u32[]{:S(2)}, u32[]{:S(2)}) collective-permute-start(bf16[1024,512]{1,0:T(8,128)(2,1)} %refs_6_.3), channel_id=1, source_target_pairs={{0,1},{1,0},{2,3},{3,2},{4,5},{5,4},{6,7},{7,6},{8,9},{9,8},{10,11... | collective-permute-start | bytes 3145736 | tf_op jit(solution)/shard_map/ppermute | solution.py:387
  0.5 7.9 %collective-permute-start = (bf16[16,4096]{1,0:T(8,128)(2,1)}, bf16[16,4096]{1,0:T(8,128)(2,1)S(1)}, u32[]{:S(2)}, u32[]{:S(2)}) collective-permute-start(bf16[16,4096]{1,0:T(8,128)(2,1)} %refs_0_.1), channel_id=1, source_target_pairs={{0,4},{1,5},{2,6},{3,7},{4,0},{5,1},{6,2},{7,3},{8,12},{9,13},{10,... | collective-permute-start | bytes 393224 | tf_op jit(solution)/shard_map/ppermute | solution.py:380
  3.5 8.3 %collective-permute-start.1 = (bf16[16,4096]{1,0:T(8,128)(2,1)}, bf16[16,4096]{1,0:T(8,128)(2,1)S(1)}, u32[]{:S(2)}, u32[]{:S(2)}) collective-permute-start(bf16[16,4096]{1,0:T(8,128)(2,1)} %refs_0_.1), channel_id=1, source_target_pairs={{0,2},{1,3},{2,0},{3,1},{4,6},{5,7},{6,4},{7,5},{8,10},{9,11},{10,... | collective-permute-start | bytes 393224 | tf_op jit(solution)/shard_map/ppermute | solution.py:376
  5.1 19.4 %collective-permute-start.5 = (bf16[16,4096]{1,0:T(8,128)(2,1)}, bf16[16,4096]{1,0:T(8,128)(2,1)S(1)}, u32[]{:S(2)}, u32[]{:S(2)}) collective-permute-start(bf16[16,4096]{1,0:T(8,128)(2,1)} %refs_0_.1), channel_id=1, source_target_pairs={{0,8},{1,9},{2,10},{3,11},{4,12},{5,13},{6,14},{7,15},{8,0},{9,1},... | collective-permute-start | bytes 393224 | tf_op jit(solution)/shard_map/ppermute | solution.py:380
  8.4 6.8 %collective-permute-start.2 = (bf16[16,4096]{1,0:T(8,128)(2,1)S(1)}, bf16[16,4096]{1,0:T(8,128)(2,1)}, u32[]{:S(2)}, u32[]{:S(2)}) collective-permute-start(bf16[16,4096]{1,0:T(8,128)(2,1)S(1)} %collective-permute-done.refs_1_), channel_id=1, source_target_pairs={{0,2},{1,3},{2,0},{3,1},{4,6},{5,7},{6,4},{7,5},{8,10},{9,11},{10,... | collective-permute-start | bytes 393224 | tf_op jit(solution)/shard_map/ppermute | solution.py:376
  11.8 20.4 %copy-start = (bf16[256,2048]{1,0:T(8,128)(2,1)S(1)}, bf16[256,2048]{1,0:T(8,128)(2,1)}, u32[]{:S(2)}) copy-start(bf16[256,2048]{1,0:T(8,128)(2,1)} %refs_2_.1) | copy-start | bytes 3145732
  11.9 12.6 %collective-permute-start.6 = (bf16[16,4096]{1,0:T(8,128)(2,1)}, bf16[16,4096]{1,0:T(8,128)(2,1)}, u32[]{:S(2)}, u32[]{:S(2)}) collective-permute-start(bf16[16,4096]{1,0:T(8,128)(2,1)} %refs_0_.1), channel_id=1, source_target_pairs={{0,12},{1,13},{2,14},{3,15},{4,8},{5,9},{6,10},{7,11},{8,4},{9,5},... | collective-permute-start | bytes 393224 | tf_op jit(solution)/shard_map/ppermute | solution.py:380
  15.2 9.3 %copy-start.3 = (bf16[1024,512]{1,0:T(8,128)(2,1)}, bf16[1024,512]{1,0:T(8,128)(2,1)S(1)}, u32[]{:S(2)}) copy-start(bf16[1024,512]{1,0:T(8,128)(2,1)S(1)} %collective-permute-done.3.refs_5_) | copy-start | bytes 3145732
  15.2 9.3 %copy-start.5 = (bf16[1024,512]{1,0:T(8,128)(2,1)}, bf16[1024,512]{1,0:T(8,128)(2,1)S(1)}, u32[]{:S(2)}) copy-start(bf16[1024,512]{1,0:T(8,128)(2,1)S(1)} %collective-permute-done.4.refs_7_) | copy-start | bytes 3145732
  24.5 28.6 %all-to-all-start = ((bf16[8,272,128]{2,1,0:T(8,128)(2,1)}), bf16[8,272,128]{2,1,0:T(8,128)(2,1)S(1)}, u32[]{:S(2)}, u32[]{:S(2)}) async-start(bf16[8,272,128]{2,1,0:T(8,128)(2,1)} %attention.2), calls=%async_computation | async-start | bytes 1114112 | tf_op jit(solution)/shard_map/all_to_all | solution.py:430
  29.1 10.1 %collective-permute-start.7 = (bf16[16,4096]{1,0:T(8,128)(2,1)S(1)}, bf16[16,4096]{1,0:T(8,128)(2,1)S(1)}, u32[]{:S(2)}, u32[]{:S(2)}) collective-permute-start(bf16[16,4096]{1,0:T(8,128)(2,1)S(1)} %collective-permute-done.5.refs_0_), channel_id=1, source_target_pairs={{0,2},{1,3},{2,0},{3,1},{4,6},{5,7},{6,4},{7,5},{8,10},{9,11},{10,... | collective-permute-start | bytes 393224 | tf_op jit(solution)/shard_map/ppermute | solution.py:376
  31.2 10.3 %collective-permute-start.8 = (bf16[16,4096]{1,0:T(8,128)(2,1)}, bf16[16,4096]{1,0:T(8,128)(2,1)S(1)}, u32[]{:S(2)}, u32[]{:S(2)}) collective-permute-start(bf16[16,4096]{1,0:T(8,128)(2,1)} %collective-permute-done.6.refs_1_), channel_id=1, source_target_pairs={{0,2},{1,3},{2,0},{3,1},{4,6},{5,7},{6,4},{7,5},{8,10},{9,11},{10,... | collective-permute-start | bytes 393224 | tf_op jit(solution)/shard_map/ppermute | solution.py:376
  32.2 58.7 %copy-start.2 = (bf16[16,2048]{1,0:T(8,128)(2,1)S(1)}, bf16[16,2048]{1,0:T(8,128)(2,1)}, u32[]{:S(2)}) copy-start(bf16[16,2048]{1,0:T(8,128)(2,1)} %residual.1) | copy-start | bytes 196612
  32.2 25.4 %collective-permute-start.9 = (bf16[256,2048]{1,0:T(8,128)(2,1)S(1)}, bf16[256,2048]{1,0:T(8,128)(2,1)S(1)}, u32[]{:S(2)}, u32[]{:S(2)}) collective-permute-start(bf16[256,2048]{1,0:T(8,128)(2,1)S(1)} %copy-done), channel_id=1, source_target_pairs={{0,1},{1,0},{2,3},{3,2},{4,5},{5,4},{6,7},{7,6},{8,9},{9,8},{10,11... | collective-permute-start | bytes 3145736 | tf_op jit(solution)/shard_map/ppermute | solution.py:441
  41.4 1.2 copy-start.4
  42.7 1.2 copy-start.6
  43.9 33.3 %copy-start.7 = (bf16[2048]{0:T(1024)(128)(2,1)S(1)}, bf16[2048]{0:T(1024)(128)(2,1)}, u32[]{:S(2)}) copy-start(bf16[2048]{0:T(1024)(128)(2,1)} %param.22) | copy-start | bytes 12292
  43.9 33.4 %copy-start.8 = (s32[16,8]{0,1:T(8,128)S(1)}, s32[16,8]{0,1:T(8,128)}, u32[]{:S(2)}) copy-start(s32[16,8]{0,1:T(8,128)} %param.23) | copy-start | bytes 1540
  52.3 0.8 copy-start.1
  53.1 18.3 %all-to-all-start.1 = ((bf16[8,272,128]{2,1,0:T(8,128)(2,1)}), bf16[8,272,128]{2,1,0:T(8,128)(2,1)S(1)}, u32[]{:S(2)}, u32[]{:S(2)}) async-start(bf16[8,272,128]{2,1,0:T(8,128)(2,1)} %copy-done.1), calls=%async_computation.1 | async-start | bytes 1114112 | tf_op jit(solution)/shard_map/all_to_all | solution.py:430
  73.5 17.4 %all-to-all-start.2 = ((bf16[8,16,2048]{2,1,0:T(8,128)(2,1)}), bf16[8,16,2048]{2,1,0:T(8,128)(2,1)S(1)}, u32[]{:S(2)}, u32[]{:S(2)}) async-start(bf16[8,16,2048]{2,1,0:T(8,128)(2,1)} %bitcast.6), calls=%async_computation.2 | async-start | bytes 1048576 | tf_op jit(solution)/shard_map/all_to_all | solution.py:443
  109.4 12.0 %copy-start.9 = (f32[16,8]{0,1:T(8,128)S(1)}, f32[16,8]{0,1:T(8,128)}, u32[]{:S(2)}) copy-start(f32[16,8]{0,1:T(8,128)} %param.24) | copy-start | bytes 1540
  117.3 18.6 %all-to-all-start.4 = ((bf16[16,8,2048]{2,1,0:T(8,128)(2,1)}), bf16[16,8,2048]{2,1,0:T(8,128)(2,1)S(1)}, u32[]{:S(2)}, u32[]{:S(2)}) async-start(bf16[16,8,2048]{2,1,0:T(8,128)(2,1)} %bitcast.10), calls=%async_computation.4 | async-start | bytes 1048576 | tf_op jit(solution)/shard_map/all_to_all | solution.py:456

commit v16 on v10

--- a/solution.py
+++ b/solution.py
@@ -29,32 +29,51 @@
 
 
 def attention_body(shape, place, *refs):
-    owners, owner_heads, home_rows, rows, cache_here, step = shape
-    *query_refs, key_own, key_other, value_own, value_other, key_fresh, value_fresh = refs[:-8]
-    lens, row_ids, out, q_rows, q_turned, hidden, scores, probs = refs[-8:]
+    steps, key_heads, owners, owner_heads, home_rows, rows, cache_here, piece = shape
+    inputs, (lens, row_ids, out) = refs[:-13], refs[-13:-10]
+    q_rows, q_turned, hidden, scores, probs, keys, values, key_new, value_new, sems = refs[-10:]
+    *query_refs, key_own, key_other, value_own, value_other, key_fresh, value_fresh = inputs
     chip, start_own, start_other, side_here, ring_here = place[0], place[1], place[2], place[4], place[5]
     near = rows // home_rows // 2
     pack = HD // rows
     groups = owner_heads // pack
-
-    @pl.when(pl.program_id(0) == 0)
-    def _():
-        lanes = lens.shape[1]
-        for part, start in enumerate((start_own, start_other)):
-            positions = start + lax.broadcasted_iota(jnp.int32, (cache_here, lanes), 0)
-            hidden[part * cache_here : (part + 1) * cache_here, :] = jnp.where(
-                positions < lens[...], 0.0, MASKED
-            )
-        token = chip * home_rows + lax.broadcasted_iota(jnp.int32, (home_rows, lanes), 0)
-        hidden[2 * cache_here :, :] = jnp.where(token == row_ids[...], 0.0, MASKED)
-
-    for k, piece in enumerate(query_refs):
+    columns = key_heads * HD
+    parts = [slice(part * cache_here, (part + 1) * cache_here) for part in range(2)]
+
+    copies = []
+
+    def copy(source, target):
+        copies.append(pltpu.make_async_copy(source, target, sems.at[len(copies)]))
+        copies[-1].start()
+        return copies[-1]
+
+    small = [copy(key_fresh, key_new), copy(value_fresh, value_new)]
+    for k, block in enumerate(query_refs):
         side = side_here if k < near else 1 - side_here
         spot = 2 * (lax.rem(ring_here, near) ^ (k % near)) + side
-        q_rows[pl.ds(pl.multiple_of(spot * home_rows, home_rows), home_rows), :] = piece[...]
-
+        place_rows = pl.ds(pl.multiple_of(spot * home_rows, home_rows), home_rows)
+        small.append(copy(block, q_rows.at[place_rows, :]))
+    key_copies, value_copies = [], []
+    for n in range(steps):
+        cols = pl.ds(n * columns, columns)
+        key_copies.append(
+            [copy(source.at[:, cols], keys.at[n, parts[p], :]) for p, source in enumerate((key_own, key_other))]
+        )
+        value_copies.append(
+            [copy(source.at[:, cols], values.at[n, parts[p], :]) for p, source in enumerate((value_own, value_other))]
+        )
+
+    for part, start in enumerate((start_own, start_other)):
+        positions = start + lax.broadcasted_iota(jnp.int32, (cache_here, HD), 0)
+        hidden[parts[part], :] = jnp.where(positions < lens[...], 0.0, MASKED)
+    token = chip * home_rows + lax.broadcasted_iota(jnp.int32, (home_rows, HD), 0)
+    hidden[2 * cache_here :, :] = jnp.where(token == row_ids[...], 0.0, MASKED)
+
+    for one in small:
+        one.wait()
     factor = LOG2E / math.sqrt(HD)
-    for n in range(owners * groups):
+    wide = owners * groups * HD
+    for n in range(steps * key_heads * owners * groups):
         block = jnp.concatenate(
             [q_rows[:, h * HD : (h + 1) * HD] for h in range(n * pack, (n + 1) * pack)], axis=0
         )
@@ -62,90 +81,110 @@
         coarse = scaled.astype(BF16)
         q_turned[:HD, n * HD : (n + 1) * HD] = coarse
         q_turned[HD:, n * HD : (n + 1) * HD] = (scaled - coarse.astype(F32)).astype(BF16)
-    wide = owners * groups * HD
-
-    def score(keys, at):
-        s = nn_dot(jnp.concatenate([keys, keys], axis=1), q_turned[...])
-        return s + jnp.concatenate([hidden[at, :]] * (owners * groups), axis=1)
-
-    s_new = score(key_fresh[...], slice(2 * cache_here, 2 * cache_here + home_rows))
-    run = jnp.max(s_new.reshape(home_rows // 8, 8, wide), axis=0)
-    pieces = [(part, i) for part in range(2) for i in range(0, cache_here, step)]
-    for part, i in pieces:
-        at = slice(part * cache_here + i, part * cache_here + i + step)
-        s = score((key_own, key_other)[part][i : i + step, :], at)
-        scores[at, :] = s
-        run = jnp.maximum(run, jnp.max(s.reshape(step // 8, 8, wide), axis=0))
-    peak = jnp.maximum(jnp.max(run, axis=0, keepdims=True), FLOOR).astype(BF16).astype(F32)
-    p_new = jnp.exp2((s_new - peak).astype(BF16))
-    for part, i in pieces:
-        at = slice(part * cache_here + i, part * cache_here + i + step)
-        probs[at, :] = jnp.exp2((scores[at, :] - peak).astype(BF16))
+
+    each = range(key_heads)
+    heads = [slice(g * HD, (g + 1) * HD) for g in each]
+    across = [slice(g * wide, (g + 1) * wide) for g in each]
+    fresh_at = slice(2 * cache_here, 2 * cache_here + home_rows)
+    pieces = [slice(i, i + piece) for i in range(0, 2 * cache_here, piece)]
     ones = jnp.ones((STATS, cache_here), BF16)
-    sums = nn_dot(jnp.concatenate([value_own[...], ones], axis=0), probs[:cache_here, :])
-    sums = sums + nn_dot(jnp.concatenate([value_other[...], ones], axis=0), probs[cache_here:, :])
-    numer = sums[:HD] + nn_dot(value_fresh[...].astype(F32).T.astype(BF16), p_new)
-    denom = sums[HD : HD + 1] + jnp.sum(p_new.astype(F32), axis=0, keepdims=True)
-    high = denom.astype(BF16).astype(F32)
-    low = denom - high
-    for owner in range(owners):
-        lanes = [slice((owner * groups + k) * HD, (owner * groups + k + 1) * HD) for k in range(groups)]
-        for k, cols in enumerate(lanes):
-            out[owner, k * HD : (k + 1) * HD, :] = numer[:, cols].astype(BF16)
-        filled = [kind[:, cols] for kind in (peak, high, low) for cols in lanes]
-        filled += [jnp.zeros_like(filled[0])] * (STATS - len(filled))
-        out[owner, groups * HD :, :] = jnp.concatenate(filled, axis=0).astype(BF16)
+
+    def most(s):
+        return jnp.max(s.reshape(s.shape[0] // 8, 8, wide), axis=0)
+
+    for n in range(steps):
+
+        def score(g, keys_here, at):
+            first = (n * key_heads + g) * wide
+            s = nn_dot(jnp.concatenate([keys_here, keys_here], axis=1), q_turned[:, first : first + wide])
+            return s + jnp.concatenate([hidden[at, :]] * (owners * groups), axis=1)
+
+        for one in key_copies[n]:
+            one.wait()
+        whole = [slice((n * key_heads + g) * HD, (n * key_heads + g + 1) * HD) for g in each]
+        s_new = [score(g, key_new[:, whole[g]], fresh_at) for g in each]
+        run = [most(s) for s in s_new]
+        for at in pieces:
+            for g in each:
+                s = score(g, keys[n, at, heads[g]], at)
+                scores[n % 2, at, across[g]] = s
+                run[g] = jnp.maximum(run[g], most(s))
+        peak = [
+            jnp.maximum(jnp.max(r, axis=0, keepdims=True), FLOOR).astype(BF16).astype(F32) for r in run
+        ]
+        for at in pieces:
+            for g in each:
+                probs[n % 2, at, across[g]] = jnp.exp2((scores[n % 2, at, across[g]] - peak[g]).astype(BF16))
+        for one in value_copies[n]:
+            one.wait()
+        for g in each:
+            sums = 0.0
+            for part in parts:
+                turned = jnp.concatenate([values[n, part, heads[g]].T, ones], axis=0)
+                sums = sums + nn_dot(turned, probs[n % 2, part, across[g]])
+            p_new = jnp.exp2((s_new[g] - peak[g]).astype(BF16))
+            fresh = value_new[:, whole[g]].astype(F32).T.astype(BF16)
+            numer = sums[:HD] + nn_dot(fresh, p_new)
+            denom = sums[HD : HD + 1] + jnp.sum(p_new.astype(F32), axis=0, keepdims=True)
+            high = denom.astype(BF16).astype(F32)
+            low = denom - high
+            for owner in range(owners):
+                spot = (n * key_heads + g) * owners + owner
+                lanes = [slice((owner * groups + k) * HD, (owner * groups + k + 1) * HD) for k in range(groups)]
+                for k, cols in enumerate(lanes):
+                    out[spot, k * HD : (k + 1) * HD, :] = numer[:, cols].astype(BF16)
+                filled = [kind[:, cols] for kind in (peak[g], high, low) for cols in lanes]
+                filled += [jnp.zeros_like(filled[0])] * (STATS - len(filled))
+                out[spot, groups * HD :, :] = jnp.concatenate(filled, axis=0).astype(BF16)
 
 
 def attention(place, query_blocks, keys, values, new_key, new_value, lens, row_ids, chips, kv_heads):
     home_rows = new_key.shape[0]
     rows = home_rows * len(query_blocks)
     cache_here = keys[0].shape[0]
+    together = 2
+    steps = kv_heads // together
     owners = chips // kv_heads
-    columns = query_blocks[0][0].shape[1] // kv_heads
-    owner_heads = columns // HD // owners
-    wide = rows * columns // HD
+    width = query_blocks[0].shape[1]
+    owner_heads = width // HD // chips
+    wide = together * owners * owner_heads * rows
     height = owner_heads * rows + STATS
-    step = 512
-    positions = 2 * cache_here + home_rows
-    kv = lambda g, place: (0, g)
-    whole = lambda g, place: (0, 0)
-    shape = (owners, owner_heads, home_rows, rows, cache_here, step)
-    work = wide * kv_heads * 2 * cache_here
+    piece = 512
+    positions = 2 * cache_here
+    shape = (steps, together, owners, owner_heads, home_rows, rows, cache_here, piece)
+    work = wide * steps * positions
+    vmem = pl.BlockSpec(memory_space=pltpu.VMEM)
+    anywhere = pl.BlockSpec(memory_space=pl.ANY)
+    inputs = [*query_blocks, *keys, *values, new_key, new_value]
     return pl.pallas_call(
         functools.partial(attention_body, shape),
-        grid_spec=pltpu.PrefetchScalarGridSpec(
-            num_scalar_prefetch=1,
-            grid=(kv_heads,),
-            in_specs=[
-                pl.BlockSpec((home_rows, columns), functools.partial(lambda n, g, place: (n, g), n))
-                for _, n in query_blocks
-            ]
-            + [pl.BlockSpec((cache_here, HD), kv)] * 2
-            + [pl.BlockSpec((HD, cache_here), lambda g, place: (g, 0))] * 2
-            + [pl.BlockSpec((home_rows, HD), kv)] * 2
-            + [pl.BlockSpec(lens.shape, whole)] * 2,
-            out_specs=pl.BlockSpec((owners, height, HD), lambda g, place: (g, 0, 0)),
-            scratch_shapes=[
-                pltpu.VMEM((rows, columns), BF16),
-                pltpu.VMEM((2 * HD, wide), BF16),
-                pltpu.VMEM((positions, HD), F32),
-                pltpu.VMEM((2 * cache_here, wide), F32),
-                pltpu.VMEM((2 * cache_here, wide), BF16),
-            ],
-        ),
+        in_specs=[pl.BlockSpec(memory_space=pltpu.SMEM)] + [anywhere] * len(inputs) + [vmem] * 2,
+        out_specs=vmem,
+        scratch_shapes=[
+            pltpu.VMEM((rows, width), BF16),
+            pltpu.VMEM((2 * HD, steps * wide), BF16),
+            pltpu.VMEM((positions + home_rows, HD), F32),
+            pltpu.VMEM((2, positions, wide), F32),
+            pltpu.VMEM((2, positions, wide), BF16),
+            pltpu.VMEM((steps, positions, together * HD), BF16),
+            pltpu.VMEM((steps, positions, together * HD), BF16),
+            pltpu.VMEM(new_key.shape, BF16),
+            pltpu.VMEM(new_value.shape, BF16),
+            pltpu.SemaphoreType.DMA((len(query_blocks) + 2 + 4 * steps,)),
+        ],
         out_shape=jax.ShapeDtypeStruct((chips, height, HD), BF16),
-        compiler_params=pltpu.CompilerParams(vmem_limit_bytes=32 * MIB),
+        compiler_params=pltpu.CompilerParams(vmem_limit_bytes=48 * MIB),
         cost_estimate=pl.CostEstimate(
             flops=6 * work * HD, bytes_accessed=8 * MIB, transcendentals=work
         ),
         name="attention",
     )(
         place,
-        *[block for block, _ in query_blocks],
+        *query_blocks,
         pltpu.with_memory_space_constraint(keys[0], pltpu.HBM),
         keys[1],
-        *values,
+        pltpu.with_memory_space_constraint(values[0], pltpu.HBM),
+        values[1],
         pltpu.with_memory_space_constraint(new_key, pltpu.HBM),
         pltpu.with_memory_space_constraint(new_value, pltpu.HBM),
         lens,
@@ -356,16 +395,13 @@
         lax.ppermute(queries, "ctx", [(i, i ^ (2 * CORES * k)) for i in range(devices)])
         for k in range(1, rings)
     ]
-    near_blocks = [(pltpu.with_memory_space_constraint(queries, pltpu.HBM), 0)]
-    near_blocks += [(block, 0) for block in by_ring[1:half]]
-    near_blocks += [(neighbour, 0)] + [(across_y(block), 0) for block in by_ring[1:half]]
-    far = jnp.concatenate(by_ring[half:], axis=0)
-    far_across = across_y(far)
-    far_blocks = [(far, k) for k in range(half)] + [(far_across, k) for k in range(half)]
+    near_blocks = [pltpu.with_memory_space_constraint(queries, pltpu.HBM), *by_ring[1:half]]
+    near_blocks += [neighbour] + [across_y(block) for block in by_ring[1:half]]
+    far_across = [across_y(block) for block in by_ring[half:]]
+    far_blocks = by_ring[half:] + far_across
     late_keys, late_values, _ = lax.optimization_barrier((key_cache, value_cache, neighbour))
     key_other = lax.ppermute(late_keys, "ctx", swap)
-    value_turned = late_values.T
-    value_other = lax.ppermute(value_turned, "ctx", swap)
+    value_other = lax.ppermute(late_values, "ctx", swap)
     place = jnp.stack([chip, index * cache_here, (index ^ 1) * cache_here, core, chip % 2, chip // 2]).astype(jnp.int32)
 
     def in_lanes(by_chip, n):
@@ -398,7 +434,7 @@
             place,
             blocks,
             (key_cache, key_other),
-            (value_turned, value_other),
+            (value_cache, value_other),
             new_key,
             new_value,
             lens[chunk],

time: 132 us -> 145 us (1.098)
  local copies, waits for them, and re-layouts: 3.58 us -> 9.73 us
  starting transfers between devices: 25.6 us -> 30 us
  waiting for transfers between devices: 52.4 us -> 54.7 us
    unnamed x13 -> x30, local copies, waits for them, and re-layouts: 0.17 us -> 6.56 us
    ppermute x3 -> x4, waiting for transfers between devices: 0.01 us -> 3.71 us  [across_y(): return lax.ppermute(block, 'ctx', across)]
    ppermute x3 -> x4, starting transfers between devices: 3.86 us -> 6.74 us  [across_y(): return lax.ppermute(block, 'ctx', across)]
    all_to_all x2, waiting for transfers between devices: 18.2 us -> 15.8 us  [on_device(): lax.all_to_all(sums, 'ctx', split_axis=0, concat_axis=0, axis_index_group...]
    all_to_all x2, starting transfers between devices: 8.86 us -> 10.6 us  [on_device(): lax.all_to_all(sums, 'ctx', split_axis=0, concat_axis=0, axis_index_group...]
    optimization_barrier x1 -> x0, local copies, waits for them, and re-layouts: 1.49 us -> none  [on_device(): lax.optimization_barrier((key_cache, value_cache, neighbour))]
  transfers between devices with their start and end apart: 13 -> 14, of which waited for: 5 -> 6; matrix products, arithmetic and copies ran while one was open for 3% -> 3% of each run, Pallas kernels for 15% -> 14%
where the time goes in v16:
time: 145 us; the launch traced here: 144 us
  waiting for transfers between devices  54.7 us (38%)
  Pallas kernels  31.3 us (22%)
  starting transfers between devices  30 us (21%)
  blocking collectives  18 us (12%)
  local copies, waits for them, and re-layouts  9.73 us (7%)
    pallas_call x2, Pallas kernels, attention(): pl.pallas_call(functools.partial(attention_body, shape), in_specs=[pl.Blo...  20 us
    all_to_all x1, blocking collectives, on_device(): lax.all_to_all(outgoing.reshape(devices, experts * MOST, width), 'ctx', s...  18 us
    all_to_all x2, waiting for transfers between devices, on_device(): lax.all_to_all(sums, 'ctx', split_axis=0, concat_axis=0, axis_index_group...  15.8 us
    all_to_all x1, waiting for transfers between devices, on_device(): lax.all_to_all(produced.reshape(devices, experts * MOST, width), 'ctx', s...  14.3 us
    all_to_all x1, waiting for transfers between devices, on_device(): lax.all_to_all(share.reshape(chips, home_rows, width), 'ctx', split_axis=...  14 us
    all_to_all x2, starting transfers between devices, on_device(): lax.all_to_all(sums, 'ctx', split_axis=0, concat_axis=0, axis_index_group...  10.6 us
    pallas_call x1, Pallas kernels, run_experts(): pl.pallas_call(functools.partial(experts_body, step), in_specs=[vmem] + [...  7.88 us
    ppermute x3, waiting for transfers between devices, on_device(): lax.ppermute(queries, 'ctx', [(i, i ^ 2 * CORES * k) for i in range(devic...  6.93 us
  transfers between devices with their start and end apart: 14, of which 6 were waited for; matrix products, arithmetic and copies ran while one was open for 3% of the time, Pallas kernels for 14%

profile of v16, /device:TPU:0, one launch (start us, length us, event | category | flops | bytes accessed | tf_op | source)
XLA Modules:
  0.0 144.4 jit_solution(17157076015781850002)
XLA Ops:
  0.0 3.0 %collective-permute-start.1 = (bf16[16,4096]{1,0:T(8,128)(2,1)}, bf16[16,4096]{1,0:T(8,128)(2,1)S(1)}, u32[]{:S(2)}, u32[]{:S(2)}) collective-permute-start(bf16[16,4096]{1,0:T(8,128)(2,1)} %refs_0_.1), channel_id=1, source_target_pairs={{0,2},{1,3},{2,0},{3,1},{4,6},{5,7},{6,4},{7,5},{8,10},{9,11},{10,... | collective-permute-start | bytes 393224 | tf_op jit(solution)/shard_map/ppermute | solution.py:391
  3.0 3.7 %collective-permute-done.1.refs_2_ = bf16[16,4096]{1,0:T(8,128)(2,1)S(1)} collective-permute-done((bf16[16,4096]{1,0:T(8,128)(2,1)}, bf16[16,4096]{1,0:T(8,128)(2,1)S(1)}, u32[]{:S(2)}, u32[]{:S(2)}) %collective-permute-start.1) | collective-permute-done | bytes 131104 | tf_op jit(solution)/shard_map/ppermute | solution.py:391
  6.7 0.5 collective-permute-start.4
  7.2 1.8 %collective-permute-start = (bf16[16,4096]{1,0:T(8,128)(2,1)}, bf16[16,4096]{1,0:T(8,128)(2,1)}, u32[]{:S(2)}, u32[]{:S(2)}) collective-permute-start(bf16[16,4096]{1,0:T(8,128)(2,1)} %refs_0_.1), channel_id=1, source_target_pairs={{0,4},{1,5},{2,6},{3,7},{4,0},{5,1},{6,2},{7,3},{8,12},{9,13},{10,... | collective-permute-start | bytes 393224 | tf_op jit(solution)/shard_map/ppermute | solution.py:395
  9.0 2.6 %collective-permute-start.5 = (bf16[16,4096]{1,0:T(8,128)(2,1)}, bf16[16,4096]{1,0:T(8,128)(2,1)S(1)}, u32[]{:S(2)}, u32[]{:S(2)}) collective-permute-start(bf16[16,4096]{1,0:T(8,128)(2,1)} %refs_0_.1), channel_id=1, source_target_pairs={{0,8},{1,9},{2,10},{3,11},{4,12},{5,13},{6,14},{7,15},{8,0},{9,1},... | collective-permute-start | bytes 393224 | tf_op jit(solution)/shard_map/ppermute | solution.py:395
  11.6 0.8 reshape.66
  12.3 2.4 %collective-permute-done.refs_1_ = bf16[16,4096]{1,0:T(8,128)(2,1)} collective-permute-done((bf16[16,4096]{1,0:T(8,128)(2,1)}, bf16[16,4096]{1,0:T(8,128)(2,1)}, u32[]{:S(2)}, u32[]{:S(2)}) %collective-permute-start) | collective-permute-done | bytes 131104 | tf_op jit(solution)/shard_map/ppermute | solution.py:395
  14.7 1.7 %collective-permute-start.2 = (bf16[16,4096]{1,0:T(8,128)(2,1)}, bf16[16,4096]{1,0:T(8,128)(2,1)}, u32[]{:S(2)}, u32[]{:S(2)}) collective-permute-start(bf16[16,4096]{1,0:T(8,128)(2,1)} %collective-permute-done.refs_1_), channel_id=1, source_target_pairs={{0,2},{1,3},{2,0},{3,1},{4,6},{5,7},{6,4},{7,5},{8,10},{9,11},{10,... | collective-permute-start | bytes 393224 | tf_op jit(solution)/shard_map/ppermute | solution.py:391
  16.5 0.1 tile.40
  16.6 0.1 tile.42.refs_10_
  16.7 0.6 constant_dynamic-slice_fusion
  17.3 0.1 tile.43
  17.4 0.1 tile.45.refs_11_
  17.4 0.1 stack.27.place
  17.5 4.6 %collective-permute-done.5.refs_0_ = bf16[16,4096]{1,0:T(8,128)(2,1)S(1)} collective-permute-done((bf16[16,4096]{1,0:T(8,128)(2,1)}, bf16[16,4096]{1,0:T(8,128)(2,1)S(1)}, u32[]{:S(2)}, u32[]{:S(2)}) %collective-permute-start.5) | collective-permute-done | bytes 131104 | tf_op jit(solution)/shard_map/ppermute | solution.py:395
  22.1 1.5 %collective-permute-start.6 = (bf16[16,4096]{1,0:T(8,128)(2,1)S(1)}, bf16[16,4096]{1,0:T(8,128)(2,1)S(1)}, u32[]{:S(2)}, u32[]{:S(2)}) collective-permute-start(bf16[16,4096]{1,0:T(8,128)(2,1)S(1)} %collective-permute-done.5.refs_0_), channel_id=1, source_target_pairs={{0,2},{1,3},{2,0},{3,1},{4,6},{5,7},{6,4},{7,5},{8,10},{9,11},{10,... | collective-permute-start | bytes 393224 | tf_op jit(solution)/shard_map/ppermute | solution.py:391
  23.6 0.5 collective-permute-start.8
  24.2 10.3 %attention.2 = bf16[8,272,128]{2,1,0:T(8,128)(2,1)} custom-call(s32[6]{0:T(128)S(1)} %stack.27.place, bf16[16,4096]{1,0:T(8,128)(2,1)} %refs_0_.1, bf16[16,4096]{1,0:T(8,128)(2,1)} %collective-permute-done.refs_1_, bf16[16,4096]{1,0:T(8,128)(2,1)S(1)} %collective-permute-done.1.refs_2_, bf16[16,4096]{1,0:T(8,128)(2,1)} %collective-permute-done.2.refs_3_, ...), custom_call_target="tpu_custom_call" | custom-call | flops 3221225472 | bytes 8388608 | tf_op jit(solution)/shard_map/attention/pallas_call | solution.py:159
  34.5 0.6 copy-done.7
  35.1 0.7 copy-done.9
  35.8 4.6 %all-to-all-start = ((bf16[8,272,128]{2,1,0:T(8,128)(2,1)}), bf16[8,272,128]{2,1,0:T(8,128)(2,1)S(1)}, u32[]{:S(2)}, u32[]{:S(2)}) async-start(bf16[8,272,128]{2,1,0:T(8,128)(2,1)} %attention.2), calls=%async_computation | async-start | bytes 1114112 | tf_op jit(solution)/shard_map/all_to_all | solution.py:450
  40.4 0.1 tile.46
  40.5 0.1 tile.48.refs_10_
  40.6 0.8 tile.49
  41.4 0.1 tile.51.refs_11_
  41.5 1.2 copy-done.4
  42.7 1.2 copy-done.6
  43.9 0.9 copy-done.8
  44.8 0.9 copy-done.10
  45.8 9.7 %attention.3 = bf16[8,272,128]{2,1,0:T(8,128)(2,1)S(1)} custom-call(s32[6]{0:T(128)S(1)} %stack.27.place, bf16[16,4096]{1,0:T(8,128)(2,1)S(1)} %collective-permute-done.5.refs_0_, bf16[16,4096]{1,0:T(8,128)(2,1)S(1)} %collective-permute-done.7.refs_1_, bf16[16,4096]{1,0:T(8,128)(2,1)S(1)} %copy-done.8, bf16[16,4096]{1,0:T(8,128)(2,1)S(1)} %copy-done.10, ...), custom_call_target="tpu_custom_call" | custom-call | flops 3221225472 | bytes 8388608 | tf_op jit(solution)/shard_map/attention/pallas_call | solution.py:159
  55.5 0.8 copy-done.1
  56.3 6.0 %all-to-all-start.1 = ((bf16[8,272,128]{2,1,0:T(8,128)(2,1)}), bf16[8,272,128]{2,1,0:T(8,128)(2,1)S(1)}, u32[]{:S(2)}, u32[]{:S(2)}) async-start(bf16[8,272,128]{2,1,0:T(8,128)(2,1)} %copy-done.1), calls=%async_computation.1 | async-start | bytes 1114112 | tf_op jit(solution)/shard_map/all_to_all | solution.py:450
  62.3 15.8 %all-to-all-done.1.refs_1_ = bf16[8,272,128]{2,1,0:T(8,128)(2,1)S(1)} async-done(((bf16[8,272,128]{2,1,0:T(8,128)(2,1)}), bf16[8,272,128]{2,1,0:T(8,128)(2,1)S(1)}, u32[]{:S(2)}, u32[]{:S(2)}) %all-to-all-start.1) | async-done | bytes 557088 | tf_op jit(solution)/shard_map/all_to_all | solution.py:450
  78.1 2.1 %project.1 = bf16[128,2048]{1,0:T(8,128)(2,1)} custom-call(s32[6]{0:T(128)S(1)} %stack.27.place, bf16[8,272,128]{2,1,0:T(8,128)(2,1)S(1)} %all-to-all-done.refs_0_, bf16[8,272,128]{2,1,0:T(8,128)(2,1)S(1)} %all-to-all-done.1.refs_1_, bf16[256,2048]{1,0:T(8,128)(2,1)S(1)} %copy-done, bf16[256,2048]{1,0:T(8,128)(2,1)S(1)} %collective-permute-done.9.refs_3_), custom_call_target="tpu_custom_call" | custom-call | flops 268435456 | bytes 4194304 | tf_op jit(solution)/shard_map/project/pallas_call | solution.py:228
  80.2 3.6 %all-to-all-start.2 = ((bf16[8,16,2048]{2,1,0:T(8,128)(2,1)}), bf16[8,16,2048]{2,1,0:T(8,128)(2,1)S(1)}, u32[]{:S(2)}, u32[]{:S(2)}) async-start(bf16[8,16,2048]{2,1,0:T(8,128)(2,1)} %bitcast.6), calls=%async_computation.2 | async-start | bytes 1048576 | tf_op jit(solution)/shard_map/all_to_all | solution.py:456
  84.0 0.1 eq.31
  84.1 0.2 convert_reduce_fusion
  84.2 0.1 reduce_sum.21
  84.3 0.1 fusion
  84.5 0.1 copy.23
  84.6 14.0 %all-to-all-done.2.parts = bf16[8,16,2048]{2,1,0:T(8,128)(2,1)S(1)} async-done(((bf16[8,16,2048]{2,1,0:T(8,128)(2,1)}), bf16[8,16,2048]{2,1,0:T(8,128)(2,1)S(1)}, u32[]{:S(2)}, u32[]{:S(2)}) %all-to-all-start.2) | async-done | bytes 524320 | tf_op jit(solution)/shard_map/all_to_all | solution.py:456
  98.6 0.4 norm_and_dispatch.1
  99.0 18.0 %all_to_all.25 = bf16[16,8,2048]{2,1,0:T(8,128)(2,1)S(1)} all-to-all(bf16[16,8,2048]{2,1,0:T(8,128)(2,1)S(1)} %bitcast.14), channel_id=1, replica_groups=mesh['groups'=2,'ctx'=16] {'ctx'}, dimensions={0} | all-to-all | bytes 1048576 | tf_op jit(solution)/shard_map/all_to_all | solution.py:465
  117.0 7.9 %experts.1 = bf16[128,2048]{1,0:T(8,128)(2,1)} custom-call(bf16[128,2048]{1,0:T(8,128)(2,1)S(1)} %bitcast.12, bf16[2,2048,768]{2,1,0:T(8,128)(2,1)} %w_gate.1, bf16[2,2048,768]{2,1,0:T(8,128)(2,1)} %w_up.1, bf16[2,768,2048]{2,1,0:T(8,128)(2,1)} %w_down.1), custom_call_target="tpu_custom_call" | custom-call | flops 2415919104 | bytes 18874368 | tf_op jit(solution)/shard_map/experts/pallas_call | solution.py:319
  124.9 4.1 %all-to-all-start.4 = ((bf16[16,8,2048]{2,1,0:T(8,128)(2,1)}), bf16[16,8,2048]{2,1,0:T(8,128)(2,1)S(1)}, u32[]{:S(2)}, u32[]{:S(2)}) async-start(bf16[16,8,2048]{2,1,0:T(8,128)(2,1)} %bitcast.10), calls=%async_computation.4 | async-start | bytes 1048576 | tf_op jit(solution)/shard_map/all_to_all | solution.py:469
  129.1 0.1 select_reduce_fusion
  129.2 14.3 %all-to-all-done.4 = bf16[16,8,2048]{2,1,0:T(8,128)(2,1)S(1)} async-done(((bf16[16,8,2048]{2,1,0:T(8,128)(2,1)}), bf16[16,8,2048]{2,1,0:T(8,128)(2,1)S(1)}, u32[]{:S(2)}, u32[]{:S(2)}) %all-to-all-start.4) | async-done | bytes 524320 | tf_op jit(solution)/shard_map/all_to_all | solution.py:469
  143.5 0.9 mix.1
  (44 shorter events, 0.4 us)
Async XLA Ops:
  0.0 6.7 %collective-permute-start.1 = (bf16[16,4096]{1,0:T(8,128)(2,1)}, bf16[16,4096]{1,0:T(8,128)(2,1)S(1)}, u32[]{:S(2)}, u32[]{:S(2)}) collective-permute-start(bf16[16,4096]{1,0:T(8,128)(2,1)} %refs_0_.1), channel_id=1, source_target_pairs={{0,2},{1,3},{2,0},{3,1},{4,6},{5,7},{6,4},{7,5},{8,10},{9,11},{10,... | collective-permute-start | bytes 393224 | tf_op jit(solution)/shard_map/ppermute | solution.py:391
  6.7 17.5 %collective-permute-start.3 = (bf16[1024,512]{1,0:T(8,128)(2,1)}, bf16[1024,512]{1,0:T(8,128)(2,1)S(1)}, u32[]{:S(2)}, u32[]{:S(2)}) collective-permute-start(bf16[1024,512]{1,0:T(8,128)(2,1)} %refs_4_.3), channel_id=1, source_target_pairs={{0,1},{1,0},{2,3},{3,2},{4,5},{5,4},{6,7},{7,6},{8,9},{9,8},{10,11... | collective-permute-start | bytes 3145736 | tf_op jit(solution)/shard_map/ppermute | solution.py:403
  6.7 17.5 %collective-permute-start.4 = (bf16[1024,512]{1,0:T(8,128)(2,1)}, bf16[1024,512]{1,0:T(8,128)(2,1)S(1)}, u32[]{:S(2)}, u32[]{:S(2)}) collective-permute-start(bf16[1024,512]{1,0:T(8,128)(2,1)} %refs_6_.3), channel_id=1, source_target_pairs={{0,1},{1,0},{2,3},{3,2},{4,5},{5,4},{6,7},{7,6},{8,9},{9,8},{10,11... | collective-permute-start | bytes 3145736 | tf_op jit(solution)/shard_map/ppermute | solution.py:404
  7.2 7.5 %collective-permute-start = (bf16[16,4096]{1,0:T(8,128)(2,1)}, bf16[16,4096]{1,0:T(8,128)(2,1)}, u32[]{:S(2)}, u32[]{:S(2)}) collective-permute-start(bf16[16,4096]{1,0:T(8,128)(2,1)} %refs_0_.1), channel_id=1, source_target_pairs={{0,4},{1,5},{2,6},{3,7},{4,0},{5,1},{6,2},{7,3},{8,12},{9,13},{10,... | collective-permute-start | bytes 393224 | tf_op jit(solution)/shard_map/ppermute | solution.py:395
  9.0 13.1 %collective-permute-start.5 = (bf16[16,4096]{1,0:T(8,128)(2,1)}, bf16[16,4096]{1,0:T(8,128)(2,1)S(1)}, u32[]{:S(2)}, u32[]{:S(2)}) collective-permute-start(bf16[16,4096]{1,0:T(8,128)(2,1)} %refs_0_.1), channel_id=1, source_target_pairs={{0,8},{1,9},{2,10},{3,11},{4,12},{5,13},{6,14},{7,15},{8,0},{9,1},... | collective-permute-start | bytes 393224 | tf_op jit(solution)/shard_map/ppermute | solution.py:395
  11.6 12.1 %collective-permute-start.7 = (bf16[16,4096]{1,0:T(8,128)(2,1)}, bf16[16,4096]{1,0:T(8,128)(2,1)S(1)}, u32[]{:S(2)}, u32[]{:S(2)}) collective-permute-start(bf16[16,4096]{1,0:T(8,128)(2,1)} %refs_0_.1), channel_id=1, source_target_pairs={{0,12},{1,13},{2,14},{3,15},{4,8},{5,9},{6,10},{7,11},{8,4},{9,5},... | collective-permute-start | bytes 393224 | tf_op jit(solution)/shard_map/ppermute | solution.py:395
  14.7 9.5 %collective-permute-start.2 = (bf16[16,4096]{1,0:T(8,128)(2,1)}, bf16[16,4096]{1,0:T(8,128)(2,1)}, u32[]{:S(2)}, u32[]{:S(2)}) collective-permute-start(bf16[16,4096]{1,0:T(8,128)(2,1)} %collective-permute-done.refs_1_), channel_id=1, source_target_pairs={{0,2},{1,3},{2,0},{3,1},{4,6},{5,7},{6,4},{7,5},{8,10},{9,11},{10,... | collective-permute-start | bytes 393224 | tf_op jit(solution)/shard_map/ppermute | solution.py:391
  17.5 23.9 %copy-start = (bf16[256,2048]{1,0:T(8,128)(2,1)S(1)}, bf16[256,2048]{1,0:T(8,128)(2,1)}, u32[]{:S(2)}) copy-start(bf16[256,2048]{1,0:T(8,128)(2,1)} %refs_2_.1) | copy-start | bytes 3145732
  22.1 12.4 %collective-permute-start.6 = (bf16[16,4096]{1,0:T(8,128)(2,1)S(1)}, bf16[16,4096]{1,0:T(8,128)(2,1)S(1)}, u32[]{:S(2)}, u32[]{:S(2)}) collective-permute-start(bf16[16,4096]{1,0:T(8,128)(2,1)S(1)} %collective-permute-done.5.refs_0_), channel_id=1, source_target_pairs={{0,2},{1,3},{2,0},{3,1},{4,6},{5,7},{6,4},{7,5},{8,10},{9,11},{10,... | collective-permute-start | bytes 393224 | tf_op jit(solution)/shard_map/ppermute | solution.py:391
  23.6 11.5 %collective-permute-start.8 = (bf16[16,4096]{1,0:T(8,128)(2,1)S(1)}, bf16[16,4096]{1,0:T(8,128)(2,1)S(1)}, u32[]{:S(2)}, u32[]{:S(2)}) collective-permute-start(bf16[16,4096]{1,0:T(8,128)(2,1)S(1)} %collective-permute-done.7.refs_1_), channel_id=1, source_target_pairs={{0,2},{1,3},{2,0},{3,1},{4,6},{5,7},{6,4},{7,5},{8,10},{9,11},{10,... | collective-permute-start | bytes 393224 | tf_op jit(solution)/shard_map/ppermute | solution.py:391
  24.1 11.6 %copy-start.3 = (bf16[1024,512]{1,0:T(8,128)(2,1)}, bf16[1024,512]{1,0:T(8,128)(2,1)S(1)}, u32[]{:S(2)}) copy-start(bf16[1024,512]{1,0:T(8,128)(2,1)S(1)} %collective-permute-done.3.refs_5_) | copy-start | bytes 3145732
  24.2 11.6 %copy-start.5 = (bf16[1024,512]{1,0:T(8,128)(2,1)}, bf16[1024,512]{1,0:T(8,128)(2,1)S(1)}, u32[]{:S(2)}) copy-start(bf16[1024,512]{1,0:T(8,128)(2,1)S(1)} %collective-permute-done.4.refs_7_) | copy-start | bytes 3145732
  34.5 0.6 copy-start.7
  35.1 0.7 copy-start.9
  35.8 20.5 %all-to-all-start = ((bf16[8,272,128]{2,1,0:T(8,128)(2,1)}), bf16[8,272,128]{2,1,0:T(8,128)(2,1)S(1)}, u32[]{:S(2)}, u32[]{:S(2)}) async-start(bf16[8,272,128]{2,1,0:T(8,128)(2,1)} %attention.2), calls=%async_computation | async-start | bytes 1114112 | tf_op jit(solution)/shard_map/all_to_all | solution.py:450
  41.4 57.1 %copy-start.2 = (bf16[16,2048]{1,0:T(8,128)(2,1)S(1)}, bf16[16,2048]{1,0:T(8,128)(2,1)}, u32[]{:S(2)}) copy-start(bf16[16,2048]{1,0:T(8,128)(2,1)} %residual.1) | copy-start | bytes 196612
  41.4 20.9 %collective-permute-start.9 = (bf16[256,2048]{1,0:T(8,128)(2,1)S(1)}, bf16[256,2048]{1,0:T(8,128)(2,1)S(1)}, u32[]{:S(2)}, u32[]{:S(2)}) collective-permute-start(bf16[256,2048]{1,0:T(8,128)(2,1)S(1)} %copy-done), channel_id=1, source_target_pairs={{0,1},{1,0},{2,3},{3,2},{4,5},{5,4},{6,7},{7,6},{8,9},{9,8},{10,11... | collective-permute-start | bytes 3145736 | tf_op jit(solution)/shard_map/ppermute | solution.py:454
  41.5 1.3 copy-start.4
  42.7 1.2 copy-start.6
  43.9 0.9 copy-start.8
  44.8 0.9 copy-start.10
  45.8 38.1 %copy-start.11 = (bf16[2048]{0:T(1024)(128)(2,1)S(1)}, bf16[2048]{0:T(1024)(128)(2,1)}, u32[]{:S(2)}) copy-start(bf16[2048]{0:T(1024)(128)(2,1)} %param.22) | copy-start | bytes 12292
  45.8 38.1 %copy-start.12 = (s32[16,8]{0,1:T(8,128)S(1)}, s32[16,8]{0,1:T(8,128)}, u32[]{:S(2)}) copy-start(s32[16,8]{0,1:T(8,128)} %param.23) | copy-start | bytes 1540
  55.5 0.8 copy-start.1
  56.3 21.8 %all-to-all-start.1 = ((bf16[8,272,128]{2,1,0:T(8,128)(2,1)}), bf16[8,272,128]{2,1,0:T(8,128)(2,1)S(1)}, u32[]{:S(2)}, u32[]{:S(2)}) async-start(bf16[8,272,128]{2,1,0:T(8,128)(2,1)} %copy-done.1), calls=%async_computation.1 | async-start | bytes 1114112 | tf_op jit(solution)/shard_map/all_to_all | solution.py:450
  80.2 18.3 %all-to-all-start.2 = ((bf16[8,16,2048]{2,1,0:T(8,128)(2,1)}), bf16[8,16,2048]{2,1,0:T(8,128)(2,1)S(1)}, u32[]{:S(2)}, u32[]{:S(2)}) async-start(bf16[8,16,2048]{2,1,0:T(8,128)(2,1)} %bitcast.6), calls=%async_computation.2 | async-start | bytes 1048576 | tf_op jit(solution)/shard_map/all_to_all | solution.py:456
  117.0 12.0 %copy-start.13 = (f32[16,8]{0,1:T(8,128)S(1)}, f32[16,8]{0,1:T(8,128)}, u32[]{:S(2)}) copy-start(f32[16,8]{0,1:T(8,128)} %param.24) | copy-start | bytes 1540
  124.9 18.6 %all-to-all-start.4 = ((bf16[16,8,2048]{2,1,0:T(8,128)(2,1)}), bf16[16,8,2048]{2,1,0:T(8,128)(2,1)S(1)}, u32[]{:S(2)}, u32[]{:S(2)}) async-start(bf16[16,8,2048]{2,1,0:T(8,128)(2,1)} %bitcast.10), calls=%async_computation.4 | async-start | bytes 1048576 | tf_op jit(solution)/shard_map/all_to_all | solution.py:469

commit v17 on v13

--- a/solution.py
+++ b/solution.py
@@ -178,8 +178,14 @@
 
 
 def project_body(rows, place, *refs):
-    *chunks, weight_own, weight_other, out, turned = refs
+    *chunks, weight_own, weight_other, out, turned, own_held, other_held, sems = refs
     core = place[3]
+    copies = [
+        pltpu.make_async_copy(weight_own, own_held, sems.at[0]),
+        pltpu.make_async_copy(weight_other, other_held, sems.at[1]),
+    ]
+    for copy in copies:
+        copy.start()
     chips, height, _ = chunks[0].shape
     base = height - STATS
     groups = base // HD
@@ -203,7 +209,9 @@
                 turned[part, near * rows : (near + 1) * rows, h * HD : (h + 1) * HD] = attended[
                     j * rows : (j + 1) * rows
                 ]
-    product = nn_dot(turned[core], weight_own[...]) + nn_dot(turned[1 - core], weight_other[...])
+    for copy in copies:
+        copy.wait()
+    product = nn_dot(turned[core], own_held[...]) + nn_dot(turned[1 - core], other_held[...])
     out[...] = product.astype(BF16)
 
 
@@ -212,16 +220,23 @@
     vmem = pl.BlockSpec(memory_space=pltpu.VMEM)
     return pl.pallas_call(
         functools.partial(project_body, rows),
-        in_specs=[pl.BlockSpec(memory_space=pltpu.SMEM)] + [vmem] * (len(chunks) + 2),
+        in_specs=[pl.BlockSpec(memory_space=pltpu.SMEM)]
+        + [vmem] * len(chunks)
+        + [pl.BlockSpec(memory_space=pl.ANY)] * 2,
         out_specs=vmem,
         out_shape=jax.ShapeDtypeStruct((2 * rows, width), BF16),
-        scratch_shapes=[pltpu.VMEM((CORES, 2 * rows, depth), BF16)],
+        scratch_shapes=[
+            pltpu.VMEM((CORES, 2 * rows, depth), BF16),
+            pltpu.VMEM((depth, width), BF16),
+            pltpu.VMEM((depth, width), BF16),
+            pltpu.SemaphoreType.DMA((2,)),
+        ],
         compiler_params=pltpu.CompilerParams(vmem_limit_bytes=32 * MIB),
         cost_estimate=pl.CostEstimate(
             flops=8 * rows * width * depth, bytes_accessed=4 * MIB, transcendentals=0
         ),
         name="project",
-    )(place, *chunks, weight_own, weight_other)
+    )(place, *chunks, pltpu.with_memory_space_constraint(weight_own, pltpu.HBM), weight_other)
 
 
 def norm_body(parts, residual, gain, chooser, middle_out, sent):
@@ -259,27 +274,28 @@
     experts, _, depth = w_gate.shape
     rows, width = arrived.shape
     pieces = [(e, f) for e in range(experts) for f in range(0, depth, step)]
-    copies = []
+    order = []
     for n, (e, f) in enumerate(pieces):
-        down = pl.ds(f, step)
-        copies.append(
-            [
-                pltpu.make_async_copy(w_gate.at[e, :, down], gate_held.at[n], sems.at[n, 0]),
-                pltpu.make_async_copy(w_up.at[e, :, down], up_held.at[n], sems.at[n, 1]),
-                pltpu.make_async_copy(w_down.at[e, down, :], down_held.at[n], sems.at[n, 2]),
-            ]
-        )
-    for piece in copies:
-        for copy in piece[:2]:
-            copy.start()
-    for piece in copies:
-        piece[2].start()
+        columns = pl.ds(f, step)
+        order.append(pltpu.make_async_copy(w_gate.at[e, :, columns], gate_held.at[n], sems.at[n, 0]))
+        order.append(pltpu.make_async_copy(w_up.at[e, :, columns], up_held.at[n], sems.at[n, 1]))
+    for n, (e, f) in enumerate(pieces):
+        order.append(pltpu.make_async_copy(w_down.at[e, pl.ds(f, step), :], down_held.at[n], sems.at[n, 2]))
+    window = 6
+    for copy in order[:window]:
+        copy.start()
+
+    def await_copy(k):
+        order[k].wait()
+        if k + window < len(order):
+            order[k + window].start()
+
     slot = lax.broadcasted_iota(jnp.int32, (rows, 1), 0)
     values = arrived[...]
     hidden = []
     for n, (e, f) in enumerate(pieces):
-        copies[n][0].wait()
-        copies[n][1].wait()
+        await_copy(2 * n)
+        await_copy(2 * n + 1)
         gate = nn_dot(values, gate_held[n])
         upward = nn_dot(values, up_held[n])
         part = gate / (1.0 + jnp.exp(-gate)) * upward
@@ -287,7 +303,7 @@
         hidden.append(jnp.where(mine, part, 0.0).astype(BF16))
     total = None
     for n in range(len(pieces)):
-        copies[n][2].wait()
+        await_copy(2 * len(pieces) + n)
         term = nn_dot(hidden[n], down_held[n])
         total = term if total is None else total + term
     out[...] = total.astype(BF16)

time: 131 us -> 133 us (1.015)
  no operation moved by 1% of the time
where the time goes in v17:
time: 133 us; the launch traced here: 132 us
  waiting for transfers between devices  52.6 us (40%)
  Pallas kernels  30.5 us (23%)
  starting transfers between devices  25.5 us (19%)
  blocking collectives  18 us (14%)
  local copies, waits for them, and re-layouts  4.83 us (4%)
    all_to_all x2, waiting for transfers between devices, on_device(): lax.all_to_all(sums, 'ctx', split_axis=0, concat_axis=0, axis_index_group...  18.2 us
    all_to_all x1, blocking collectives, on_device(): lax.all_to_all(outgoing.reshape(devices, experts * MOST, width), 'ctx', s...  18 us
    pallas_call x2, Pallas kernels, attention(): pl.pallas_call(functools.partial(attention_body, shape), grid_spec=pltpu....  18 us
    all_to_all x1, waiting for transfers between devices, on_device(): lax.all_to_all(produced.reshape(devices, experts * MOST, width), 'ctx', s...  14.3 us
    all_to_all x1, waiting for transfers between devices, on_device(): lax.all_to_all(share.reshape(chips, home_rows, width), 'ctx', split_axis=...  13.8 us
    all_to_all x2, starting transfers between devices, on_device(): lax.all_to_all(sums, 'ctx', split_axis=0, concat_axis=0, axis_index_group...  8.86 us
    pallas_call x1, Pallas kernels, run_experts(): pl.pallas_call(functools.partial(experts_body, step), in_specs=[vmem] + [...  8.13 us
    ppermute x3, waiting for transfers between devices, on_device(): lax.ppermute(queries, 'ctx', [(i, i ^ 2 * CORES * k) for i in range(devic...  6.34 us
  transfers between devices with their start and end apart: 13, of which 5 were waited for; matrix products, arithmetic and copies ran while one was open for 3% of the time, Pallas kernels for 14%

profile of v17, /device:TPU:0, one launch (start us, length us, event | category | flops | bytes accessed | tf_op | source)
XLA Modules:
  0.0 132.0 jit_solution(1920342855485901367)
XLA Ops:
  0.0 3.0 %collective-permute-start.1 = (bf16[16,4096]{1,0:T(8,128)(2,1)}, bf16[16,4096]{1,0:T(8,128)(2,1)S(1)}, u32[]{:S(2)}, u32[]{:S(2)}) collective-permute-start(bf16[16,4096]{1,0:T(8,128)(2,1)} %refs_0_.1), channel_id=1, source_target_pairs={{0,2},{1,3},{2,0},{3,1},{4,6},{5,7},{6,4},{7,5},{8,10},{9,11},{10,... | collective-permute-start | bytes 393224 | tf_op jit(solution)/shard_map/ppermute | solution.py:392
  3.0 1.6 %collective-permute-start = (bf16[16,4096]{1,0:T(8,128)(2,1)}, bf16[16,4096]{1,0:T(8,128)(2,1)S(1)}, u32[]{:S(2)}, u32[]{:S(2)}) collective-permute-start(bf16[16,4096]{1,0:T(8,128)(2,1)} %refs_0_.1), channel_id=1, source_target_pairs={{0,4},{1,5},{2,6},{3,7},{4,0},{5,1},{6,2},{7,3},{8,12},{9,13},{10,... | collective-permute-start | bytes 393224 | tf_op jit(solution)/shard_map/ppermute | solution.py:396
  4.5 2.6 %collective-permute-start.5 = (bf16[16,4096]{1,0:T(8,128)(2,1)}, bf16[16,4096]{1,0:T(8,128)(2,1)S(1)}, u32[]{:S(2)}, u32[]{:S(2)}) collective-permute-start(bf16[16,4096]{1,0:T(8,128)(2,1)} %refs_0_.1), channel_id=1, source_target_pairs={{0,8},{1,9},{2,10},{3,11},{4,12},{5,13},{6,14},{7,15},{8,0},{9,1},... | collective-permute-start | bytes 393224 | tf_op jit(solution)/shard_map/ppermute | solution.py:396
  7.1 0.2 collective-permute-start.6
  7.4 0.8 reshape.66
  8.1 0.1 collective-permute-start.3
  8.2 1.5 %copy.23 = bf16[1024,512]{0,1:T(8,128)(2,1)S(1)} copy(bf16[1024,512]{1,0:T(8,128)(2,1)} %param.18) | data formatting | bytes 2097152 | tf_op jit(solution)/shard_map/optimization_barrier | solution.py:405
  9.7 0.6 collective-permute-start.4
  10.2 0.1 fusion.2
  10.3 0.1 tile.40
  10.4 0.1 tile.42.refs_10_
  10.5 0.1 tile.43
  10.6 0.1 tile.45.refs_11_
  10.7 0.1 stack.27.place
  10.8 0.0 collective-permute-done.refs_1_
  10.8 0.3 collective-permute-start.2
  11.1 6.3 %collective-permute-done.5 = bf16[16,4096]{1,0:T(8,128)(2,1)S(1)} collective-permute-done((bf16[16,4096]{1,0:T(8,128)(2,1)}, bf16[16,4096]{1,0:T(8,128)(2,1)S(1)}, u32[]{:S(2)}, u32[]{:S(2)}) %collective-permute-start.5) | collective-permute-done | bytes 131104 | tf_op jit(solution)/shard_map/ppermute | solution.py:396
  17.5 0.6 collective-permute-start.7
  18.0 0.0 collective-permute-done.2.refs_3_
  18.0 0.0 collective-permute-done.3.refs_5_
  18.1 9.0 %attention.2 = bf16[8,272,128]{2,1,0:T(8,128)(2,1)} custom-call(s32[6]{0:T(128)S(1)} %stack.27.place, bf16[16,4096]{1,0:T(8,128)(2,1)} %refs_0_.1, bf16[16,4096]{1,0:T(8,128)(2,1)S(1)} %collective-permute-done.refs_1_, bf16[16,4096]{1,0:T(8,128)(2,1)S(1)} %collective-permute-done.1.refs_2_, bf16[16,4096]{1,0:T(8,128)(2,1)S(1)} %collective-permute-done.2.refs_3_, ...), custom_call_target="tpu_custom_call" | custom-call | flops 3221225472 | bytes 8388608 | tf_op jit(solution)/shard_map/attention/pallas_call | solution.py:139
  27.1 5.2 %all-to-all-start = ((bf16[8,272,128]{2,1,0:T(8,128)(2,1)}), bf16[8,272,128]{2,1,0:T(8,128)(2,1)S(1)}, u32[]{:S(2)}, u32[]{:S(2)}) async-start(bf16[8,272,128]{2,1,0:T(8,128)(2,1)} %attention.2), calls=%async_computation | async-start | bytes 1114112 | tf_op jit(solution)/shard_map/all_to_all | solution.py:454
  32.2 0.1 tile.46
  32.3 0.1 tile.48.refs_10_
  32.4 0.1 tile.49
  32.5 0.1 tile.51.refs_11_
  32.6 1.2 copy-done.2
  33.9 9.0 %attention.3 = bf16[8,272,128]{2,1,0:T(8,128)(2,1)} custom-call(s32[6]{0:T(128)S(1)} %stack.27.place, bf16[32,4096]{1,0:T(8,128)(2,1)S(1)} %constant_dynamic-update-slice_fusion.refs_0_.refs_1_, bf16[32,4096]{1,0:T(8,128)(2,1)S(1)} %constant_dynamic-update-slice_fusion.refs_0_.refs_1_, bf16[32,4096]{1,0:T(8,128)(2,1)S(1)} %collective-permute-done.7.refs_2_.refs_3_, ...), custom_call_target="tpu_custom_call" | custom-call | flops 3221225472 | bytes 8388608 | tf_op jit(solution)/shard_map/attention/pallas_call | solution.py:139
  42.8 3.2 %all-to-all-done.refs_0_ = bf16[8,272,128]{2,1,0:T(8,128)(2,1)S(1)} async-done(((bf16[8,272,128]{2,1,0:T(8,128)(2,1)}), bf16[8,272,128]{2,1,0:T(8,128)(2,1)S(1)}, u32[]{:S(2)}, u32[]{:S(2)}) %all-to-all-start) | async-done | bytes 557088 | tf_op jit(solution)/shard_map/all_to_all | solution.py:454
  46.1 3.7 %all-to-all-start.1 = ((bf16[8,272,128]{2,1,0:T(8,128)(2,1)}), bf16[8,272,128]{2,1,0:T(8,128)(2,1)S(1)}, u32[]{:S(2)}, u32[]{:S(2)}) async-start(bf16[8,272,128]{2,1,0:T(8,128)(2,1)} %attention.3), calls=%async_computation.1 | async-start | bytes 1114112 | tf_op jit(solution)/shard_map/all_to_all | solution.py:454
  49.7 14.9 %all-to-all-done.1.refs_1_ = bf16[8,272,128]{2,1,0:T(8,128)(2,1)S(1)} async-done(((bf16[8,272,128]{2,1,0:T(8,128)(2,1)}), bf16[8,272,128]{2,1,0:T(8,128)(2,1)S(1)}, u32[]{:S(2)}, u32[]{:S(2)}) %all-to-all-start.1) | async-done | bytes 557088 | tf_op jit(solution)/shard_map/all_to_all | solution.py:454
  64.7 3.0 %project.1 = bf16[128,2048]{1,0:T(8,128)(2,1)} custom-call(s32[6]{0:T(128)S(1)} %stack.27.place, bf16[8,272,128]{2,1,0:T(8,128)(2,1)S(1)} %all-to-all-done.refs_0_, bf16[8,272,128]{2,1,0:T(8,128)(2,1)S(1)} %all-to-all-done.1.refs_1_, bf16[256,2048]{1,0:T(8,128)(2,1)} %refs_2_.1, bf16[256,2048]{1,0:T(8,128)(2,1)S(1)} %collective-permute-done.8.refs_3_), custom_call_target="tpu_custom_call" | custom-call | flops 268435456 | bytes 4194304 | tf_op jit(solution)/shard_map/project/pallas_call | solution.py:221
  67.7 3.6 %all-to-all-start.2 = ((bf16[8,16,2048]{2,1,0:T(8,128)(2,1)}), bf16[8,16,2048]{2,1,0:T(8,128)(2,1)S(1)}, u32[]{:S(2)}, u32[]{:S(2)}) async-start(bf16[8,16,2048]{2,1,0:T(8,128)(2,1)} %bitcast.7), calls=%async_computation.2 | async-start | bytes 1048576 | tf_op jit(solution)/shard_map/all_to_all | solution.py:460
  71.4 0.1 copy.24
  71.5 0.1 eq.31
  71.6 0.2 convert_reduce_fusion
  71.7 0.1 reduce_sum.21
  71.8 0.1 fusion
  72.0 0.1 copy.26
  72.1 13.8 %all-to-all-done.2.parts = bf16[8,16,2048]{2,1,0:T(8,128)(2,1)S(1)} async-done(((bf16[8,16,2048]{2,1,0:T(8,128)(2,1)}), bf16[8,16,2048]{2,1,0:T(8,128)(2,1)S(1)}, u32[]{:S(2)}, u32[]{:S(2)}) %all-to-all-start.2) | async-done | bytes 524320 | tf_op jit(solution)/shard_map/all_to_all | solution.py:460
  85.9 0.4 norm_and_dispatch.1
  86.4 18.0 %all_to_all.25 = bf16[16,8,2048]{2,1,0:T(8,128)(2,1)S(1)} all-to-all(bf16[16,8,2048]{2,1,0:T(8,128)(2,1)S(1)} %bitcast.18), channel_id=1, replica_groups=mesh['groups'=2,'ctx'=16] {'ctx'}, dimensions={0} | all-to-all | bytes 1048576 | tf_op jit(solution)/shard_map/all_to_all | solution.py:469
  104.4 8.1 %experts.1 = bf16[128,2048]{1,0:T(8,128)(2,1)} custom-call(bf16[128,2048]{1,0:T(8,128)(2,1)S(1)} %bitcast.13, bf16[2,2048,768]{2,1,0:T(8,128)(2,1)} %w_gate.1, bf16[2,2048,768]{2,1,0:T(8,128)(2,1)} %w_up.1, bf16[2,768,2048]{2,1,0:T(8,128)(2,1)} %w_down.1), custom_call_target="tpu_custom_call" | custom-call | flops 2415919104 | bytes 18874368 | tf_op jit(solution)/shard_map/experts/pallas_call | solution.py:320
  112.5 4.1 %all-to-all-start.4 = ((bf16[16,8,2048]{2,1,0:T(8,128)(2,1)}), bf16[16,8,2048]{2,1,0:T(8,128)(2,1)S(1)}, u32[]{:S(2)}, u32[]{:S(2)}) async-start(bf16[16,8,2048]{2,1,0:T(8,128)(2,1)} %bitcast.11), calls=%async_computation.4 | async-start | bytes 1048576 | tf_op jit(solution)/shard_map/all_to_all | solution.py:473
  116.7 0.1 copy.27
  116.7 0.1 select_reduce_fusion
  116.9 14.3 %all-to-all-done.4 = bf16[16,8,2048]{2,1,0:T(8,128)(2,1)S(1)} async-done(((bf16[16,8,2048]{2,1,0:T(8,128)(2,1)}), bf16[16,8,2048]{2,1,0:T(8,128)(2,1)S(1)}, u32[]{:S(2)}, u32[]{:S(2)}) %all-to-all-start.4) | async-done | bytes 524320 | tf_op jit(solution)/shard_map/all_to_all | solution.py:473
  131.1 0.9 mix.1
  (29 shorter events, 0.1 us)
Async XLA Ops:
  0.0 8.1 %collective-permute-start.1 = (bf16[16,4096]{1,0:T(8,128)(2,1)}, bf16[16,4096]{1,0:T(8,128)(2,1)S(1)}, u32[]{:S(2)}, u32[]{:S(2)}) collective-permute-start(bf16[16,4096]{1,0:T(8,128)(2,1)} %refs_0_.1), channel_id=1, source_target_pairs={{0,2},{1,3},{2,0},{3,1},{4,6},{5,7},{6,4},{7,5},{8,10},{9,11},{10,... | collective-permute-start | bytes 393224 | tf_op jit(solution)/shard_map/ppermute | solution.py:392
  3.0 7.8 %collective-permute-start = (bf16[16,4096]{1,0:T(8,128)(2,1)}, bf16[16,4096]{1,0:T(8,128)(2,1)S(1)}, u32[]{:S(2)}, u32[]{:S(2)}) collective-permute-start(bf16[16,4096]{1,0:T(8,128)(2,1)} %refs_0_.1), channel_id=1, source_target_pairs={{0,4},{1,5},{2,6},{3,7},{4,0},{5,1},{6,2},{7,3},{8,12},{9,13},{10,... | collective-permute-start | bytes 393224 | tf_op jit(solution)/shard_map/ppermute | solution.py:396
  4.5 12.9 %collective-permute-start.5 = (bf16[16,4096]{1,0:T(8,128)(2,1)}, bf16[16,4096]{1,0:T(8,128)(2,1)S(1)}, u32[]{:S(2)}, u32[]{:S(2)}) collective-permute-start(bf16[16,4096]{1,0:T(8,128)(2,1)} %refs_0_.1), channel_id=1, source_target_pairs={{0,8},{1,9},{2,10},{3,11},{4,12},{5,13},{6,14},{7,15},{8,0},{9,1},... | collective-permute-start | bytes 393224 | tf_op jit(solution)/shard_map/ppermute | solution.py:396
  7.1 10.3 %collective-permute-start.6 = (bf16[16,4096]{1,0:T(8,128)(2,1)}, bf16[16,4096]{1,0:T(8,128)(2,1)S(1)}, u32[]{:S(2)}, u32[]{:S(2)}) collective-permute-start(bf16[16,4096]{1,0:T(8,128)(2,1)} %refs_0_.1), channel_id=1, source_target_pairs={{0,12},{1,13},{2,14},{3,15},{4,8},{5,9},{6,10},{7,11},{8,4},{9,5},... | collective-permute-start | bytes 393224 | tf_op jit(solution)/shard_map/ppermute | solution.py:396
  8.1 9.9 %collective-permute-start.3 = (bf16[1024,512]{1,0:T(8,128)(2,1)}, bf16[1024,512]{1,0:T(8,128)(2,1)S(1)}, u32[]{:S(2)}, u32[]{:S(2)}) collective-permute-start(bf16[1024,512]{1,0:T(8,128)(2,1)} %refs_4_.3), channel_id=1, source_target_pairs={{0,1},{1,0},{2,3},{3,2},{4,5},{5,4},{6,7},{7,6},{8,9},{9,8},{10,11... | collective-permute-start | bytes 3145736 | tf_op jit(solution)/shard_map/ppermute | solution.py:406
  9.7 8.4 %collective-permute-start.4 = (bf16[512,1024]{1,0:T(8,128)(2,1)S(1)}, bf16[512,1024]{1,0:T(8,128)(2,1)}, u32[]{:S(2)}, u32[]{:S(2)}) collective-permute-start(bf16[512,1024]{1,0:T(8,128)(2,1)S(1)} %bitcast.15), channel_id=1, source_target_pairs={{0,1},{1,0},{2,3},{3,2},{4,5},{5,4},{6,7},{7,6},{8,9},{9,8},{10,11... | collective-permute-start | bytes 3145736 | tf_op jit(solution)/shard_map/ppermute | solution.py:408
  10.8 7.3 %collective-permute-start.2 = (bf16[16,4096]{1,0:T(8,128)(2,1)S(1)}, bf16[16,4096]{1,0:T(8,128)(2,1)S(1)}, u32[]{:S(2)}, u32[]{:S(2)}) collective-permute-start(bf16[16,4096]{1,0:T(8,128)(2,1)S(1)} %collective-permute-done.refs_1_), channel_id=1, source_target_pairs={{0,2},{1,3},{2,0},{3,1},{4,6},{5,7},{6,4},{7,5},{8,10},{9,11},{10,... | collective-permute-start | bytes 393224 | tf_op jit(solution)/shard_map/ppermute | solution.py:392
  17.5 9.6 %collective-permute-start.7 = (bf16[32,4096]{1,0:T(8,128)(2,1)S(1)}, bf16[32,4096]{1,0:T(8,128)(2,1)S(1)}, u32[]{:S(2)}, u32[]{:S(2)}) collective-permute-start(bf16[32,4096]{1,0:T(8,128)(2,1)S(1)} %constant_dynamic-update-slice_fusion.refs_0_.refs_1_), channel_id=1, source_target_pairs={{0,2},{1,3},{2,0},{3,1},{4,6},{5,7},{6,4},{7,5},{8,10},{9,11},{10,... | collective-permute-start | bytes 786440 | tf_op jit(solution)/shard_map/ppermute | solution.py:392
  18.0 9.0 %copy-start.1 = (bf16[1024,512]{1,0:T(8,128)(2,1)}, bf16[1024,512]{1,0:T(8,128)(2,1)S(1)}, u32[]{:S(2)}) copy-start(bf16[1024,512]{1,0:T(8,128)(2,1)S(1)} %collective-permute-done.3.refs_5_) | copy-start | bytes 3145732
  27.1 19.0 %all-to-all-start = ((bf16[8,272,128]{2,1,0:T(8,128)(2,1)}), bf16[8,272,128]{2,1,0:T(8,128)(2,1)S(1)}, u32[]{:S(2)}, u32[]{:S(2)}) async-start(bf16[8,272,128]{2,1,0:T(8,128)(2,1)} %attention.2), calls=%async_computation | async-start | bytes 1114112 | tf_op jit(solution)/shard_map/all_to_all | solution.py:454
  32.6 53.4 %copy-start = (bf16[16,2048]{1,0:T(8,128)(2,1)S(1)}, bf16[16,2048]{1,0:T(8,128)(2,1)}, u32[]{:S(2)}) copy-start(bf16[16,2048]{1,0:T(8,128)(2,1)} %residual.1) | copy-start | bytes 196612
  32.6 17.2 %collective-permute-start.8 = (bf16[256,2048]{1,0:T(8,128)(2,1)}, bf16[256,2048]{1,0:T(8,128)(2,1)S(1)}, u32[]{:S(2)}, u32[]{:S(2)}) collective-permute-start(bf16[256,2048]{1,0:T(8,128)(2,1)} %refs_2_.1), channel_id=1, source_target_pairs={{0,1},{1,0},{2,3},{3,2},{4,5},{5,4},{6,7},{7,6},{8,9},{9,8},{10,11... | collective-permute-start | bytes 3145736 | tf_op jit(solution)/shard_map/ppermute | solution.py:458
  32.6 1.3 copy-start.2
  33.9 37.5 %copy-start.3 = (bf16[2048]{0:T(1024)(128)(2,1)S(1)}, bf16[2048]{0:T(1024)(128)(2,1)}, u32[]{:S(2)}) copy-start(bf16[2048]{0:T(1024)(128)(2,1)} %param.22) | copy-start | bytes 12292
  33.9 37.5 %copy-start.4 = (s32[16,8]{0,1:T(8,128)S(1)}, s32[16,8]{0,1:T(8,128)}, u32[]{:S(2)}) copy-start(s32[16,8]{0,1:T(8,128)} %param.23) | copy-start | bytes 1540
  46.1 18.6 %all-to-all-start.1 = ((bf16[8,272,128]{2,1,0:T(8,128)(2,1)}), bf16[8,272,128]{2,1,0:T(8,128)(2,1)S(1)}, u32[]{:S(2)}, u32[]{:S(2)}) async-start(bf16[8,272,128]{2,1,0:T(8,128)(2,1)} %attention.3), calls=%async_computation.1 | async-start | bytes 1114112 | tf_op jit(solution)/shard_map/all_to_all | solution.py:454
  67.7 18.2 %all-to-all-start.2 = ((bf16[8,16,2048]{2,1,0:T(8,128)(2,1)}), bf16[8,16,2048]{2,1,0:T(8,128)(2,1)S(1)}, u32[]{:S(2)}, u32[]{:S(2)}) async-start(bf16[8,16,2048]{2,1,0:T(8,128)(2,1)} %bitcast.7), calls=%async_computation.2 | async-start | bytes 1048576 | tf_op jit(solution)/shard_map/all_to_all | solution.py:460
  104.4 12.3 %copy-start.5 = (f32[16,8]{0,1:T(8,128)S(1)}, f32[16,8]{0,1:T(8,128)}, u32[]{:S(2)}) copy-start(f32[16,8]{0,1:T(8,128)} %param.24) | copy-start | bytes 1540
  112.5 18.6 %all-to-all-start.4 = ((bf16[16,8,2048]{2,1,0:T(8,128)(2,1)}), bf16[16,8,2048]{2,1,0:T(8,128)(2,1)S(1)}, u32[]{:S(2)}, u32[]{:S(2)}) async-start(bf16[16,8,2048]{2,1,0:T(8,128)(2,1)} %bitcast.11), calls=%async_computation.4 | async-start | bytes 1048576 | tf_op jit(solution)/shard_map/all_to_all | solution.py:473

commit v18 on v13

--- a/solution.py
+++ b/solution.py
@@ -94,12 +94,12 @@
             probs[at, across[g]] = jnp.exp2((scores[at, across[g]] - peak[g]).astype(BF16))
     ones = jnp.ones((STATS, cache_here), BF16)
     sums = [
-        nn_dot(jnp.concatenate([value_own[heads[g], :], ones], axis=0), probs[:cache_here, across[g]])
+        nn_dot(jnp.concatenate([value_own[:, heads[g]].T, ones], axis=0), probs[:cache_here, across[g]])
         for g in each
     ]
     sums = [
         sums[g]
-        + nn_dot(jnp.concatenate([value_other[heads[g], :], ones], axis=0), probs[cache_here:, across[g]])
+        + nn_dot(jnp.concatenate([value_other[:, heads[g]].T, ones], axis=0), probs[cache_here:, across[g]])
         for g in each
     ]
     for g in each:
@@ -145,8 +145,7 @@
                 pl.BlockSpec((home_rows, columns), functools.partial(lambda n, g, place: (n, g), n))
                 for _, n in query_blocks
             ]
-            + [pl.BlockSpec((cache_here, together * HD), kv)] * 2
-            + [pl.BlockSpec((together * HD, cache_here), lambda g, place: (g, 0))] * 2
+            + [pl.BlockSpec((cache_here, together * HD), kv)] * 4
             + [pl.BlockSpec((home_rows, together * HD), kv)] * 2
             + [pl.BlockSpec(lens.shape, whole)] * 2,
             out_specs=pl.BlockSpec((together * owners, height, HD), lambda g, place: (g, 0, 0)),
@@ -169,7 +168,8 @@
         *[block for block, _ in query_blocks],
         pltpu.with_memory_space_constraint(keys[0], pltpu.HBM),
         keys[1],
-        *values,
+        pltpu.with_memory_space_constraint(values[0], pltpu.HBM),
+        values[1],
         pltpu.with_memory_space_constraint(new_key, pltpu.HBM),
         pltpu.with_memory_space_constraint(new_value, pltpu.HBM),
         lens,
@@ -372,24 +372,27 @@
     half = rings // 2
     chunk_rows = 2 * half * home_rows
 
+    def from_peer(block, ring, side):
+        far_end = 2 * CORES * ring + CORES * side
+        return lax.ppermute(block, "ctx", [(i, i ^ far_end) for i in range(devices)])
+
     def across_y(block):
-        return lax.ppermute(block, "ctx", across)
-
-    neighbour = across_y(queries)
-    by_ring = [queries] + [
-        lax.ppermute(queries, "ctx", [(i, i ^ (2 * CORES * k)) for i in range(devices)])
-        for k in range(1, rings)
-    ]
+        return from_peer(block, 0, 1)
+
+    by_ring = [queries] + [None] * (half - 1) + [from_peer(queries, k, 0) for k in range(half, rings)]
+    key_other = lax.ppermute(key_cache, "ctx", swap)
+    late_queries, key_other = lax.optimization_barrier((queries, key_other))
+    neighbour = across_y(late_queries)
+    by_ring[1:half] = [from_peer(late_queries, k, 0) for k in range(1, half)]
     near_blocks = [(pltpu.with_memory_space_constraint(queries, pltpu.HBM), 0)]
-    near_blocks += [(block, 0) for block in by_ring[1:half]]
-    near_blocks += [(neighbour, 0)] + [(across_y(block), 0) for block in by_ring[1:half]]
+    near = by_ring[1:half] + [neighbour] + [from_peer(late_queries, k, 1) for k in range(1, half)]
+    near, by_ring[half:] = lax.optimization_barrier((near, by_ring[half:]))
+    near_blocks += [(block, 0) for block in near]
     far = jnp.concatenate(by_ring[half:], axis=0)
     far_across = across_y(far)
     far_blocks = [(far, k) for k in range(half)] + [(far_across, k) for k in range(half)]
-    late_keys, late_values, _ = lax.optimization_barrier((key_cache, value_cache, neighbour))
-    key_other = lax.ppermute(late_keys, "ctx", swap)
-    value_turned = late_values.T
-    value_other = lax.ppermute(value_turned, "ctx", swap)
+    late_values, neighbour = lax.optimization_barrier((value_cache, neighbour))
+    value_other = lax.ppermute(late_values, "ctx", swap)
     place = jnp.stack([chip, index * cache_here, (index ^ 1) * cache_here, core, chip % 2, chip // 2]).astype(jnp.int32)
 
     def in_lanes(by_chip, n):
@@ -422,7 +425,7 @@
             place,
             blocks,
             (key_cache, key_other),
-            (value_turned, value_other),
+            (value_cache, value_other),
             new_key,
             new_value,
             lens[chunk],

time: 131 us -> 138 us (1.053)
  waiting for transfers between devices: 52.6 us -> 58.5 us
    ppermute x8, waiting for transfers between devices: 6.35 us -> 12.1 us  [the longest x6 9.64 us: from_peer(): lax.ppermute(block, 'ctx', [(i, i ^ far_end) for i in range(devices)])]
    unnamed x13 -> x19, local copies, waits for them, and re-layouts: 0.17 us -> 2.24 us
    ppermute x8, starting transfers between devices: 8.86 us -> 10.9 us  [the longest x6 10.4 us: from_peer(): lax.ppermute(block, 'ctx', [(i, i ^ far_end) for i in range(devices)])]
    optimization_barrier x1 -> x0, local copies, waits for them, and re-layouts: 1.49 us -> none  [on_device(): lax.optimization_barrier((key_cache, value_cache, neighbour))]
  transfers between devices with their start and end apart: 13 -> 13, of which waited for: 5 -> 8; matrix products, arithmetic and copies ran while one was open for 3% -> 2% of each run, Pallas kernels for 14% -> 13%
where the time goes in v18:
time: 138 us; the launch traced here: 137 us
  waiting for transfers between devices  58.5 us (42%)
  Pallas kernels  29 us (21%)
  starting transfers between devices  26.8 us (19%)
  blocking collectives  18 us (13%)
  local copies, waits for them, and re-layouts  4.15 us (3%)
    all_to_all x2, waiting for transfers between devices, on_device(): lax.all_to_all(sums, 'ctx', split_axis=0, concat_axis=0, axis_index_group...  18.2 us
    all_to_all x1, blocking collectives, on_device(): lax.all_to_all(outgoing.reshape(devices, experts * MOST, width), 'ctx', s...  18 us
    pallas_call x2, Pallas kernels, attention(): pl.pallas_call(functools.partial(attention_body, shape), grid_spec=pltpu....  17.8 us
    all_to_all x1, waiting for transfers between devices, on_device(): lax.all_to_all(produced.reshape(devices, experts * MOST, width), 'ctx', s...  14.3 us
    all_to_all x1, waiting for transfers between devices, on_device(): lax.all_to_all(share.reshape(chips, home_rows, width), 'ctx', split_axis=...  13.8 us
    ppermute x6, starting transfers between devices, from_peer(): lax.ppermute(block, 'ctx', [(i, i ^ far_end) for i in range(devices)])  10.4 us
    ppermute x6, waiting for transfers between devices, from_peer(): lax.ppermute(block, 'ctx', [(i, i ^ far_end) for i in range(devices)])  9.64 us
    all_to_all x2, starting transfers between devices, on_device(): lax.all_to_all(sums, 'ctx', split_axis=0, concat_axis=0, axis_index_group...  8.19 us
  transfers between devices with their start and end apart: 13, of which 8 were waited for; matrix products, arithmetic and copies ran while one was open for 2% of the time, Pallas kernels for 13%

profile of v18, /device:TPU:0, one launch (start us, length us, event | category | flops | bytes accessed | tf_op | source)
XLA Modules:
  0.0 137.0 jit_solution(1131589622376373352)
XLA Ops:
  0.0 0.5 collective-permute-start
  0.5 2.5 %collective-permute-done.refs_5_ = bf16[1024,512]{1,0:T(8,128)(2,1)S(1)} collective-permute-done((bf16[1024,512]{1,0:T(8,128)(2,1)}, bf16[1024,512]{1,0:T(8,128)(2,1)S(1)}, u32[]{:S(2)}, u32[]{:S(2)}) %collective-permute-start) | collective-permute-done | bytes 1048608 | tf_op jit(solution)/shard_map/ppermute | solution.py:383
  3.0 2.9 %collective-permute-start.2 = (bf16[16,4096]{1,0:T(8,128)(2,1)}, bf16[16,4096]{1,0:T(8,128)(2,1)S(1)}, u32[]{:S(2)}, u32[]{:S(2)}) collective-permute-start(bf16[16,4096]{1,0:T(8,128)(2,1)} %refs_0_.1), channel_id=1, source_target_pairs={{0,2},{1,3},{2,0},{3,1},{4,6},{5,7},{6,4},{7,5},{8,10},{9,11},{10,... | collective-permute-start | bytes 393224 | tf_op jit(solution)/shard_map/ppermute | solution.py:377
  5.8 2.6 %collective-permute-start.4 = (bf16[16,4096]{1,0:T(8,128)(2,1)}, bf16[16,4096]{1,0:T(8,128)(2,1)S(1)}, u32[]{:S(2)}, u32[]{:S(2)}) collective-permute-start(bf16[16,4096]{1,0:T(8,128)(2,1)} %refs_0_.1), channel_id=1, source_target_pairs={{0,8},{1,9},{2,10},{3,11},{4,12},{5,13},{6,14},{7,15},{8,0},{9,1},... | collective-permute-start | bytes 393224 | tf_op jit(solution)/shard_map/ppermute | solution.py:377
  8.4 1.3 collective-permute-start.5
  9.8 0.8 reshape.66
  10.5 0.2 collective-permute-start.1
  10.8 1.7 %collective-permute-start.3 = (bf16[16,4096]{1,0:T(8,128)(2,1)}, bf16[16,4096]{1,0:T(8,128)(2,1)S(1)}, u32[]{:S(2)}, u32[]{:S(2)}) collective-permute-start(bf16[16,4096]{1,0:T(8,128)(2,1)} %refs_0_.1), channel_id=1, source_target_pairs={{0,6},{1,7},{2,4},{3,5},{4,2},{5,3},{6,0},{7,1},{8,14},{9,15},{10,... | collective-permute-start | bytes 393224 | tf_op jit(solution)/shard_map/ppermute | solution.py:377
  12.5 0.1 fusion.2
  12.6 0.1 tile.40
  12.7 0.1 tile.42.refs_10_
  12.8 0.1 tile.43
  12.9 0.1 tile.45.refs_11_
  13.0 0.1 stack.27.place
  13.0 5.9 %collective-permute-done.4 = bf16[16,4096]{1,0:T(8,128)(2,1)S(1)} collective-permute-done((bf16[16,4096]{1,0:T(8,128)(2,1)}, bf16[16,4096]{1,0:T(8,128)(2,1)S(1)}, u32[]{:S(2)}, u32[]{:S(2)}) %collective-permute-start.4) | collective-permute-done | bytes 131104 | tf_op jit(solution)/shard_map/ppermute | solution.py:377
  19.0 1.8 %collective-permute-done.1.refs_1_ = bf16[16,4096]{1,0:T(8,128)(2,1)S(1)} collective-permute-done((bf16[16,4096]{1,0:T(8,128)(2,1)}, bf16[16,4096]{1,0:T(8,128)(2,1)S(1)}, u32[]{:S(2)}, u32[]{:S(2)}) %collective-permute-start.1) | collective-permute-done | bytes 131104 | tf_op jit(solution)/shard_map/ppermute | solution.py:377
  20.8 1.9 %collective-permute-done.3.refs_3_ = bf16[16,4096]{1,0:T(8,128)(2,1)S(1)} collective-permute-done((bf16[16,4096]{1,0:T(8,128)(2,1)}, bf16[16,4096]{1,0:T(8,128)(2,1)S(1)}, u32[]{:S(2)}, u32[]{:S(2)}) %collective-permute-start.3) | collective-permute-done | bytes 131104 | tf_op jit(solution)/shard_map/ppermute | solution.py:377
  22.7 1.6 %collective-permute-start.7 = (bf16[32,4096]{1,0:T(8,128)(2,1)S(1)}, bf16[32,4096]{1,0:T(8,128)(2,1)S(1)}, u32[]{:S(2)}, u32[]{:S(2)}) collective-permute-start(bf16[32,4096]{1,0:T(8,128)(2,1)S(1)} %constant_dynamic-update-slice_fusion.refs_0_.refs_1_), channel_id=1, source_target_pairs={{0,2},{1,3},{2,0},{3,1},{4,6},{5,7},{6,4},{7,5},{8,10},{9,11},{10,... | collective-permute-start | bytes 786440 | tf_op jit(solution)/shard_map/ppermute | solution.py:377
  24.3 9.2 %attention.2 = bf16[8,272,128]{2,1,0:T(8,128)(2,1)} custom-call(s32[6]{0:T(128)S(1)} %stack.27.place, bf16[16,4096]{1,0:T(8,128)(2,1)} %refs_0_.1, bf16[16,4096]{1,0:T(8,128)(2,1)S(1)} %collective-permute-done.1.refs_1_, bf16[16,4096]{1,0:T(8,128)(2,1)S(1)} %collective-permute-done.2.refs_2_, bf16[16,4096]{1,0:T(8,128)(2,1)S(1)} %collective-permute-done.3.refs_3_, ...), custom_call_target="tpu_custom_call" | custom-call | flops 3221225472 | bytes 8388608 | tf_op jit(solution)/shard_map/attention/pallas_call | solution.py:139
  33.6 4.6 %all-to-all-start = ((bf16[8,272,128]{2,1,0:T(8,128)(2,1)}), bf16[8,272,128]{2,1,0:T(8,128)(2,1)S(1)}, u32[]{:S(2)}, u32[]{:S(2)}) async-start(bf16[8,272,128]{2,1,0:T(8,128)(2,1)} %attention.2), calls=%async_computation | async-start | bytes 1114112 | tf_op jit(solution)/shard_map/all_to_all | solution.py:441
  38.1 0.1 tile.46
  38.2 0.1 tile.48.refs_10_
  38.3 0.1 tile.49
  38.4 0.1 tile.51.refs_11_
  38.5 0.0 collective-permute-start.8
  38.5 1.2 copy-done.4
  39.8 8.6 %attention.3 = bf16[8,272,128]{2,1,0:T(8,128)(2,1)S(1)} custom-call(s32[6]{0:T(128)S(1)} %stack.27.place, bf16[32,4096]{1,0:T(8,128)(2,1)S(1)} %constant_dynamic-update-slice_fusion.refs_0_.refs_1_, bf16[32,4096]{1,0:T(8,128)(2,1)S(1)} %constant_dynamic-update-slice_fusion.refs_0_.refs_1_, bf16[32,4096]{1,0:T(8,128)(2,1)S(1)} %collective-permute-done.7.refs_2_.refs_3_, ...), custom_call_target="tpu_custom_call" | custom-call | flops 3221225472 | bytes 8388608 | tf_op jit(solution)/shard_map/attention/pallas_call | solution.py:139
  48.3 0.8 copy-done.1
  49.1 3.3 %all-to-all-done.refs_0_ = bf16[8,272,128]{2,1,0:T(8,128)(2,1)S(1)} async-done(((bf16[8,272,128]{2,1,0:T(8,128)(2,1)}), bf16[8,272,128]{2,1,0:T(8,128)(2,1)S(1)}, u32[]{:S(2)}, u32[]{:S(2)}) %all-to-all-start) | async-done | bytes 557088 | tf_op jit(solution)/shard_map/all_to_all | solution.py:441
  52.5 3.6 %all-to-all-start.1 = ((bf16[8,272,128]{2,1,0:T(8,128)(2,1)}), bf16[8,272,128]{2,1,0:T(8,128)(2,1)S(1)}, u32[]{:S(2)}, u32[]{:S(2)}) async-start(bf16[8,272,128]{2,1,0:T(8,128)(2,1)} %copy-done.1), calls=%async_computation.1 | async-start | bytes 1114112 | tf_op jit(solution)/shard_map/all_to_all | solution.py:441
  56.1 14.9 %all-to-all-done.1.refs_1_ = bf16[8,272,128]{2,1,0:T(8,128)(2,1)S(1)} async-done(((bf16[8,272,128]{2,1,0:T(8,128)(2,1)}), bf16[8,272,128]{2,1,0:T(8,128)(2,1)S(1)}, u32[]{:S(2)}, u32[]{:S(2)}) %all-to-all-start.1) | async-done | bytes 557088 | tf_op jit(solution)/shard_map/all_to_all | solution.py:441
  71.0 2.1 %project.1 = bf16[128,2048]{1,0:T(8,128)(2,1)} custom-call(s32[6]{0:T(128)S(1)} %stack.27.place, bf16[8,272,128]{2,1,0:T(8,128)(2,1)S(1)} %all-to-all-done.refs_0_, bf16[8,272,128]{2,1,0:T(8,128)(2,1)S(1)} %all-to-all-done.1.refs_1_, bf16[256,2048]{1,0:T(8,128)(2,1)S(1)} %copy-done, bf16[256,2048]{1,0:T(8,128)(2,1)S(1)} %collective-permute-done.8.refs_3_), custom_call_target="tpu_custom_call" | custom-call | flops 268435456 | bytes 4194304 | tf_op jit(solution)/shard_map/project/pallas_call | solution.py:213
  73.1 3.6 %all-to-all-start.2 = ((bf16[8,16,2048]{2,1,0:T(8,128)(2,1)}), bf16[8,16,2048]{2,1,0:T(8,128)(2,1)S(1)}, u32[]{:S(2)}, u32[]{:S(2)}) async-start(bf16[8,16,2048]{2,1,0:T(8,128)(2,1)} %bitcast.6), calls=%async_computation.2 | async-start | bytes 1048576 | tf_op jit(solution)/shard_map/all_to_all | solution.py:447
  76.7 0.1 copy.21
  76.8 0.1 eq.31
  76.9 0.2 convert_reduce_fusion
  77.1 0.1 reduce_sum.21
  77.2 0.1 fusion
  77.3 0.1 copy.23
  77.4 13.8 %all-to-all-done.2.parts = bf16[8,16,2048]{2,1,0:T(8,128)(2,1)S(1)} async-done(((bf16[8,16,2048]{2,1,0:T(8,128)(2,1)}), bf16[8,16,2048]{2,1,0:T(8,128)(2,1)S(1)}, u32[]{:S(2)}, u32[]{:S(2)}) %all-to-all-start.2) | async-done | bytes 524320 | tf_op jit(solution)/shard_map/all_to_all | solution.py:447
  91.2 0.4 norm_and_dispatch.1
  91.7 18.0 %all_to_all.25 = bf16[16,8,2048]{2,1,0:T(8,128)(2,1)S(1)} all-to-all(bf16[16,8,2048]{2,1,0:T(8,128)(2,1)S(1)} %bitcast.14), channel_id=1, replica_groups=mesh['groups'=2,'ctx'=16] {'ctx'}, dimensions={0} | all-to-all | bytes 1048576 | tf_op jit(solution)/shard_map/all_to_all | solution.py:456
  109.7 7.9 %experts.1 = bf16[128,2048]{1,0:T(8,128)(2,1)} custom-call(bf16[128,2048]{1,0:T(8,128)(2,1)S(1)} %bitcast.12, bf16[2,2048,768]{2,1,0:T(8,128)(2,1)} %w_gate.1, bf16[2,2048,768]{2,1,0:T(8,128)(2,1)} %w_up.1, bf16[2,768,2048]{2,1,0:T(8,128)(2,1)} %w_down.1), custom_call_target="tpu_custom_call" | custom-call | flops 2415919104 | bytes 18874368 | tf_op jit(solution)/shard_map/experts/pallas_call | solution.py:304
  117.6 4.1 %all-to-all-start.4 = ((bf16[16,8,2048]{2,1,0:T(8,128)(2,1)}), bf16[16,8,2048]{2,1,0:T(8,128)(2,1)S(1)}, u32[]{:S(2)}, u32[]{:S(2)}) async-start(bf16[16,8,2048]{2,1,0:T(8,128)(2,1)} %bitcast.10), calls=%async_computation.4 | async-start | bytes 1048576 | tf_op jit(solution)/shard_map/all_to_all | solution.py:460
  121.7 0.1 copy.24
  121.8 0.1 select_reduce_fusion
  121.9 14.3 %all-to-all-done.4 = bf16[16,8,2048]{2,1,0:T(8,128)(2,1)S(1)} async-done(((bf16[16,8,2048]{2,1,0:T(8,128)(2,1)}), bf16[16,8,2048]{2,1,0:T(8,128)(2,1)S(1)}, u32[]{:S(2)}, u32[]{:S(2)}) %all-to-all-start.4) | async-done | bytes 524320 | tf_op jit(solution)/shard_map/all_to_all | solution.py:460
  136.1 0.9 mix.1
  (32 shorter events, 0.1 us)
Async XLA Ops:
  0.0 3.0 %collective-permute-start = (bf16[1024,512]{1,0:T(8,128)(2,1)}, bf16[1024,512]{1,0:T(8,128)(2,1)S(1)}, u32[]{:S(2)}, u32[]{:S(2)}) collective-permute-start(bf16[1024,512]{1,0:T(8,128)(2,1)} %refs_4_.3), channel_id=1, source_target_pairs={{0,1},{1,0},{2,3},{3,2},{4,5},{5,4},{6,7},{7,6},{8,9},{9,8},{10,11... | collective-permute-start | bytes 3145736 | tf_op jit(solution)/shard_map/ppermute | solution.py:383
  3.0 30.6 %copy-start.3 = (bf16[1024,512]{1,0:T(8,128)(2,1)}, bf16[1024,512]{1,0:T(8,128)(2,1)S(1)}, u32[]{:S(2)}) copy-start(bf16[1024,512]{1,0:T(8,128)(2,1)S(1)} %collective-permute-done.refs_5_) | copy-start | bytes 3145732
  3.0 9.6 %collective-permute-start.2 = (bf16[16,4096]{1,0:T(8,128)(2,1)}, bf16[16,4096]{1,0:T(8,128)(2,1)S(1)}, u32[]{:S(2)}, u32[]{:S(2)}) collective-permute-start(bf16[16,4096]{1,0:T(8,128)(2,1)} %refs_0_.1), channel_id=1, source_target_pairs={{0,2},{1,3},{2,0},{3,1},{4,6},{5,7},{6,4},{7,5},{8,10},{9,11},{10,... | collective-permute-start | bytes 393224 | tf_op jit(solution)/shard_map/ppermute | solution.py:377
  5.8 13.1 %collective-permute-start.4 = (bf16[16,4096]{1,0:T(8,128)(2,1)}, bf16[16,4096]{1,0:T(8,128)(2,1)S(1)}, u32[]{:S(2)}, u32[]{:S(2)}) collective-permute-start(bf16[16,4096]{1,0:T(8,128)(2,1)} %refs_0_.1), channel_id=1, source_target_pairs={{0,8},{1,9},{2,10},{3,11},{4,12},{5,13},{6,14},{7,15},{8,0},{9,1},... | collective-permute-start | bytes 393224 | tf_op jit(solution)/shard_map/ppermute | solution.py:377
  8.4 10.6 %collective-permute-start.5 = (bf16[16,4096]{1,0:T(8,128)(2,1)}, bf16[16,4096]{1,0:T(8,128)(2,1)S(1)}, u32[]{:S(2)}, u32[]{:S(2)}) collective-permute-start(bf16[16,4096]{1,0:T(8,128)(2,1)} %refs_0_.1), channel_id=1, source_target_pairs={{0,12},{1,13},{2,14},{3,15},{4,8},{5,9},{6,10},{7,11},{8,4},{9,5},... | collective-permute-start | bytes 393224 | tf_op jit(solution)/shard_map/ppermute | solution.py:377
  10.5 10.3 %collective-permute-start.1 = (bf16[16,4096]{1,0:T(8,128)(2,1)}, bf16[16,4096]{1,0:T(8,128)(2,1)S(1)}, u32[]{:S(2)}, u32[]{:S(2)}) collective-permute-start(bf16[16,4096]{1,0:T(8,128)(2,1)} %refs_0_.1), channel_id=1, source_target_pairs={{0,4},{1,5},{2,6},{3,7},{4,0},{5,1},{6,2},{7,3},{8,12},{9,13},{10,... | collective-permute-start | bytes 393224 | tf_op jit(solution)/shard_map/ppermute | solution.py:377
  10.8 11.9 %collective-permute-start.3 = (bf16[16,4096]{1,0:T(8,128)(2,1)}, bf16[16,4096]{1,0:T(8,128)(2,1)S(1)}, u32[]{:S(2)}, u32[]{:S(2)}) collective-permute-start(bf16[16,4096]{1,0:T(8,128)(2,1)} %refs_0_.1), channel_id=1, source_target_pairs={{0,6},{1,7},{2,4},{3,5},{4,2},{5,3},{6,0},{7,1},{8,14},{9,15},{10,... | collective-permute-start | bytes 393224 | tf_op jit(solution)/shard_map/ppermute | solution.py:377
  12.5 11.8 %collective-permute-start.6 = (bf16[1024,512]{1,0:T(8,128)(2,1)}, bf16[1024,512]{1,0:T(8,128)(2,1)}, u32[]{:S(2)}, u32[]{:S(2)}) collective-permute-start(bf16[1024,512]{1,0:T(8,128)(2,1)} %refs_6_.3), channel_id=1, source_target_pairs={{0,1},{1,0},{2,3},{3,2},{4,5},{5,4},{6,7},{7,6},{8,9},{9,8},{10,11... | collective-permute-start | bytes 3145736 | tf_op jit(solution)/shard_map/ppermute | solution.py:395
  22.7 15.8 %copy-start = (bf16[256,2048]{1,0:T(8,128)(2,1)S(1)}, bf16[256,2048]{1,0:T(8,128)(2,1)}, u32[]{:S(2)}) copy-start(bf16[256,2048]{1,0:T(8,128)(2,1)} %refs_2_.1) | copy-start | bytes 3145732
  22.7 10.9 %collective-permute-start.7 = (bf16[32,4096]{1,0:T(8,128)(2,1)S(1)}, bf16[32,4096]{1,0:T(8,128)(2,1)S(1)}, u32[]{:S(2)}, u32[]{:S(2)}) collective-permute-start(bf16[32,4096]{1,0:T(8,128)(2,1)S(1)} %constant_dynamic-update-slice_fusion.refs_0_.refs_1_), channel_id=1, source_target_pairs={{0,2},{1,3},{2,0},{3,1},{4,6},{5,7},{6,4},{7,5},{8,10},{9,11},{10,... | collective-permute-start | bytes 786440 | tf_op jit(solution)/shard_map/ppermute | solution.py:377
  33.6 18.9 %all-to-all-start = ((bf16[8,272,128]{2,1,0:T(8,128)(2,1)}), bf16[8,272,128]{2,1,0:T(8,128)(2,1)S(1)}, u32[]{:S(2)}, u32[]{:S(2)}) async-start(bf16[8,272,128]{2,1,0:T(8,128)(2,1)} %attention.2), calls=%async_computation | async-start | bytes 1114112 | tf_op jit(solution)/shard_map/all_to_all | solution.py:441
  38.5 52.8 %copy-start.2 = (bf16[16,2048]{1,0:T(8,128)(2,1)S(1)}, bf16[16,2048]{1,0:T(8,128)(2,1)}, u32[]{:S(2)}) copy-start(bf16[16,2048]{1,0:T(8,128)(2,1)} %residual.1) | copy-start | bytes 196612
  38.5 17.6 %collective-permute-start.8 = (bf16[256,2048]{1,0:T(8,128)(2,1)S(1)}, bf16[256,2048]{1,0:T(8,128)(2,1)S(1)}, u32[]{:S(2)}, u32[]{:S(2)}) collective-permute-start(bf16[256,2048]{1,0:T(8,128)(2,1)S(1)} %copy-done), channel_id=1, source_target_pairs={{0,1},{1,0},{2,3},{3,2},{4,5},{5,4},{6,7},{7,6},{8,9},{9,8},{10,11... | collective-permute-start | bytes 3145736 | tf_op jit(solution)/shard_map/ppermute | solution.py:445
  38.5 1.3 copy-start.4
  39.7 36.9 %copy-start.5 = (bf16[2048]{0:T(1024)(128)(2,1)S(1)}, bf16[2048]{0:T(1024)(128)(2,1)}, u32[]{:S(2)}) copy-start(bf16[2048]{0:T(1024)(128)(2,1)} %param.22) | copy-start | bytes 12292
  39.8 37.0 %copy-start.6 = (s32[16,8]{0,1:T(8,128)S(1)}, s32[16,8]{0,1:T(8,128)}, u32[]{:S(2)}) copy-start(s32[16,8]{0,1:T(8,128)} %param.23) | copy-start | bytes 1540
  48.3 0.8 copy-start.1
  52.5 18.6 %all-to-all-start.1 = ((bf16[8,272,128]{2,1,0:T(8,128)(2,1)}), bf16[8,272,128]{2,1,0:T(8,128)(2,1)S(1)}, u32[]{:S(2)}, u32[]{:S(2)}) async-start(bf16[8,272,128]{2,1,0:T(8,128)(2,1)} %copy-done.1), calls=%async_computation.1 | async-start | bytes 1114112 | tf_op jit(solution)/shard_map/all_to_all | solution.py:441
  73.1 18.1 %all-to-all-start.2 = ((bf16[8,16,2048]{2,1,0:T(8,128)(2,1)}), bf16[8,16,2048]{2,1,0:T(8,128)(2,1)S(1)}, u32[]{:S(2)}, u32[]{:S(2)}) async-start(bf16[8,16,2048]{2,1,0:T(8,128)(2,1)} %bitcast.6), calls=%async_computation.2 | async-start | bytes 1048576 | tf_op jit(solution)/shard_map/all_to_all | solution.py:447
  109.7 12.0 %copy-start.7 = (f32[16,8]{0,1:T(8,128)S(1)}, f32[16,8]{0,1:T(8,128)}, u32[]{:S(2)}) copy-start(f32[16,8]{0,1:T(8,128)} %param.24) | copy-start | bytes 1540
  117.6 18.6 %all-to-all-start.4 = ((bf16[16,8,2048]{2,1,0:T(8,128)(2,1)}), bf16[16,8,2048]{2,1,0:T(8,128)(2,1)S(1)}, u32[]{:S(2)}, u32[]{:S(2)}) async-start(bf16[16,8,2048]{2,1,0:T(8,128)(2,1)} %bitcast.10), calls=%async_computation.4 | async-start | bytes 1048576 | tf_op jit(solution)/shard_map/all_to_all | solution.py:460

commit v19 on v13

--- a/solution.py
+++ b/solution.py
@@ -94,12 +94,12 @@
             probs[at, across[g]] = jnp.exp2((scores[at, across[g]] - peak[g]).astype(BF16))
     ones = jnp.ones((STATS, cache_here), BF16)
     sums = [
-        nn_dot(jnp.concatenate([value_own[heads[g], :], ones], axis=0), probs[:cache_here, across[g]])
+        nn_dot(jnp.concatenate([value_own[:, heads[g]].T, ones], axis=0), probs[:cache_here, across[g]])
         for g in each
     ]
     sums = [
         sums[g]
-        + nn_dot(jnp.concatenate([value_other[heads[g], :], ones], axis=0), probs[cache_here:, across[g]])
+        + nn_dot(jnp.concatenate([value_other[:, heads[g]].T, ones], axis=0), probs[cache_here:, across[g]])
         for g in each
     ]
     for g in each:
@@ -145,8 +145,7 @@
                 pl.BlockSpec((home_rows, columns), functools.partial(lambda n, g, place: (n, g), n))
                 for _, n in query_blocks
             ]
-            + [pl.BlockSpec((cache_here, together * HD), kv)] * 2
-            + [pl.BlockSpec((together * HD, cache_here), lambda g, place: (g, 0))] * 2
+            + [pl.BlockSpec((cache_here, together * HD), kv)] * 4
             + [pl.BlockSpec((home_rows, together * HD), kv)] * 2
             + [pl.BlockSpec(lens.shape, whole)] * 2,
             out_specs=pl.BlockSpec((together * owners, height, HD), lambda g, place: (g, 0, 0)),
@@ -169,7 +168,8 @@
         *[block for block, _ in query_blocks],
         pltpu.with_memory_space_constraint(keys[0], pltpu.HBM),
         keys[1],
-        *values,
+        pltpu.with_memory_space_constraint(values[0], pltpu.HBM),
+        values[1],
         pltpu.with_memory_space_constraint(new_key, pltpu.HBM),
         pltpu.with_memory_space_constraint(new_value, pltpu.HBM),
         lens,
@@ -388,8 +388,7 @@
     far_blocks = [(far, k) for k in range(half)] + [(far_across, k) for k in range(half)]
     late_keys, late_values, _ = lax.optimization_barrier((key_cache, value_cache, neighbour))
     key_other = lax.ppermute(late_keys, "ctx", swap)
-    value_turned = late_values.T
-    value_other = lax.ppermute(value_turned, "ctx", swap)
+    value_other = lax.ppermute(late_values, "ctx", swap)
     place = jnp.stack([chip, index * cache_here, (index ^ 1) * cache_here, core, chip % 2, chip // 2]).astype(jnp.int32)
 
     def in_lanes(by_chip, n):
@@ -422,7 +421,7 @@
             place,
             blocks,
             (key_cache, key_other),
-            (value_turned, value_other),
+            (value_cache, value_other),
             new_key,
             new_value,
             lens[chunk],

time: 131 us -> 132 us (level)
  waiting for transfers between devices: 52.6 us -> 54.3 us
    unnamed x13 -> x19, local copies, waits for them, and re-layouts: 0.17 us -> 2.24 us
    ppermute x3, waiting for transfers between devices: 6.34 us -> 7.89 us  [on_device(): lax.ppermute(queries, 'ctx', [(i, i ^ 2 * CORES * k) for i in range(devic...]
    optimization_barrier x1 -> x0, local copies, waits for them, and re-layouts: 1.49 us -> none  [on_device(): lax.optimization_barrier((key_cache, value_cache, neighbour))]
  transfers between devices with their start and end apart: 13 -> 13, of which waited for: 5 -> 6; matrix products, arithmetic and copies ran while one was open for 3% -> 2% of each run, Pallas kernels for 14% -> 14%
where the time goes in v19:
time: 132 us; the launch traced here: 131 us
  waiting for transfers between devices  54.3 us (41%)
  Pallas kernels  29 us (22%)
  starting transfers between devices  25.4 us (19%)
  blocking collectives  18 us (14%)
  local copies, waits for them, and re-layouts  4.15 us (3%)
    all_to_all x2, waiting for transfers between devices, on_device(): lax.all_to_all(sums, 'ctx', split_axis=0, concat_axis=0, axis_index_group...  18.1 us
    all_to_all x1, blocking collectives, on_device(): lax.all_to_all(outgoing.reshape(devices, experts * MOST, width), 'ctx', s...  18 us
    pallas_call x2, Pallas kernels, attention(): pl.pallas_call(functools.partial(attention_body, shape), grid_spec=pltpu....  17.8 us
    all_to_all x1, waiting for transfers between devices, on_device(): lax.all_to_all(produced.reshape(devices, experts * MOST, width), 'ctx', s...  14.3 us
    all_to_all x1, waiting for transfers between devices, on_device(): lax.all_to_all(share.reshape(chips, home_rows, width), 'ctx', split_axis=...  13.9 us
    all_to_all x2, starting transfers between devices, on_device(): lax.all_to_all(sums, 'ctx', split_axis=0, concat_axis=0, axis_index_group...  8.86 us
    ppermute x3, waiting for transfers between devices, on_device(): lax.ppermute(queries, 'ctx', [(i, i ^ 2 * CORES * k) for i in range(devic...  7.89 us
    pallas_call x1, Pallas kernels, run_experts(): pl.pallas_call(functools.partial(experts_body, step), in_specs=[vmem] + [...  7.86 us
  transfers between devices with their start and end apart: 13, of which 6 were waited for; matrix products, arithmetic and copies ran while one was open for 2% of the time, Pallas kernels for 14%

profile of v19, /device:TPU:0, one launch (start us, length us, event | category | flops | bytes accessed | tf_op | source)
XLA Modules:
  0.0 131.5 jit_solution(13918157211536116142)
XLA Ops:
  0.0 3.0 %collective-permute-start.1 = (bf16[16,4096]{1,0:T(8,128)(2,1)}, bf16[16,4096]{1,0:T(8,128)(2,1)S(1)}, u32[]{:S(2)}, u32[]{:S(2)}) collective-permute-start(bf16[16,4096]{1,0:T(8,128)(2,1)} %refs_0_.1), channel_id=1, source_target_pairs={{0,2},{1,3},{2,0},{3,1},{4,6},{5,7},{6,4},{7,5},{8,10},{9,11},{10,... | collective-permute-start | bytes 393224 | tf_op jit(solution)/shard_map/ppermute | solution.py:376
  3.0 1.6 %collective-permute-start = (bf16[16,4096]{1,0:T(8,128)(2,1)}, bf16[16,4096]{1,0:T(8,128)(2,1)S(1)}, u32[]{:S(2)}, u32[]{:S(2)}) collective-permute-start(bf16[16,4096]{1,0:T(8,128)(2,1)} %refs_0_.1), channel_id=1, source_target_pairs={{0,4},{1,5},{2,6},{3,7},{4,0},{5,1},{6,2},{7,3},{8,12},{9,13},{10,... | collective-permute-start | bytes 393224 | tf_op jit(solution)/shard_map/ppermute | solution.py:380
  4.5 2.6 %collective-permute-start.5 = (bf16[16,4096]{1,0:T(8,128)(2,1)}, bf16[16,4096]{1,0:T(8,128)(2,1)S(1)}, u32[]{:S(2)}, u32[]{:S(2)}) collective-permute-start(bf16[16,4096]{1,0:T(8,128)(2,1)} %refs_0_.1), channel_id=1, source_target_pairs={{0,8},{1,9},{2,10},{3,11},{4,12},{5,13},{6,14},{7,15},{8,0},{9,1},... | collective-permute-start | bytes 393224 | tf_op jit(solution)/shard_map/ppermute | solution.py:380
  7.1 0.2 collective-permute-start.6
  7.4 0.8 reshape.66
  8.1 0.1 collective-permute-start.3
  8.2 0.5 collective-permute-start.4
  8.7 0.1 fusion.2
  8.8 0.1 tile.40
  8.9 0.1 tile.42.refs_10_
  8.9 0.1 tile.43
  9.0 0.1 tile.45.refs_11_
  9.1 0.1 stack.27.place
  9.2 0.4 collective-permute-done.refs_1_
  9.6 0.3 collective-permute-start.2
  9.9 7.5 %collective-permute-done.5 = bf16[16,4096]{1,0:T(8,128)(2,1)S(1)} collective-permute-done((bf16[16,4096]{1,0:T(8,128)(2,1)}, bf16[16,4096]{1,0:T(8,128)(2,1)S(1)}, u32[]{:S(2)}, u32[]{:S(2)}) %collective-permute-start.5) | collective-permute-done | bytes 131104 | tf_op jit(solution)/shard_map/ppermute | solution.py:380
  17.5 0.0 copy-start
  17.5 0.6 collective-permute-start.7
  18.1 9.2 %attention.2 = bf16[8,272,128]{2,1,0:T(8,128)(2,1)} custom-call(s32[6]{0:T(128)S(1)} %stack.27.place, bf16[16,4096]{1,0:T(8,128)(2,1)} %refs_0_.1, bf16[16,4096]{1,0:T(8,128)(2,1)S(1)} %collective-permute-done.refs_1_, bf16[16,4096]{1,0:T(8,128)(2,1)S(1)} %collective-permute-done.1.refs_2_, bf16[16,4096]{1,0:T(8,128)(2,1)S(1)} %collective-permute-done.2.refs_3_, ...), custom_call_target="tpu_custom_call" | custom-call | flops 3221225472 | bytes 8388608 | tf_op jit(solution)/shard_map/attention/pallas_call | solution.py:139
  27.3 5.2 %all-to-all-start = ((bf16[8,272,128]{2,1,0:T(8,128)(2,1)}), bf16[8,272,128]{2,1,0:T(8,128)(2,1)S(1)}, u32[]{:S(2)}, u32[]{:S(2)}) async-start(bf16[8,272,128]{2,1,0:T(8,128)(2,1)} %attention.2), calls=%async_computation | async-start | bytes 1114112 | tf_op jit(solution)/shard_map/all_to_all | solution.py:437
  32.5 0.1 tile.46
  32.6 0.1 tile.48.refs_10_
  32.7 0.1 tile.49
  32.7 0.1 tile.51.refs_11_
  32.8 0.0 collective-permute-start.8
  32.9 1.2 copy-done.4
  34.1 8.6 %attention.3 = bf16[8,272,128]{2,1,0:T(8,128)(2,1)S(1)} custom-call(s32[6]{0:T(128)S(1)} %stack.27.place, bf16[32,4096]{1,0:T(8,128)(2,1)S(1)} %constant_dynamic-update-slice_fusion.refs_0_.refs_1_, bf16[32,4096]{1,0:T(8,128)(2,1)S(1)} %constant_dynamic-update-slice_fusion.refs_0_.refs_1_, bf16[32,4096]{1,0:T(8,128)(2,1)S(1)} %collective-permute-done.7.refs_2_.refs_3_, ...), custom_call_target="tpu_custom_call" | custom-call | flops 3221225472 | bytes 8388608 | tf_op jit(solution)/shard_map/attention/pallas_call | solution.py:139
  42.7 0.8 copy-done.1
  43.5 2.8 %all-to-all-done.refs_0_ = bf16[8,272,128]{2,1,0:T(8,128)(2,1)S(1)} async-done(((bf16[8,272,128]{2,1,0:T(8,128)(2,1)}), bf16[8,272,128]{2,1,0:T(8,128)(2,1)S(1)}, u32[]{:S(2)}, u32[]{:S(2)}) %all-to-all-start) | async-done | bytes 557088 | tf_op jit(solution)/shard_map/all_to_all | solution.py:437
  46.3 3.7 %all-to-all-start.1 = ((bf16[8,272,128]{2,1,0:T(8,128)(2,1)}), bf16[8,272,128]{2,1,0:T(8,128)(2,1)S(1)}, u32[]{:S(2)}, u32[]{:S(2)}) async-start(bf16[8,272,128]{2,1,0:T(8,128)(2,1)} %copy-done.1), calls=%async_computation.1 | async-start | bytes 1114112 | tf_op jit(solution)/shard_map/all_to_all | solution.py:437
  50.0 15.3 %all-to-all-done.1.refs_1_ = bf16[8,272,128]{2,1,0:T(8,128)(2,1)S(1)} async-done(((bf16[8,272,128]{2,1,0:T(8,128)(2,1)}), bf16[8,272,128]{2,1,0:T(8,128)(2,1)S(1)}, u32[]{:S(2)}, u32[]{:S(2)}) %all-to-all-start.1) | async-done | bytes 557088 | tf_op jit(solution)/shard_map/all_to_all | solution.py:437
  65.3 2.1 %project.1 = bf16[128,2048]{1,0:T(8,128)(2,1)} custom-call(s32[6]{0:T(128)S(1)} %stack.27.place, bf16[8,272,128]{2,1,0:T(8,128)(2,1)S(1)} %all-to-all-done.refs_0_, bf16[8,272,128]{2,1,0:T(8,128)(2,1)S(1)} %all-to-all-done.1.refs_1_, bf16[256,2048]{1,0:T(8,128)(2,1)S(1)} %copy-done, bf16[256,2048]{1,0:T(8,128)(2,1)S(1)} %collective-permute-done.8.refs_3_), custom_call_target="tpu_custom_call" | custom-call | flops 268435456 | bytes 4194304 | tf_op jit(solution)/shard_map/project/pallas_call | solution.py:213
  67.4 3.6 %all-to-all-start.2 = ((bf16[8,16,2048]{2,1,0:T(8,128)(2,1)}), bf16[8,16,2048]{2,1,0:T(8,128)(2,1)S(1)}, u32[]{:S(2)}, u32[]{:S(2)}) async-start(bf16[8,16,2048]{2,1,0:T(8,128)(2,1)} %bitcast.6), calls=%async_computation.2 | async-start | bytes 1048576 | tf_op jit(solution)/shard_map/all_to_all | solution.py:443
  71.1 0.1 copy.21
  71.1 0.1 eq.31
  71.2 0.2 convert_reduce_fusion
  71.4 0.1 reduce_sum.21
  71.5 0.1 fusion
  71.6 0.1 copy.23
  71.8 13.9 %all-to-all-done.2.parts = bf16[8,16,2048]{2,1,0:T(8,128)(2,1)S(1)} async-done(((bf16[8,16,2048]{2,1,0:T(8,128)(2,1)}), bf16[8,16,2048]{2,1,0:T(8,128)(2,1)S(1)}, u32[]{:S(2)}, u32[]{:S(2)}) %all-to-all-start.2) | async-done | bytes 524320 | tf_op jit(solution)/shard_map/all_to_all | solution.py:443
  85.7 0.4 norm_and_dispatch.1
  86.1 18.0 %all_to_all.25 = bf16[16,8,2048]{2,1,0:T(8,128)(2,1)S(1)} all-to-all(bf16[16,8,2048]{2,1,0:T(8,128)(2,1)S(1)} %bitcast.14), channel_id=1, replica_groups=mesh['groups'=2,'ctx'=16] {'ctx'}, dimensions={0} | all-to-all | bytes 1048576 | tf_op jit(solution)/shard_map/all_to_all | solution.py:452
  104.2 7.9 %experts.1 = bf16[128,2048]{1,0:T(8,128)(2,1)} custom-call(bf16[128,2048]{1,0:T(8,128)(2,1)S(1)} %bitcast.12, bf16[2,2048,768]{2,1,0:T(8,128)(2,1)} %w_gate.1, bf16[2,2048,768]{2,1,0:T(8,128)(2,1)} %w_up.1, bf16[2,768,2048]{2,1,0:T(8,128)(2,1)} %w_down.1), custom_call_target="tpu_custom_call" | custom-call | flops 2415919104 | bytes 18874368 | tf_op jit(solution)/shard_map/experts/pallas_call | solution.py:304
  112.0 4.1 %all-to-all-start.4 = ((bf16[16,8,2048]{2,1,0:T(8,128)(2,1)}), bf16[16,8,2048]{2,1,0:T(8,128)(2,1)S(1)}, u32[]{:S(2)}, u32[]{:S(2)}) async-start(bf16[16,8,2048]{2,1,0:T(8,128)(2,1)} %bitcast.10), calls=%async_computation.4 | async-start | bytes 1048576 | tf_op jit(solution)/shard_map/all_to_all | solution.py:456
  116.1 0.1 copy.24
  116.2 0.1 select_reduce_fusion
  116.3 14.3 %all-to-all-done.4 = bf16[16,8,2048]{2,1,0:T(8,128)(2,1)S(1)} async-done(((bf16[16,8,2048]{2,1,0:T(8,128)(2,1)}), bf16[16,8,2048]{2,1,0:T(8,128)(2,1)S(1)}, u32[]{:S(2)}, u32[]{:S(2)}) %all-to-all-start.4) | async-done | bytes 524320 | tf_op jit(solution)/shard_map/all_to_all | solution.py:456
  130.6 0.9 mix.1
  (32 shorter events, 0.1 us)
Async XLA Ops:
  0.0 8.1 %collective-permute-start.1 = (bf16[16,4096]{1,0:T(8,128)(2,1)}, bf16[16,4096]{1,0:T(8,128)(2,1)S(1)}, u32[]{:S(2)}, u32[]{:S(2)}) collective-permute-start(bf16[16,4096]{1,0:T(8,128)(2,1)} %refs_0_.1), channel_id=1, source_target_pairs={{0,2},{1,3},{2,0},{3,1},{4,6},{5,7},{6,4},{7,5},{8,10},{9,11},{10,... | collective-permute-start | bytes 393224 | tf_op jit(solution)/shard_map/ppermute | solution.py:376
  3.0 6.6 %collective-permute-start = (bf16[16,4096]{1,0:T(8,128)(2,1)}, bf16[16,4096]{1,0:T(8,128)(2,1)S(1)}, u32[]{:S(2)}, u32[]{:S(2)}) collective-permute-start(bf16[16,4096]{1,0:T(8,128)(2,1)} %refs_0_.1), channel_id=1, source_target_pairs={{0,4},{1,5},{2,6},{3,7},{4,0},{5,1},{6,2},{7,3},{8,12},{9,13},{10,... | collective-permute-start | bytes 393224 | tf_op jit(solution)/shard_map/ppermute | solution.py:380
  4.5 12.9 %collective-permute-start.5 = (bf16[16,4096]{1,0:T(8,128)(2,1)}, bf16[16,4096]{1,0:T(8,128)(2,1)S(1)}, u32[]{:S(2)}, u32[]{:S(2)}) collective-permute-start(bf16[16,4096]{1,0:T(8,128)(2,1)} %refs_0_.1), channel_id=1, source_target_pairs={{0,8},{1,9},{2,10},{3,11},{4,12},{5,13},{6,14},{7,15},{8,0},{9,1},... | collective-permute-start | bytes 393224 | tf_op jit(solution)/shard_map/ppermute | solution.py:380
  7.1 10.3 %collective-permute-start.6 = (bf16[16,4096]{1,0:T(8,128)(2,1)}, bf16[16,4096]{1,0:T(8,128)(2,1)S(1)}, u32[]{:S(2)}, u32[]{:S(2)}) collective-permute-start(bf16[16,4096]{1,0:T(8,128)(2,1)} %refs_0_.1), channel_id=1, source_target_pairs={{0,12},{1,13},{2,14},{3,15},{4,8},{5,9},{6,10},{7,11},{8,4},{9,5},... | collective-permute-start | bytes 393224 | tf_op jit(solution)/shard_map/ppermute | solution.py:380
  8.1 9.9 %collective-permute-start.3 = (bf16[1024,512]{1,0:T(8,128)(2,1)}, bf16[1024,512]{1,0:T(8,128)(2,1)S(1)}, u32[]{:S(2)}, u32[]{:S(2)}) collective-permute-start(bf16[1024,512]{1,0:T(8,128)(2,1)} %refs_4_.3), channel_id=1, source_target_pairs={{0,1},{1,0},{2,3},{3,2},{4,5},{5,4},{6,7},{7,6},{8,9},{9,8},{10,11... | collective-permute-start | bytes 3145736 | tf_op jit(solution)/shard_map/ppermute | solution.py:390
  8.2 9.9 %collective-permute-start.4 = (bf16[1024,512]{1,0:T(8,128)(2,1)}, bf16[1024,512]{1,0:T(8,128)(2,1)}, u32[]{:S(2)}, u32[]{:S(2)}) collective-permute-start(bf16[1024,512]{1,0:T(8,128)(2,1)} %refs_6_.3), channel_id=1, source_target_pairs={{0,1},{1,0},{2,3},{3,2},{4,5},{5,4},{6,7},{7,6},{8,9},{9,8},{10,11... | collective-permute-start | bytes 3145736 | tf_op jit(solution)/shard_map/ppermute | solution.py:391
  9.6 8.4 %collective-permute-start.2 = (bf16[16,4096]{1,0:T(8,128)(2,1)S(1)}, bf16[16,4096]{1,0:T(8,128)(2,1)S(1)}, u32[]{:S(2)}, u32[]{:S(2)}) collective-permute-start(bf16[16,4096]{1,0:T(8,128)(2,1)S(1)} %collective-permute-done.refs_1_), channel_id=1, source_target_pairs={{0,2},{1,3},{2,0},{3,1},{4,6},{5,7},{6,4},{7,5},{8,10},{9,11},{10,... | collective-permute-start | bytes 393224 | tf_op jit(solution)/shard_map/ppermute | solution.py:376
  17.5 15.4 %copy-start = (bf16[256,2048]{1,0:T(8,128)(2,1)S(1)}, bf16[256,2048]{1,0:T(8,128)(2,1)}, u32[]{:S(2)}) copy-start(bf16[256,2048]{1,0:T(8,128)(2,1)} %refs_2_.1) | copy-start | bytes 3145732
  17.5 9.8 %collective-permute-start.7 = (bf16[32,4096]{1,0:T(8,128)(2,1)S(1)}, bf16[32,4096]{1,0:T(8,128)(2,1)S(1)}, u32[]{:S(2)}, u32[]{:S(2)}) collective-permute-start(bf16[32,4096]{1,0:T(8,128)(2,1)S(1)} %constant_dynamic-update-slice_fusion.refs_0_.refs_1_), channel_id=1, source_target_pairs={{0,2},{1,3},{2,0},{3,1},{4,6},{5,7},{6,4},{7,5},{8,10},{9,11},{10,... | collective-permute-start | bytes 786440 | tf_op jit(solution)/shard_map/ppermute | solution.py:376
  18.0 9.3 %copy-start.3 = (bf16[1024,512]{1,0:T(8,128)(2,1)}, bf16[1024,512]{1,0:T(8,128)(2,1)S(1)}, u32[]{:S(2)}) copy-start(bf16[1024,512]{1,0:T(8,128)(2,1)S(1)} %collective-permute-done.3.refs_5_) | copy-start | bytes 3145732
  27.3 19.0 %all-to-all-start = ((bf16[8,272,128]{2,1,0:T(8,128)(2,1)}), bf16[8,272,128]{2,1,0:T(8,128)(2,1)S(1)}, u32[]{:S(2)}, u32[]{:S(2)}) async-start(bf16[8,272,128]{2,1,0:T(8,128)(2,1)} %attention.2), calls=%async_computation | async-start | bytes 1114112 | tf_op jit(solution)/shard_map/all_to_all | solution.py:437
  32.8 52.9 %copy-start.2 = (bf16[16,2048]{1,0:T(8,128)(2,1)S(1)}, bf16[16,2048]{1,0:T(8,128)(2,1)}, u32[]{:S(2)}) copy-start(bf16[16,2048]{1,0:T(8,128)(2,1)} %residual.1) | copy-start | bytes 196612
  32.8 17.2 %collective-permute-start.8 = (bf16[256,2048]{1,0:T(8,128)(2,1)S(1)}, bf16[256,2048]{1,0:T(8,128)(2,1)S(1)}, u32[]{:S(2)}, u32[]{:S(2)}) collective-permute-start(bf16[256,2048]{1,0:T(8,128)(2,1)S(1)} %copy-done), channel_id=1, source_target_pairs={{0,1},{1,0},{2,3},{3,2},{4,5},{5,4},{6,7},{7,6},{8,9},{9,8},{10,11... | collective-permute-start | bytes 3145736 | tf_op jit(solution)/shard_map/ppermute | solution.py:441
  32.8 1.3 copy-start.4
  34.1 36.9 %copy-start.5 = (bf16[2048]{0:T(1024)(128)(2,1)S(1)}, bf16[2048]{0:T(1024)(128)(2,1)}, u32[]{:S(2)}) copy-start(bf16[2048]{0:T(1024)(128)(2,1)} %param.22) | copy-start | bytes 12292
  34.1 36.9 %copy-start.6 = (s32[16,8]{0,1:T(8,128)S(1)}, s32[16,8]{0,1:T(8,128)}, u32[]{:S(2)}) copy-start(s32[16,8]{0,1:T(8,128)} %param.23) | copy-start | bytes 1540
  42.7 0.8 copy-start.1
  46.3 19.0 %all-to-all-start.1 = ((bf16[8,272,128]{2,1,0:T(8,128)(2,1)}), bf16[8,272,128]{2,1,0:T(8,128)(2,1)S(1)}, u32[]{:S(2)}, u32[]{:S(2)}) async-start(bf16[8,272,128]{2,1,0:T(8,128)(2,1)} %copy-done.1), calls=%async_computation.1 | async-start | bytes 1114112 | tf_op jit(solution)/shard_map/all_to_all | solution.py:437
  67.4 18.3 %all-to-all-start.2 = ((bf16[8,16,2048]{2,1,0:T(8,128)(2,1)}), bf16[8,16,2048]{2,1,0:T(8,128)(2,1)S(1)}, u32[]{:S(2)}, u32[]{:S(2)}) async-start(bf16[8,16,2048]{2,1,0:T(8,128)(2,1)} %bitcast.6), calls=%async_computation.2 | async-start | bytes 1048576 | tf_op jit(solution)/shard_map/all_to_all | solution.py:443
  104.2 12.0 %copy-start.7 = (f32[16,8]{0,1:T(8,128)S(1)}, f32[16,8]{0,1:T(8,128)}, u32[]{:S(2)}) copy-start(f32[16,8]{0,1:T(8,128)} %param.24) | copy-start | bytes 1540
  112.0 18.6 %all-to-all-start.4 = ((bf16[16,8,2048]{2,1,0:T(8,128)(2,1)}), bf16[16,8,2048]{2,1,0:T(8,128)(2,1)S(1)}, u32[]{:S(2)}, u32[]{:S(2)}) async-start(bf16[16,8,2048]{2,1,0:T(8,128)(2,1)} %bitcast.10), calls=%async_computation.4 | async-start | bytes 1048576 | tf_op jit(solution)/shard_map/all_to_all | solution.py:456

commit v20 on v19

--- a/solution.py
+++ b/solution.py
@@ -130,7 +130,7 @@
     owner_heads = columns // HD // owners // together
     wide = rows * columns // HD
     height = owner_heads * rows + STATS
-    step = 512
+    step = 1024
     positions = 2 * cache_here + home_rows
     kv = lambda g, place: (0, g)
     whole = lambda g, place: (0, 0)

time: 132 us -> 132 us (level)
  no operation moved by 1% of the time
where the time goes in v20:
time: 132 us
  waiting for transfers between devices  54.2 us (41%)
  Pallas kernels  29.1 us (22%)
  starting transfers between devices  25.4 us (19%)
  blocking collectives  18 us (14%)
  local copies, waits for them, and re-layouts  4.15 us (3%)
    all_to_all x2, waiting for transfers between devices, on_device(): lax.all_to_all(sums, 'ctx', split_axis=0, concat_axis=0, axis_index_group...  18.1 us
    all_to_all x1, blocking collectives, on_device(): lax.all_to_all(outgoing.reshape(devices, experts * MOST, width), 'ctx', s...  18 us
    pallas_call x2, Pallas kernels, attention(): pl.pallas_call(functools.partial(attention_body, shape), grid_spec=pltpu....  17.8 us
    all_to_all x1, waiting for transfers between devices, on_device(): lax.all_to_all(produced.reshape(devices, experts * MOST, width), 'ctx', s...  14.3 us
    all_to_all x1, waiting for transfers between devices, on_device(): lax.all_to_all(share.reshape(chips, home_rows, width), 'ctx', split_axis=...  13.9 us
    all_to_all x2, starting transfers between devices, on_device(): lax.all_to_all(sums, 'ctx', split_axis=0, concat_axis=0, axis_index_group...  8.86 us
    ppermute x3, waiting for transfers between devices, on_device(): lax.ppermute(queries, 'ctx', [(i, i ^ 2 * CORES * k) for i in range(devic...  7.89 us
    pallas_call x1, Pallas kernels, run_experts(): pl.pallas_call(functools.partial(experts_body, step), in_specs=[vmem] + [...  7.86 us
  transfers between devices with their start and end apart: 13, of which 6 were waited for; matrix products, arithmetic and copies ran while one was open for 2% of the time, Pallas kernels for 14%

profile of v20, /device:TPU:0, one launch (start us, length us, event | category | flops | bytes accessed | tf_op | source)
XLA Modules:
  0.0 131.5 jit_solution(3304408894366840204)
XLA Ops:
  0.0 3.0 %collective-permute-start.1 = (bf16[16,4096]{1,0:T(8,128)(2,1)}, bf16[16,4096]{1,0:T(8,128)(2,1)S(1)}, u32[]{:S(2)}, u32[]{:S(2)}) collective-permute-start(bf16[16,4096]{1,0:T(8,128)(2,1)} %refs_0_.1), channel_id=1, source_target_pairs={{0,2},{1,3},{2,0},{3,1},{4,6},{5,7},{6,4},{7,5},{8,10},{9,11},{10,... | collective-permute-start | bytes 393224 | tf_op jit(solution)/shard_map/ppermute | solution.py:376
  3.0 1.6 %collective-permute-start = (bf16[16,4096]{1,0:T(8,128)(2,1)}, bf16[16,4096]{1,0:T(8,128)(2,1)S(1)}, u32[]{:S(2)}, u32[]{:S(2)}) collective-permute-start(bf16[16,4096]{1,0:T(8,128)(2,1)} %refs_0_.1), channel_id=1, source_target_pairs={{0,4},{1,5},{2,6},{3,7},{4,0},{5,1},{6,2},{7,3},{8,12},{9,13},{10,... | collective-permute-start | bytes 393224 | tf_op jit(solution)/shard_map/ppermute | solution.py:380
  4.5 2.6 %collective-permute-start.5 = (bf16[16,4096]{1,0:T(8,128)(2,1)}, bf16[16,4096]{1,0:T(8,128)(2,1)S(1)}, u32[]{:S(2)}, u32[]{:S(2)}) collective-permute-start(bf16[16,4096]{1,0:T(8,128)(2,1)} %refs_0_.1), channel_id=1, source_target_pairs={{0,8},{1,9},{2,10},{3,11},{4,12},{5,13},{6,14},{7,15},{8,0},{9,1},... | collective-permute-start | bytes 393224 | tf_op jit(solution)/shard_map/ppermute | solution.py:380
  7.1 0.2 collective-permute-start.6
  7.4 0.8 reshape.66
  8.1 0.1 collective-permute-start.3
  8.2 0.5 collective-permute-start.4
  8.7 0.1 fusion.2
  8.8 0.1 tile.40
  8.9 0.1 tile.42.refs_10_
  8.9 0.1 tile.43
  9.0 0.1 tile.45.refs_11_
  9.1 0.1 stack.27.place
  9.2 0.4 collective-permute-done.refs_1_
  9.6 0.3 collective-permute-start.2
  9.9 7.5 %collective-permute-done.5 = bf16[16,4096]{1,0:T(8,128)(2,1)S(1)} collective-permute-done((bf16[16,4096]{1,0:T(8,128)(2,1)}, bf16[16,4096]{1,0:T(8,128)(2,1)S(1)}, u32[]{:S(2)}, u32[]{:S(2)}) %collective-permute-start.5) | collective-permute-done | bytes 131104 | tf_op jit(solution)/shard_map/ppermute | solution.py:380
  17.5 0.0 copy-start
  17.5 0.6 collective-permute-start.7
  18.1 9.3 %attention.2 = bf16[8,272,128]{2,1,0:T(8,128)(2,1)} custom-call(s32[6]{0:T(128)S(1)} %stack.27.place, bf16[16,4096]{1,0:T(8,128)(2,1)} %refs_0_.1, bf16[16,4096]{1,0:T(8,128)(2,1)S(1)} %collective-permute-done.refs_1_, bf16[16,4096]{1,0:T(8,128)(2,1)S(1)} %collective-permute-done.1.refs_2_, bf16[16,4096]{1,0:T(8,128)(2,1)S(1)} %collective-permute-done.2.refs_3_, ...), custom_call_target="tpu_custom_call" | custom-call | flops 3221225472 | bytes 8388608 | tf_op jit(solution)/shard_map/attention/pallas_call | solution.py:139
  27.3 5.2 %all-to-all-start = ((bf16[8,272,128]{2,1,0:T(8,128)(2,1)}), bf16[8,272,128]{2,1,0:T(8,128)(2,1)S(1)}, u32[]{:S(2)}, u32[]{:S(2)}) async-start(bf16[8,272,128]{2,1,0:T(8,128)(2,1)} %attention.2), calls=%async_computation | async-start | bytes 1114112 | tf_op jit(solution)/shard_map/all_to_all | solution.py:437
  32.5 0.1 tile.46
  32.6 0.1 tile.48.refs_10_
  32.7 0.1 tile.49
  32.8 0.1 tile.51.refs_11_
  32.9 0.0 collective-permute-start.8
  32.9 1.2 copy-done.4
  34.1 8.6 %attention.3 = bf16[8,272,128]{2,1,0:T(8,128)(2,1)S(1)} custom-call(s32[6]{0:T(128)S(1)} %stack.27.place, bf16[32,4096]{1,0:T(8,128)(2,1)S(1)} %constant_dynamic-update-slice_fusion.refs_0_.refs_1_, bf16[32,4096]{1,0:T(8,128)(2,1)S(1)} %constant_dynamic-update-slice_fusion.refs_0_.refs_1_, bf16[32,4096]{1,0:T(8,128)(2,1)S(1)} %collective-permute-done.7.refs_2_.refs_3_, ...), custom_call_target="tpu_custom_call" | custom-call | flops 3221225472 | bytes 8388608 | tf_op jit(solution)/shard_map/attention/pallas_call | solution.py:139
  42.7 0.8 copy-done.1
  43.5 2.8 %all-to-all-done.refs_0_ = bf16[8,272,128]{2,1,0:T(8,128)(2,1)S(1)} async-done(((bf16[8,272,128]{2,1,0:T(8,128)(2,1)}), bf16[8,272,128]{2,1,0:T(8,128)(2,1)S(1)}, u32[]{:S(2)}, u32[]{:S(2)}) %all-to-all-start) | async-done | bytes 557088 | tf_op jit(solution)/shard_map/all_to_all | solution.py:437
  46.3 3.7 %all-to-all-start.1 = ((bf16[8,272,128]{2,1,0:T(8,128)(2,1)}), bf16[8,272,128]{2,1,0:T(8,128)(2,1)S(1)}, u32[]{:S(2)}, u32[]{:S(2)}) async-start(bf16[8,272,128]{2,1,0:T(8,128)(2,1)} %copy-done.1), calls=%async_computation.1 | async-start | bytes 1114112 | tf_op jit(solution)/shard_map/all_to_all | solution.py:437
  50.0 15.4 %all-to-all-done.1.refs_1_ = bf16[8,272,128]{2,1,0:T(8,128)(2,1)S(1)} async-done(((bf16[8,272,128]{2,1,0:T(8,128)(2,1)}), bf16[8,272,128]{2,1,0:T(8,128)(2,1)S(1)}, u32[]{:S(2)}, u32[]{:S(2)}) %all-to-all-start.1) | async-done | bytes 557088 | tf_op jit(solution)/shard_map/all_to_all | solution.py:437
  65.4 2.1 %project.1 = bf16[128,2048]{1,0:T(8,128)(2,1)} custom-call(s32[6]{0:T(128)S(1)} %stack.27.place, bf16[8,272,128]{2,1,0:T(8,128)(2,1)S(1)} %all-to-all-done.refs_0_, bf16[8,272,128]{2,1,0:T(8,128)(2,1)S(1)} %all-to-all-done.1.refs_1_, bf16[256,2048]{1,0:T(8,128)(2,1)S(1)} %copy-done, bf16[256,2048]{1,0:T(8,128)(2,1)S(1)} %collective-permute-done.8.refs_3_), custom_call_target="tpu_custom_call" | custom-call | flops 268435456 | bytes 4194304 | tf_op jit(solution)/shard_map/project/pallas_call | solution.py:213
  67.4 3.6 %all-to-all-start.2 = ((bf16[8,16,2048]{2,1,0:T(8,128)(2,1)}), bf16[8,16,2048]{2,1,0:T(8,128)(2,1)S(1)}, u32[]{:S(2)}, u32[]{:S(2)}) async-start(bf16[8,16,2048]{2,1,0:T(8,128)(2,1)} %bitcast.6), calls=%async_computation.2 | async-start | bytes 1048576 | tf_op jit(solution)/shard_map/all_to_all | solution.py:443
  71.1 0.1 copy.21
  71.2 0.1 eq.31
  71.3 0.2 convert_reduce_fusion
  71.4 0.1 reduce_sum.21
  71.5 0.1 fusion
  71.7 0.1 copy.23
  71.8 13.9 %all-to-all-done.2.parts = bf16[8,16,2048]{2,1,0:T(8,128)(2,1)S(1)} async-done(((bf16[8,16,2048]{2,1,0:T(8,128)(2,1)}), bf16[8,16,2048]{2,1,0:T(8,128)(2,1)S(1)}, u32[]{:S(2)}, u32[]{:S(2)}) %all-to-all-start.2) | async-done | bytes 524320 | tf_op jit(solution)/shard_map/all_to_all | solution.py:443
  85.7 0.4 norm_and_dispatch.1
  86.2 18.0 %all_to_all.25 = bf16[16,8,2048]{2,1,0:T(8,128)(2,1)S(1)} all-to-all(bf16[16,8,2048]{2,1,0:T(8,128)(2,1)S(1)} %bitcast.14), channel_id=1, replica_groups=mesh['groups'=2,'ctx'=16] {'ctx'}, dimensions={0} | all-to-all | bytes 1048576 | tf_op jit(solution)/shard_map/all_to_all | solution.py:452
  104.2 7.9 %experts.1 = bf16[128,2048]{1,0:T(8,128)(2,1)} custom-call(bf16[128,2048]{1,0:T(8,128)(2,1)S(1)} %bitcast.12, bf16[2,2048,768]{2,1,0:T(8,128)(2,1)} %w_gate.1, bf16[2,2048,768]{2,1,0:T(8,128)(2,1)} %w_up.1, bf16[2,768,2048]{2,1,0:T(8,128)(2,1)} %w_down.1), custom_call_target="tpu_custom_call" | custom-call | flops 2415919104 | bytes 18874368 | tf_op jit(solution)/shard_map/experts/pallas_call | solution.py:304
  112.1 4.1 %all-to-all-start.4 = ((bf16[16,8,2048]{2,1,0:T(8,128)(2,1)}), bf16[16,8,2048]{2,1,0:T(8,128)(2,1)S(1)}, u32[]{:S(2)}, u32[]{:S(2)}) async-start(bf16[16,8,2048]{2,1,0:T(8,128)(2,1)} %bitcast.10), calls=%async_computation.4 | async-start | bytes 1048576 | tf_op jit(solution)/shard_map/all_to_all | solution.py:456
  116.2 0.1 copy.24
  116.3 0.1 select_reduce_fusion
  116.4 14.3 %all-to-all-done.4 = bf16[16,8,2048]{2,1,0:T(8,128)(2,1)S(1)} async-done(((bf16[16,8,2048]{2,1,0:T(8,128)(2,1)}), bf16[16,8,2048]{2,1,0:T(8,128)(2,1)S(1)}, u32[]{:S(2)}, u32[]{:S(2)}) %all-to-all-start.4) | async-done | bytes 524320 | tf_op jit(solution)/shard_map/all_to_all | solution.py:456
  130.6 0.9 mix.1
  (32 shorter events, 0.1 us)
Async XLA Ops:
  0.0 8.1 %collective-permute-start.1 = (bf16[16,4096]{1,0:T(8,128)(2,1)}, bf16[16,4096]{1,0:T(8,128)(2,1)S(1)}, u32[]{:S(2)}, u32[]{:S(2)}) collective-permute-start(bf16[16,4096]{1,0:T(8,128)(2,1)} %refs_0_.1), channel_id=1, source_target_pairs={{0,2},{1,3},{2,0},{3,1},{4,6},{5,7},{6,4},{7,5},{8,10},{9,11},{10,... | collective-permute-start | bytes 393224 | tf_op jit(solution)/shard_map/ppermute | solution.py:376
  3.0 6.6 %collective-permute-start = (bf16[16,4096]{1,0:T(8,128)(2,1)}, bf16[16,4096]{1,0:T(8,128)(2,1)S(1)}, u32[]{:S(2)}, u32[]{:S(2)}) collective-permute-start(bf16[16,4096]{1,0:T(8,128)(2,1)} %refs_0_.1), channel_id=1, source_target_pairs={{0,4},{1,5},{2,6},{3,7},{4,0},{5,1},{6,2},{7,3},{8,12},{9,13},{10,... | collective-permute-start | bytes 393224 | tf_op jit(solution)/shard_map/ppermute | solution.py:380
  4.5 12.9 %collective-permute-start.5 = (bf16[16,4096]{1,0:T(8,128)(2,1)}, bf16[16,4096]{1,0:T(8,128)(2,1)S(1)}, u32[]{:S(2)}, u32[]{:S(2)}) collective-permute-start(bf16[16,4096]{1,0:T(8,128)(2,1)} %refs_0_.1), channel_id=1, source_target_pairs={{0,8},{1,9},{2,10},{3,11},{4,12},{5,13},{6,14},{7,15},{8,0},{9,1},... | collective-permute-start | bytes 393224 | tf_op jit(solution)/shard_map/ppermute | solution.py:380
  7.1 10.3 %collective-permute-start.6 = (bf16[16,4096]{1,0:T(8,128)(2,1)}, bf16[16,4096]{1,0:T(8,128)(2,1)S(1)}, u32[]{:S(2)}, u32[]{:S(2)}) collective-permute-start(bf16[16,4096]{1,0:T(8,128)(2,1)} %refs_0_.1), channel_id=1, source_target_pairs={{0,12},{1,13},{2,14},{3,15},{4,8},{5,9},{6,10},{7,11},{8,4},{9,5},... | collective-permute-start | bytes 393224 | tf_op jit(solution)/shard_map/ppermute | solution.py:380
  8.1 9.9 %collective-permute-start.3 = (bf16[1024,512]{1,0:T(8,128)(2,1)}, bf16[1024,512]{1,0:T(8,128)(2,1)S(1)}, u32[]{:S(2)}, u32[]{:S(2)}) collective-permute-start(bf16[1024,512]{1,0:T(8,128)(2,1)} %refs_4_.3), channel_id=1, source_target_pairs={{0,1},{1,0},{2,3},{3,2},{4,5},{5,4},{6,7},{7,6},{8,9},{9,8},{10,11... | collective-permute-start | bytes 3145736 | tf_op jit(solution)/shard_map/ppermute | solution.py:390
  8.2 9.9 %collective-permute-start.4 = (bf16[1024,512]{1,0:T(8,128)(2,1)}, bf16[1024,512]{1,0:T(8,128)(2,1)}, u32[]{:S(2)}, u32[]{:S(2)}) collective-permute-start(bf16[1024,512]{1,0:T(8,128)(2,1)} %refs_6_.3), channel_id=1, source_target_pairs={{0,1},{1,0},{2,3},{3,2},{4,5},{5,4},{6,7},{7,6},{8,9},{9,8},{10,11... | collective-permute-start | bytes 3145736 | tf_op jit(solution)/shard_map/ppermute | solution.py:391
  9.6 8.4 %collective-permute-start.2 = (bf16[16,4096]{1,0:T(8,128)(2,1)S(1)}, bf16[16,4096]{1,0:T(8,128)(2,1)S(1)}, u32[]{:S(2)}, u32[]{:S(2)}) collective-permute-start(bf16[16,4096]{1,0:T(8,128)(2,1)S(1)} %collective-permute-done.refs_1_), channel_id=1, source_target_pairs={{0,2},{1,3},{2,0},{3,1},{4,6},{5,7},{6,4},{7,5},{8,10},{9,11},{10,... | collective-permute-start | bytes 393224 | tf_op jit(solution)/shard_map/ppermute | solution.py:376
  17.5 15.4 %copy-start = (bf16[256,2048]{1,0:T(8,128)(2,1)S(1)}, bf16[256,2048]{1,0:T(8,128)(2,1)}, u32[]{:S(2)}) copy-start(bf16[256,2048]{1,0:T(8,128)(2,1)} %refs_2_.1) | copy-start | bytes 3145732
  17.5 9.8 %collective-permute-start.7 = (bf16[32,4096]{1,0:T(8,128)(2,1)S(1)}, bf16[32,4096]{1,0:T(8,128)(2,1)S(1)}, u32[]{:S(2)}, u32[]{:S(2)}) collective-permute-start(bf16[32,4096]{1,0:T(8,128)(2,1)S(1)} %constant_dynamic-update-slice_fusion.refs_0_.refs_1_), channel_id=1, source_target_pairs={{0,2},{1,3},{2,0},{3,1},{4,6},{5,7},{6,4},{7,5},{8,10},{9,11},{10,... | collective-permute-start | bytes 786440 | tf_op jit(solution)/shard_map/ppermute | solution.py:376
  18.0 9.3 %copy-start.3 = (bf16[1024,512]{1,0:T(8,128)(2,1)}, bf16[1024,512]{1,0:T(8,128)(2,1)S(1)}, u32[]{:S(2)}) copy-start(bf16[1024,512]{1,0:T(8,128)(2,1)S(1)} %collective-permute-done.3.refs_5_) | copy-start | bytes 3145732
  27.3 19.0 %all-to-all-start = ((bf16[8,272,128]{2,1,0:T(8,128)(2,1)}), bf16[8,272,128]{2,1,0:T(8,128)(2,1)S(1)}, u32[]{:S(2)}, u32[]{:S(2)}) async-start(bf16[8,272,128]{2,1,0:T(8,128)(2,1)} %attention.2), calls=%async_computation | async-start | bytes 1114112 | tf_op jit(solution)/shard_map/all_to_all | solution.py:437
  32.9 52.9 %copy-start.2 = (bf16[16,2048]{1,0:T(8,128)(2,1)S(1)}, bf16[16,2048]{1,0:T(8,128)(2,1)}, u32[]{:S(2)}) copy-start(bf16[16,2048]{1,0:T(8,128)(2,1)} %residual.1) | copy-start | bytes 196612
  32.9 17.2 %collective-permute-start.8 = (bf16[256,2048]{1,0:T(8,128)(2,1)S(1)}, bf16[256,2048]{1,0:T(8,128)(2,1)S(1)}, u32[]{:S(2)}, u32[]{:S(2)}) collective-permute-start(bf16[256,2048]{1,0:T(8,128)(2,1)S(1)} %copy-done), channel_id=1, source_target_pairs={{0,1},{1,0},{2,3},{3,2},{4,5},{5,4},{6,7},{7,6},{8,9},{9,8},{10,11... | collective-permute-start | bytes 3145736 | tf_op jit(solution)/shard_map/ppermute | solution.py:441
  32.9 1.3 copy-start.4
  34.1 36.9 %copy-start.5 = (bf16[2048]{0:T(1024)(128)(2,1)S(1)}, bf16[2048]{0:T(1024)(128)(2,1)}, u32[]{:S(2)}) copy-start(bf16[2048]{0:T(1024)(128)(2,1)} %param.22) | copy-start | bytes 12292
  34.1 37.0 %copy-start.6 = (s32[16,8]{0,1:T(8,128)S(1)}, s32[16,8]{0,1:T(8,128)}, u32[]{:S(2)}) copy-start(s32[16,8]{0,1:T(8,128)} %param.23) | copy-start | bytes 1540
  42.7 0.8 copy-start.1
  46.3 19.0 %all-to-all-start.1 = ((bf16[8,272,128]{2,1,0:T(8,128)(2,1)}), bf16[8,272,128]{2,1,0:T(8,128)(2,1)S(1)}, u32[]{:S(2)}, u32[]{:S(2)}) async-start(bf16[8,272,128]{2,1,0:T(8,128)(2,1)} %copy-done.1), calls=%async_computation.1 | async-start | bytes 1114112 | tf_op jit(solution)/shard_map/all_to_all | solution.py:437
  67.4 18.3 %all-to-all-start.2 = ((bf16[8,16,2048]{2,1,0:T(8,128)(2,1)}), bf16[8,16,2048]{2,1,0:T(8,128)(2,1)S(1)}, u32[]{:S(2)}, u32[]{:S(2)}) async-start(bf16[8,16,2048]{2,1,0:T(8,128)(2,1)} %bitcast.6), calls=%async_computation.2 | async-start | bytes 1048576 | tf_op jit(solution)/shard_map/all_to_all | solution.py:443
  104.2 12.0 %copy-start.7 = (f32[16,8]{0,1:T(8,128)S(1)}, f32[16,8]{0,1:T(8,128)}, u32[]{:S(2)}) copy-start(f32[16,8]{0,1:T(8,128)} %param.24) | copy-start | bytes 1540
  112.1 18.6 %all-to-all-start.4 = ((bf16[16,8,2048]{2,1,0:T(8,128)(2,1)}), bf16[16,8,2048]{2,1,0:T(8,128)(2,1)S(1)}, u32[]{:S(2)}, u32[]{:S(2)}) async-start(bf16[16,8,2048]{2,1,0:T(8,128)(2,1)} %bitcast.10), calls=%async_computation.4 | async-start | bytes 1048576 | tf_op jit(solution)/shard_map/all_to_all | solution.py:456

commit v21 on v13

--- a/solution.py
+++ b/solution.py
@@ -221,7 +221,7 @@
             flops=8 * rows * width * depth, bytes_accessed=4 * MIB, transcendentals=0
         ),
         name="project",
-    )(place, *chunks, weight_own, weight_other)
+    )(place, *chunks, pltpu.with_memory_space_constraint(weight_own, pltpu.VMEM), weight_other)
 
 
 def norm_body(parts, residual, gain, chooser, middle_out, sent):

time: 131 us -> 131 us (level)
  no operation moved by 1% of the time
where the time goes in v21:
time: 131 us
  waiting for transfers between devices  52.6 us (40%)
  Pallas kernels  30.2 us (23%)
  starting transfers between devices  25.5 us (19%)
  blocking collectives  18 us (14%)
  local copies, waits for them, and re-layouts  3.58 us (3%)
    all_to_all x2, waiting for transfers between devices, on_device(): lax.all_to_all(sums, 'ctx', split_axis=0, concat_axis=0, axis_index_group...  18.7 us
    pallas_call x2, Pallas kernels, attention(): pl.pallas_call(functools.partial(attention_body, shape), grid_spec=pltpu....  18.3 us
    all_to_all x1, blocking collectives, on_device(): lax.all_to_all(outgoing.reshape(devices, experts * MOST, width), 'ctx', s...  18 us
    all_to_all x1, waiting for transfers between devices, on_device(): lax.all_to_all(produced.reshape(devices, experts * MOST, width), 'ctx', s...  14.3 us
    all_to_all x1, waiting for transfers between devices, on_device(): lax.all_to_all(share.reshape(chips, home_rows, width), 'ctx', split_axis=...  13.4 us
    all_to_all x2, starting transfers between devices, on_device(): lax.all_to_all(sums, 'ctx', split_axis=0, concat_axis=0, axis_index_group...  8.85 us
    pallas_call x1, Pallas kernels, run_experts(): pl.pallas_call(functools.partial(experts_body, step), in_specs=[vmem] + [...  7.86 us
    ppermute x3, waiting for transfers between devices, on_device(): lax.ppermute(queries, 'ctx', [(i, i ^ 2 * CORES * k) for i in range(devic...  6.34 us
  transfers between devices with their start and end apart: 13, of which 5 were waited for; matrix products, arithmetic and copies ran while one was open for 3% of the time, Pallas kernels for 14%

profile of v21, /device:TPU:0, one launch (start us, length us, event | category | flops | bytes accessed | tf_op | source)
XLA Modules:
  0.0 130.6 jit_solution(3359488877205657053)
XLA Ops:
  0.0 3.0 %collective-permute-start.1 = (bf16[16,4096]{1,0:T(8,128)(2,1)}, bf16[16,4096]{1,0:T(8,128)(2,1)S(1)}, u32[]{:S(2)}, u32[]{:S(2)}) collective-permute-start(bf16[16,4096]{1,0:T(8,128)(2,1)} %refs_0_.1), channel_id=1, source_target_pairs={{0,2},{1,3},{2,0},{3,1},{4,6},{5,7},{6,4},{7,5},{8,10},{9,11},{10,... | collective-permute-start | bytes 393224 | tf_op jit(solution)/shard_map/ppermute | solution.py:376
  3.0 1.6 %collective-permute-start = (bf16[16,4096]{1,0:T(8,128)(2,1)}, bf16[16,4096]{1,0:T(8,128)(2,1)S(1)}, u32[]{:S(2)}, u32[]{:S(2)}) collective-permute-start(bf16[16,4096]{1,0:T(8,128)(2,1)} %refs_0_.1), channel_id=1, source_target_pairs={{0,4},{1,5},{2,6},{3,7},{4,0},{5,1},{6,2},{7,3},{8,12},{9,13},{10,... | collective-permute-start | bytes 393224 | tf_op jit(solution)/shard_map/ppermute | solution.py:380
  4.5 2.6 %collective-permute-start.5 = (bf16[16,4096]{1,0:T(8,128)(2,1)}, bf16[16,4096]{1,0:T(8,128)(2,1)S(1)}, u32[]{:S(2)}, u32[]{:S(2)}) collective-permute-start(bf16[16,4096]{1,0:T(8,128)(2,1)} %refs_0_.1), channel_id=1, source_target_pairs={{0,8},{1,9},{2,10},{3,11},{4,12},{5,13},{6,14},{7,15},{8,0},{9,1},... | collective-permute-start | bytes 393224 | tf_op jit(solution)/shard_map/ppermute | solution.py:380
  7.1 0.2 collective-permute-start.6
  7.4 0.8 reshape.66
  8.1 0.1 collective-permute-start.3
  8.2 1.5 %copy.23 = bf16[1024,512]{0,1:T(8,128)(2,1)S(1)} copy(bf16[1024,512]{1,0:T(8,128)(2,1)} %param.18) | data formatting | bytes 2097152 | tf_op jit(solution)/shard_map/optimization_barrier | solution.py:389
  9.7 0.6 collective-permute-start.4
  10.2 0.1 fusion.2
  10.3 0.1 tile.40
  10.4 0.1 tile.42.refs_10_
  10.5 0.1 tile.43
  10.6 0.1 tile.45.refs_11_
  10.7 0.1 stack.27.place
  10.8 0.3 collective-permute-start.2
  11.1 6.3 %collective-permute-done.5 = bf16[16,4096]{1,0:T(8,128)(2,1)S(1)} collective-permute-done((bf16[16,4096]{1,0:T(8,128)(2,1)}, bf16[16,4096]{1,0:T(8,128)(2,1)S(1)}, u32[]{:S(2)}, u32[]{:S(2)}) %collective-permute-start.5) | collective-permute-done | bytes 131104 | tf_op jit(solution)/shard_map/ppermute | solution.py:380
  17.4 0.0 collective-permute-done.6
  17.5 0.0 copy-start
  17.5 0.6 collective-permute-start.7
  18.0 0.0 collective-permute-done.2.refs_3_
  18.1 9.2 %attention.2 = bf16[8,272,128]{2,1,0:T(8,128)(2,1)} custom-call(s32[6]{0:T(128)S(1)} %stack.27.place, bf16[16,4096]{1,0:T(8,128)(2,1)} %refs_0_.1, bf16[16,4096]{1,0:T(8,128)(2,1)S(1)} %collective-permute-done.refs_1_, bf16[16,4096]{1,0:T(8,128)(2,1)S(1)} %collective-permute-done.1.refs_2_, bf16[16,4096]{1,0:T(8,128)(2,1)S(1)} %collective-permute-done.2.refs_3_, ...), custom_call_target="tpu_custom_call" | custom-call | flops 3221225472 | bytes 8388608 | tf_op jit(solution)/shard_map/attention/pallas_call | solution.py:139
  27.2 5.2 %all-to-all-start = ((bf16[8,272,128]{2,1,0:T(8,128)(2,1)}), bf16[8,272,128]{2,1,0:T(8,128)(2,1)S(1)}, u32[]{:S(2)}, u32[]{:S(2)}) async-start(bf16[8,272,128]{2,1,0:T(8,128)(2,1)} %attention.2), calls=%async_computation | async-start | bytes 1114112 | tf_op jit(solution)/shard_map/all_to_all | solution.py:438
  32.4 0.1 tile.46
  32.5 0.1 tile.48.refs_10_
  32.6 0.1 tile.49
  32.6 0.1 tile.51.refs_11_
  32.7 0.1 collective-permute-start.8
  32.8 9.1 %attention.3 = bf16[8,272,128]{2,1,0:T(8,128)(2,1)} custom-call(s32[6]{0:T(128)S(1)} %stack.27.place, bf16[32,4096]{1,0:T(8,128)(2,1)S(1)} %constant_dynamic-update-slice_fusion.refs_0_.refs_1_, bf16[32,4096]{1,0:T(8,128)(2,1)S(1)} %constant_dynamic-update-slice_fusion.refs_0_.refs_1_, bf16[32,4096]{1,0:T(8,128)(2,1)S(1)} %collective-permute-done.7.refs_2_.refs_3_, ...), custom_call_target="tpu_custom_call" | custom-call | flops 3221225472 | bytes 8388608 | tf_op jit(solution)/shard_map/attention/pallas_call | solution.py:139
  42.0 4.2 %all-to-all-done.refs_0_ = bf16[8,272,128]{2,1,0:T(8,128)(2,1)S(1)} async-done(((bf16[8,272,128]{2,1,0:T(8,128)(2,1)}), bf16[8,272,128]{2,1,0:T(8,128)(2,1)S(1)}, u32[]{:S(2)}, u32[]{:S(2)}) %all-to-all-start) | async-done | bytes 557088 | tf_op jit(solution)/shard_map/all_to_all | solution.py:438
  46.2 3.7 %all-to-all-start.1 = ((bf16[8,272,128]{2,1,0:T(8,128)(2,1)}), bf16[8,272,128]{2,1,0:T(8,128)(2,1)S(1)}, u32[]{:S(2)}, u32[]{:S(2)}) async-start(bf16[8,272,128]{2,1,0:T(8,128)(2,1)} %attention.3), calls=%async_computation.1 | async-start | bytes 1114112 | tf_op jit(solution)/shard_map/all_to_all | solution.py:438
  49.9 14.4 %all-to-all-done.1.refs_1_ = bf16[8,272,128]{2,1,0:T(8,128)(2,1)S(1)} async-done(((bf16[8,272,128]{2,1,0:T(8,128)(2,1)}), bf16[8,272,128]{2,1,0:T(8,128)(2,1)S(1)}, u32[]{:S(2)}, u32[]{:S(2)}) %all-to-all-start.1) | async-done | bytes 557088 | tf_op jit(solution)/shard_map/all_to_all | solution.py:438
  64.3 2.8 %project.1 = bf16[128,2048]{1,0:T(8,128)(2,1)} custom-call(s32[6]{0:T(128)S(1)} %stack.27.place, bf16[8,272,128]{2,1,0:T(8,128)(2,1)S(1)} %all-to-all-done.refs_0_, bf16[8,272,128]{2,1,0:T(8,128)(2,1)S(1)} %all-to-all-done.1.refs_1_, bf16[256,2048]{1,0:T(8,128)(2,1)S(1)} %copy-done, bf16[256,2048]{1,0:T(8,128)(2,1)} %collective-permute-done.8.refs_3_), custom_call_target="tpu_custom_call" | custom-call | flops 268435456 | bytes 4194304 | tf_op jit(solution)/shard_map/project/pallas_call | solution.py:213
  67.1 3.6 %all-to-all-start.2 = ((bf16[8,16,2048]{2,1,0:T(8,128)(2,1)}), bf16[8,16,2048]{2,1,0:T(8,128)(2,1)S(1)}, u32[]{:S(2)}, u32[]{:S(2)}) async-start(bf16[8,16,2048]{2,1,0:T(8,128)(2,1)} %bitcast.7), calls=%async_computation.2 | async-start | bytes 1048576 | tf_op jit(solution)/shard_map/all_to_all | solution.py:444
  70.7 0.1 copy.24
  70.8 0.1 eq.31
  70.9 0.2 convert_reduce_fusion
  71.1 0.1 reduce_sum.21
  71.2 0.1 fusion
  71.3 0.1 copy.26
  71.4 13.4 %all-to-all-done.2.parts = bf16[8,16,2048]{2,1,0:T(8,128)(2,1)S(1)} async-done(((bf16[8,16,2048]{2,1,0:T(8,128)(2,1)}), bf16[8,16,2048]{2,1,0:T(8,128)(2,1)S(1)}, u32[]{:S(2)}, u32[]{:S(2)}) %all-to-all-start.2) | async-done | bytes 524320 | tf_op jit(solution)/shard_map/all_to_all | solution.py:444
  84.8 0.4 norm_and_dispatch.1
  85.2 18.0 %all_to_all.25 = bf16[16,8,2048]{2,1,0:T(8,128)(2,1)S(1)} all-to-all(bf16[16,8,2048]{2,1,0:T(8,128)(2,1)S(1)} %bitcast.18), channel_id=1, replica_groups=mesh['groups'=2,'ctx'=16] {'ctx'}, dimensions={0} | all-to-all | bytes 1048576 | tf_op jit(solution)/shard_map/all_to_all | solution.py:453
  103.2 7.9 %experts.1 = bf16[128,2048]{1,0:T(8,128)(2,1)} custom-call(bf16[128,2048]{1,0:T(8,128)(2,1)S(1)} %bitcast.13, bf16[2,2048,768]{2,1,0:T(8,128)(2,1)} %w_gate.1, bf16[2,2048,768]{2,1,0:T(8,128)(2,1)} %w_up.1, bf16[2,768,2048]{2,1,0:T(8,128)(2,1)} %w_down.1), custom_call_target="tpu_custom_call" | custom-call | flops 2415919104 | bytes 18874368 | tf_op jit(solution)/shard_map/experts/pallas_call | solution.py:304
  111.1 4.1 %all-to-all-start.4 = ((bf16[16,8,2048]{2,1,0:T(8,128)(2,1)}), bf16[16,8,2048]{2,1,0:T(8,128)(2,1)S(1)}, u32[]{:S(2)}, u32[]{:S(2)}) async-start(bf16[16,8,2048]{2,1,0:T(8,128)(2,1)} %bitcast.11), calls=%async_computation.4 | async-start | bytes 1048576 | tf_op jit(solution)/shard_map/all_to_all | solution.py:457
  115.2 0.1 copy.27
  115.3 0.1 select_reduce_fusion
  115.4 14.3 %all-to-all-done.4 = bf16[16,8,2048]{2,1,0:T(8,128)(2,1)S(1)} async-done(((bf16[16,8,2048]{2,1,0:T(8,128)(2,1)}), bf16[16,8,2048]{2,1,0:T(8,128)(2,1)S(1)}, u32[]{:S(2)}, u32[]{:S(2)}) %all-to-all-start.4) | async-done | bytes 524320 | tf_op jit(solution)/shard_map/all_to_all | solution.py:457
  129.7 0.9 mix.1
  (27 shorter events, 0.1 us)
Async XLA Ops:
  0.0 8.1 %collective-permute-start.1 = (bf16[16,4096]{1,0:T(8,128)(2,1)}, bf16[16,4096]{1,0:T(8,128)(2,1)S(1)}, u32[]{:S(2)}, u32[]{:S(2)}) collective-permute-start(bf16[16,4096]{1,0:T(8,128)(2,1)} %refs_0_.1), channel_id=1, source_target_pairs={{0,2},{1,3},{2,0},{3,1},{4,6},{5,7},{6,4},{7,5},{8,10},{9,11},{10,... | collective-permute-start | bytes 393224 | tf_op jit(solution)/shard_map/ppermute | solution.py:376
  3.0 7.8 %collective-permute-start = (bf16[16,4096]{1,0:T(8,128)(2,1)}, bf16[16,4096]{1,0:T(8,128)(2,1)S(1)}, u32[]{:S(2)}, u32[]{:S(2)}) collective-permute-start(bf16[16,4096]{1,0:T(8,128)(2,1)} %refs_0_.1), channel_id=1, source_target_pairs={{0,4},{1,5},{2,6},{3,7},{4,0},{5,1},{6,2},{7,3},{8,12},{9,13},{10,... | collective-permute-start | bytes 393224 | tf_op jit(solution)/shard_map/ppermute | solution.py:380
  4.5 12.9 %collective-permute-start.5 = (bf16[16,4096]{1,0:T(8,128)(2,1)}, bf16[16,4096]{1,0:T(8,128)(2,1)S(1)}, u32[]{:S(2)}, u32[]{:S(2)}) collective-permute-start(bf16[16,4096]{1,0:T(8,128)(2,1)} %refs_0_.1), channel_id=1, source_target_pairs={{0,8},{1,9},{2,10},{3,11},{4,12},{5,13},{6,14},{7,15},{8,0},{9,1},... | collective-permute-start | bytes 393224 | tf_op jit(solution)/shard_map/ppermute | solution.py:380
  7.1 10.3 %collective-permute-start.6 = (bf16[16,4096]{1,0:T(8,128)(2,1)}, bf16[16,4096]{1,0:T(8,128)(2,1)S(1)}, u32[]{:S(2)}, u32[]{:S(2)}) collective-permute-start(bf16[16,4096]{1,0:T(8,128)(2,1)} %refs_0_.1), channel_id=1, source_target_pairs={{0,12},{1,13},{2,14},{3,15},{4,8},{5,9},{6,10},{7,11},{8,4},{9,5},... | collective-permute-start | bytes 393224 | tf_op jit(solution)/shard_map/ppermute | solution.py:380
  8.1 9.9 %collective-permute-start.3 = (bf16[1024,512]{1,0:T(8,128)(2,1)}, bf16[1024,512]{1,0:T(8,128)(2,1)}, u32[]{:S(2)}, u32[]{:S(2)}) collective-permute-start(bf16[1024,512]{1,0:T(8,128)(2,1)} %refs_4_.3), channel_id=1, source_target_pairs={{0,1},{1,0},{2,3},{3,2},{4,5},{5,4},{6,7},{7,6},{8,9},{9,8},{10,11... | collective-permute-start | bytes 3145736 | tf_op jit(solution)/shard_map/ppermute | solution.py:390
  9.7 8.4 %collective-permute-start.4 = (bf16[512,1024]{1,0:T(8,128)(2,1)S(1)}, bf16[512,1024]{1,0:T(8,128)(2,1)}, u32[]{:S(2)}, u32[]{:S(2)}) collective-permute-start(bf16[512,1024]{1,0:T(8,128)(2,1)S(1)} %bitcast.15), channel_id=1, source_target_pairs={{0,1},{1,0},{2,3},{3,2},{4,5},{5,4},{6,7},{7,6},{8,9},{9,8},{10,11... | collective-permute-start | bytes 3145736 | tf_op jit(solution)/shard_map/ppermute | solution.py:392
  10.8 7.3 %collective-permute-start.2 = (bf16[16,4096]{1,0:T(8,128)(2,1)S(1)}, bf16[16,4096]{1,0:T(8,128)(2,1)S(1)}, u32[]{:S(2)}, u32[]{:S(2)}) collective-permute-start(bf16[16,4096]{1,0:T(8,128)(2,1)S(1)} %collective-permute-done.refs_1_), channel_id=1, source_target_pairs={{0,2},{1,3},{2,0},{3,1},{4,6},{5,7},{6,4},{7,5},{8,10},{9,11},{10,... | collective-permute-start | bytes 393224 | tf_op jit(solution)/shard_map/ppermute | solution.py:376
  17.5 15.3 %copy-start = (bf16[256,2048]{1,0:T(8,128)(2,1)S(1)}, bf16[256,2048]{1,0:T(8,128)(2,1)}, u32[]{:S(2)}) copy-start(bf16[256,2048]{1,0:T(8,128)(2,1)} %refs_2_.1) | copy-start | bytes 3145732
  17.5 9.7 %collective-permute-start.7 = (bf16[32,4096]{1,0:T(8,128)(2,1)S(1)}, bf16[32,4096]{1,0:T(8,128)(2,1)S(1)}, u32[]{:S(2)}, u32[]{:S(2)}) collective-permute-start(bf16[32,4096]{1,0:T(8,128)(2,1)S(1)} %constant_dynamic-update-slice_fusion.refs_0_.refs_1_), channel_id=1, source_target_pairs={{0,2},{1,3},{2,0},{3,1},{4,6},{5,7},{6,4},{7,5},{8,10},{9,11},{10,... | collective-permute-start | bytes 786440 | tf_op jit(solution)/shard_map/ppermute | solution.py:376
  27.2 19.0 %all-to-all-start = ((bf16[8,272,128]{2,1,0:T(8,128)(2,1)}), bf16[8,272,128]{2,1,0:T(8,128)(2,1)S(1)}, u32[]{:S(2)}, u32[]{:S(2)}) async-start(bf16[8,272,128]{2,1,0:T(8,128)(2,1)} %attention.2), calls=%async_computation | async-start | bytes 1114112 | tf_op jit(solution)/shard_map/all_to_all | solution.py:438
  32.7 38.0 %copy-start.2 = (bf16[2048]{0:T(1024)(128)(2,1)S(1)}, bf16[2048]{0:T(1024)(128)(2,1)}, u32[]{:S(2)}) copy-start(bf16[2048]{0:T(1024)(128)(2,1)} %param.22) | copy-start | bytes 12292
  32.7 38.0 %copy-start.3 = (s32[16,8]{0,1:T(8,128)S(1)}, s32[16,8]{0,1:T(8,128)}, u32[]{:S(2)}) copy-start(s32[16,8]{0,1:T(8,128)} %param.23) | copy-start | bytes 1540
  32.7 52.1 %copy-start.1 = (bf16[16,2048]{1,0:T(8,128)(2,1)S(1)}, bf16[16,2048]{1,0:T(8,128)(2,1)}, u32[]{:S(2)}) copy-start(bf16[16,2048]{1,0:T(8,128)(2,1)} %residual.1) | copy-start | bytes 196612
  32.7 17.1 %collective-permute-start.8 = (bf16[256,2048]{1,0:T(8,128)(2,1)S(1)}, bf16[256,2048]{1,0:T(8,128)(2,1)}, u32[]{:S(2)}, u32[]{:S(2)}) collective-permute-start(bf16[256,2048]{1,0:T(8,128)(2,1)S(1)} %copy-done), channel_id=1, source_target_pairs={{0,1},{1,0},{2,3},{3,2},{4,5},{5,4},{6,7},{7,6},{8,9},{9,8},{10,11... | collective-permute-start | bytes 3145736 | tf_op jit(solution)/shard_map/ppermute | solution.py:442
  46.2 18.1 %all-to-all-start.1 = ((bf16[8,272,128]{2,1,0:T(8,128)(2,1)}), bf16[8,272,128]{2,1,0:T(8,128)(2,1)S(1)}, u32[]{:S(2)}, u32[]{:S(2)}) async-start(bf16[8,272,128]{2,1,0:T(8,128)(2,1)} %attention.3), calls=%async_computation.1 | async-start | bytes 1114112 | tf_op jit(solution)/shard_map/all_to_all | solution.py:438
  67.1 17.7 %all-to-all-start.2 = ((bf16[8,16,2048]{2,1,0:T(8,128)(2,1)}), bf16[8,16,2048]{2,1,0:T(8,128)(2,1)S(1)}, u32[]{:S(2)}, u32[]{:S(2)}) async-start(bf16[8,16,2048]{2,1,0:T(8,128)(2,1)} %bitcast.7), calls=%async_computation.2 | async-start | bytes 1048576 | tf_op jit(solution)/shard_map/all_to_all | solution.py:444
  103.2 12.0 %copy-start.4 = (f32[16,8]{0,1:T(8,128)S(1)}, f32[16,8]{0,1:T(8,128)}, u32[]{:S(2)}) copy-start(f32[16,8]{0,1:T(8,128)} %param.24) | copy-start | bytes 1540
  111.1 18.6 %all-to-all-start.4 = ((bf16[16,8,2048]{2,1,0:T(8,128)(2,1)}), bf16[16,8,2048]{2,1,0:T(8,128)(2,1)S(1)}, u32[]{:S(2)}, u32[]{:S(2)}) async-start(bf16[16,8,2048]{2,1,0:T(8,128)(2,1)} %bitcast.11), calls=%async_computation.4 | async-start | bytes 1048576 | tf_op jit(solution)/shard_map/all_to_all | solution.py:457
